TPU v7x, 512 devices: a whole 4x4x16 slice. The times are simulated.
512 devices in a mesh: dp: 32 (over z_lo, x), tensor: 16 (over y, z_hi, core).
Axes of the slice: x: 4, y: 4, z: 16 (z_hi: 2, z_lo: 8; z = z_hi * 8 + z_lo), core: 2. Of those that a mesh axis runs over, the one named last changes fastest.
Arguments:
- gate_pre: bfloat16 [4096, 14336], P('dp', 'tensor'), may hold values from -6 to 6
- up_pre: bfloat16 [4096, 14336], P('dp', 'tensor'), may hold values from -6 to 6
- weight: bfloat16 [14336, 8192], P('tensor', 'dp'), may hold values from -0.046875 to 0.046875
- basis: bfloat16 [8192, 512], P('dp'), may hold values from -0.0625 to 0.0625
- cotangent: bfloat16 [4096, 8192], P(('dp', 'tensor')), may hold values from -6 to 6
- moment1: float32 [14336, 512], P(('tensor', 'dp')), may hold values from -6 to 6
- moment2: float32 [14336, 512], P(('tensor', 'dp')), may hold values from 0.05 to 2
Outputs:
- layer_out: bfloat16 [4096, 8192], P(('dp', 'tensor'))
- grad_gate: bfloat16 [4096, 14336], P('dp', 'tensor')
- grad_up: bfloat16 [4096, 14336], P('dp', 'tensor')
- moment1_new: float32 [14336, 512], P(('tensor', 'dp'))
- moment2_new: float32 [14336, 512], P(('tensor', 'dp'))
- expansion: float32 [14336, 8192], P('tensor', 'dp')
All inputs are finite; a program needn't handle non-finite values.
Results may differ from a plain program's by a relative error of at most 0.034.
Values may be sent and summed in bfloat16 or wider, within the bound.
No kernel may reach another device: no remote copies, remote signals or barrier semaphores. Data moves between devices by JAX's collectives and lax.ppermute only.
A program may use at most 128 MiB of HBM per device.

v0:
```python
import jax
import jax.numpy as jnp
from jax import lax
from jax.sharding import PartitionSpec as P

corr_first = 1.0 - 0.9**10
corr_second = 1.0 - 0.999**10


def body(gate_pre, up_pre, weight, basis, cotangent, moment1, moment2):
    gate_float = gate_pre.astype(jnp.float32)
    up_float = up_pre.astype(jnp.float32)
    sigmoid_gate = jax.nn.sigmoid(gate_float)
    hidden = (gate_float * sigmoid_gate * up_float).astype(jnp.bfloat16)
    weight_full = lax.all_gather(weight, "dp", axis=1, tiled=True)
    forward_term = jnp.dot(hidden, weight_full, preferred_element_type=jnp.float32)
    layer_out = lax.psum_scatter(
        forward_term.astype(jnp.bfloat16), "tensor", scatter_dimension=0, tiled=True
    )
    basis_full = lax.all_gather(basis, "dp", axis=0, tiled=True)
    cotangent_full = lax.all_gather(cotangent, "tensor", axis=0, tiled=True)
    grad_hidden = lax.dot_general(
        cotangent_full, weight_full, (((1,), (1,)), ((), ())), preferred_element_type=jnp.float32
    )
    grad_up = (grad_hidden * gate_float * sigmoid_gate).astype(jnp.bfloat16)
    grad_gate = (
        grad_hidden * up_float * sigmoid_gate * (1.0 + gate_float * (1.0 - sigmoid_gate))
    ).astype(jnp.bfloat16)
    reduced = jnp.dot(cotangent_full, basis_full, preferred_element_type=jnp.float32).astype(
        jnp.bfloat16
    )
    projected = lax.psum_scatter(
        lax.dot_general(
            hidden, reduced, (((0,), (0,)), ((), ())), preferred_element_type=jnp.float32
        ).astype(jnp.bfloat16),
        "dp",
        scatter_dimension=0,
        tiled=True,
    ).astype(jnp.float32)
    moment1_new = 0.9 * moment1 + 0.1 * projected
    moment2_new = 0.999 * moment2 + 0.001 * projected * projected
    step = (moment1_new / corr_first / (jnp.sqrt(moment2_new / corr_second) + 1e-08)).astype(
        jnp.bfloat16
    )
    step_full = lax.all_gather(step, "dp", axis=0, tiled=True)
    expansion = lax.dot_general(
        step_full, basis, (((1,), (1,)), ((), ())), preferred_element_type=jnp.float32
    )
    return (layer_out, grad_gate, grad_up, moment1_new, moment2_new, expansion)


def solution(mesh):
    placed = (
        P("dp", "tensor"),
        P("dp", "tensor"),
        P("tensor", "dp"),
        P("dp", None),
        P(("dp", "tensor"), None),
        P(("tensor", "dp"), None),
        P(("tensor", "dp"), None),
    )
    return jax.shard_map(
        body,
        mesh=mesh,
        in_specs=placed,
        out_specs=(
            P(("dp", "tensor"), None),
            P("dp", "tensor"),
            P("dp", "tensor"),
            P(("tensor", "dp"), None),
            P(("tensor", "dp"), None),
            P("tensor", "dp"),
        ),
        check_vma=False,
    )
```

profile of v0, /device:TPU:24, one launch (start us, length us, event | category | flops | bytes accessed | tf_op | source)
XLA Modules:
  0.0 882.1 jit_solution(13198256765409054352)
XLA Ops:
  7.2 0.0 all-gather.5.cloned.1.call-start
  7.2 0.7 all-gather.5.cloned.1.call-update
  7.9 0.0 all-gather.7.cloned.1.call-start
  7.9 0.7 all-gather.7.cloned.1.call-update
  8.6 0.0 all-gather.9.cloned.1.call-start
  8.7 0.7 all-gather.9.cloned.1.call-update
  9.4 0.0 reduce-scatter.4.cloned.1.call-start
  9.5 254.6 %all-gather.5.cloned.1.call-done = bf16[896,8192]{1,0:T(8,128)(2,1)} async-done(((bf16[896,256]{1,0:T(8,128)(2,1)}), bf16[896,8192]{1,0:T(8,128)(2,1)}) %all-gather.5.cloned.1.call-update) | async-done | bytes 14680080 | tf_op jit(solution)/shard_map/all_gather | solution.py:15
  264.0 9.2 %convolution_convert_fusion = bf16[128,8192]{1,0:T(8,128)(2,1)} fusion(bf16[896,8192]{1,0:T(8,128)(2,1)} %all-gather.5.cloned.1.call-done, bf16[128,896]{1,0:T(8,128)(2,1)} %param.8, bf16[128,896]{1,0:T(8,128)(2,1)} %param.7), kind=kOutput, calls=%fused_computation | convolution fusion | flops 1881014272 | bytes 17235968 | tf_op jit(solution)/shard_map/dot_general | solution.py:16
  273.3 82.9 %all-gather.7.cloned.1.call-done = bf16[128,8192]{1,0:T(8,128)(2,1)} async-done(((bf16[8,8192]{1,0:T(8,128)(2,1)}), bf16[128,8192]{1,0:T(8,128)(2,1)}) %all-gather.7.cloned.1.call-update) | async-done | bytes 2097168 | tf_op jit(solution)/shard_map/all_gather | solution.py:21
  356.2 230.1 %all-gather.9.cloned.1.call-done = bf16[8192,512]{1,0:T(8,128)(2,1)} async-done(((bf16[256,512]{1,0:T(8,128)(2,1)}), bf16[8192,512]{1,0:T(8,128)(2,1)}) %all-gather.9.cloned.1.call-update) | async-done | bytes 8388624 | tf_op jit(solution)/shard_map/all_gather | solution.py:20
  586.3 5.7 convolution_convert_fusion.1
  592.0 138.3 %fusion = bf16[32,512]{1,0:T(8,128)(2,1)S(1)} fusion(bf16[896,512]{1,0:T(8,128)(2,1)S(1)} %convolution_convert_fusion.1), kind=kCustom, calls=%all-reduce-scatter | all-reduce-scatter fusion | flops 524289 | bytes 952320
  730.3 1.3 collective-permute-start.2
  731.6 1.3 collective-permute-start.1
  732.9 1.3 collective-permute-start
  734.2 1.3 collective-permute-start.3
  735.5 1.3 dynamic-slice.4
  737.5 0.6 concatenate
  738.1 0.7 fusion.13
  738.8 123.8 %all-gather = bf16[32,28,512]{2,1,0:T(8,128)(2,1)S(1)} all-gather(bf16[1,28,512]{2,1,0:T(8,128)(2,1)S(1)} %get-tuple-element.6), channel_id=1, replica_groups=mesh['dp'=32,'tensor'=16] {'dp'}, dimensions={0}, use_global_device_ids=true | all-gather | bytes 946176 | tf_op jit(solution)/shard_map/all_gather | solution.py:45
  862.6 0.2 reshape.13
  862.8 1.4 fusion.18
  864.2 11.3 %fusion.10 = (bf16[128,896]{1,0:T(8,128)(2,1)}, bf16[128,896]{1,0:T(8,128)(2,1)}) fusion(bf16[128,896]{1,0:T(8,128)(2,1)S(1)} %copy-done.2, bf16[128,896]{1,0:T(8,128)(2,1)S(1)} %copy-done.1, bf16[128,8192]{1,0:T(8,128)(2,1)} %all-gather.7.cloned.1.call-done, bf16[896,8192]{1,0:T(8,128)(2,1)} %all-gather.5.cloned.1.call-done), kind=kOutput, calls=%fused_computation.18 | convolution fusion | flops 1880768512 | bytes 17694720 | tf_op jit(solution)/shard_map/dot_general | solution.py:22
  (17 shorter events, 0.1 us)
Async XLA Ops:
  7.2 256.9 %all-gather.5.cloned.1.call-start = ((), (), s32[]{:S(2)}) async-start(), calls=%async_computation.1 | async-start | bytes 15138816 | tf_op jit(solution)/shard_map/all_gather | solution.py:15
  7.9 348.3 %all-gather.7.cloned.1.call-start = ((), (), s32[]{:S(2)}) async-start(), calls=%async_computation.3 | async-start | bytes 2228224 | tf_op jit(solution)/shard_map/all_gather | solution.py:21
  8.6 577.7 %all-gather.9.cloned.1.call-start = ((), (), s32[]{:S(2)}) async-start(), calls=%async_computation.4 | async-start | bytes 8650752 | tf_op jit(solution)/shard_map/all_gather | solution.py:20
  9.4 576.9 %copy-start.1 = (bf16[128,896]{1,0:T(8,128)(2,1)S(1)}, bf16[128,896]{1,0:T(8,128)(2,1)}, u32[]{:S(2)}) copy-start(bf16[128,896]{1,0:T(8,128)(2,1)} %param.8) | copy-start | bytes 688132
  9.4 576.9 %copy-start.2 = (bf16[128,896]{1,0:T(8,128)(2,1)S(1)}, bf16[128,896]{1,0:T(8,128)(2,1)}, u32[]{:S(2)}) copy-start(bf16[128,896]{1,0:T(8,128)(2,1)} %param.7) | copy-start | bytes 688132
  9.4 866.1 %reduce-scatter.4.cloned.1.call-start = ((), (), s32[]{:S(2)}) async-start(), calls=%async_computation.2 | async-start | bytes 2228224 | tf_op jit(solution)/shard_map/reduce_scatter | solution.py:17
  273.2 464.9 %copy-start.3 = (f32[28,512]{1,0:T(8,128)S(1)}, f32[28,512]{1,0:T(8,128)}, u32[]{:S(2)}) copy-start(f32[28,512]{1,0:T(8,128)} %param.13) | copy-start | bytes 172036
  273.2 464.9 %copy-start.4 = (f32[28,512]{1,0:T(8,128)S(1)}, f32[28,512]{1,0:T(8,128)}, u32[]{:S(2)}) copy-start(f32[28,512]{1,0:T(8,128)} %param.12) | copy-start | bytes 172036
  273.3 589.5 %copy-start = (bf16[256,512]{1,0:T(8,128)(2,1)S(1)}, bf16[256,512]{1,0:T(8,128)(2,1)}, u32[]{:S(2)}) copy-start(bf16[256,512]{1,0:T(8,128)(2,1)} %param.10) | copy-start | bytes 786436
  730.3 7.2 collective-permute-start.2
  731.6 5.9 collective-permute-start.1
  732.9 4.6 collective-permute-start
  734.2 3.2 collective-permute-start.3
Sparse Core Ops, SparseCore 0:
  10.0 253.9 all-gather.4
  267.3 88.8 all-gather.6
  358.3 227.9 all-gather.8
  591.5 122.1 reduce-scatter.3
where the time goes:
time: 882 us
  waiting for transfers between devices  570 us (65%)
  blocking collectives  262 us (30%)
  matrix products  27.6 us (3%)
  between operations  14.6 us (2%)
    all_gather x1, waiting for transfers between devices, body(): weight_full = lax.all_gather(weight, 'dp', axis=1, tiled=True)  255 us
    all_gather x1, waiting for transfers between devices, body(): basis_full = lax.all_gather(basis, 'dp', axis=0, tiled=True)  230 us
    unnamed x1, blocking collectives  138 us
    all_gather x1, blocking collectives, body(): step_full = lax.all_gather(step, 'dp', axis=0, tiled=True)  124 us
    all_gather x1, waiting for transfers between devices, body(): cotangent_full = lax.all_gather(cotangent, 'tensor', axis=0, tiled=True)  82.9 us
  transfers between devices with their start and end apart: 8, of which 3 were waited for; matrix products, arithmetic and copies ran while one was open for 19% of the time, Pallas kernels for 0%

commit v1 on v0

v1 whole, which is shorter than its diff:
```python
import jax
import jax.numpy as jnp
from jax import lax
from jax.sharding import Mesh, PartitionSpec as P

corr_first = 1.0 - 0.9**10
corr_second = 1.0 - 0.999**10

NZ, NX, NY, NH, NC = 8, 4, 4, 2, 2
ORDER = (0, 2, 4, 6, 7, 5, 3, 1)
PLACE = tuple(ORDER.index(i) for i in range(NZ))
RING = [(ORDER[i], ORDER[(i + 1) % NZ]) for i in range(NZ)]
bf16, f32 = jnp.bfloat16, jnp.float32


def shift(value, axis, size, by):
    return lax.ppermute(value, axis, [(i, (i + by) % size) for i in range(size)])


def dot(a, b, contract):
    return lax.dot_general(a, b, (contract, ((), ())), preferred_element_type=f32)


def gather_ring(value, axis, size):
    index = lax.axis_index(axis)
    parts = jnp.zeros((size,) + value.shape, value.dtype)
    parts = lax.dynamic_update_index_in_dim(parts, value, index, 0)
    for by in range(1, size):
        arrived = shift(value, axis, size, by)
        parts = lax.dynamic_update_index_in_dim(parts, arrived, (index - by) % size, 0)
    return parts


def scatter_sum(parts, axis, size):
    index = lax.axis_index(axis)
    total = lax.dynamic_index_in_dim(parts, index, 0, keepdims=False).astype(f32)
    for by in range(1, size):
        piece = lax.dynamic_index_in_dim(parts, (index + by) % size, 0, keepdims=False)
        total = total + shift(piece, axis, size, by).astype(f32)
    return total


def body(gate_pre, up_pre, weight, basis, cotangent, moment1, moment2):
    zl = lax.axis_index("zl")
    order = jnp.asarray(ORDER, jnp.int32)
    place = jnp.asarray(PLACE, jnp.int32)[zl]

    gate = gate_pre.astype(f32)
    up = up_pre.astype(f32)
    sig = jax.nn.sigmoid(gate)
    hidden = (gate * sig * up).astype(bf16)
    rows, ff = hidden.shape
    mine, width = cotangent.shape
    cols = width // NZ
    rank = basis.shape[1]

    parts = cotangent.reshape(mine, NZ, cols).transpose(1, 0, 2)
    parts = jnp.broadcast_to(parts[:, None], (NZ, NH, mine, cols)).reshape(NZ * NH, mine, cols)
    got = lax.all_to_all(parts, ("zl", "zh"), 0, 0, tiled=True)
    got = gather_ring(got, "y", NY)
    other = shift(got, "c", NC, 1)
    low = lax.axis_index("c") == 0
    pair = jnp.stack([jnp.where(low, got, other), jnp.where(low, other, got)])
    cot = pair.reshape(NC, NY, NZ, NH, mine, cols).transpose(2, 1, 3, 0, 4, 5)
    cot = cot.reshape(NZ * rows, cols)

    weight_tile = gather_ring(weight, "x", NX)
    weight_tile = weight_tile.transpose(1, 0, 2).reshape(ff, cols)
    basis_tile = gather_ring(basis, "x", NX).reshape(cols, rank)

    tile = jnp.zeros((NZ, rows, ff), bf16)
    tile = lax.dynamic_update_index_in_dim(tile, hidden, zl, 0)
    moving = hidden
    for hop in range(1, NZ):
        moving = lax.ppermute(moving, "zl", RING)
        tile = lax.dynamic_update_index_in_dim(tile, moving, order[(place - hop) % NZ], 0)
    tile = tile.reshape(NZ * rows, ff)

    reduced = dot(cot, basis_tile, ((1,), (0,))).astype(bf16)
    projected = dot(tile, reduced, ((0,), (0,))).astype(bf16)
    own = moment1.shape[0]
    projected = projected.reshape(NZ, NX, own, rank).transpose(1, 0, 2, 3)
    projected = scatter_sum(projected, "x", NX).astype(bf16)
    projected = lax.all_to_all(projected, "zl", 0, 0, tiled=True).astype(f32).sum(0)
    moment1_new = 0.9 * moment1 + 0.1 * projected
    moment2_new = 0.999 * moment2 + 0.001 * projected * projected
    step = (moment1_new / corr_first / (jnp.sqrt(moment2_new / corr_second) + 1e-08)).astype(bf16)
    steps = lax.all_to_all(
        jnp.broadcast_to(step[None], (NZ, own, rank)), "zl", 0, 0, tiled=True
    )
    steps = gather_ring(steps, "x", NX).transpose(1, 0, 2, 3).reshape(ff, rank)
    expansion = dot(steps, basis, ((1,), (1,)))

    partial = dot(cot, weight_tile, ((1,), (1,))).reshape(NZ, rows, ff)
    sums = []
    half = rows // 2
    for part in range(2):
        lines = partial[:, part * half : (part + 1) * half]
        total = lax.dynamic_index_in_dim(lines, order[(place - 1) % NZ], 0, keepdims=False)
        for hop in range(NZ - 1):
            arrived = lax.ppermute(total.astype(bf16), "zl", RING)
            total = arrived.astype(f32) + lax.dynamic_index_in_dim(
                lines, order[(place - 2 - hop) % NZ], 0, keepdims=False
            )
        sums.append(total)
    grad_hidden = jnp.concatenate(sums, 0)
    grad_up = (grad_hidden * gate * sig).astype(bf16)
    grad_gate = (grad_hidden * up * sig * (1.0 + gate * (1.0 - sig))).astype(bf16)

    term = dot(tile, weight_tile, ((1,), (0,))).astype(bf16)
    term = term.reshape(NZ, NY, NH, NC, mine, cols).transpose(3, 1, 0, 2, 4, 5)
    term = scatter_sum(term, "c", NC).astype(bf16)
    term = scatter_sum(term, "y", NY).astype(bf16)
    term = lax.all_to_all(term.reshape(NZ * NH, mine, cols), ("zl", "zh"), 0, 0, tiled=True)
    term = term.reshape(NZ, NH, mine, cols).astype(f32).sum(1).astype(bf16)
    layer_out = term.transpose(1, 0, 2).reshape(mine, width)
    return (layer_out, grad_gate, grad_up, moment1_new, moment2_new, expansion)


def solution(mesh):
    fine = Mesh(mesh.devices.reshape(NZ, NX, NY, NH, NC), ("zl", "x", "y", "zh", "c"))
    dp, tensor = ("zl", "x"), ("y", "zh", "c")
    placed = (
        P(dp, tensor),
        P(dp, tensor),
        P(tensor, dp),
        P(dp, None),
        P(dp + tensor, None),
        P(tensor + dp, None),
        P(tensor + dp, None),
    )
    return jax.shard_map(
        body,
        mesh=fine,
        in_specs=placed,
        out_specs=(
            P(dp + tensor, None),
            P(dp, tensor),
            P(dp, tensor),
            P(tensor + dp, None),
            P(tensor + dp, None),
            P(tensor, dp),
        ),
        check_vma=False,
    )
```

time: 882 us -> 373 us (0.42)
  waiting for transfers between devices: 570 us -> 33.1 us
  blocking collectives: 262 us -> 0 us
  starting transfers between devices: 5.32 us -> 199 us
  local copies, waits for them, and re-layouts: 2.11 us -> 80.7 us
  other arithmetic: 0.7 us -> 20.4 us
  matrix products: 27.6 us -> 13.1 us
    all_gather x3 -> x0, waiting for transfers between devices: 568 us -> none  [the longest x1 255 us: body(): weight_full = lax.all_gather(weight, 'dp', axis=1, tiled=True)]
    ppermute x0 -> x41, starting transfers between devices: none -> 164 us  [the longest x20 63.3 us: shift(): lax.ppermute(value, axis, [(i, (i + by) % size) for i in range(size)])]
    unnamed x1 -> x0, blocking collectives: 138 us -> none
    all_gather x1 -> x0, blocking collectives: 124 us -> none  [body(): step_full = lax.all_gather(step, 'dp', axis=0, tiled=True)]
    dynamic_update_slice x0 -> x24, local copies, waits for them, and re-layouts: none -> 54.8 us  [the longest x12 43.3 us: gather_ring(): lax.dynamic_update_index_in_dim(parts, arrived, (index - by) % size, 0)]
    all_to_all x0 -> x4, starting transfers between devices: none -> 35.4 us  [the longest x1 13.4 us: body(): got = lax.all_to_all(parts, ('zl', 'zh'), 0, 0, tiled=True)]
    ppermute x0 -> x41, waiting for transfers between devices: none -> 22.9 us  [the longest x20 11.4 us: shift(): lax.ppermute(value, axis, [(i, (i + by) % size) for i in range(size)])]
    convert_element_type x0 -> x17, other arithmetic: none -> 16.4 us  [the longest x12 10.2 us: body(): arrived = lax.ppermute(total.astype(bf16), 'zl', RING)]
  transfers between devices with their start and end apart: 8 -> 45, of which waited for: 3 -> 12; matrix products, arithmetic and copies ran while one was open for 19% -> 29% of each run, Pallas kernels for 0% -> 0%
where the time goes in v1:
time: 373 us; the launch traced here: 369 us
  starting transfers between devices  199 us (53%)
  local copies, waits for them, and re-layouts  80.7 us (22%)
  waiting for transfers between devices  33.1 us (9%)
  between operations  22.2 us (6%)
  other arithmetic  20.4 us (5%)
  matrix products  13.1 us (4%)
    ppermute x20, starting transfers between devices, shift(): lax.ppermute(value, axis, [(i, (i + by) % size) for i in range(size)])  63.3 us
    ppermute x14, starting transfers between devices, body(): arrived = lax.ppermute(total.astype(bf16), 'zl', RING)  61.6 us
    dynamic_update_slice x12, local copies, waits for them, and re-layouts, gather_ring(): lax.dynamic_update_index_in_dim(parts, arrived, (index - by) % size, 0)  43.3 us
    ppermute x7, starting transfers between devices, body(): moving = lax.ppermute(moving, 'zl', RING)  38.8 us
    all_to_all x1, starting transfers between devices, body(): got = lax.all_to_all(parts, ('zl', 'zh'), 0, 0, tiled=True)  13.4 us
    dot_general x4, matrix products, dot(): lax.dot_general(a, b, (contract, ((), ())), preferred_element_type=f32)  13.1 us
    ppermute x20, waiting for transfers between devices, shift(): lax.ppermute(value, axis, [(i, (i + by) % size) for i in range(size)])  11.4 us
    ppermute x7, waiting for transfers between devices, body(): moving = lax.ppermute(moving, 'zl', RING)  10.4 us
  transfers between devices with their start and end apart: 45, of which 12 were waited for; matrix products, arithmetic and copies ran while one was open for 29% of the time, Pallas kernels for 0%

profile of v1, /device:TPU:24, one launch (start us, length us, event | category | flops | bytes accessed | tf_op | source)
XLA Modules:
  0.0 368.7 jit_solution(11603156223391037234)
XLA Ops:
  14.7 5.1 %collective-permute-start = (bf16[128,896]{1,0:T(8,128)(2,1)}, bf16[128,896]{1,0:T(8,128)(2,1)}, u32[]{:S(2)}, u32[]{:S(2)}) collective-permute-start(bf16[128,896]{1,0:T(8,128)(2,1)} %get-tuple-element.10), channel_id=1, source_target_pairs={{0,128},{128,256},{256,384},{384,448},{448,320},{320,192},{192,64}... | collective-permute-start | bytes 688136 | tf_op jit(solution)/shard_map/ppermute | solution.py:75
  20.6 13.4 %all-to-all-start.1 = ((bf16[16,8,1024]{2,1,0:T(8,128)(2,1)}), bf16[16,8,1024]{2,1,0:T(8,128)(2,1)S(1)}, u32[]{:S(2)}, u32[]{:S(2)}) async-start(bf16[16,8,1024]{2,1,0:T(8,128)(2,1)} %bitcast.43), calls=%async_computation.1 | async-start | bytes 524288 | tf_op jit(solution)/shard_map/all_to_all | solution.py:59
  89.3 11.7 %dynamic_update_slice.86 = bf16[4,896,256]{2,0,1:T(4,128)(2,1)S(1)} dynamic-update-slice(bf16[4,896,256]{2,0,1:T(4,128)(2,1)S(1)} %copy.29, bf16[1,896,256]{2,0,1:T(2,128)(2,1)S(1)} %copy.30, s32[]{:T(128)S(6)} %select_n.314, s32[]{:T(128)} %constant.345.clone.1, s32[]{:T(128)} %constant.345.clone.1) | dynamic-update-slice | bytes 917508 | tf_op jit(solution)/shard_map/jit(dynamic_update_index_in_dim)/dynamic_update_slice | solution.py:30
  101.0 16.7 %dynamic_update_slice.87 = bf16[4,896,256]{2,0,1:T(4,128)(2,1)S(1)} dynamic-update-slice(bf16[4,896,256]{2,0,1:T(4,128)(2,1)S(1)} %dynamic_update_slice.86, bf16[1,896,256]{2,0,1:T(2,128)(2,1)} %copy.31, s32[]{:T(128)S(6)} %select_n.316, s32[]{:T(128)} %constant.345.clone.1, s32[]{:T(128)} %constant.345.clone.1) | dynamic-update-slice | bytes 917508 | tf_op jit(solution)/shard_map/jit(dynamic_update_index_in_dim)/dynamic_update_slice | solution.py:30
  117.7 11.7 %dynamic_update_slice.88 = bf16[4,896,256]{2,0,1:T(4,128)(2,1)S(1)} dynamic-update-slice(bf16[4,896,256]{2,0,1:T(4,128)(2,1)S(1)} %dynamic_update_slice.87, bf16[1,896,256]{2,0,1:T(2,128)(2,1)S(1)} %copy-done.1, s32[]{:T(128)S(6)} %select_n.318, s32[]{:T(128)} %constant.345.clone.1, s32[]{:T(128)} %constant.345.clone.1) | dynamic-update-slice | bytes 917508 | tf_op jit(solution)/shard_map/jit(dynamic_update_index_in_dim)/dynamic_update_slice | solution.py:30
  133.4 5.4 %collective-permute-start.2 = (bf16[128,896]{1,0:T(8,128)(2,1)}, bf16[128,896]{1,0:T(8,128)(2,1)S(1)}, u32[]{:S(2)}, u32[]{:S(2)}) collective-permute-start(bf16[128,896]{1,0:T(8,128)(2,1)} %collective-permute-done.1), channel_id=1, source_target_pairs={{0,128},{128,256},{256,384},{384,448},{448,320},{320,192},{192,64}... | collective-permute-start | bytes 688136 | tf_op jit(solution)/shard_map/ppermute | solution.py:75
  142.6 5.2 %collective-permute-start.3 = (bf16[128,896]{1,0:T(8,128)(2,1)S(1)}, bf16[128,896]{1,0:T(8,128)(2,1)S(1)}, u32[]{:S(2)}, u32[]{:S(2)}) collective-permute-start(bf16[128,896]{1,0:T(8,128)(2,1)S(1)} %collective-permute-done.2), channel_id=1, source_target_pairs={{0,128},{128,256},{256,384},{384,448},{448,320},{320,192},{192,64}... | collective-permute-start | bytes 688136 | tf_op jit(solution)/shard_map/ppermute | solution.py:75
  151.3 6.0 %collective-permute-start.4 = (bf16[128,896]{1,0:T(8,128)(2,1)S(1)}, bf16[128,896]{1,0:T(8,128)(2,1)S(1)}, u32[]{:S(2)}, u32[]{:S(2)}) collective-permute-start(bf16[128,896]{1,0:T(8,128)(2,1)S(1)} %collective-permute-done.3), channel_id=1, source_target_pairs={{0,128},{128,256},{256,384},{384,448},{448,320},{320,192},{192,64}... | collective-permute-start | bytes 688136 | tf_op jit(solution)/shard_map/ppermute | solution.py:75
  166.8 6.7 %collective-permute-start.5 = (bf16[128,896]{1,0:T(8,128)(2,1)S(1)}, bf16[128,896]{1,0:T(8,128)(2,1)S(1)}, u32[]{:S(2)}, u32[]{:S(2)}) collective-permute-start(bf16[128,896]{1,0:T(8,128)(2,1)S(1)} %collective-permute-done.4), channel_id=1, source_target_pairs={{0,128},{128,256},{256,384},{384,448},{448,320},{320,192},{192,64}... | collective-permute-start | bytes 688136 | tf_op jit(solution)/shard_map/ppermute | solution.py:75
  177.0 5.7 %collective-permute-start.6 = (bf16[128,896]{1,0:T(8,128)(2,1)S(1)}, bf16[128,896]{1,0:T(8,128)(2,1)S(1)}, u32[]{:S(2)}, u32[]{:S(2)}) collective-permute-start(bf16[128,896]{1,0:T(8,128)(2,1)S(1)} %collective-permute-done.5), channel_id=1, source_target_pairs={{0,128},{128,256},{256,384},{384,448},{448,320},{320,192},{192,64}... | collective-permute-start | bytes 688136 | tf_op jit(solution)/shard_map/ppermute | solution.py:75
  203.2 5.3 %collective-permute-start.25 = (bf16[64,896]{1,0:T(8,128)(2,1)}, bf16[64,896]{1,0:T(8,128)(2,1)}, u32[]{:S(2)}, u32[]{:S(2)}) collective-permute-start(bf16[64,896]{1,0:T(8,128)(2,1)} %fusion.30), channel_id=1, source_target_pairs={{0,128},{128,256},{256,384},{384,448},{448,320},{320,192},{192,64}... | collective-permute-start | bytes 344072 | tf_op jit(solution)/shard_map/ppermute | solution.py:101
  212.0 5.5 %convolution_convert_fusion.2 = bf16[896,512]{1,0:T(8,128)(2,1)} fusion(bf16[1024,896]{1,0:T(8,128)(2,1)} %bitcast.22, bf16[1024,1024]{1,0:T(8,128)(2,1)} %bitcast.193, bf16[1024,512]{1,0:T(8,128)(2,1)} %bitcast.75), kind=kOutput, calls=%fused_computation.5 | convolution fusion | flops 2014248960 | bytes 5898240 | tf_op jit(solution)/shard_map/dot_general | solution.py:21
  218.8 6.4 %collective-permute-start.37 = (bf16[8,28,512]{2,1,0:T(8,128)(2,1)S(1)}, bf16[8,28,512]{2,1,0:T(8,128)(2,1)S(1)}, u32[]{:S(2)}, u32[]{:S(2)}) collective-permute-start(bf16[8,28,512]{2,1,0:T(8,128)(2,1)S(1)} %get-tuple-element.16), channel_id=1, source_target_pairs={{0,48},{16,0},{32,16},{48,32},{1,49},{17,1},{33,17},{49,33},{2,50}... | collective-permute-start | bytes 688136 | tf_op jit(solution)/shard_map/ppermute | solution.py:17
  253.1 5.5 %collective-permute-start.20 = (bf16[64,896]{1,0:T(8,128)(2,1)S(1)}, bf16[64,896]{1,0:T(8,128)(2,1)S(1)}, u32[]{:S(2)}, u32[]{:S(2)}) collective-permute-start(bf16[64,896]{1,0:T(8,128)(2,1)S(1)} %fusion.27), channel_id=1, source_target_pairs={{0,128},{128,256},{256,384},{384,448},{448,320},{320,192},{192,64}... | collective-permute-start | bytes 344072 | tf_op jit(solution)/shard_map/ppermute | solution.py:101
  259.6 5.7 %collective-permute-start.28 = (bf16[64,896]{1,0:T(8,128)(2,1)S(1)}, bf16[64,896]{1,0:T(8,128)(2,1)S(1)}, u32[]{:S(2)}, u32[]{:S(2)}) collective-permute-start(bf16[64,896]{1,0:T(8,128)(2,1)S(1)} %fusion.20), channel_id=1, source_target_pairs={{0,128},{128,256},{256,384},{384,448},{448,320},{320,192},{192,64}... | collective-permute-start | bytes 344072 | tf_op jit(solution)/shard_map/ppermute | solution.py:101
  265.3 6.5 %collective-permute-start.21 = (bf16[64,896]{1,0:T(8,128)(2,1)S(1)}, bf16[64,896]{1,0:T(8,128)(2,1)S(1)}, u32[]{:S(2)}, u32[]{:S(2)}) collective-permute-start(bf16[64,896]{1,0:T(8,128)(2,1)S(1)} %fusion.26), channel_id=1, source_target_pairs={{0,128},{128,256},{256,384},{384,448},{448,320},{320,192},{192,64}... | collective-permute-start | bytes 344072 | tf_op jit(solution)/shard_map/ppermute | solution.py:101
  275.8 5.1 %collective-permute-start.12 = (bf16[8,2,8,1024]{3,2,1,0:T(8,128)(2,1)S(1)}, bf16[8,2,8,1024]{3,2,1,0:T(8,128)(2,1)S(1)}, u32[]{:S(2)}, u32[]{:S(2)}) collective-permute-start(bf16[8,2,8,1024]{3,2,1,0:T(8,128)(2,1)S(1)} %get-tuple-element.20), channel_id=1, source_target_pairs={{0,8},{4,12},{8,0},{12,4},{1,9},{5,13},{9,1},{13,5},{2,10},{6,14},... | collective-permute-start | bytes 786440 | tf_op jit(solution)/shard_map/ppermute | solution.py:17
  293.6 5.1 %collective-permute-start.30 = (bf16[64,896]{1,0:T(8,128)(2,1)}, bf16[64,896]{1,0:T(8,128)(2,1)}, u32[]{:S(2)}, u32[]{:S(2)}) collective-permute-start(bf16[64,896]{1,0:T(8,128)(2,1)} %fusion.18), channel_id=1, source_target_pairs={{0,128},{128,256},{256,384},{384,448},{448,320},{320,192},{192,64}... | collective-permute-start | bytes 344072 | tf_op jit(solution)/shard_map/ppermute | solution.py:101
  299.7 9.7 %all-to-all-start = ((bf16[16,8,1024]{2,1,0:T(8,128)(2,1)}), bf16[16,8,1024]{2,1,0:T(8,128)(2,1)S(1)}, u32[]{:S(2)}, u32[]{:S(2)}) async-start(bf16[16,8,1024]{2,1,0:T(8,128)(2,1)} %bitcast.37), calls=%async_computation | async-start | bytes 524288 | tf_op jit(solution)/shard_map/all_to_all | solution.py:114
  310.3 4.9 %collective-permute-start.23 = (bf16[64,896]{1,0:T(8,128)(2,1)S(1)}, bf16[64,896]{1,0:T(8,128)(2,1)S(1)}, u32[]{:S(2)}, u32[]{:S(2)}) collective-permute-start(bf16[64,896]{1,0:T(8,128)(2,1)S(1)} %fusion.24), channel_id=1, source_target_pairs={{0,128},{128,256},{256,384},{384,448},{448,320},{320,192},{192,64}... | collective-permute-start | bytes 344072 | tf_op jit(solution)/shard_map/ppermute | solution.py:101
  316.2 5.5 %collective-permute-start.31 = (bf16[64,896]{1,0:T(8,128)(2,1)S(1)}, bf16[64,896]{1,0:T(8,128)(2,1)}, u32[]{:S(2)}, u32[]{:S(2)}) collective-permute-start(bf16[64,896]{1,0:T(8,128)(2,1)S(1)} %fusion.17), channel_id=1, source_target_pairs={{0,128},{128,256},{256,384},{384,448},{448,320},{320,192},{192,64}... | collective-permute-start | bytes 344072 | tf_op jit(solution)/shard_map/ppermute | solution.py:101
  321.8 5.2 %collective-permute-start.24 = (bf16[64,896]{1,0:T(8,128)(2,1)S(1)}, bf16[64,896]{1,0:T(8,128)(2,1)}, u32[]{:S(2)}, u32[]{:S(2)}) collective-permute-start(bf16[64,896]{1,0:T(8,128)(2,1)S(1)} %fusion.23), channel_id=1, source_target_pairs={{0,128},{128,256},{256,384},{384,448},{448,320},{320,192},{192,64}... | collective-permute-start | bytes 344072 | tf_op jit(solution)/shard_map/ppermute | solution.py:101
  330.1 8.9 %all-to-all-start.3 = ((bf16[8,28,512]{2,1,0:T(8,128)(2,1)}), bf16[8,28,512]{2,1,0:T(8,128)(2,1)S(1)}, u32[]{:S(2)}, u32[]{:S(2)}) async-start(bf16[8,28,512]{2,1,0:T(8,128)(2,1)} %broadcast_in_dim.130), calls=%async_computation.3 | async-start | bytes 524288 | tf_op jit(solution)/shard_map/all_to_all | solution.py:88
  342.7 9.3 %all-to-all-done.3 = bf16[8,28,512]{2,1,0:T(8,128)(2,1)S(1)} async-done(((bf16[8,28,512]{2,1,0:T(8,128)(2,1)}), bf16[8,28,512]{2,1,0:T(8,128)(2,1)S(1)}, u32[]{:S(2)}, u32[]{:S(2)}) %all-to-all-start.3) | async-done | bytes 229408 | tf_op jit(solution)/shard_map/all_to_all | solution.py:88
  (171 shorter events, 170.3 us)
Async XLA Ops:
  0.7 80.7 %collective-permute-start.7 = (bf16[896,256]{1,0:T(8,128)(2,1)}, bf16[896,256]{1,0:T(8,128)(2,1)S(1)}, u32[]{:S(2)}, u32[]{:S(2)}) collective-permute-start(bf16[896,256]{1,0:T(8,128)(2,1)} %param.11), channel_id=1, source_target_pairs={{0,16},{16,32},{32,48},{48,0},{1,17},{17,33},{33,49},{49,1},{2,18}... | collective-permute-start | bytes 1376264 | tf_op jit(solution)/shard_map/ppermute | solution.py:17
  4.2 79.7 %collective-permute-start.8 = (bf16[896,256]{1,0:T(8,128)(2,1)}, bf16[896,256]{1,0:T(8,128)(2,1)}, u32[]{:S(2)}, u32[]{:S(2)}) collective-permute-start(bf16[896,256]{1,0:T(8,128)(2,1)} %param.11), channel_id=1, source_target_pairs={{0,32},{16,48},{32,0},{48,16},{1,33},{17,49},{33,1},{49,17},{2,34}... | collective-permute-start | bytes 1376264 | tf_op jit(solution)/shard_map/ppermute | solution.py:17
  8.9 77.7 %collective-permute-start.9 = (bf16[896,256]{1,0:T(8,128)(2,1)}, bf16[896,256]{1,0:T(8,128)(2,1)}, u32[]{:S(2)}, u32[]{:S(2)}) collective-permute-start(bf16[896,256]{1,0:T(8,128)(2,1)} %param.11), channel_id=1, source_target_pairs={{0,48},{16,0},{32,16},{48,32},{1,49},{17,1},{33,17},{49,33},{2,50}... | collective-permute-start | bytes 1376264 | tf_op jit(solution)/shard_map/ppermute | solution.py:17
  14.7 50.6 %collective-permute-start = (bf16[128,896]{1,0:T(8,128)(2,1)}, bf16[128,896]{1,0:T(8,128)(2,1)}, u32[]{:S(2)}, u32[]{:S(2)}) collective-permute-start(bf16[128,896]{1,0:T(8,128)(2,1)} %get-tuple-element.10), channel_id=1, source_target_pairs={{0,128},{128,256},{256,384},{384,448},{448,320},{320,192},{192,64}... | collective-permute-start | bytes 688136 | tf_op jit(solution)/shard_map/ppermute | solution.py:75
  20.6 137.4 %all-to-all-start.1 = ((bf16[16,8,1024]{2,1,0:T(8,128)(2,1)}), bf16[16,8,1024]{2,1,0:T(8,128)(2,1)S(1)}, u32[]{:S(2)}, u32[]{:S(2)}) async-start(bf16[16,8,1024]{2,1,0:T(8,128)(2,1)} %bitcast.43), calls=%async_computation.1 | async-start | bytes 524288 | tf_op jit(solution)/shard_map/all_to_all | solution.py:59
  34.0 35.8 %collective-permute-start.32 = (bf16[256,512]{1,0:T(8,128)(2,1)S(1)}, bf16[256,512]{1,0:T(8,128)(2,1)}, u32[]{:S(2)}, u32[]{:S(2)}) collective-permute-start(bf16[256,512]{1,0:T(8,128)(2,1)S(1)} %copy-done.6), channel_id=1, source_target_pairs={{0,16},{16,32},{32,48},{48,0},{1,17},{17,33},{33,49},{49,1},{2,18}... | collective-permute-start | bytes 786440 | tf_op jit(solution)/shard_map/ppermute | solution.py:17
  75.2 58.2 %collective-permute-start.1 = (bf16[128,896]{1,0:T(8,128)(2,1)}, bf16[128,896]{1,0:T(8,128)(2,1)}, u32[]{:S(2)}, u32[]{:S(2)}) collective-permute-start(bf16[128,896]{1,0:T(8,128)(2,1)} %collective-permute-done), channel_id=1, source_target_pairs={{0,128},{128,256},{256,384},{384,448},{448,320},{320,192},{192,64}... | collective-permute-start | bytes 688136 | tf_op jit(solution)/shard_map/ppermute | solution.py:75
  174.3 21.7 %collective-permute-start.17 = (bf16[4,16,8,1024]{3,2,1,0:T(8,128)(2,1)S(1)}, bf16[4,16,8,1024]{3,2,1,0:T(8,128)(2,1)S(1)}, u32[]{:S(2)}, u32[]{:S(2)}) collective-permute-start(bf16[4,16,8,1024]{3,2,1,0:T(8,128)(2,1)S(1)} %bitcast_dynamic-update-slice_fusion.9), channel_id=1, source_target_pairs={{0,1},{1,0},{2,3},{3,2},{4,5},{5,4},{6,7},{7,6},{8,9},{9,8},{10,11... | collective-permute-start | bytes 3145736 | tf_op jit(solution)/shard_map/ppermute | solution.py:17
  193.9 78.0 %collective-permute-start.10 = (bf16[4,8,2,8,1024]{4,3,2,0,1:T(8,128)(2,1)}, bf16[4,8,2,8,1024]{4,3,2,0,1:T(8,128)(2,1)}, u32[]{:S(2)}, u32[]{:S(2)}) collective-permute-start(bf16[4,8,2,8,1024]{4,3,2,0,1:T(8,128)(2,1)} %dynamic-slice_bitcast_fusion), channel_id=1, source_target_pairs={{0,1},{1,0},{2,3},{3,2},{4,5},{5,4},{6,7},{7,6},{8,9},{9,8},{10,11... | collective-permute-start | bytes 3145736 | tf_op jit(solution)/shard_map/ppermute | solution.py:17
  203.2 24.0 %collective-permute-start.25 = (bf16[64,896]{1,0:T(8,128)(2,1)}, bf16[64,896]{1,0:T(8,128)(2,1)}, u32[]{:S(2)}, u32[]{:S(2)}) collective-permute-start(bf16[64,896]{1,0:T(8,128)(2,1)} %fusion.30), channel_id=1, source_target_pairs={{0,128},{128,256},{256,384},{384,448},{448,320},{320,192},{192,64}... | collective-permute-start | bytes 344072 | tf_op jit(solution)/shard_map/ppermute | solution.py:101
  208.5 23.1 %collective-permute-start.18 = (bf16[64,896]{1,0:T(8,128)(2,1)S(1)}, bf16[64,896]{1,0:T(8,128)(2,1)}, u32[]{:S(2)}, u32[]{:S(2)}) collective-permute-start(bf16[64,896]{1,0:T(8,128)(2,1)S(1)} %fusion.29), channel_id=1, source_target_pairs={{0,128},{128,256},{256,384},{384,448},{448,320},{320,192},{192,64}... | collective-permute-start | bytes 344072 | tf_op jit(solution)/shard_map/ppermute | solution.py:101
  218.8 17.7 %collective-permute-start.37 = (bf16[8,28,512]{2,1,0:T(8,128)(2,1)S(1)}, bf16[8,28,512]{2,1,0:T(8,128)(2,1)S(1)}, u32[]{:S(2)}, u32[]{:S(2)}) collective-permute-start(bf16[8,28,512]{2,1,0:T(8,128)(2,1)S(1)} %get-tuple-element.16), channel_id=1, source_target_pairs={{0,48},{16,0},{32,16},{48,32},{1,49},{17,1},{33,17},{49,33},{2,50}... | collective-permute-start | bytes 688136 | tf_op jit(solution)/shard_map/ppermute | solution.py:17
  243.0 56.7 %all-to-all-start.2 = ((bf16[8,28,512]{2,1,0:T(8,128)(2,1)}), bf16[8,28,512]{2,1,0:T(8,128)(2,1)S(1)}, u32[]{:S(2)}, u32[]{:S(2)}) async-start(bf16[8,28,512]{2,1,0:T(8,128)(2,1)} %fusion.3), calls=%async_computation.2 | async-start | bytes 524288 | tf_op jit(solution)/shard_map/all_to_all | solution.py:84
  259.6 24.5 %collective-permute-start.28 = (bf16[64,896]{1,0:T(8,128)(2,1)S(1)}, bf16[64,896]{1,0:T(8,128)(2,1)S(1)}, u32[]{:S(2)}, u32[]{:S(2)}) collective-permute-start(bf16[64,896]{1,0:T(8,128)(2,1)S(1)} %fusion.20), channel_id=1, source_target_pairs={{0,128},{128,256},{256,384},{384,448},{448,320},{320,192},{192,64}... | collective-permute-start | bytes 344072 | tf_op jit(solution)/shard_map/ppermute | solution.py:101
  265.3 23.6 %collective-permute-start.21 = (bf16[64,896]{1,0:T(8,128)(2,1)S(1)}, bf16[64,896]{1,0:T(8,128)(2,1)S(1)}, u32[]{:S(2)}, u32[]{:S(2)}) collective-permute-start(bf16[64,896]{1,0:T(8,128)(2,1)S(1)} %fusion.26), channel_id=1, source_target_pairs={{0,128},{128,256},{256,384},{384,448},{448,320},{320,192},{192,64}... | collective-permute-start | bytes 344072 | tf_op jit(solution)/shard_map/ppermute | solution.py:101
  273.9 24.9 %collective-permute-start.13 = (bf16[8,2,8,1024]{3,2,1,0:T(8,128)(2,1)S(1)}, bf16[8,2,8,1024]{3,2,1,0:T(8,128)(2,1)S(1)}, u32[]{:S(2)}, u32[]{:S(2)}) collective-permute-start(bf16[8,2,8,1024]{3,2,1,0:T(8,128)(2,1)S(1)} %get-tuple-element.19), channel_id=1, source_target_pairs={{0,12},{4,0},{8,4},{12,8},{1,13},{5,1},{9,5},{13,9},{2,14},{6,2},{... | collective-permute-start | bytes 786440 | tf_op jit(solution)/shard_map/ppermute | solution.py:17
  275.8 23.0 %collective-permute-start.12 = (bf16[8,2,8,1024]{3,2,1,0:T(8,128)(2,1)S(1)}, bf16[8,2,8,1024]{3,2,1,0:T(8,128)(2,1)S(1)}, u32[]{:S(2)}, u32[]{:S(2)}) collective-permute-start(bf16[8,2,8,1024]{3,2,1,0:T(8,128)(2,1)S(1)} %get-tuple-element.20), channel_id=1, source_target_pairs={{0,8},{4,12},{8,0},{12,4},{1,9},{5,13},{9,1},{13,5},{2,10},{6,14},... | collective-permute-start | bytes 786440 | tf_op jit(solution)/shard_map/ppermute | solution.py:17
  280.9 17.8 %collective-permute-start.11 = (bf16[8,2,8,1024]{3,2,1,0:T(8,128)(2,1)S(1)}, bf16[8,2,8,1024]{3,2,1,0:T(8,128)(2,1)S(1)}, u32[]{:S(2)}, u32[]{:S(2)}) collective-permute-start(bf16[8,2,8,1024]{3,2,1,0:T(8,128)(2,1)S(1)} %get-tuple-element.18), channel_id=1, source_target_pairs={{0,4},{4,8},{8,12},{12,0},{1,5},{5,9},{9,13},{13,1},{2,6},{6,10},{... | collective-permute-start | bytes 786440 | tf_op jit(solution)/shard_map/ppermute | solution.py:17
  289.0 20.4 %collective-permute-start.22 = (bf16[64,896]{1,0:T(8,128)(2,1)S(1)}, bf16[64,896]{1,0:T(8,128)(2,1)}, u32[]{:S(2)}, u32[]{:S(2)}) collective-permute-start(bf16[64,896]{1,0:T(8,128)(2,1)S(1)} %fusion.25), channel_id=1, source_target_pairs={{0,128},{128,256},{256,384},{384,448},{448,320},{320,192},{192,64}... | collective-permute-start | bytes 344072 | tf_op jit(solution)/shard_map/ppermute | solution.py:101
  293.6 21.5 %collective-permute-start.30 = (bf16[64,896]{1,0:T(8,128)(2,1)}, bf16[64,896]{1,0:T(8,128)(2,1)}, u32[]{:S(2)}, u32[]{:S(2)}) collective-permute-start(bf16[64,896]{1,0:T(8,128)(2,1)} %fusion.18), channel_id=1, source_target_pairs={{0,128},{128,256},{256,384},{384,448},{448,320},{320,192},{192,64}... | collective-permute-start | bytes 344072 | tf_op jit(solution)/shard_map/ppermute | solution.py:101
  299.7 29.7 %all-to-all-start = ((bf16[16,8,1024]{2,1,0:T(8,128)(2,1)}), bf16[16,8,1024]{2,1,0:T(8,128)(2,1)S(1)}, u32[]{:S(2)}, u32[]{:S(2)}) async-start(bf16[16,8,1024]{2,1,0:T(8,128)(2,1)} %bitcast.37), calls=%async_computation | async-start | bytes 524288 | tf_op jit(solution)/shard_map/all_to_all | solution.py:114
  316.2 22.8 %collective-permute-start.31 = (bf16[64,896]{1,0:T(8,128)(2,1)S(1)}, bf16[64,896]{1,0:T(8,128)(2,1)}, u32[]{:S(2)}, u32[]{:S(2)}) collective-permute-start(bf16[64,896]{1,0:T(8,128)(2,1)S(1)} %fusion.17), channel_id=1, source_target_pairs={{0,128},{128,256},{256,384},{384,448},{448,320},{320,192},{192,64}... | collective-permute-start | bytes 344072 | tf_op jit(solution)/shard_map/ppermute | solution.py:101
  321.8 18.3 %collective-permute-start.24 = (bf16[64,896]{1,0:T(8,128)(2,1)S(1)}, bf16[64,896]{1,0:T(8,128)(2,1)}, u32[]{:S(2)}, u32[]{:S(2)}) collective-permute-start(bf16[64,896]{1,0:T(8,128)(2,1)S(1)} %fusion.23), channel_id=1, source_target_pairs={{0,128},{128,256},{256,384},{384,448},{448,320},{320,192},{192,64}... | collective-permute-start | bytes 344072 | tf_op jit(solution)/shard_map/ppermute | solution.py:101
  330.1 21.9 %all-to-all-start.3 = ((bf16[8,28,512]{2,1,0:T(8,128)(2,1)}), bf16[8,28,512]{2,1,0:T(8,128)(2,1)S(1)}, u32[]{:S(2)}, u32[]{:S(2)}) async-start(bf16[8,28,512]{2,1,0:T(8,128)(2,1)} %broadcast_in_dim.130), calls=%async_computation.3 | async-start | bytes 524288 | tf_op jit(solution)/shard_map/all_to_all | solution.py:88
  (36 other events, 436.1 us)

commit v2 on v0

v2 whole, which is shorter than its diff:
```python
import jax
import jax.numpy as jnp
from jax import lax
from jax.experimental import pallas as pl
from jax.experimental.pallas import tpu as pltpu
from jax.sharding import Mesh, PartitionSpec as P

corr_first = 1.0 - 0.9**10
corr_second = 1.0 - 0.999**10

NZ, NX, NY, NH, NC = 8, 4, 4, 2, 2
bf16, f32 = jnp.bfloat16, jnp.float32
VMEM = pl.BlockSpec(memory_space=pltpu.VMEM)
SMEM = pl.BlockSpec(memory_space=pltpu.SMEM)


def shift(value, axis, size, by):
    return lax.ppermute(value, axis, [(i, (i - by) % size) for i in range(size)])


def dot(a, b, contract):
    return lax.dot_general(a, b, (contract, ((), ())), preferred_element_type=f32)


def call(kernel, n_in, outs, scratch=(), flops=0, limit=32):
    return pl.pallas_call(
        kernel,
        out_shape=tuple(jax.ShapeDtypeStruct(*o) for o in outs),
        in_specs=[SMEM] + [VMEM] * n_in,
        out_specs=tuple(VMEM for _ in outs),
        scratch_shapes=[pltpu.VMEM(*s) for s in scratch],
        compiler_params=pltpu.CompilerParams(vmem_limit_bytes=limit << 20),
        cost_estimate=pl.CostEstimate(flops=flops, bytes_accessed=4 << 20, transcendentals=0),
    )


def prepare(pos, gate, up, cot, hidden, pack, natural):
    x, y, c = pos[0], pos[1], pos[2]
    g = gate[...].astype(f32)
    natural[...] = g * jax.nn.sigmoid(g) * up[...].astype(f32)
    for cr in range(NC):
        for yr in range(NY):
            first = (lax.rem(y + yr, NY) * 4 + lax.rem(c + cr, NC)) * 8
            pair = [natural[pl.ds(pl.multiple_of(first + zh * 16, 8), 8), :] for zh in range(NH)]
            hidden[pl.ds((cr * NY + yr) * 16, 16), :] = jnp.concatenate(pair, 0).astype(bf16)
    for r in range(NX):
        block = lax.rem(x + r, NX) * 256
        for zl in range(NZ):
            piece = cot[:, pl.ds(pl.multiple_of(zl * 1024 + block, 256), 256)]
            for zh in range(NH):
                pack[zl * NH + zh, :, r * 256 : (r + 1) * 256] = piece


def backward(pos, *refs):
    cots, weights, bases = refs[:8], refs[8:12], refs[12:16]
    grad, reduced, tile = refs[16:]
    for piece in range(8):
        for zl in range(NZ):
            tile[pl.ds(zl * 128 + piece * 16, 16), :] = cots[piece][pl.ds(zl * 16, 16), :]

    def rows(step, _):
        at = pl.ds(pl.multiple_of(step * 256, 256), 256)
        total, low = None, None
        for r in range(NX):
            part = tile[at, r * 256 : (r + 1) * 256]
            more = dot(part, weights[r][...], ((1,), (1,)))
            total = more if total is None else total + more
            more = dot(part, bases[r][...], ((1,), (0,)))
            low = more if low is None else low + more
        grad[at, :] = total.astype(bf16)
        reduced[at, :] = low.astype(bf16)
        return 0

    lax.fori_loop(0, 4, rows, 0)


def project(pos, tile, reduced, out, total):
    x = pos[0]
    total[...] = dot(tile[...], reduced[...], ((0,), (0,)))
    for xs in range(NX):
        to = lax.rem(xs - x + NX, NX)
        for zl in range(NZ):
            out[to, zl, :, :] = total[zl * 112 + xs * 28 : zl * 112 + xs * 28 + 28, :].astype(bf16)


def forward(pos, tile, w0, w1, w2, w3, out):
    def rows(step, _):
        at = pl.ds(pl.multiple_of(step * 256, 256), 256)
        part = tile[at, :]
        for r, w in enumerate((w0, w1, w2, w3)):
            term = dot(part, w[...], ((1,), (0,))).astype(bf16)
            for half in range(2):
                for piece in range(8):
                    first = half * 128 + piece * 16
                    to = pl.ds(pl.multiple_of((step * 2 + half) * 16, 16), 16)
                    out[piece // 4, piece % 4, to, r * 256 : (r + 1) * 256] = term[first : first + 16, :]
        return 0

    lax.fori_loop(0, 4, rows, 0)


def finish_out(pos, parts, out):
    x = pos[0]
    for zl in range(NZ):
        both = (parts[zl * NH].astype(f32) + parts[zl * NH + 1].astype(f32)).astype(bf16)
        for r in range(NX):
            block = zl * 1024 + lax.rem(x + r, NX) * 256
            out[:, pl.ds(pl.multiple_of(block, 256), 256)] = both[:, r * 256 : (r + 1) * 256]


def finish_grad(pos, total, gate, up, grad_gate, grad_up, relative, natural):
    y, c = pos[1], pos[2]
    relative[...] = total[...].astype(f32)
    for ys in range(NY):
        yr = lax.rem(ys - y + NY, NY)
        for zh in range(NH):
            for cs in range(NC):
                cr = lax.rem(cs + c, NC)
                first = ((cr * NY + yr) * NH + zh) * 8
                natural[((ys * NH + zh) * NC + cs) * 8 : ((ys * NH + zh) * NC + cs) * 8 + 8, :] = (
                    relative[pl.ds(pl.multiple_of(first, 8), 8), :]
                )
    g, u, d = gate[...].astype(f32), up[...].astype(f32), natural[...]
    s = jax.nn.sigmoid(g)
    grad_up[...] = (d * g * s).astype(bf16)
    grad_gate[...] = (d * u * s * (1.0 + g * (1.0 - s))).astype(bf16)


def expand(pos, s0, s1, s2, s3, basis, out, pieces, steps):
    x = pos[0]
    for r, piece in enumerate((s0, s1, s2, s3)):
        pieces[lax.rem(x + r, NX)] = piece[...].astype(f32)
    for xs in range(NX):
        for zl in range(NZ):
            steps[zl * 112 + xs * 28 : zl * 112 + xs * 28 + 28, :] = pieces[xs, zl]
    out[...] = dot(steps[...].astype(bf16), basis[...], ((1,), (1,)))


def body(gate, up, weight, basis, cotangent, moment1, moment2):
    pos = jnp.stack([lax.axis_index(a).astype(jnp.int32) for a in ("x", "y", "c")])
    rows, ff = gate.shape
    mine, width = cotangent.shape
    cols = width // NZ
    rank = basis.shape[1]
    own = moment1.shape[0]

    hidden, pack = call(
        prepare, 3, [((rows, ff), bf16), ((NZ * NH, mine, cols), bf16)], [((rows, ff), f32)]
    )(pos, gate, up, cotangent)
    tile = lax.all_gather(hidden, "zl", axis=0, tiled=True)

    got = lax.all_to_all(pack, ("zl", "zh"), 0, 0, tiled=True).reshape(rows, cols)
    cots = [got] + [shift(got, "y", NY, by) for by in range(1, NY)]
    cots = cots + [shift(piece, "c", NC, 1) for piece in cots]
    bases = [basis] + [shift(basis, "x", NX, by) for by in range(1, NX)]
    weights = [weight] + [shift(weight, "x", NX, by) for by in range(1, NX)]

    partial, reduced = call(
        backward,
        16,
        [((NZ * rows, ff), bf16), ((NZ * rows, rank), bf16)],
        [((NZ * rows, cols), bf16)],
        flops=3 * 10**9,
    )(pos, *cots, *weights, *bases)
    grad_hidden = lax.psum_scatter(partial, "zl", scatter_dimension=0, tiled=True)
    grad_gate, grad_up = call(
        finish_grad,
        3,
        [((rows, ff), bf16), ((rows, ff), bf16)],
        [((rows, ff), f32), ((rows, ff), f32)],
    )(pos, grad_hidden, gate, up)

    (parts,) = call(
        project, 2, [((NX, NZ, own, rank), bf16)], [((ff, rank), f32)], flops=10**9
    )(pos, tile, reduced)
    projected = parts[0].astype(f32)
    for by in range(1, NX):
        projected = projected + shift(parts[by], "x", NX, -by).astype(f32)
    projected = lax.all_to_all(projected.astype(bf16), "zl", 0, 0, tiled=True).astype(f32).sum(0)
    moment1_new = 0.9 * moment1 + 0.1 * projected
    moment2_new = 0.999 * moment2 + 0.001 * projected * projected
    step = (moment1_new / corr_first / (jnp.sqrt(moment2_new / corr_second) + 1e-08)).astype(bf16)
    steps = lax.all_to_all(
        jnp.broadcast_to(step[None], (NZ, own, rank)), "zl", 0, 0, tiled=True
    )
    steps = [steps] + [shift(steps, "x", NX, by) for by in range(1, NX)]
    (expansion,) = call(
        expand,
        5,
        [((ff, basis.shape[0]), f32)],
        [((NX, NZ, own, rank), f32), ((ff, rank), f32)],
        flops=3 * 10**8,
    )(pos, *steps, basis)

    (term,) = call(forward, 5, [((NC, NY, rows, cols), bf16)], flops=2 * 10**9)(
        pos, tile, *weights
    )
    term = (term[0].astype(f32) + shift(term[1], "c", NC, 1).astype(f32)).astype(bf16)
    total = term[0].astype(f32)
    for by in range(1, NY):
        total = total + shift(term[by], "y", NY, -by).astype(f32)
    total = total.astype(bf16).reshape(NZ * NH, mine, cols)
    total = lax.all_to_all(total, ("zl", "zh"), 0, 0, tiled=True)
    (layer_out,) = call(finish_out, 1, [((mine, width), bf16)])(pos, total)
    return (layer_out, grad_gate, grad_up, moment1_new, moment2_new, expansion)


def solution(mesh):
    fine = Mesh(mesh.devices.reshape(NZ, NX, NY, NH, NC), ("zl", "x", "y", "zh", "c"))
    dp, tensor = ("zl", "x"), ("y", "zh", "c")
    placed = (
        P(dp, tensor),
        P(dp, tensor),
        P(tensor, dp),
        P(dp, None),
        P(dp + tensor, None),
        P(tensor + dp, None),
        P(tensor + dp, None),
    )
    return jax.shard_map(
        body,
        mesh=fine,
        in_specs=placed,
        out_specs=(
            P(dp + tensor, None),
            P(dp, tensor),
            P(dp, tensor),
            P(tensor + dp, None),
            P(tensor + dp, None),
            P(tensor, dp),
        ),
        check_vma=False,
    )
```

time: 882 us -> 228 us (0.26)
  waiting for transfers between devices: 570 us -> 62.5 us
  blocking collectives: 262 us -> 0 us
  starting transfers between devices: 5.32 us -> 108 us
  matrix products: 27.6 us -> 0 us
  Pallas kernels: 0 us -> 17.7 us
  local copies, waits for them, and re-layouts: 2.11 us -> 17.3 us
    all_gather x3 -> x1, waiting for transfers between devices: 568 us -> 0.02 us  [body(): tile = lax.all_gather(hidden, 'zl', axis=0, tiled=True)]
    unnamed x1 -> x0, blocking collectives: 138 us -> none
    all_gather x1 -> x0, blocking collectives: 124 us -> none  [body(): step_full = lax.all_gather(step, 'dp', axis=0, tiled=True)]
    ppermute x0 -> x23, starting transfers between devices: none -> 72.9 us  [shift(): lax.ppermute(value, axis, [(i, (i - by) % size) for i in range(size)])]
    all_to_all x0 -> x4, starting transfers between devices: none -> 35.3 us  [the longest x1 15.2 us: body(): lax.all_to_all(pack, ('zl', 'zh'), 0, 0, tiled=True).reshape(rows, cols)]
    ppermute x0 -> x23, waiting for transfers between devices: none -> 33.7 us  [shift(): lax.ppermute(value, axis, [(i, (i - by) % size) for i in range(size)])]
    all_to_all x0 -> x4, waiting for transfers between devices: none -> 28.8 us  [the longest x1 26 us: body(): lax.all_to_all(projected.astype(bf16), 'zl', 0, 0, tiled=True).astype(f32)]
    dot_general x4 -> x0, matrix products: 27.6 us -> none  [the longest x1 11.3 us: body(): lax.dot_general(cotangent_full, weight_full, (((1,), (1,)), ((), ())), pr...]
  transfers between devices with their start and end apart: 8 -> 29, of which waited for: 3 -> 9; matrix products, arithmetic and copies ran while one was open for 19% -> 3% of each run, Pallas kernels for 0% -> 6%
where the time goes in v2:
time: 228 us; the launch traced here: 226 us
  starting transfers between devices  108 us (47%)
  waiting for transfers between devices  62.5 us (27%)
  Pallas kernels  17.7 us (8%)
  local copies, waits for them, and re-layouts  17.3 us (8%)
  between operations  14.6 us (6%)
  other arithmetic  5.21 us (2%)
    ppermute x23, starting transfers between devices, shift(): lax.ppermute(value, axis, [(i, (i - by) % size) for i in range(size)])  72.9 us
    ppermute x23, waiting for transfers between devices, shift(): lax.ppermute(value, axis, [(i, (i - by) % size) for i in range(size)])  33.7 us
    all_to_all x1, waiting for transfers between devices, body(): lax.all_to_all(projected.astype(bf16), 'zl', 0, 0, tiled=True).astype(f32)  26 us
    all_to_all x1, starting transfers between devices, body(): lax.all_to_all(pack, ('zl', 'zh'), 0, 0, tiled=True).reshape(rows, cols)  15.2 us
    unnamed x44, local copies, waits for them, and re-layouts  14.6 us
    all_to_all x1, starting transfers between devices, body(): lax.all_to_all(projected.astype(bf16), 'zl', 0, 0, tiled=True).astype(f32)  9.52 us
    all_to_all x1, starting transfers between devices, body(): total = lax.all_to_all(total, ('zl', 'zh'), 0, 0, tiled=True)  7.13 us
    pallas_call x1, Pallas kernels, body(): call(backward, 16, [((NZ * rows, ff), bf16), ((NZ * rows, rank), bf16)],...  5.92 us
  transfers between devices with their start and end apart: 29, of which 9 were waited for; matrix products, arithmetic and copies ran while one was open for 3% of the time, Pallas kernels for 6%

profile of v2, /device:TPU:24, one launch (start us, length us, event | category | flops | bytes accessed | tf_op | source)
XLA Modules:
  0.0 225.5 jit_solution(3248253915225681187)
XLA Ops:
  11.6 15.2 %all-to-all-start.1 = ((bf16[16,8,1024]{2,1,0:T(8,128)(2,1)}), bf16[16,8,1024]{2,1,0:T(8,128)(2,1)S(1)}, u32[]{:S(2)}, u32[]{:S(2)}) async-start(bf16[16,8,1024]{2,1,0:T(8,128)(2,1)} %get-tuple-element.13), calls=%async_computation.1 | async-start | bytes 524288 | tf_op jit(solution)/shard_map/all_to_all | solution.py:152
  26.8 4.7 %collective-permute-start = (bf16[896,256]{1,0:T(8,128)(2,1)}, bf16[896,256]{1,0:T(8,128)(2,1)S(1)}, u32[]{:S(2)}, u32[]{:S(2)}) collective-permute-start(bf16[896,256]{1,0:T(8,128)(2,1)} %refs_8_.1), channel_id=1, source_target_pairs={{0,48},{16,0},{32,16},{48,32},{1,49},{17,1},{33,17},{49,33},{2,50}... | collective-permute-start | bytes 1376264 | tf_op jit(solution)/shard_map/ppermute | solution.py:18
  31.5 2.7 %collective-permute-start.14 = (bf16[256,512]{1,0:T(8,128)(2,1)}, bf16[256,512]{1,0:T(8,128)(2,1)S(1)}, u32[]{:S(2)}, u32[]{:S(2)}) collective-permute-start(bf16[256,512]{1,0:T(8,128)(2,1)} %basis.1), channel_id=1, source_target_pairs={{0,48},{16,0},{32,16},{48,32},{1,49},{17,1},{33,17},{49,33},{2,50}... | collective-permute-start | bytes 786440 | tf_op jit(solution)/shard_map/ppermute | solution.py:18
  36.7 2.8 %collective-permute-start.16 = (bf16[256,512]{1,0:T(8,128)(2,1)}, bf16[256,512]{1,0:T(8,128)(2,1)S(1)}, u32[]{:S(2)}, u32[]{:S(2)}) collective-permute-start(bf16[256,512]{1,0:T(8,128)(2,1)} %basis.1), channel_id=1, source_target_pairs={{0,16},{16,32},{32,48},{48,0},{1,17},{17,33},{33,49},{49,1},{2,18}... | collective-permute-start | bytes 786440 | tf_op jit(solution)/shard_map/ppermute | solution.py:18
  39.5 5.9 %collective-permute-start.1 = (bf16[896,256]{1,0:T(8,128)(2,1)}, bf16[896,256]{1,0:T(8,128)(2,1)S(1)}, u32[]{:S(2)}, u32[]{:S(2)}) collective-permute-start(bf16[896,256]{1,0:T(8,128)(2,1)} %refs_8_.1), channel_id=1, source_target_pairs={{0,32},{16,48},{32,0},{48,16},{1,33},{17,49},{33,1},{49,17},{2,34}... | collective-permute-start | bytes 1376264 | tf_op jit(solution)/shard_map/ppermute | solution.py:18
  45.4 17.1 %collective-permute-done.14.refs_13_ = bf16[256,512]{1,0:T(8,128)(2,1)S(1)} collective-permute-done((bf16[256,512]{1,0:T(8,128)(2,1)}, bf16[256,512]{1,0:T(8,128)(2,1)S(1)}, u32[]{:S(2)}, u32[]{:S(2)}) %collective-permute-start.14) | collective-permute-done | bytes 262176 | tf_op jit(solution)/shard_map/ppermute | solution.py:18
  65.1 2.8 %collective-permute-start.8 = (bf16[128,1024]{1,0:T(8,128)(2,1)S(1)}, bf16[128,1024]{1,0:T(8,128)(2,1)S(1)}, u32[]{:S(2)}, u32[]{:S(2)}) collective-permute-start(bf16[128,1024]{1,0:T(8,128)(2,1)S(1)} %bitcast.36), channel_id=1, source_target_pairs={{0,8},{4,12},{8,0},{12,4},{1,9},{5,13},{9,1},{13,5},{2,10},{6,14},... | collective-permute-start | bytes 786440 | tf_op jit(solution)/shard_map/ppermute | solution.py:18
  68.6 4.1 %collective-permute-start.9 = (bf16[128,1024]{1,0:T(8,128)(2,1)S(1)}, bf16[128,1024]{1,0:T(8,128)(2,1)S(1)}, u32[]{:S(2)}, u32[]{:S(2)}) collective-permute-start(bf16[128,1024]{1,0:T(8,128)(2,1)S(1)} %bitcast.37), channel_id=1, source_target_pairs={{0,4},{4,8},{8,12},{12,0},{1,5},{5,9},{9,13},{13,1},{2,6},{6,10},{... | collective-permute-start | bytes 786440 | tf_op jit(solution)/shard_map/ppermute | solution.py:18
  88.0 5.9 %shard_map.121 = (bf16[1024,896]{1,0:T(8,128)(2,1)}, bf16[1024,512]{1,0:T(8,128)(2,1)S(1)}) custom-call(s32[3]{0:T(128)S(1)} %pad_add_fusion.pos, bf16[128,1024]{1,0:T(8,128)(2,1)S(1)} %bitcast.39, bf16[128,1024]{1,0:T(8,128)(2,1)S(1)} %collective-permute-done.7.refs_1_, bf16[128,1024]{1,0:T(8,128)(2,1)S(1)} %collective-permute-done.8.refs_2_, ...), custom_call_target="tpu_custom_call" | custom-call | flops 3000000000 | bytes 4194304 | tf_op jit(solution)/shard_map/pallas_call | solution.py:158
  100.0 6.4 %collective-permute-start.18 = (bf16[8,28,512]{2,1,0:T(8,128)(2,1)}, bf16[8,28,512]{2,1,0:T(8,128)(2,1)}, u32[]{:S(2)}, u32[]{:S(2)}) collective-permute-start(bf16[8,28,512]{2,1,0:T(8,128)(2,1)} %get-tuple-element.23), channel_id=1, source_target_pairs={{0,32},{16,48},{32,0},{48,16},{1,33},{17,49},{33,1},{49,17},{2,34}... | collective-permute-start | bytes 688136 | tf_op jit(solution)/shard_map/ppermute | solution.py:18
  106.4 4.5 %collective-permute-start.19 = (bf16[8,28,512]{2,1,0:T(8,128)(2,1)}, bf16[8,28,512]{2,1,0:T(8,128)(2,1)}, u32[]{:S(2)}, u32[]{:S(2)}) collective-permute-start(bf16[8,28,512]{2,1,0:T(8,128)(2,1)} %get-tuple-element.22), channel_id=1, source_target_pairs={{0,48},{16,0},{32,16},{48,32},{1,49},{17,1},{33,17},{49,33},{2,50}... | collective-permute-start | bytes 688136 | tf_op jit(solution)/shard_map/ppermute | solution.py:18
  116.6 3.5 %shard_map.119 = bf16[2,4,128,1024]{3,2,1,0:T(8,128)(2,1)S(1)} custom-call(s32[3]{0:T(128)S(1)} %pad_add_fusion.pos, bf16[1024,896]{1,0:T(8,128)(2,1)S(1)} %copy-done.1, bf16[896,256]{1,0:T(8,128)(2,1)S(1)} %copy-done.11, bf16[896,256]{1,0:T(8,128)(2,1)S(1)} %copy-done.13, bf16[896,256]{1,0:T(8,128)(2,1)S(1)} %copy-done.15, bf16[896,256]{1,0:T(8,128)(2,1)S(1)} %copy-done.17), custom_call_target="tpu_custom_call" | custom-call | flops 2000000000 | bytes 4194304 | tf_op jit(solution)/shard_map/pallas_call | solution.py:195
  122.0 9.5 %all-to-all-start.2 = ((bf16[8,28,512]{2,1,0:T(8,128)(2,1)}), bf16[8,28,512]{2,1,0:T(8,128)(2,1)S(1)}, u32[]{:S(2)}, u32[]{:S(2)}) async-start(bf16[8,28,512]{2,1,0:T(8,128)(2,1)} %fusion.3), calls=%async_computation.3 | async-start | bytes 524288 | tf_op jit(solution)/shard_map/all_to_all | solution.py:179
  134.5 26.0 %all-to-all-done.2 = bf16[8,28,512]{2,1,0:T(8,128)(2,1)S(1)} async-done(((bf16[8,28,512]{2,1,0:T(8,128)(2,1)}), bf16[8,28,512]{2,1,0:T(8,128)(2,1)S(1)}, u32[]{:S(2)}, u32[]{:S(2)}) %all-to-all-start.2) | async-done | bytes 229408 | tf_op jit(solution)/shard_map/all_to_all | solution.py:179
  162.0 3.4 %all-to-all-start.3 = ((bf16[8,28,512]{2,1,0:T(8,128)(2,1)}), bf16[8,28,512]{2,1,0:T(8,128)(2,1)S(1)}, u32[]{:S(2)}, u32[]{:S(2)}) async-start(bf16[8,28,512]{2,1,0:T(8,128)(2,1)} %broadcast_in_dim.2), calls=%async_computation.4 | async-start | bytes 524288 | tf_op jit(solution)/shard_map/all_to_all | solution.py:183
  169.9 3.1 %collective-permute-start.5 = (bf16[128,1024]{1,0:T(8,128)(2,1)S(1)}, bf16[128,1024]{1,0:T(8,128)(2,1)S(1)}, u32[]{:S(2)}, u32[]{:S(2)}) collective-permute-start(bf16[128,1024]{1,0:T(8,128)(2,1)S(1)} %get-tuple-element.26), channel_id=1, source_target_pairs={{0,8},{4,12},{8,0},{12,4},{1,9},{5,13},{9,1},{13,5},{2,10},{6,14},... | collective-permute-start | bytes 786440 | tf_op jit(solution)/shard_map/ppermute | solution.py:18
  173.1 3.1 %collective-permute-start.6 = (bf16[128,1024]{1,0:T(8,128)(2,1)S(1)}, bf16[128,1024]{1,0:T(8,128)(2,1)S(1)}, u32[]{:S(2)}, u32[]{:S(2)}) collective-permute-start(bf16[128,1024]{1,0:T(8,128)(2,1)S(1)} %get-tuple-element.25), channel_id=1, source_target_pairs={{0,12},{4,0},{8,4},{12,8},{1,13},{5,1},{9,5},{13,9},{2,14},{6,2},{... | collective-permute-start | bytes 786440 | tf_op jit(solution)/shard_map/ppermute | solution.py:18
  178.1 3.8 %collective-permute-done.5 = bf16[128,1024]{1,0:T(8,128)(2,1)S(1)} collective-permute-done((bf16[128,1024]{1,0:T(8,128)(2,1)S(1)}, bf16[128,1024]{1,0:T(8,128)(2,1)S(1)}, u32[]{:S(2)}, u32[]{:S(2)}) %collective-permute-start.5) | collective-permute-done | bytes 262176 | tf_op jit(solution)/shard_map/ppermute | solution.py:18
  182.0 2.7 %collective-permute-done.6 = bf16[128,1024]{1,0:T(8,128)(2,1)S(1)} collective-permute-done((bf16[128,1024]{1,0:T(8,128)(2,1)S(1)}, bf16[128,1024]{1,0:T(8,128)(2,1)S(1)}, u32[]{:S(2)}, u32[]{:S(2)}) %collective-permute-start.6) | collective-permute-done | bytes 262176 | tf_op jit(solution)/shard_map/ppermute | solution.py:18
  185.6 2.8 %all-to-all-done.3.s0 = bf16[8,28,512]{2,1,0:T(8,128)(2,1)S(1)} async-done(((bf16[8,28,512]{2,1,0:T(8,128)(2,1)}), bf16[8,28,512]{2,1,0:T(8,128)(2,1)S(1)}, u32[]{:S(2)}, u32[]{:S(2)}) %all-to-all-start.3) | async-done | bytes 229408 | tf_op jit(solution)/shard_map/all_to_all | solution.py:183
  188.3 7.1 %all-to-all-start = ((bf16[16,8,1024]{2,1,0:T(8,128)(2,1)}), bf16[16,8,1024]{2,1,0:T(8,128)(2,1)S(1)}, u32[]{:S(2)}, u32[]{:S(2)}) async-start(bf16[16,8,1024]{2,1,0:T(8,128)(2,1)} %fusion.7), calls=%async_computation | async-start | bytes 524288 | tf_op jit(solution)/shard_map/all_to_all | solution.py:203
  195.5 3.5 %collective-permute-start.20 = (bf16[8,28,512]{2,1,0:T(8,128)(2,1)S(1)}, bf16[8,28,512]{2,1,0:T(8,128)(2,1)S(1)}, u32[]{:S(2)}, u32[]{:S(2)}) collective-permute-start(bf16[8,28,512]{2,1,0:T(8,128)(2,1)S(1)} %all-to-all-done.3.s0), channel_id=1, source_target_pairs={{0,48},{16,0},{32,16},{48,32},{1,49},{17,1},{33,17},{49,33},{2,50}... | collective-permute-start | bytes 688136 | tf_op jit(solution)/shard_map/ppermute | solution.py:18
  199.0 5.0 %collective-permute-start.21 = (bf16[8,28,512]{2,1,0:T(8,128)(2,1)S(1)}, bf16[8,28,512]{2,1,0:T(8,128)(2,1)S(1)}, u32[]{:S(2)}, u32[]{:S(2)}) collective-permute-start(bf16[8,28,512]{2,1,0:T(8,128)(2,1)S(1)} %all-to-all-done.3.s0), channel_id=1, source_target_pairs={{0,32},{16,48},{32,0},{48,16},{1,33},{17,49},{33,1},{49,17},{2,34}... | collective-permute-start | bytes 688136 | tf_op jit(solution)/shard_map/ppermute | solution.py:18
  211.1 4.2 %collective-permute-done.22.s3 = bf16[8,28,512]{2,1,0:T(8,128)(2,1)S(1)} collective-permute-done((bf16[8,28,512]{2,1,0:T(8,128)(2,1)S(1)}, bf16[8,28,512]{2,1,0:T(8,128)(2,1)S(1)}, u32[]{:S(2)}, u32[]{:S(2)}) %collective-permute-start.22) | collective-permute-done | bytes 229408 | tf_op jit(solution)/shard_map/ppermute | solution.py:18
  (97 shorter events, 61.0 us)
Async XLA Ops:
  7.2 86.8 %all-gather.2.cloned.1.call-start = ((), (), s32[]{:S(2)}) async-start(), calls=%async_computation.5 | async-start | bytes 2064384 | tf_op jit(solution)/shard_map/all_gather | solution.py:150
  11.6 50.8 %all-to-all-start.1 = ((bf16[16,8,1024]{2,1,0:T(8,128)(2,1)}), bf16[16,8,1024]{2,1,0:T(8,128)(2,1)S(1)}, u32[]{:S(2)}, u32[]{:S(2)}) async-start(bf16[16,8,1024]{2,1,0:T(8,128)(2,1)} %get-tuple-element.13), calls=%async_computation.1 | async-start | bytes 524288 | tf_op jit(solution)/shard_map/all_to_all | solution.py:152
  26.8 179.2 %reduce-scatter.2.cloned.1.call-start = ((), (), s32[]{:S(2)}) async-start(), calls=%async_computation.6 | async-start | bytes 2064384 | tf_op jit(solution)/shard_map/reduce_scatter | solution.py:165
  26.8 45.9 %collective-permute-start = (bf16[896,256]{1,0:T(8,128)(2,1)}, bf16[896,256]{1,0:T(8,128)(2,1)S(1)}, u32[]{:S(2)}, u32[]{:S(2)}) collective-permute-start(bf16[896,256]{1,0:T(8,128)(2,1)} %refs_8_.1), channel_id=1, source_target_pairs={{0,48},{16,0},{32,16},{48,32},{1,49},{17,1},{33,17},{49,33},{2,50}... | collective-permute-start | bytes 1376264 | tf_op jit(solution)/shard_map/ppermute | solution.py:18
  31.5 30.9 %collective-permute-start.14 = (bf16[256,512]{1,0:T(8,128)(2,1)}, bf16[256,512]{1,0:T(8,128)(2,1)S(1)}, u32[]{:S(2)}, u32[]{:S(2)}) collective-permute-start(bf16[256,512]{1,0:T(8,128)(2,1)} %basis.1), channel_id=1, source_target_pairs={{0,48},{16,0},{32,16},{48,32},{1,49},{17,1},{33,17},{49,33},{2,50}... | collective-permute-start | bytes 786440 | tf_op jit(solution)/shard_map/ppermute | solution.py:18
  34.3 30.8 %collective-permute-start.15 = (bf16[256,512]{1,0:T(8,128)(2,1)}, bf16[256,512]{1,0:T(8,128)(2,1)S(1)}, u32[]{:S(2)}, u32[]{:S(2)}) collective-permute-start(bf16[256,512]{1,0:T(8,128)(2,1)} %basis.1), channel_id=1, source_target_pairs={{0,32},{16,48},{32,0},{48,16},{1,33},{17,49},{33,1},{49,17},{2,34}... | collective-permute-start | bytes 786440 | tf_op jit(solution)/shard_map/ppermute | solution.py:18
  36.7 31.2 %collective-permute-start.16 = (bf16[256,512]{1,0:T(8,128)(2,1)}, bf16[256,512]{1,0:T(8,128)(2,1)S(1)}, u32[]{:S(2)}, u32[]{:S(2)}) collective-permute-start(bf16[256,512]{1,0:T(8,128)(2,1)} %basis.1), channel_id=1, source_target_pairs={{0,16},{16,32},{32,48},{48,0},{1,17},{17,33},{33,49},{49,1},{2,18}... | collective-permute-start | bytes 786440 | tf_op jit(solution)/shard_map/ppermute | solution.py:18
  39.5 35.2 %collective-permute-start.1 = (bf16[896,256]{1,0:T(8,128)(2,1)}, bf16[896,256]{1,0:T(8,128)(2,1)S(1)}, u32[]{:S(2)}, u32[]{:S(2)}) collective-permute-start(bf16[896,256]{1,0:T(8,128)(2,1)} %refs_8_.1), channel_id=1, source_target_pairs={{0,32},{16,48},{32,0},{48,16},{1,33},{17,49},{33,1},{49,17},{2,34}... | collective-permute-start | bytes 1376264 | tf_op jit(solution)/shard_map/ppermute | solution.py:18
  62.4 14.2 %collective-permute-start.7 = (bf16[128,1024]{1,0:T(8,128)(2,1)S(1)}, bf16[128,1024]{1,0:T(8,128)(2,1)S(1)}, u32[]{:S(2)}, u32[]{:S(2)}) collective-permute-start(bf16[128,1024]{1,0:T(8,128)(2,1)S(1)} %bitcast.35), channel_id=1, source_target_pairs={{0,12},{4,0},{8,4},{12,8},{1,13},{5,1},{9,5},{13,9},{2,14},{6,2},{... | collective-permute-start | bytes 786440 | tf_op jit(solution)/shard_map/ppermute | solution.py:18
  65.1 14.0 %collective-permute-start.8 = (bf16[128,1024]{1,0:T(8,128)(2,1)S(1)}, bf16[128,1024]{1,0:T(8,128)(2,1)S(1)}, u32[]{:S(2)}, u32[]{:S(2)}) collective-permute-start(bf16[128,1024]{1,0:T(8,128)(2,1)S(1)} %bitcast.36), channel_id=1, source_target_pairs={{0,8},{4,12},{8,0},{12,4},{1,9},{5,13},{9,1},{13,5},{2,10},{6,14},... | collective-permute-start | bytes 786440 | tf_op jit(solution)/shard_map/ppermute | solution.py:18
  68.6 12.4 %collective-permute-start.9 = (bf16[128,1024]{1,0:T(8,128)(2,1)S(1)}, bf16[128,1024]{1,0:T(8,128)(2,1)S(1)}, u32[]{:S(2)}, u32[]{:S(2)}) collective-permute-start(bf16[128,1024]{1,0:T(8,128)(2,1)S(1)} %bitcast.37), channel_id=1, source_target_pairs={{0,4},{4,8},{8,12},{12,0},{1,5},{5,9},{9,13},{13,1},{2,6},{6,10},{... | collective-permute-start | bytes 786440 | tf_op jit(solution)/shard_map/ppermute | solution.py:18
  72.8 12.1 %collective-permute-start.2 = (bf16[896,256]{1,0:T(8,128)(2,1)}, bf16[896,256]{1,0:T(8,128)(2,1)S(1)}, u32[]{:S(2)}, u32[]{:S(2)}) collective-permute-start(bf16[896,256]{1,0:T(8,128)(2,1)} %refs_8_.1), channel_id=1, source_target_pairs={{0,16},{16,32},{32,48},{48,0},{1,17},{17,33},{33,49},{49,1},{2,18}... | collective-permute-start | bytes 1376264 | tf_op jit(solution)/shard_map/ppermute | solution.py:18
  98.1 22.0 %collective-permute-start.17 = (bf16[8,28,512]{2,1,0:T(8,128)(2,1)}, bf16[8,28,512]{2,1,0:T(8,128)(2,1)S(1)}, u32[]{:S(2)}, u32[]{:S(2)}) collective-permute-start(bf16[8,28,512]{2,1,0:T(8,128)(2,1)} %get-tuple-element.21), channel_id=1, source_target_pairs={{0,16},{16,32},{32,48},{48,0},{1,17},{17,33},{33,49},{49,1},{2,18}... | collective-permute-start | bytes 688136 | tf_op jit(solution)/shard_map/ppermute | solution.py:18
  100.0 20.1 %collective-permute-start.18 = (bf16[8,28,512]{2,1,0:T(8,128)(2,1)}, bf16[8,28,512]{2,1,0:T(8,128)(2,1)}, u32[]{:S(2)}, u32[]{:S(2)}) collective-permute-start(bf16[8,28,512]{2,1,0:T(8,128)(2,1)} %get-tuple-element.23), channel_id=1, source_target_pairs={{0,32},{16,48},{32,0},{48,16},{1,33},{17,49},{33,1},{49,17},{2,34}... | collective-permute-start | bytes 688136 | tf_op jit(solution)/shard_map/ppermute | solution.py:18
  106.4 13.7 %collective-permute-start.19 = (bf16[8,28,512]{2,1,0:T(8,128)(2,1)}, bf16[8,28,512]{2,1,0:T(8,128)(2,1)}, u32[]{:S(2)}, u32[]{:S(2)}) collective-permute-start(bf16[8,28,512]{2,1,0:T(8,128)(2,1)} %get-tuple-element.22), channel_id=1, source_target_pairs={{0,48},{16,0},{32,16},{48,32},{1,49},{17,1},{33,17},{49,33},{2,50}... | collective-permute-start | bytes 688136 | tf_op jit(solution)/shard_map/ppermute | solution.py:18
  122.0 38.5 %all-to-all-start.2 = ((bf16[8,28,512]{2,1,0:T(8,128)(2,1)}), bf16[8,28,512]{2,1,0:T(8,128)(2,1)S(1)}, u32[]{:S(2)}, u32[]{:S(2)}) async-start(bf16[8,28,512]{2,1,0:T(8,128)(2,1)} %fusion.3), calls=%async_computation.3 | async-start | bytes 524288 | tf_op jit(solution)/shard_map/all_to_all | solution.py:179
  132.6 32.8 %collective-permute-start.3 = (bf16[4,128,1024]{2,1,0:T(8,128)(2,1)}, bf16[4,128,1024]{2,1,0:T(8,128)(2,1)}, u32[]{:S(2)}, u32[]{:S(2)}) collective-permute-start(bf16[4,128,1024]{2,1,0:T(8,128)(2,1)} %slice_bitcast_fusion), channel_id=1, source_target_pairs={{0,1},{1,0},{2,3},{3,2},{4,5},{5,4},{6,7},{7,6},{8,9},{9,8},{10,11... | collective-permute-start | bytes 3145736 | tf_op jit(solution)/shard_map/ppermute | solution.py:18
  162.0 26.3 %all-to-all-start.3 = ((bf16[8,28,512]{2,1,0:T(8,128)(2,1)}), bf16[8,28,512]{2,1,0:T(8,128)(2,1)S(1)}, u32[]{:S(2)}, u32[]{:S(2)}) async-start(bf16[8,28,512]{2,1,0:T(8,128)(2,1)} %broadcast_in_dim.2), calls=%async_computation.4 | async-start | bytes 524288 | tf_op jit(solution)/shard_map/all_to_all | solution.py:183
  169.9 12.1 %collective-permute-start.5 = (bf16[128,1024]{1,0:T(8,128)(2,1)S(1)}, bf16[128,1024]{1,0:T(8,128)(2,1)S(1)}, u32[]{:S(2)}, u32[]{:S(2)}) collective-permute-start(bf16[128,1024]{1,0:T(8,128)(2,1)S(1)} %get-tuple-element.26), channel_id=1, source_target_pairs={{0,8},{4,12},{8,0},{12,4},{1,9},{5,13},{9,1},{13,5},{2,10},{6,14},... | collective-permute-start | bytes 786440 | tf_op jit(solution)/shard_map/ppermute | solution.py:18
  173.1 11.6 %collective-permute-start.6 = (bf16[128,1024]{1,0:T(8,128)(2,1)S(1)}, bf16[128,1024]{1,0:T(8,128)(2,1)S(1)}, u32[]{:S(2)}, u32[]{:S(2)}) collective-permute-start(bf16[128,1024]{1,0:T(8,128)(2,1)S(1)} %get-tuple-element.25), channel_id=1, source_target_pairs={{0,12},{4,0},{8,4},{12,8},{1,13},{5,1},{9,5},{13,9},{2,14},{6,2},{... | collective-permute-start | bytes 786440 | tf_op jit(solution)/shard_map/ppermute | solution.py:18
  188.3 29.1 %all-to-all-start = ((bf16[16,8,1024]{2,1,0:T(8,128)(2,1)}), bf16[16,8,1024]{2,1,0:T(8,128)(2,1)S(1)}, u32[]{:S(2)}, u32[]{:S(2)}) async-start(bf16[16,8,1024]{2,1,0:T(8,128)(2,1)} %fusion.7), calls=%async_computation | async-start | bytes 524288 | tf_op jit(solution)/shard_map/all_to_all | solution.py:203
  195.5 13.2 %collective-permute-start.20 = (bf16[8,28,512]{2,1,0:T(8,128)(2,1)S(1)}, bf16[8,28,512]{2,1,0:T(8,128)(2,1)S(1)}, u32[]{:S(2)}, u32[]{:S(2)}) collective-permute-start(bf16[8,28,512]{2,1,0:T(8,128)(2,1)S(1)} %all-to-all-done.3.s0), channel_id=1, source_target_pairs={{0,48},{16,0},{32,16},{48,32},{1,49},{17,1},{33,17},{49,33},{2,50}... | collective-permute-start | bytes 688136 | tf_op jit(solution)/shard_map/ppermute | solution.py:18
  199.0 12.1 %collective-permute-start.21 = (bf16[8,28,512]{2,1,0:T(8,128)(2,1)S(1)}, bf16[8,28,512]{2,1,0:T(8,128)(2,1)S(1)}, u32[]{:S(2)}, u32[]{:S(2)}) collective-permute-start(bf16[8,28,512]{2,1,0:T(8,128)(2,1)S(1)} %all-to-all-done.3.s0), channel_id=1, source_target_pairs={{0,32},{16,48},{32,0},{48,16},{1,33},{17,49},{33,1},{49,17},{2,34}... | collective-permute-start | bytes 688136 | tf_op jit(solution)/shard_map/ppermute | solution.py:18
  204.0 11.2 %collective-permute-start.22 = (bf16[8,28,512]{2,1,0:T(8,128)(2,1)S(1)}, bf16[8,28,512]{2,1,0:T(8,128)(2,1)S(1)}, u32[]{:S(2)}, u32[]{:S(2)}) collective-permute-start(bf16[8,28,512]{2,1,0:T(8,128)(2,1)S(1)} %all-to-all-done.3.s0), channel_id=1, source_target_pairs={{0,16},{16,32},{32,48},{48,0},{1,17},{17,33},{33,49},{49,1},{2,18}... | collective-permute-start | bytes 688136 | tf_op jit(solution)/shard_map/ppermute | solution.py:18
  (27 other events, 310.1 us)
Sparse Core Ops, SparseCore 0:
  11.7 76.8 all-gather.1
  111.1 73.6 reduce-scatter.1

commit v3 on v0

v3 whole, which is shorter than its diff:
```python
import jax
import jax.numpy as jnp
from jax import lax
from jax.experimental import pallas as pl
from jax.experimental.pallas import tpu as pltpu
from jax.sharding import Mesh, PartitionSpec as P

corr_first = 1.0 - 0.9**10
corr_second = 1.0 - 0.999**10

NA, NB, NX, NY, NH, NC = 2, 4, 4, 4, 2, 2
NZ = NA * NB
bf16, f32 = jnp.bfloat16, jnp.float32
VMEM = pl.BlockSpec(memory_space=pltpu.VMEM)
SMEM = pl.BlockSpec(memory_space=pltpu.SMEM)


def spread(value, axes, size):
    copies = jnp.broadcast_to(value[None], (size,) + value.shape)
    return lax.all_to_all(copies, axes, 0, 0, tiled=True)


def swap(value, axis):
    return lax.ppermute(value, axis, [(0, 1), (1, 0)])


def dot(a, b, contract):
    return lax.dot_general(a, b, (contract, ((), ())), preferred_element_type=f32)


def call(kernel, n_in, outs, scratch=(), flops=0, limit=32):
    return pl.pallas_call(
        kernel,
        out_shape=tuple(jax.ShapeDtypeStruct(*o) for o in outs),
        in_specs=[SMEM] + [VMEM] * n_in,
        out_specs=tuple(VMEM for _ in outs),
        scratch_shapes=[pltpu.VMEM(*s) for s in scratch],
        compiler_params=pltpu.CompilerParams(vmem_limit_bytes=limit << 20),
        cost_estimate=pl.CostEstimate(flops=flops, bytes_accessed=4 << 20, transcendentals=0),
    )


def prepare(pos, gate, up, cot, hidden, pack, plain):
    c = pos[1]
    g = gate[...].astype(f32)
    plain[...] = g * jax.nn.sigmoid(g) * up[...].astype(f32)
    for cr in range(NC):
        for y in range(NY):
            first = (y * 4 + lax.rem(c + cr, NC)) * 8
            pair = [plain[pl.ds(pl.multiple_of(first + zh * 16, 8), 8), :] for zh in range(NH)]
            hidden[pl.ds((cr * NY + y) * 16, 16), :] = jnp.concatenate(pair, 0).astype(bf16)
    for za in range(NA):
        for x in range(NX):
            for zb in range(NB):
                block = ((za * NB + zb) * NX + x) * 256
                piece = cot[:, block : block + 256]
                for zh in range(NH):
                    pack[(za * NX + x) * NH + zh, :, zb * 256 : (zb + 1) * 256] = piece


def project(pos, cot_own, cot_other, basis_own, basis_other, hidden, tile, out, basis, reduced, total):
    za, c = pos[0], pos[1]
    for hr, part in enumerate((basis_own, basis_other)):
        for zb in range(NB):
            first = zb * 256 + lax.rem(c + hr, NC) * 128
            basis[pl.ds(pl.multiple_of(first, 128), 128), :] = part[zb]
    for x in range(NX):
        for ar in range(NA):
            at = pl.ds(pl.multiple_of((lax.rem(za + ar, NA) * NX + x) * 16, 16), 16)
            for cr, cot in enumerate((cot_own, cot_other)):
                for y in range(NY):
                    to = (x * NA + ar) * 128 + (cr * NY + y) * 16
                    tile[to : to + 16, :] = cot[y, at, :]

    def rows(step, _):
        at = pl.ds(pl.multiple_of(step * 256, 256), 256)
        reduced[at, :] = dot(tile[at, :], basis[...], ((1,), (0,))).astype(bf16)
        return 0

    lax.fori_loop(0, 4, rows, 0)
    total[...] = dot(hidden[...], reduced[...], ((0,), (0,)))
    spare = jnp.zeros((4, total.shape[1]), f32)
    for x in range(NX):
        for zl in range(NZ):
            first = zl * 112 + x * 28
            block = jnp.concatenate([total[first : first + 28, :], spare], 0)
            out[x, zl * 32 : zl * 32 + 32, :] = block.astype(bf16)


def backward(pos, tile, weight, out):
    def rows(x, _):
        at = pl.ds(pl.multiple_of(x * 256, 256), 256)
        total = None
        for zb in range(NB):
            more = dot(tile[at, zb * 256 : (zb + 1) * 256], weight[zb], ((1,), (1,)))
            total = more if total is None else total + more
        out[x] = total.astype(bf16)
        return 0

    lax.fori_loop(0, NX, rows, 0)


def forward(pos, hidden, weight, out):
    za = pos[0]

    def rows(x, _):
        part = hidden[pl.ds(pl.multiple_of(x * 256, 256), 256), :]
        for zb in range(NB):
            term = dot(part, weight[zb], ((1,), (0,))).astype(bf16)
            for ar in range(NA):
                to = (lax.rem(za + ar, NA) * NX + x) * 16
                to = pl.ds(pl.multiple_of(to, 16), 16)
                for piece in range(8):
                    first = ar * 128 + piece * 16
                    out[piece // 4, piece % 4, to, zb * 256 : (zb + 1) * 256] = term[first : first + 16, :]
        return 0

    lax.fori_loop(0, NX, rows, 0)


def finish_out(pos, parts, out):
    for za in range(NA):
        for x in range(NX):
            at = (za * NX + x) * NH
            both = (parts[at].astype(f32) + parts[at + 1].astype(f32)).astype(bf16)
            for zb in range(NB):
                block = ((za * NB + zb) * NX + x) * 256
                out[:, block : block + 256] = both[:, zb * 256 : (zb + 1) * 256]


def finish_grad(pos, parts, arrived, gate, up, grad_gate, grad_up, relative, plain):
    c = pos[1]
    total = arrived[...].astype(f32)
    for x in range(NX):
        total = total + parts[x, :128, :].astype(f32)
    relative[...] = total
    for y in range(NY):
        for zh in range(NH):
            for cs in range(NC):
                cr = lax.rem(cs + c, NC)
                first = ((cr * NY + y) * NH + zh) * 8
                to = ((y * NH + zh) * NC + cs) * 8
                plain[to : to + 8, :] = relative[pl.ds(pl.multiple_of(first, 8), 8), :]
    g, u, d = gate[...].astype(f32), up[...].astype(f32), plain[...]
    s = jax.nn.sigmoid(g)
    grad_up[...] = (d * g * s).astype(bf16)
    grad_gate[...] = (d * u * s * (1.0 + g * (1.0 - s))).astype(bf16)


def expand(pos, parts, basis, out, steps):
    for x in range(NX):
        for zl in range(NZ):
            first = zl * 112 + x * 28
            steps[first : first + 28, :] = parts[x, zl * 32 : zl * 32 + 32, :].astype(f32)[:28]
    out[...] = dot(steps[...].astype(bf16), basis[...], ((1,), (1,)))


def body(gate, up, weight, basis, cotangent, moment1, moment2):
    za, c = lax.axis_index("za"), lax.axis_index("c")
    pos = jnp.stack([za, c]).astype(jnp.int32)
    rows, ff = gate.shape
    mine, width = cotangent.shape
    deep, rank = basis.shape
    cols = NB * deep
    own, slot = moment1.shape[0], 32
    square = ("za", "x", "zh")
    line = ("za", "zb")

    hidden, pack = call(
        prepare, 3, [((rows, ff), bf16), ((NA * NX * NH, mine, cols), bf16)], [((rows, ff), f32)]
    )(pos, gate, up, cotangent)

    cot = lax.all_to_all(pack, square, 0, 0, tiled=True).reshape(rows, cols)
    half = deep // NC
    basis_part = spread(lax.dynamic_slice_in_dim(basis, c * half, half, 0), "zb", NB)
    pair = jnp.concatenate([hidden, swap(hidden, "za")], 0)
    weights = spread(weight, "zb", NB)
    cot = spread(cot, "y", NY)
    tile_hidden = spread(pair, "x", NX).reshape(NX * NA * rows, ff)

    tile, parts = call(
        project,
        5,
        [((NX * NA * rows, cols), bf16), ((NX, NZ * slot, rank), bf16)],
        [((cols, rank), bf16), ((NX * NA * rows, rank), bf16), ((ff, rank), f32)],
        flops=2 * 10**9,
    )(pos, cot, swap(cot, "c"), basis_part, swap(basis_part, "c"), tile_hidden)

    parts = lax.all_to_all(parts, "x", 0, 0, tiled=True).astype(f32).sum(0).astype(bf16)
    parts = lax.all_to_all(parts, line, 0, 0, tiled=True).reshape(NZ, slot, rank)
    projected = parts.astype(f32).sum(0)[:own]
    moment1_new = 0.9 * moment1 + 0.1 * projected
    moment2_new = 0.999 * moment2 + 0.001 * projected * projected
    step = (moment1_new / corr_first / (jnp.sqrt(moment2_new / corr_second) + 1e-08)).astype(bf16)
    step = jnp.pad(step, ((0, slot - own), (0, 0)))
    steps = spread(spread(step, line, NZ).reshape(NZ * slot, rank), "x", NX)
    (expansion,) = call(
        expand, 2, [((ff, deep), f32)], [((ff, rank), f32)], flops=3 * 10**8
    )(pos, steps, basis)

    (partial,) = call(backward, 2, [((NX, NA * rows, ff), bf16)], flops=2 * 10**9)(
        pos, tile, weights
    )
    partial = lax.all_to_all(partial, "x", 0, 0, tiled=True)
    arrived = swap(partial[:, rows:].astype(f32).sum(0).astype(bf16), "za")
    grad_gate, grad_up = call(
        finish_grad,
        4,
        [((rows, ff), bf16), ((rows, ff), bf16)],
        [((rows, ff), f32), ((rows, ff), f32)],
    )(pos, partial, arrived, gate, up)

    (term,) = call(forward, 2, [((NC, NY, rows, cols), bf16)], flops=2 * 10**9)(
        pos, tile_hidden, weights
    )
    term = (term[0].astype(f32) + swap(term[1], "c").astype(f32)).astype(bf16)
    term = lax.all_to_all(term, "y", 0, 0, tiled=True).astype(f32).sum(0).astype(bf16)
    term = lax.all_to_all(
        term.reshape(NA * NX * NH, mine, cols), square, 0, 0, tiled=True
    )
    (layer_out,) = call(finish_out, 1, [((mine, width), bf16)])(pos, term)
    return (layer_out, grad_gate, grad_up, moment1_new, moment2_new, expansion)


def solution(mesh):
    names = ("za", "zb", "x", "y", "zh", "c")
    fine = Mesh(mesh.devices.reshape(NA, NB, NX, NY, NH, NC), names)
    dp, tensor = ("za", "zb", "x"), ("y", "zh", "c")
    placed = (
        P(dp, tensor),
        P(dp, tensor),
        P(tensor, dp),
        P(dp, None),
        P(dp + tensor, None),
        P(tensor + dp, None),
        P(tensor + dp, None),
    )
    return jax.shard_map(
        body,
        mesh=fine,
        in_specs=placed,
        out_specs=(
            P(dp + tensor, None),
            P(dp, tensor),
            P(dp, tensor),
            P(tensor + dp, None),
            P(tensor + dp, None),
            P(tensor, dp),
        ),
        check_vma=False,
    )
```

time: 882 us -> 340 us (0.39)
  waiting for transfers between devices: 570 us -> 154 us
  blocking collectives: 262 us -> 55 us
  starting transfers between devices: 5.32 us -> 82.7 us
  matrix products: 27.6 us -> 0 us
  Pallas kernels: 0 us -> 18.4 us
  local copies, waits for them, and re-layouts: 2.11 us -> 19.9 us
  between operations: 14.6 us -> 0.88 us
    all_gather x3 -> x0, waiting for transfers between devices: 568 us -> none  [the longest x1 255 us: body(): weight_full = lax.all_gather(weight, 'dp', axis=1, tiled=True)]
    unnamed x1 -> x0, blocking collectives: 138 us -> none
    all_gather x1 -> x0, blocking collectives: 124 us -> none  [body(): step_full = lax.all_gather(step, 'dp', axis=0, tiled=True)]
    all_to_all x0 -> x9, waiting for transfers between devices: none -> 108 us  [the longest x5 71.7 us: spread(): return lax.all_to_all(copies, axes, 0, 0, tiled=True)]
    all_to_all x0 -> x9, starting transfers between devices: none -> 65.7 us  [the longest x5 22.3 us: spread(): return lax.all_to_all(copies, axes, 0, 0, tiled=True)]
    all_to_all x0 -> x3, blocking collectives: none -> 55 us  [the longest x1 19.2 us: spread(): return lax.all_to_all(copies, axes, 0, 0, tiled=True)]
    ppermute x0 -> x5, waiting for transfers between devices: none -> 46.5 us  [swap(): return lax.ppermute(value, axis, [(0, 1), (1, 0)])]
    dot_general x4 -> x0, matrix products: 27.6 us -> none  [the longest x1 11.3 us: body(): lax.dot_general(cotangent_full, weight_full, (((1,), (1,)), ((), ())), pr...]
  transfers between devices with their start and end apart: 8 -> 14, of which waited for: 3 -> 9; matrix products, arithmetic and copies ran while one was open for 19% -> 3% of each run, Pallas kernels for 0% -> 3%
where the time goes in v3:
time: 340 us; the launch traced here: 337 us
  waiting for transfers between devices  154 us (45%)
  starting transfers between devices  82.7 us (24%)
  blocking collectives  55 us (16%)
  local copies, waits for them, and re-layouts  19.9 us (6%)
  Pallas kernels  18.4 us (5%)
  other arithmetic  6.01 us (2%)
    all_to_all x5, waiting for transfers between devices, spread(): return lax.all_to_all(copies, axes, 0, 0, tiled=True)  71.7 us
    ppermute x5, waiting for transfers between devices, swap(): return lax.ppermute(value, axis, [(0, 1), (1, 0)])  46.5 us
    all_to_all x5, starting transfers between devices, spread(): return lax.all_to_all(copies, axes, 0, 0, tiled=True)  22.3 us
    all_to_all x1, blocking collectives, spread(): return lax.all_to_all(copies, axes, 0, 0, tiled=True)  19.2 us
    all_to_all x1, waiting for transfers between devices, body(): cot = lax.all_to_all(pack, square, 0, 0, tiled=True).reshape(rows, cols)  19.1 us
    all_to_all x1, blocking collectives, body(): lax.all_to_all(parts, line, 0, 0, tiled=True).reshape(NZ, slot, rank)  18.8 us
    all_to_all x1, starting transfers between devices, body(): cot = lax.all_to_all(pack, square, 0, 0, tiled=True).reshape(rows, cols)  17.7 us
    all_to_all x1, starting transfers between devices, body(): lax.all_to_all(term.reshape(NA * NX * NH, mine, cols), square, 0, 0, tile...  17.4 us
  transfers between devices with their start and end apart: 14, of which 9 were waited for; matrix products, arithmetic and copies ran while one was open for 3% of the time, Pallas kernels for 3%

profile of v3, /device:TPU:24, one launch (start us, length us, event | category | flops | bytes accessed | tf_op | source)
XLA Modules:
  0.0 336.9 jit_solution(6857484927965988494)
XLA Ops:
  4.8 17.7 %all-to-all-start.4 = ((bf16[16,8,1024]{2,1,0:T(8,128)(2,1)}), bf16[16,8,1024]{2,1,0:T(8,128)(2,1)S(1)}, u32[]{:S(2)}, u32[]{:S(2)}) async-start(bf16[16,8,1024]{2,1,0:T(8,128)(2,1)} %get-tuple-element.13), calls=%async_computation.4 | async-start | bytes 524288 | tf_op jit(solution)/shard_map/all_to_all | solution.py:173
  23.4 19.1 %all-to-all-done.4 = bf16[16,8,1024]{2,1,0:T(8,128)(2,1)S(1)} async-done(((bf16[16,8,1024]{2,1,0:T(8,128)(2,1)}), bf16[16,8,1024]{2,1,0:T(8,128)(2,1)S(1)}, u32[]{:S(2)}, u32[]{:S(2)}) %all-to-all-start.4) | async-done | bytes 262176 | tf_op jit(solution)/shard_map/all_to_all | solution.py:173
  42.5 19.2 %all_to_all.64.basis_own = bf16[4,128,512]{2,1,0:T(8,128)(2,1)S(1)} all-to-all(bf16[4,128,512]{2,1,0:T(8,128)(2,1)S(1)} %broadcast_in_dim.20), channel_id=1, replica_groups=mesh['za'=2,'zb'=4,'x'=4,'y'=4,'zh'=2,'c'=2] {'zb'}, dimensions={0} | all-to-all | bytes 1048576 | tf_op jit(solution)/shard_map/all_to_all | solution.py:20
  62.9 4.7 %all-to-all-start.5 = ((bf16[4,128,1024]{2,1,0:T(8,128)(2,1)}), bf16[4,128,1024]{2,1,0:T(8,128)(2,1)S(1)}, u32[]{:S(2)}, u32[]{:S(2)}) async-start(bf16[4,128,1024]{2,1,0:T(8,128)(2,1)} %broadcast_in_dim.19), calls=%async_computation.5 | async-start | bytes 2097152 | tf_op jit(solution)/shard_map/all_to_all | solution.py:20
  70.6 22.0 %collective-permute-done = bf16[128,896]{1,0:T(8,128)(2,1)S(1)} collective-permute-done((bf16[128,896]{1,0:T(8,128)(2,1)S(1)}, bf16[128,896]{1,0:T(8,128)(2,1)S(1)}, u32[]{:S(2)}, u32[]{:S(2)}) %collective-permute-start) | collective-permute-done | bytes 229408 | tf_op jit(solution)/shard_map/ppermute | solution.py:24
  94.0 4.1 %all-to-all-start = ((bf16[4,256,896]{2,1,0:T(8,128)(2,1)}), bf16[4,256,896]{2,1,0:T(8,128)(2,1)S(1)}, u32[]{:S(2)}, u32[]{:S(2)}) async-start(bf16[4,256,896]{2,1,0:T(8,128)(2,1)} %broadcast_in_dim.16), calls=%async_computation | async-start | bytes 3670016 | tf_op jit(solution)/shard_map/all_to_all | solution.py:20
  102.5 19.4 %all-to-all-done = bf16[4,256,896]{2,1,0:T(8,128)(2,1)S(1)} async-done(((bf16[4,256,896]{2,1,0:T(8,128)(2,1)}), bf16[4,256,896]{2,1,0:T(8,128)(2,1)S(1)}, u32[]{:S(2)}, u32[]{:S(2)}) %all-to-all-start) | async-done | bytes 1835040 | tf_op jit(solution)/shard_map/all_to_all | solution.py:20
  121.9 5.1 %shard_map.121 = (bf16[1024,1024]{1,0:T(8,128)(2,1)S(1)}, bf16[4,256,512]{2,1,0:T(8,128)(2,1)S(1)}) custom-call(s32[2]{0:T(128)S(1)} %pad_add_fusion.pos, bf16[4,128,1024]{2,1,0:T(8,128)(2,1)S(1)} %all-to-all-done.5.cot_own, bf16[4,128,1024]{2,1,0:T(8,128)(2,1)} %collective-permute-done.2.cot_other, bf16[4,128,512]{2,1,0:T(8,128)(2,1)S(1)} %all_to_all.64.basis_own, ...), custom_call_target="tpu_custom_call" | custom-call | flops 2000000000 | bytes 4194304 | tf_op jit(solution)/shard_map/pallas_call | solution.py:181
  128.4 16.9 %all_to_all.65 = bf16[4,256,512]{2,1,0:T(8,128)(2,1)S(1)} all-to-all(bf16[4,256,512]{2,1,0:T(8,128)(2,1)S(1)} %get-tuple-element.17), channel_id=1, replica_groups=mesh['za'=2,'zb'=4,'x'=4,'y'=4,'zh'=2,'c'=2] {'x'}, dimensions={0} | all-to-all | bytes 2097152 | tf_op jit(solution)/shard_map/all_to_all | solution.py:189
  145.6 18.8 %all_to_all.66 = bf16[8,32,512]{2,1,0:T(8,128)(2,1)S(1)} all-to-all(bf16[8,32,512]{2,1,0:T(8,128)(2,1)S(1)} %bitcast.19), channel_id=1, replica_groups=mesh['za'=2,'zb'=4,'x'=4,'y'=4,'zh'=2,'c'=2] {'za','zb'}, dimensions={0} | all-to-all | bytes 524288 | tf_op jit(solution)/shard_map/all_to_all | solution.py:190
  165.8 3.7 %all-to-all-start.1 = ((bf16[4,896,256]{2,1,0:T(8,128)(2,1)}), bf16[4,896,256]{2,1,0:T(8,128)(2,1)S(1)}, u32[]{:S(2)}, u32[]{:S(2)}) async-start(bf16[4,896,256]{2,1,0:T(8,128)(2,1)} %broadcast_in_dim.17), calls=%async_computation.1 | async-start | bytes 3670016 | tf_op jit(solution)/shard_map/all_to_all | solution.py:20
  170.3 38.5 %all-to-all-done.1.weight = bf16[4,896,256]{2,1,0:T(8,128)(2,1)S(1)} async-done(((bf16[4,896,256]{2,1,0:T(8,128)(2,1)}), bf16[4,896,256]{2,1,0:T(8,128)(2,1)S(1)}, u32[]{:S(2)}, u32[]{:S(2)}) %all-to-all-start.1) | async-done | bytes 1835040 | tf_op jit(solution)/shard_map/all_to_all | solution.py:20
  210.8 6.2 %all-to-all-start.10 = ((bf16[8,32,512]{2,1,0:T(8,128)(2,1)}), bf16[8,32,512]{2,1,0:T(8,128)(2,1)S(1)}, u32[]{:S(2)}, u32[]{:S(2)}) async-start(bf16[8,32,512]{2,1,0:T(8,128)(2,1)} %broadcast_in_dim.21), calls=%async_computation.10 | async-start | bytes 524288 | tf_op jit(solution)/shard_map/all_to_all | solution.py:20
  220.0 3.5 %shard_map.119 = bf16[2,4,128,1024]{3,2,1,0:T(8,128)(2,1)S(1)} custom-call(s32[2]{0:T(128)S(1)} %pad_add_fusion.pos, bf16[1024,896]{1,0:T(8,128)(2,1)S(1)} %bitcast.15, bf16[4,896,256]{2,1,0:T(8,128)(2,1)S(1)} %copy-done.3), custom_call_target="tpu_custom_call" | custom-call | flops 2000000000 | bytes 4194304 | tf_op jit(solution)/shard_map/pallas_call | solution.py:213
  226.5 5.5 %all-to-all-done.10 = bf16[8,32,512]{2,1,0:T(8,128)(2,1)S(1)} async-done(((bf16[8,32,512]{2,1,0:T(8,128)(2,1)}), bf16[8,32,512]{2,1,0:T(8,128)(2,1)S(1)}, u32[]{:S(2)}, u32[]{:S(2)}) %all-to-all-start.10) | async-done | bytes 262176 | tf_op jit(solution)/shard_map/all_to_all | solution.py:20
  233.1 3.5 %all-to-all-start.11 = ((bf16[4,256,512]{2,1,0:T(8,128)(2,1)}), bf16[4,256,512]{2,1,0:T(8,128)(2,1)S(1)}, u32[]{:S(2)}, u32[]{:S(2)}) async-start(bf16[4,256,512]{2,1,0:T(8,128)(2,1)} %broadcast_in_dim.45), calls=%async_computation.11 | async-start | bytes 2097152 | tf_op jit(solution)/shard_map/all_to_all | solution.py:20
  239.2 8.2 %all-to-all-done.11.parts = bf16[4,256,512]{2,1,0:T(8,128)(2,1)S(1)} async-done(((bf16[4,256,512]{2,1,0:T(8,128)(2,1)}), bf16[4,256,512]{2,1,0:T(8,128)(2,1)S(1)}, u32[]{:S(2)}, u32[]{:S(2)}) %all-to-all-start.11) | async-done | bytes 1048608 | tf_op jit(solution)/shard_map/all_to_all | solution.py:20
  247.5 4.8 %all-to-all-start.2 = ((bf16[4,128,1024]{2,1,0:T(8,128)(2,1)}), bf16[4,128,1024]{2,1,0:T(8,128)(2,1)}, u32[]{:S(2)}, u32[]{:S(2)}) async-start(bf16[4,128,1024]{2,1,0:T(8,128)(2,1)} %fusion), calls=%async_computation.2 | async-start | bytes 2097152 | tf_op jit(solution)/shard_map/all_to_all | solution.py:217
  253.8 3.5 %shard_map.122 = bf16[4,256,896]{2,1,0:T(8,128)(2,1)S(1)} custom-call(s32[2]{0:T(128)S(1)} %pad_add_fusion.pos, bf16[1024,1024]{1,0:T(8,128)(2,1)S(1)} %copy-done.13, bf16[4,896,256]{2,1,0:T(8,128)(2,1)S(1)} %copy-done.4), custom_call_target="tpu_custom_call" | custom-call | flops 2000000000 | bytes 4194304 | tf_op jit(solution)/shard_map/pallas_call | solution.py:201
  261.2 3.6 %all-to-all-start.7 = ((bf16[4,256,896]{2,1,0:T(8,128)(2,1)}), bf16[4,256,896]{2,1,0:T(8,128)(2,1)S(1)}, u32[]{:S(2)}, u32[]{:S(2)}) async-start(bf16[4,256,896]{2,1,0:T(8,128)(2,1)} %copy-done.5), calls=%async_computation.7 | async-start | bytes 3670016 | tf_op jit(solution)/shard_map/all_to_all | solution.py:204
  267.0 14.2 %all-to-all-done.7.parts = bf16[4,256,896]{2,1,0:T(8,128)(2,1)S(1)} async-done(((bf16[4,256,896]{2,1,0:T(8,128)(2,1)}), bf16[4,256,896]{2,1,0:T(8,128)(2,1)S(1)}, u32[]{:S(2)}, u32[]{:S(2)}) %all-to-all-start.7) | async-done | bytes 1835040 | tf_op jit(solution)/shard_map/all_to_all | solution.py:204
  281.1 17.4 %all-to-all-start.3 = ((bf16[16,8,1024]{2,1,0:T(8,128)(2,1)}), bf16[16,8,1024]{2,1,0:T(8,128)(2,1)S(1)}, u32[]{:S(2)}, u32[]{:S(2)}) async-start(bf16[16,8,1024]{2,1,0:T(8,128)(2,1)} %bitcast.16), calls=%async_computation.3 | async-start | bytes 524288 | tf_op jit(solution)/shard_map/all_to_all | solution.py:218
  298.7 7.7 %collective-permute-start.4 = (bf16[128,896]{1,0:T(8,128)(2,1)S(1)}, bf16[128,896]{1,0:T(8,128)(2,1)S(1)}, u32[]{:S(2)}, u32[]{:S(2)}) collective-permute-start(bf16[128,896]{1,0:T(8,128)(2,1)S(1)} %slice_reduce_fusion), channel_id=1, source_target_pairs={{0,256},{256,0},{1,257},{257,1},{2,258},{258,2},{3,259},{259,3},{4... | collective-permute-start | bytes 688136 | tf_op jit(solution)/shard_map/ppermute | solution.py:24
  309.3 24.5 %collective-permute-done.4.arrived = bf16[128,896]{1,0:T(8,128)(2,1)S(1)} collective-permute-done((bf16[128,896]{1,0:T(8,128)(2,1)S(1)}, bf16[128,896]{1,0:T(8,128)(2,1)S(1)}, u32[]{:S(2)}, u32[]{:S(2)}) %collective-permute-start.4) | collective-permute-done | bytes 229408 | tf_op jit(solution)/shard_map/ppermute | solution.py:24
  (65 shorter events, 44.0 us)
Async XLA Ops:
  4.8 37.7 %all-to-all-start.4 = ((bf16[16,8,1024]{2,1,0:T(8,128)(2,1)}), bf16[16,8,1024]{2,1,0:T(8,128)(2,1)S(1)}, u32[]{:S(2)}, u32[]{:S(2)}) async-start(bf16[16,8,1024]{2,1,0:T(8,128)(2,1)} %get-tuple-element.13), calls=%async_computation.4 | async-start | bytes 524288 | tf_op jit(solution)/shard_map/all_to_all | solution.py:173
  62.9 29.8 %all-to-all-start.5 = ((bf16[4,128,1024]{2,1,0:T(8,128)(2,1)}), bf16[4,128,1024]{2,1,0:T(8,128)(2,1)S(1)}, u32[]{:S(2)}, u32[]{:S(2)}) async-start(bf16[4,128,1024]{2,1,0:T(8,128)(2,1)} %broadcast_in_dim.19), calls=%async_computation.5 | async-start | bytes 2097152 | tf_op jit(solution)/shard_map/all_to_all | solution.py:20
  67.5 25.0 %collective-permute-start = (bf16[128,896]{1,0:T(8,128)(2,1)S(1)}, bf16[128,896]{1,0:T(8,128)(2,1)S(1)}, u32[]{:S(2)}, u32[]{:S(2)}) collective-permute-start(bf16[128,896]{1,0:T(8,128)(2,1)S(1)} %get-tuple-element.12), channel_id=1, source_target_pairs={{0,256},{256,0},{1,257},{257,1},{2,258},{258,2},{3,259},{259,3},{4... | collective-permute-start | bytes 688136 | tf_op jit(solution)/shard_map/ppermute | solution.py:24
  94.0 27.8 %all-to-all-start = ((bf16[4,256,896]{2,1,0:T(8,128)(2,1)}), bf16[4,256,896]{2,1,0:T(8,128)(2,1)S(1)}, u32[]{:S(2)}, u32[]{:S(2)}) async-start(bf16[4,256,896]{2,1,0:T(8,128)(2,1)} %broadcast_in_dim.16), calls=%async_computation | async-start | bytes 3670016 | tf_op jit(solution)/shard_map/all_to_all | solution.py:20
  98.2 23.7 %collective-permute-start.2 = (bf16[4,128,1024]{2,1,0:T(8,128)(2,1)S(1)}, bf16[4,128,1024]{2,1,0:T(8,128)(2,1)}, u32[]{:S(2)}, u32[]{:S(2)}) collective-permute-start(bf16[4,128,1024]{2,1,0:T(8,128)(2,1)S(1)} %all-to-all-done.5.cot_own), channel_id=1, source_target_pairs={{0,1},{1,0},{2,3},{3,2},{4,5},{5,4},{6,7},{7,6},{8,9},{9,8},{10,11... | collective-permute-start | bytes 3145736 | tf_op jit(solution)/shard_map/ppermute | solution.py:24
  100.1 21.8 %collective-permute-start.3 = (bf16[4,128,512]{2,1,0:T(8,128)(2,1)S(1)}, bf16[4,128,512]{2,1,0:T(8,128)(2,1)}, u32[]{:S(2)}, u32[]{:S(2)}) collective-permute-start(bf16[4,128,512]{2,1,0:T(8,128)(2,1)S(1)} %all_to_all.64.basis_own), channel_id=1, source_target_pairs={{0,1},{1,0},{2,3},{3,2},{4,5},{5,4},{6,7},{7,6},{8,9},{9,8},{10,11... | collective-permute-start | bytes 1572872 | tf_op jit(solution)/shard_map/ppermute | solution.py:24
  121.9 5.2 %copy-start = (bf16[4,256,896]{2,1,0:T(8,128)(2,1)}, bf16[4,256,896]{2,1,0:T(8,128)(2,1)S(1)}, u32[]{:S(2)}) copy-start(bf16[4,256,896]{2,1,0:T(8,128)(2,1)S(1)} %all-to-all-done) | copy-start | bytes 5505028
  128.4 36.0 %copy-start.14 = (bf16[896,256]{1,0:T(8,128)(2,1)S(1)}, bf16[896,256]{1,0:T(8,128)(2,1)}, u32[]{:S(2)}) copy-start(bf16[896,256]{1,0:T(8,128)(2,1)} %param.9) | copy-start | bytes 1376260
  165.8 3.8 %copy-start.15 = (f32[28,512]{1,0:T(8,128)S(1)}, f32[28,512]{1,0:T(8,128)}, u32[]{:S(2)}) copy-start(f32[28,512]{1,0:T(8,128)} %param.13) | copy-start | bytes 172036
  165.8 3.8 %copy-start.16 = (f32[28,512]{1,0:T(8,128)S(1)}, f32[28,512]{1,0:T(8,128)}, u32[]{:S(2)}) copy-start(f32[28,512]{1,0:T(8,128)} %param.12) | copy-start | bytes 172036
  165.8 43.0 %all-to-all-start.1 = ((bf16[4,896,256]{2,1,0:T(8,128)(2,1)}), bf16[4,896,256]{2,1,0:T(8,128)(2,1)S(1)}, u32[]{:S(2)}, u32[]{:S(2)}) async-start(bf16[4,896,256]{2,1,0:T(8,128)(2,1)} %broadcast_in_dim.17), calls=%async_computation.1 | async-start | bytes 3670016 | tf_op jit(solution)/shard_map/all_to_all | solution.py:20
  210.8 21.2 %all-to-all-start.10 = ((bf16[8,32,512]{2,1,0:T(8,128)(2,1)}), bf16[8,32,512]{2,1,0:T(8,128)(2,1)S(1)}, u32[]{:S(2)}, u32[]{:S(2)}) async-start(bf16[8,32,512]{2,1,0:T(8,128)(2,1)} %broadcast_in_dim.21), calls=%async_computation.10 | async-start | bytes 524288 | tf_op jit(solution)/shard_map/all_to_all | solution.py:20
  217.0 1.5 copy-start.1
  218.5 1.5 copy-start.3
  224.6 12.0 %collective-permute-start.1 = (bf16[4,128,1024]{2,1,0:T(8,128)(2,1)}, bf16[4,128,1024]{2,1,0:T(8,128)(2,1)}, u32[]{:S(2)}, u32[]{:S(2)}) collective-permute-start(bf16[4,128,1024]{2,1,0:T(8,128)(2,1)} %slice_bitcast_fusion), channel_id=1, source_target_pairs={{0,1},{1,0},{2,3},{3,2},{4,5},{5,4},{6,7},{7,6},{8,9},{9,8},{10,11... | collective-permute-start | bytes 3145736 | tf_op jit(solution)/shard_map/ppermute | solution.py:24
  233.1 14.4 %all-to-all-start.11 = ((bf16[4,256,512]{2,1,0:T(8,128)(2,1)}), bf16[4,256,512]{2,1,0:T(8,128)(2,1)S(1)}, u32[]{:S(2)}, u32[]{:S(2)}) async-start(bf16[4,256,512]{2,1,0:T(8,128)(2,1)} %broadcast_in_dim.45), calls=%async_computation.11 | async-start | bytes 2097152 | tf_op jit(solution)/shard_map/all_to_all | solution.py:20
  239.2 13.0 %copy-start.4 = (bf16[4,896,256]{2,1,0:T(8,128)(2,1)S(1)}, bf16[4,896,256]{2,1,0:T(8,128)(2,1)}, u32[]{:S(2)}) copy-start(bf16[4,896,256]{2,1,0:T(8,128)(2,1)} %copy-done.2) | copy-start | bytes 5505028
  247.5 13.7 %all-to-all-start.2 = ((bf16[4,128,1024]{2,1,0:T(8,128)(2,1)}), bf16[4,128,1024]{2,1,0:T(8,128)(2,1)}, u32[]{:S(2)}, u32[]{:S(2)}) async-start(bf16[4,128,1024]{2,1,0:T(8,128)(2,1)} %fusion), calls=%async_computation.2 | async-start | bytes 2097152 | tf_op jit(solution)/shard_map/all_to_all | solution.py:217
  252.3 1.6 copy-start.13
  261.2 20.0 %all-to-all-start.7 = ((bf16[4,256,896]{2,1,0:T(8,128)(2,1)}), bf16[4,256,896]{2,1,0:T(8,128)(2,1)S(1)}, u32[]{:S(2)}, u32[]{:S(2)}) async-start(bf16[4,256,896]{2,1,0:T(8,128)(2,1)} %copy-done.5), calls=%async_computation.7 | async-start | bytes 3670016 | tf_op jit(solution)/shard_map/all_to_all | solution.py:204
  267.0 66.8 %copy-start.7 = (bf16[128,896]{1,0:T(8,128)(2,1)S(1)}, bf16[128,896]{1,0:T(8,128)(2,1)}, u32[]{:S(2)}) copy-start(bf16[128,896]{1,0:T(8,128)(2,1)} %gate.3) | copy-start | bytes 688132
  281.1 54.5 %all-to-all-start.3 = ((bf16[16,8,1024]{2,1,0:T(8,128)(2,1)}), bf16[16,8,1024]{2,1,0:T(8,128)(2,1)S(1)}, u32[]{:S(2)}, u32[]{:S(2)}) async-start(bf16[16,8,1024]{2,1,0:T(8,128)(2,1)} %bitcast.16), calls=%async_computation.3 | async-start | bytes 524288 | tf_op jit(solution)/shard_map/all_to_all | solution.py:218
  298.6 35.3 %copy-start.9 = (bf16[128,896]{1,0:T(8,128)(2,1)S(1)}, bf16[128,896]{1,0:T(8,128)(2,1)}, u32[]{:S(2)}) copy-start(bf16[128,896]{1,0:T(8,128)(2,1)} %up.3) | copy-start | bytes 688132
  298.7 35.1 %collective-permute-start.4 = (bf16[128,896]{1,0:T(8,128)(2,1)S(1)}, bf16[128,896]{1,0:T(8,128)(2,1)S(1)}, u32[]{:S(2)}, u32[]{:S(2)}) collective-permute-start(bf16[128,896]{1,0:T(8,128)(2,1)S(1)} %slice_reduce_fusion), channel_id=1, source_target_pairs={{0,256},{256,0},{1,257},{257,1},{2,258},{258,2},{3,259},{259,3},{4... | collective-permute-start | bytes 688136 | tf_op jit(solution)/shard_map/ppermute | solution.py:24
  (7 other events, 7.6 us)

commit v4 on v3

v4 whole, which is shorter than its diff:
```python
import jax
import jax.numpy as jnp
from jax import lax
from jax.experimental import pallas as pl
from jax.experimental.pallas import tpu as pltpu
from jax.sharding import Mesh, PartitionSpec as P

corr_first = 1.0 - 0.9**10
corr_second = 1.0 - 0.999**10

NA, NB, NX, NY, NH, NC = 2, 4, 4, 4, 2, 2
NZ = NA * NB
ORDER = (0, 1, 3, 2)
RING = [(ORDER[i], ORDER[(i + 1) % NB]) for i in range(NB)]
bf16, f32 = jnp.bfloat16, jnp.float32
VMEM = pl.BlockSpec(memory_space=pltpu.VMEM)
SMEM = pl.BlockSpec(memory_space=pltpu.SMEM)


def shift(value, axis, size, by):
    return lax.ppermute(value, axis, [(i, (i - by) % size) for i in range(size)])


def swap(value, axis):
    return lax.ppermute(value, axis, [(0, 1), (1, 0)])


def dot(a, b, contract):
    return lax.dot_general(a, b, (contract, ((), ())), preferred_element_type=f32)


def call(kernel, n_in, outs, scratch=(), flops=0, limit=32):
    return pl.pallas_call(
        kernel,
        out_shape=tuple(jax.ShapeDtypeStruct(*o) for o in outs),
        in_specs=[SMEM] + [VMEM] * n_in,
        out_specs=tuple(VMEM for _ in outs),
        scratch_shapes=[pltpu.VMEM(*s) for s in scratch],
        compiler_params=pltpu.CompilerParams(vmem_limit_bytes=limit << 20),
        cost_estimate=pl.CostEstimate(flops=flops, bytes_accessed=4 << 20, transcendentals=0),
    )


def ring_block(zb, hop):
    place = ((zb ^ (zb >> 1)) - hop) & (NB - 1)
    return place ^ (place >> 1)


def prepare(pos, gate, up, cot, weight, basis, hidden, pack, both, plain):
    y, c = pos[2], pos[3]
    for za in range(NA):
        for x in range(NX):
            for r in range(NB):
                block = ((za * NB + ring_block(pos[4], r)) * NX + x) * 256
                piece = cot[:, pl.ds(pl.multiple_of(block, 256), 256)]
                for zh in range(NH):
                    pack[(za * NX + x) * NH + zh, :, r * 256 : (r + 1) * 256] = piece
    both[:896, :] = weight[...]
    both[896:1152, :] = basis[:, :256]
    both[1152:, :] = basis[:, 256:]
    g = gate[...].astype(f32)
    plain[...] = g * jax.nn.sigmoid(g) * up[...].astype(f32)
    for cr in range(NC):
        for yr in range(NY):
            first = (lax.rem(y + yr, NY) * 4 + lax.rem(c + cr, NC)) * 8
            pair = [plain[pl.ds(pl.multiple_of(first + zh * 16, 8), 8), :] for zh in range(NH)]
            hidden[pl.ds((cr * NY + yr) * 16, 16), :] = jnp.concatenate(pair, 0).astype(bf16)


def project(pos, *refs):
    cots, boths, hiddens = refs[:8], refs[8:12], refs[12:16]
    tile, outs, reduced, total, blocks = refs[16], refs[17:21], *refs[21:]
    za, x = pos[0], pos[1]
    for xr in range(NX):
        for ar in range(NA):
            at = (lax.rem(za + ar, NA) * NX + lax.rem(x + xr, NX)) * 16
            at = pl.ds(pl.multiple_of(at, 16), 16)
            for piece in range(8):
                to = (xr * NA + ar) * 128 + piece * 16
                tile[to : to + 16, :] = cots[piece][at, :]

    def rows(step, _):
        at = pl.ds(pl.multiple_of(step * 256, 256), 256)
        for side in range(2):
            low = None
            for r in range(NB):
                part = boths[r][896 + side * 256 : 1152 + side * 256, :]
                more = dot(tile[at, r * 256 : (r + 1) * 256], part, ((1,), (0,)))
                low = more if low is None else low + more
            reduced[at, side * 256 : (side + 1) * 256] = low.astype(bf16)
        return 0

    lax.fori_loop(0, 4, rows, 0)
    for xr in range(NX):
        more = dot(hiddens[xr][...], reduced[xr * 256 : (xr + 1) * 256, :], ((0,), (0,)))
        total[...] = more if xr == 0 else total[...] + more
    spare = jnp.zeros((4, total.shape[1]), f32)
    for xs in range(NX):
        for zl in range(NZ):
            first = zl * 112 + xs * 28
            block = jnp.concatenate([total[first : first + 28, :], spare], 0)
            blocks[xs, zl * 32 : zl * 32 + 32, :] = block.astype(bf16)
    for xr, out in enumerate(outs):
        out[...] = blocks[lax.rem(x + xr, NX)]


def backward(pos, tile, b0, b1, b2, b3, *outs):
    for xr, out in enumerate(outs):
        total = None
        for r, both in enumerate((b0, b1, b2, b3)):
            part = tile[xr * 256 : (xr + 1) * 256, r * 256 : (r + 1) * 256]
            more = dot(part, both[:896, :], ((1,), (1,)))
            total = more if total is None else total + more
        out[...] = total.astype(bf16)


def forward(pos, b0, b1, b2, b3, h0, h1, h2, h3, o0, o1, o2, o3, leave):
    za, x = pos[0], pos[1]
    for xr, hidden in enumerate((h0, h1, h2, h3)):
        for r, both in enumerate((b0, b1, b2, b3)):
            term = dot(hidden[...], both[:896, :], ((1,), (0,))).astype(bf16)
            for ar in range(NA):
                to = (lax.rem(za + ar, NA) * NX + lax.rem(x + xr, NX)) * 16
                to = pl.ds(pl.multiple_of(to, 16), 16)
                for piece in range(8):
                    first = ar * 128 + piece * 16
                    block = term[first : first + 16, :]
                    if piece < NY:
                        (o0, o1, o2, o3)[piece][to, r * 256 : (r + 1) * 256] = block
                    else:
                        leave[piece - NY, to, r * 256 : (r + 1) * 256] = block


def finish_out(pos, parts, out):
    for za in range(NA):
        for x in range(NX):
            at = (za * NX + x) * NH
            pair = (parts[at].astype(f32) + parts[at + 1].astype(f32)).astype(bf16)
            for r in range(NB):
                block = ((za * NB + ring_block(pos[4], r)) * NX + x) * 256
                to = pl.ds(pl.multiple_of(block, 256), 256)
                out[:, to] = pair[:, r * 256 : (r + 1) * 256]


def finish_grad(pos, p0, p1, p2, p3, arrived, gate, up, grad_gate, grad_up, relative, plain):
    y, c = pos[2], pos[3]
    total = arrived[...].astype(f32)
    for part in (p0, p1, p2, p3):
        total = total + part[:128, :].astype(f32)
    relative[...] = total
    for ys in range(NY):
        yr = lax.rem(ys - y + NY, NY)
        for zh in range(NH):
            for cs in range(NC):
                cr = lax.rem(cs + c, NC)
                first = ((cr * NY + yr) * NH + zh) * 8
                to = ((ys * NH + zh) * NC + cs) * 8
                plain[to : to + 8, :] = relative[pl.ds(pl.multiple_of(first, 8), 8), :]
    g, u, d = gate[...].astype(f32), up[...].astype(f32), plain[...]
    s = jax.nn.sigmoid(g)
    grad_up[...] = (d * g * s).astype(bf16)
    grad_gate[...] = (d * u * s * (1.0 + g * (1.0 - s))).astype(bf16)


def expand(pos, s0, s1, s2, s3, basis, out, pieces, steps):
    x = pos[1]
    for xr, piece in enumerate((s0, s1, s2, s3)):
        pieces[lax.rem(x + xr, NX)] = piece[...].astype(f32)
    for xs in range(NX):
        for zl in range(NZ):
            first = zl * 112 + xs * 28
            steps[first : first + 28, :] = pieces[xs, zl * 32 : zl * 32 + 28, :]
    out[...] = dot(steps[...].astype(bf16), basis[...], ((1,), (1,)))


def body(gate, up, weight, basis, cotangent, moment1, moment2):
    pos = jnp.stack([lax.axis_index(a) for a in ("za", "x", "y", "c", "zb")]).astype(jnp.int32)
    rows, ff = gate.shape
    mine, width = cotangent.shape
    deep, rank = basis.shape
    cols = NB * deep
    own, slot = moment1.shape[0], 32
    square = ("za", "x", "zh")
    line = ("za", "zb")

    hidden, pack, both = call(
        prepare,
        5,
        [
            ((rows, ff), bf16),
            ((NA * NX * NH, mine, cols), bf16),
            ((ff + 2 * deep, deep), bf16),
        ],
        [((rows, ff), f32)],
    )(pos, gate, up, cotangent, weight, basis)

    cot = lax.all_to_all(pack, square, 0, 0, tiled=True).reshape(rows, cols)
    pair = jnp.concatenate([hidden, swap(hidden, "za")], 0)
    boths = [both]
    for _ in range(1, NB):
        boths.append(lax.ppermute(boths[-1], "zb", RING))
    hiddens = [pair] + [shift(pair, "x", NX, by) for by in range(1, NX)]
    cots = [cot] + [shift(cot, "y", NY, by) for by in range(1, NY)]
    cots = cots + [swap(piece, "c") for piece in cots]

    tile, *parts = call(
        project,
        16,
        [((NX * NA * rows, cols), bf16)] + [((NZ * slot, rank), bf16)] * NX,
        [((NX * NA * rows, rank), bf16), ((ff, rank), f32), ((NX, NZ * slot, rank), bf16)],
        flops=2 * 10**9,
    )(pos, *cots, *boths, *hiddens)

    total = parts[0].astype(f32)
    for by in range(1, NX):
        total = total + shift(parts[by], "x", NX, -by).astype(f32)
    total = lax.all_to_all(total.astype(bf16), line, 0, 0, tiled=True).reshape(NZ, slot, rank)
    projected = total.astype(f32).sum(0)[:own]
    moment1_new = 0.9 * moment1 + 0.1 * projected
    moment2_new = 0.999 * moment2 + 0.001 * projected * projected
    step = (moment1_new / corr_first / (jnp.sqrt(moment2_new / corr_second) + 1e-08)).astype(bf16)
    step = jnp.pad(step, ((0, slot - own), (0, 0)))
    step = jnp.broadcast_to(step[None], (NZ, slot, rank))
    step = lax.all_to_all(step, line, 0, 0, tiled=True).reshape(NZ * slot, rank)
    steps = [step] + [shift(step, "x", NX, by) for by in range(1, NX)]
    (expansion,) = call(
        expand,
        5,
        [((ff, deep), f32)],
        [((NX, NZ * slot, rank), f32), ((ff, rank), f32)],
        flops=3 * 10**8,
    )(pos, *steps, basis)

    partial = call(backward, 5, [((NA * rows, ff), bf16)] * NX, flops=2 * 10**9)(
        pos, tile, *boths
    )
    partials = [partial[0]] + [shift(partial[by], "x", NX, -by) for by in range(1, NX)]
    leave = partials[0][rows:].astype(f32)
    for part in partials[1:]:
        leave = leave + part[rows:].astype(f32)
    arrived = swap(leave.astype(bf16), "za")
    grad_gate, grad_up = call(
        finish_grad,
        7,
        [((rows, ff), bf16), ((rows, ff), bf16)],
        [((rows, ff), f32), ((rows, ff), f32)],
    )(pos, *partials, arrived, gate, up)

    *term, leave = call(
        forward, 8, [((rows, cols), bf16)] * NY + [((NY, rows, cols), bf16)], flops=2 * 10**9
    )(pos, *boths, *hiddens)
    arrived = swap(leave, "c")
    term = [(term[yr].astype(f32) + arrived[yr].astype(f32)).astype(bf16) for yr in range(NY)]
    total = term[0].astype(f32)
    for by in range(1, NY):
        total = total + shift(term[by], "y", NY, -by).astype(f32)
    total = total.astype(bf16).reshape(NA * NX * NH, mine, cols)
    total = lax.all_to_all(total, square, 0, 0, tiled=True)
    (layer_out,) = call(finish_out, 1, [((mine, width), bf16)])(pos, total)
    return (layer_out, grad_gate, grad_up, moment1_new, moment2_new, expansion)


def solution(mesh):
    names = ("za", "zb", "x", "y", "zh", "c")
    fine = Mesh(mesh.devices.reshape(NA, NB, NX, NY, NH, NC), names)
    dp, tensor = ("za", "zb", "x"), ("y", "zh", "c")
    placed = (
        P(dp, tensor),
        P(dp, tensor),
        P(tensor, dp),
        P(dp, None),
        P(dp + tensor, None),
        P(tensor + dp, None),
        P(tensor + dp, None),
    )
    return jax.shard_map(
        body,
        mesh=fine,
        in_specs=placed,
        out_specs=(
            P(dp + tensor, None),
            P(dp, tensor),
            P(dp, tensor),
            P(tensor + dp, None),
            P(tensor + dp, None),
            P(tensor, dp),
        ),
        check_vma=False,
    )
```

time: 340 us -> 278 us (0.82)
  waiting for transfers between devices: 154 us -> 72.7 us
  starting transfers between devices: 82.7 us -> 162 us
  blocking collectives: 55 us -> 0 us
  local copies, waits for them, and re-layouts: 19.9 us -> 11.9 us
    ppermute x0 -> x21, starting transfers between devices: none -> 88.2 us  [the longest x18 57.4 us: shift(): lax.ppermute(value, axis, [(i, (i - by) % size) for i in range(size)])]
    all_to_all x8 -> x3, waiting for transfers between devices: 88.4 us -> 7.78 us  [the longest x1 7.78 us: body(): lax.all_to_all(total.astype(bf16), line, 0, 0, tiled=True)]
    all_to_all x3 -> x0, blocking collectives: 55 us -> none  [the longest x1 19.2 us: spread(): return lax.all_to_all(copies, axes, 0, 0, tiled=True)]
    ppermute x0 -> x21, waiting for transfers between devices: none -> 36 us  [the longest x18 35.3 us: shift(): lax.ppermute(value, axis, [(i, (i - by) % size) for i in range(size)])]
    all_to_all x8 -> x3, starting transfers between devices: 48 us -> 28.1 us  [the longest x1 15.7 us: body(): total = lax.all_to_all(total, square, 0, 0, tiled=True)]
    all_to_all x1, waiting for transfers between devices: 19.1 us -> 0.01 us  [body(): cot = lax.all_to_all(pack, square, 0, 0, tiled=True).reshape(rows, cols)]
    ppermute x5 -> x7, waiting for transfers between devices: 46.5 us -> 28.9 us  [swap(): return lax.ppermute(value, axis, [(0, 1), (1, 0)])]
    ppermute x5 -> x7, starting transfers between devices: 17 us -> 29.2 us  [swap(): return lax.ppermute(value, axis, [(0, 1), (1, 0)])]
  transfers between devices with their start and end apart: 14 -> 32, of which waited for: 9 -> 15; matrix products, arithmetic and copies ran while one was open for 3% -> 2% of each run, Pallas kernels for 3% -> 4%
where the time goes in v4:
time: 278 us; the launch traced here: 273 us
  starting transfers between devices  162 us (58%)
  waiting for transfers between devices  72.7 us (26%)
  Pallas kernels  18.8 us (7%)
  local copies, waits for them, and re-layouts  11.9 us (4%)
  other arithmetic  5.87 us (2%)
    ppermute x18, starting transfers between devices, shift(): lax.ppermute(value, axis, [(i, (i - by) % size) for i in range(size)])  57.4 us
    ppermute x18, waiting for transfers between devices, shift(): lax.ppermute(value, axis, [(i, (i - by) % size) for i in range(size)])  35.3 us
    ppermute x3, starting transfers between devices, body(): boths.append(lax.ppermute(boths[-1], 'zb', RING))  30.8 us
    ppermute x7, starting transfers between devices, swap(): return lax.ppermute(value, axis, [(0, 1), (1, 0)])  29.2 us
    ppermute x7, waiting for transfers between devices, swap(): return lax.ppermute(value, axis, [(0, 1), (1, 0)])  28.9 us
    all_to_all x1, starting transfers between devices, body(): cot = lax.all_to_all(pack, square, 0, 0, tiled=True).reshape(rows, cols)  16.8 us
    all_to_all x1, starting transfers between devices, body(): total = lax.all_to_all(total, square, 0, 0, tiled=True)  15.7 us
    unnamed x33, local copies, waits for them, and re-layouts  11 us
  transfers between devices with their start and end apart: 32, of which 15 were waited for; matrix products, arithmetic and copies ran while one was open for 2% of the time, Pallas kernels for 4%

profile of v4, /device:TPU:24, one launch (start us, length us, event | category | flops | bytes accessed | tf_op | source)
XLA Modules:
  0.0 272.5 jit_solution(17462026244638183843)
XLA Ops:
  6.9 3.8 %collective-permute-start = (bf16[1408,256]{1,0:T(8,128)(2,1)S(1)}, bf16[1408,256]{1,0:T(8,128)(2,1)S(1)}, u32[]{:S(2)}, u32[]{:S(2)}) collective-permute-start(bf16[1408,256]{1,0:T(8,128)(2,1)S(1)} %get-tuple-element.25.b0.refs_8_), channel_id=1, source_target_pairs={{0,64},{64,192},{192,128},{128,0},{1,65},{65,193},{193,129},{129,1... | collective-permute-start | bytes 2162696 | tf_op jit(solution)/shard_map/ppermute | solution.py:201
  10.7 16.8 %all-to-all-start.1 = ((bf16[16,8,1024]{2,1,0:T(8,128)(2,1)}), bf16[16,8,1024]{2,1,0:T(8,128)(2,1)S(1)}, u32[]{:S(2)}, u32[]{:S(2)}) async-start(bf16[16,8,1024]{2,1,0:T(8,128)(2,1)} %get-tuple-element.32), calls=%async_computation.1 | async-start | bytes 524288 | tf_op jit(solution)/shard_map/all_to_all | solution.py:197
  28.2 6.4 %collective-permute-start.1 = (bf16[1408,256]{1,0:T(8,128)(2,1)S(1)}, bf16[1408,256]{1,0:T(8,128)(2,1)S(1)}, u32[]{:S(2)}, u32[]{:S(2)}) collective-permute-start(bf16[1408,256]{1,0:T(8,128)(2,1)S(1)} %collective-permute-done.b1.refs_9_), channel_id=1, source_target_pairs={{0,64},{64,192},{192,128},{128,0},{1,65},{65,193},{193,129},{129,1... | collective-permute-start | bytes 2162696 | tf_op jit(solution)/shard_map/ppermute | solution.py:201
  34.6 12.3 %collective-permute-start.3 = (bf16[128,896]{1,0:T(8,128)(2,1)S(1)}, bf16[128,896]{1,0:T(8,128)(2,1)S(1)}, u32[]{:S(2)}, u32[]{:S(2)}) collective-permute-start(bf16[128,896]{1,0:T(8,128)(2,1)S(1)} %get-tuple-element.26), channel_id=1, source_target_pairs={{0,256},{256,0},{1,257},{257,1},{2,258},{258,2},{3,259},{259,3},{4... | collective-permute-start | bytes 688136 | tf_op jit(solution)/shard_map/ppermute | solution.py:25
  46.9 10.9 %collective-permute-done.3 = bf16[128,896]{1,0:T(8,128)(2,1)S(1)} collective-permute-done((bf16[128,896]{1,0:T(8,128)(2,1)S(1)}, bf16[128,896]{1,0:T(8,128)(2,1)S(1)}, u32[]{:S(2)}, u32[]{:S(2)}) %collective-permute-start.3) | collective-permute-done | bytes 229408 | tf_op jit(solution)/shard_map/ppermute | solution.py:25
  57.8 3.7 %collective-permute-start.6 = (bf16[256,896]{1,0:T(8,128)(2,1)S(1)}, bf16[256,896]{1,0:T(8,128)(2,1)}, u32[]{:S(2)}, u32[]{:S(2)}) collective-permute-start(bf16[256,896]{1,0:T(8,128)(2,1)S(1)} %constant_dynamic-update-slice_fusion.h0.refs_12_), channel_id=1, source_target_pairs={{0,16},{16,32},{32,48},{48,0},{1,17},{17,33},{33,49},{49,1},{2,18}... | collective-permute-start | bytes 1376264 | tf_op jit(solution)/shard_map/ppermute | solution.py:21
  61.6 4.7 %collective-permute-start.5 = (bf16[256,896]{1,0:T(8,128)(2,1)S(1)}, bf16[256,896]{1,0:T(8,128)(2,1)}, u32[]{:S(2)}, u32[]{:S(2)}) collective-permute-start(bf16[256,896]{1,0:T(8,128)(2,1)S(1)} %constant_dynamic-update-slice_fusion.h0.refs_12_), channel_id=1, source_target_pairs={{0,32},{16,48},{32,0},{48,16},{1,33},{17,49},{33,1},{49,17},{2,34}... | collective-permute-start | bytes 1376264 | tf_op jit(solution)/shard_map/ppermute | solution.py:21
  69.7 20.5 %collective-permute-start.2 = (bf16[1408,256]{1,0:T(8,128)(2,1)S(1)}, bf16[1408,256]{1,0:T(8,128)(2,1)}, u32[]{:S(2)}, u32[]{:S(2)}) collective-permute-start(bf16[1408,256]{1,0:T(8,128)(2,1)S(1)} %collective-permute-done.1.b2.refs_10_), channel_id=1, source_target_pairs={{0,64},{64,192},{192,128},{128,0},{1,65},{65,193},{193,129},{129,1... | collective-permute-start | bytes 2162696 | tf_op jit(solution)/shard_map/ppermute | solution.py:201
  92.4 4.5 %collective-permute-start.12 = (bf16[128,1024]{1,0:T(8,128)(2,1)S(1)}, bf16[128,1024]{1,0:T(8,128)(2,1)S(1)}, u32[]{:S(2)}, u32[]{:S(2)}) collective-permute-start(bf16[128,1024]{1,0:T(8,128)(2,1)S(1)} %bitcast.35), channel_id=1, source_target_pairs={{0,8},{4,12},{8,0},{12,4},{1,9},{5,13},{9,1},{13,5},{2,10},{6,14},... | collective-permute-start | bytes 786440 | tf_op jit(solution)/shard_map/ppermute | solution.py:21
  111.8 4.6 %shard_map.121 = (bf16[1024,1024]{1,0:T(8,128)(2,1)S(1)}, bf16[256,512]{1,0:T(8,128)(2,1)S(1)}, bf16[256,512]{1,0:T(8,128)(2,1)S(1)}, bf16[256,512]{1,0:T(8,128)(2,1)S(1)}, bf16[256,512]{1,0:T(8,128)(2,1)S(1)}) custom-call(s32[5]{0:T(128)S(1)} %stack.23.pos, bf16[128,1024]{1,0:T(8,128)(2,1)S(1)} %bitcast.38, ...), custom_call_target="tpu_custom_call" | custom-call | flops 2000000000 | bytes 4194304 | tf_op jit(solution)/shard_map/pallas_call | solution.py:206
  126.7 8.0 %collective-permute-done.22 = bf16[256,512]{1,0:T(8,128)(2,1)S(1)} collective-permute-done((bf16[256,512]{1,0:T(8,128)(2,1)S(1)}, bf16[256,512]{1,0:T(8,128)(2,1)S(1)}, u32[]{:S(2)}, u32[]{:S(2)}) %collective-permute-start.22) | collective-permute-done | bytes 262176 | tf_op jit(solution)/shard_map/ppermute | solution.py:21
  138.2 7.3 %all-to-all-start.2 = ((bf16[8,32,512]{2,1,0:T(8,128)(2,1)}), bf16[8,32,512]{2,1,0:T(8,128)(2,1)S(1)}, u32[]{:S(2)}, u32[]{:S(2)}) async-start(bf16[8,32,512]{2,1,0:T(8,128)(2,1)} %bitcast.11), calls=%async_computation.2 | async-start | bytes 524288 | tf_op jit(solution)/shard_map/all_to_all | solution.py:217
  147.7 3.9 %shard_map.119 = (bf16[128,1024]{1,0:T(8,128)(2,1)S(1)}, bf16[128,1024]{1,0:T(8,128)(2,1)S(1)}, bf16[128,1024]{1,0:T(8,128)(2,1)S(1)}, bf16[128,1024]{1,0:T(8,128)(2,1)S(1)}, bf16[4,128,1024]{2,1,0:T(8,128)(2,1)S(1)}) custom-call(s32[5]{0:T(128)S(1)} %stack.23.pos, bf16[1408,256]{1,0:T(8,128)(2,1)S(1)} %get-tuple-element.25.b0.refs_8_, ...), custom_call_target="tpu_custom_call" | custom-call | flops 2000000000 | bytes 4194304 | tf_op jit(solution)/shard_map/pallas_call | solution.py:249
  153.6 7.8 %all-to-all-done.2 = bf16[8,32,512]{2,1,0:T(8,128)(2,1)S(1)} async-done(((bf16[8,32,512]{2,1,0:T(8,128)(2,1)}), bf16[8,32,512]{2,1,0:T(8,128)(2,1)S(1)}, u32[]{:S(2)}, u32[]{:S(2)}) %all-to-all-start.2) | async-done | bytes 262176 | tf_op jit(solution)/shard_map/all_to_all | solution.py:217
  163.7 5.1 %all-to-all-start.3 = ((bf16[8,32,512]{2,1,0:T(8,128)(2,1)}), bf16[8,32,512]{2,1,0:T(8,128)(2,1)S(1)}, u32[]{:S(2)}, u32[]{:S(2)}) async-start(bf16[8,32,512]{2,1,0:T(8,128)(2,1)} %broadcast_in_dim.2), calls=%async_computation.3 | async-start | bytes 524288 | tf_op jit(solution)/shard_map/all_to_all | solution.py:224
  170.2 3.6 %collective-permute-start.8 = (bf16[128,1024]{1,0:T(8,128)(2,1)S(1)}, bf16[128,1024]{1,0:T(8,128)(2,1)S(1)}, u32[]{:S(2)}, u32[]{:S(2)}) collective-permute-start(bf16[128,1024]{1,0:T(8,128)(2,1)S(1)} %get-tuple-element.47), channel_id=1, source_target_pairs={{0,4},{4,8},{8,12},{12,0},{1,5},{5,9},{9,13},{13,1},{2,6},{6,10},{... | collective-permute-start | bytes 786440 | tf_op jit(solution)/shard_map/ppermute | solution.py:21
  179.5 10.2 %collective-permute-done.10 = bf16[128,1024]{1,0:T(8,128)(2,1)S(1)} collective-permute-done((bf16[128,1024]{1,0:T(8,128)(2,1)S(1)}, bf16[128,1024]{1,0:T(8,128)(2,1)S(1)}, u32[]{:S(2)}, u32[]{:S(2)}) %collective-permute-start.10) | collective-permute-done | bytes 262176 | tf_op jit(solution)/shard_map/ppermute | solution.py:21
  191.5 15.7 %all-to-all-start = ((bf16[16,8,1024]{2,1,0:T(8,128)(2,1)}), bf16[16,8,1024]{2,1,0:T(8,128)(2,1)S(1)}, u32[]{:S(2)}, u32[]{:S(2)}) async-start(bf16[16,8,1024]{2,1,0:T(8,128)(2,1)} %fusion.4), calls=%async_computation | async-start | bytes 524288 | tf_op jit(solution)/shard_map/all_to_all | solution.py:258
  213.4 4.0 %collective-permute-start.18 = (bf16[256,896]{1,0:T(8,128)(2,1)S(1)}, bf16[256,896]{1,0:T(8,128)(2,1)S(1)}, u32[]{:S(2)}, u32[]{:S(2)}) collective-permute-start(bf16[256,896]{1,0:T(8,128)(2,1)S(1)} %get-tuple-element.35), channel_id=1, source_target_pairs={{0,16},{16,32},{32,48},{48,0},{1,17},{17,33},{33,49},{49,1},{2,18}... | collective-permute-start | bytes 1376264 | tf_op jit(solution)/shard_map/ppermute | solution.py:21
  217.4 4.6 %collective-permute-start.19 = (bf16[256,896]{1,0:T(8,128)(2,1)S(1)}, bf16[256,896]{1,0:T(8,128)(2,1)S(1)}, u32[]{:S(2)}, u32[]{:S(2)}) collective-permute-start(bf16[256,896]{1,0:T(8,128)(2,1)S(1)} %get-tuple-element.36), channel_id=1, source_target_pairs={{0,32},{16,48},{32,0},{48,16},{1,33},{17,49},{33,1},{49,17},{2,34}... | collective-permute-start | bytes 1376264 | tf_op jit(solution)/shard_map/ppermute | solution.py:21
  230.7 4.8 %collective-permute-done.18.p1 = bf16[256,896]{1,0:T(8,128)(2,1)S(1)} collective-permute-done((bf16[256,896]{1,0:T(8,128)(2,1)S(1)}, bf16[256,896]{1,0:T(8,128)(2,1)S(1)}, u32[]{:S(2)}, u32[]{:S(2)}) %collective-permute-start.18) | collective-permute-done | bytes 458784 | tf_op jit(solution)/shard_map/ppermute | solution.py:21
  237.4 4.3 %collective-permute-done.19.p2 = bf16[256,896]{1,0:T(8,128)(2,1)S(1)} collective-permute-done((bf16[256,896]{1,0:T(8,128)(2,1)S(1)}, bf16[256,896]{1,0:T(8,128)(2,1)S(1)}, u32[]{:S(2)}, u32[]{:S(2)}) %collective-permute-start.19) | collective-permute-done | bytes 458784 | tf_op jit(solution)/shard_map/ppermute | solution.py:21
  243.2 7.4 %collective-permute-start.21 = (bf16[128,896]{1,0:T(8,128)(2,1)S(1)}, bf16[128,896]{1,0:T(8,128)(2,1)S(1)}, u32[]{:S(2)}, u32[]{:S(2)}) collective-permute-start(bf16[128,896]{1,0:T(8,128)(2,1)S(1)} %add_convert_fusion.2), channel_id=1, source_target_pairs={{0,256},{256,0},{1,257},{257,1},{2,258},{258,2},{3,259},{259,3},{4... | collective-permute-start | bytes 688136 | tf_op jit(solution)/shard_map/ppermute | solution.py:25
  250.6 16.6 %collective-permute-done.21.arrived = bf16[128,896]{1,0:T(8,128)(2,1)S(1)} collective-permute-done((bf16[128,896]{1,0:T(8,128)(2,1)S(1)}, bf16[128,896]{1,0:T(8,128)(2,1)S(1)}, u32[]{:S(2)}, u32[]{:S(2)}) %collective-permute-start.21) | collective-permute-done | bytes 229408 | tf_op jit(solution)/shard_map/ppermute | solution.py:25
  (90 shorter events, 80.0 us)
Async XLA Ops:
  6.9 21.3 %collective-permute-start = (bf16[1408,256]{1,0:T(8,128)(2,1)S(1)}, bf16[1408,256]{1,0:T(8,128)(2,1)S(1)}, u32[]{:S(2)}, u32[]{:S(2)}) collective-permute-start(bf16[1408,256]{1,0:T(8,128)(2,1)S(1)} %get-tuple-element.25.b0.refs_8_), channel_id=1, source_target_pairs={{0,64},{64,192},{192,128},{128,0},{1,65},{65,193},{193,129},{129,1... | collective-permute-start | bytes 2162696 | tf_op jit(solution)/shard_map/ppermute | solution.py:201
  10.7 79.5 %all-to-all-start.1 = ((bf16[16,8,1024]{2,1,0:T(8,128)(2,1)}), bf16[16,8,1024]{2,1,0:T(8,128)(2,1)S(1)}, u32[]{:S(2)}, u32[]{:S(2)}) async-start(bf16[16,8,1024]{2,1,0:T(8,128)(2,1)} %get-tuple-element.32), calls=%async_computation.1 | async-start | bytes 524288 | tf_op jit(solution)/shard_map/all_to_all | solution.py:197
  28.2 41.5 %collective-permute-start.1 = (bf16[1408,256]{1,0:T(8,128)(2,1)S(1)}, bf16[1408,256]{1,0:T(8,128)(2,1)S(1)}, u32[]{:S(2)}, u32[]{:S(2)}) collective-permute-start(bf16[1408,256]{1,0:T(8,128)(2,1)S(1)} %collective-permute-done.b1.refs_9_), channel_id=1, source_target_pairs={{0,64},{64,192},{192,128},{128,0},{1,65},{65,193},{193,129},{129,1... | collective-permute-start | bytes 2162696 | tf_op jit(solution)/shard_map/ppermute | solution.py:201
  34.6 23.2 %collective-permute-start.3 = (bf16[128,896]{1,0:T(8,128)(2,1)S(1)}, bf16[128,896]{1,0:T(8,128)(2,1)S(1)}, u32[]{:S(2)}, u32[]{:S(2)}) collective-permute-start(bf16[128,896]{1,0:T(8,128)(2,1)S(1)} %get-tuple-element.26), channel_id=1, source_target_pairs={{0,256},{256,0},{1,257},{257,1},{2,258},{258,2},{3,259},{259,3},{4... | collective-permute-start | bytes 688136 | tf_op jit(solution)/shard_map/ppermute | solution.py:25
  57.8 34.6 %collective-permute-start.6 = (bf16[256,896]{1,0:T(8,128)(2,1)S(1)}, bf16[256,896]{1,0:T(8,128)(2,1)}, u32[]{:S(2)}, u32[]{:S(2)}) collective-permute-start(bf16[256,896]{1,0:T(8,128)(2,1)S(1)} %constant_dynamic-update-slice_fusion.h0.refs_12_), channel_id=1, source_target_pairs={{0,16},{16,32},{32,48},{48,0},{1,17},{17,33},{33,49},{49,1},{2,18}... | collective-permute-start | bytes 1376264 | tf_op jit(solution)/shard_map/ppermute | solution.py:21
  61.6 35.3 %collective-permute-start.5 = (bf16[256,896]{1,0:T(8,128)(2,1)S(1)}, bf16[256,896]{1,0:T(8,128)(2,1)}, u32[]{:S(2)}, u32[]{:S(2)}) collective-permute-start(bf16[256,896]{1,0:T(8,128)(2,1)S(1)} %constant_dynamic-update-slice_fusion.h0.refs_12_), channel_id=1, source_target_pairs={{0,32},{16,48},{32,0},{48,16},{1,33},{17,49},{33,1},{49,17},{2,34}... | collective-permute-start | bytes 1376264 | tf_op jit(solution)/shard_map/ppermute | solution.py:21
  66.3 32.6 %collective-permute-start.4 = (bf16[256,896]{1,0:T(8,128)(2,1)S(1)}, bf16[256,896]{1,0:T(8,128)(2,1)}, u32[]{:S(2)}, u32[]{:S(2)}) collective-permute-start(bf16[256,896]{1,0:T(8,128)(2,1)S(1)} %constant_dynamic-update-slice_fusion.h0.refs_12_), channel_id=1, source_target_pairs={{0,48},{16,0},{32,16},{48,32},{1,49},{17,1},{33,17},{49,33},{2,50}... | collective-permute-start | bytes 1376264 | tf_op jit(solution)/shard_map/ppermute | solution.py:21
  69.7 42.0 %collective-permute-start.2 = (bf16[1408,256]{1,0:T(8,128)(2,1)S(1)}, bf16[1408,256]{1,0:T(8,128)(2,1)}, u32[]{:S(2)}, u32[]{:S(2)}) collective-permute-start(bf16[1408,256]{1,0:T(8,128)(2,1)S(1)} %collective-permute-done.1.b2.refs_10_), channel_id=1, source_target_pairs={{0,64},{64,192},{192,128},{128,0},{1,65},{65,193},{193,129},{129,1... | collective-permute-start | bytes 2162696 | tf_op jit(solution)/shard_map/ppermute | solution.py:201
  117.7 17.1 %collective-permute-start.22 = (bf16[256,512]{1,0:T(8,128)(2,1)S(1)}, bf16[256,512]{1,0:T(8,128)(2,1)S(1)}, u32[]{:S(2)}, u32[]{:S(2)}) collective-permute-start(bf16[256,512]{1,0:T(8,128)(2,1)S(1)} %get-tuple-element.41), channel_id=1, source_target_pairs={{0,16},{16,32},{32,48},{48,0},{1,17},{17,33},{33,49},{49,1},{2,18}... | collective-permute-start | bytes 786440 | tf_op jit(solution)/shard_map/ppermute | solution.py:21
  120.2 14.6 %collective-permute-start.23 = (bf16[256,512]{1,0:T(8,128)(2,1)S(1)}, bf16[256,512]{1,0:T(8,128)(2,1)S(1)}, u32[]{:S(2)}, u32[]{:S(2)}) collective-permute-start(bf16[256,512]{1,0:T(8,128)(2,1)S(1)} %get-tuple-element.42), channel_id=1, source_target_pairs={{0,32},{16,48},{32,0},{48,16},{1,33},{17,49},{33,1},{49,17},{2,34}... | collective-permute-start | bytes 786440 | tf_op jit(solution)/shard_map/ppermute | solution.py:21
  123.3 14.0 %collective-permute-start.24 = (bf16[256,512]{1,0:T(8,128)(2,1)S(1)}, bf16[256,512]{1,0:T(8,128)(2,1)S(1)}, u32[]{:S(2)}, u32[]{:S(2)}) collective-permute-start(bf16[256,512]{1,0:T(8,128)(2,1)S(1)} %get-tuple-element.43), channel_id=1, source_target_pairs={{0,48},{16,0},{32,16},{48,32},{1,49},{17,1},{33,17},{49,33},{2,50}... | collective-permute-start | bytes 786440 | tf_op jit(solution)/shard_map/ppermute | solution.py:21
  138.2 23.2 %all-to-all-start.2 = ((bf16[8,32,512]{2,1,0:T(8,128)(2,1)}), bf16[8,32,512]{2,1,0:T(8,128)(2,1)S(1)}, u32[]{:S(2)}, u32[]{:S(2)}) async-start(bf16[8,32,512]{2,1,0:T(8,128)(2,1)} %bitcast.11), calls=%async_computation.2 | async-start | bytes 524288 | tf_op jit(solution)/shard_map/all_to_all | solution.py:217
  151.6 17.1 %collective-permute-start.7 = (bf16[4,128,1024]{2,1,0:T(8,128)(2,1)S(1)}, bf16[4,128,1024]{2,1,0:T(8,128)(2,1)}, u32[]{:S(2)}, u32[]{:S(2)}) collective-permute-start(bf16[4,128,1024]{2,1,0:T(8,128)(2,1)S(1)} %get-tuple-element.28), channel_id=1, source_target_pairs={{0,1},{1,0},{2,3},{3,2},{4,5},{5,4},{6,7},{7,6},{8,9},{9,8},{10,11... | collective-permute-start | bytes 3145736 | tf_op jit(solution)/shard_map/ppermute | solution.py:25
  163.7 27.8 %all-to-all-start.3 = ((bf16[8,32,512]{2,1,0:T(8,128)(2,1)}), bf16[8,32,512]{2,1,0:T(8,128)(2,1)S(1)}, u32[]{:S(2)}, u32[]{:S(2)}) async-start(bf16[8,32,512]{2,1,0:T(8,128)(2,1)} %broadcast_in_dim.2), calls=%async_computation.3 | async-start | bytes 524288 | tf_op jit(solution)/shard_map/all_to_all | solution.py:224
  173.9 15.8 %collective-permute-start.10 = (bf16[128,1024]{1,0:T(8,128)(2,1)S(1)}, bf16[128,1024]{1,0:T(8,128)(2,1)S(1)}, u32[]{:S(2)}, u32[]{:S(2)}) collective-permute-start(bf16[128,1024]{1,0:T(8,128)(2,1)S(1)} %get-tuple-element.48), channel_id=1, source_target_pairs={{0,12},{4,0},{8,4},{12,8},{1,13},{5,1},{9,5},{13,9},{2,14},{6,2},{... | collective-permute-start | bytes 786440 | tf_op jit(solution)/shard_map/ppermute | solution.py:21
  176.1 13.6 %collective-permute-start.9 = (bf16[128,1024]{1,0:T(8,128)(2,1)S(1)}, bf16[128,1024]{1,0:T(8,128)(2,1)S(1)}, u32[]{:S(2)}, u32[]{:S(2)}) collective-permute-start(bf16[128,1024]{1,0:T(8,128)(2,1)S(1)} %get-tuple-element.49), channel_id=1, source_target_pairs={{0,8},{4,12},{8,0},{12,4},{1,9},{5,13},{9,1},{13,5},{2,10},{6,14},... | collective-permute-start | bytes 786440 | tf_op jit(solution)/shard_map/ppermute | solution.py:21
  191.5 77.5 %all-to-all-start = ((bf16[16,8,1024]{2,1,0:T(8,128)(2,1)}), bf16[16,8,1024]{2,1,0:T(8,128)(2,1)S(1)}, u32[]{:S(2)}, u32[]{:S(2)}) async-start(bf16[16,8,1024]{2,1,0:T(8,128)(2,1)} %fusion.4), calls=%async_computation | async-start | bytes 524288 | tf_op jit(solution)/shard_map/all_to_all | solution.py:258
  213.4 22.0 %collective-permute-start.18 = (bf16[256,896]{1,0:T(8,128)(2,1)S(1)}, bf16[256,896]{1,0:T(8,128)(2,1)S(1)}, u32[]{:S(2)}, u32[]{:S(2)}) collective-permute-start(bf16[256,896]{1,0:T(8,128)(2,1)S(1)} %get-tuple-element.35), channel_id=1, source_target_pairs={{0,16},{16,32},{32,48},{48,0},{1,17},{17,33},{33,49},{49,1},{2,18}... | collective-permute-start | bytes 1376264 | tf_op jit(solution)/shard_map/ppermute | solution.py:21
  217.4 24.3 %collective-permute-start.19 = (bf16[256,896]{1,0:T(8,128)(2,1)S(1)}, bf16[256,896]{1,0:T(8,128)(2,1)S(1)}, u32[]{:S(2)}, u32[]{:S(2)}) collective-permute-start(bf16[256,896]{1,0:T(8,128)(2,1)S(1)} %get-tuple-element.36), channel_id=1, source_target_pairs={{0,32},{16,48},{32,0},{48,16},{1,33},{17,49},{33,1},{49,17},{2,34}... | collective-permute-start | bytes 1376264 | tf_op jit(solution)/shard_map/ppermute | solution.py:21
  222.0 21.1 %collective-permute-start.20 = (bf16[256,896]{1,0:T(8,128)(2,1)S(1)}, bf16[256,896]{1,0:T(8,128)(2,1)S(1)}, u32[]{:S(2)}, u32[]{:S(2)}) collective-permute-start(bf16[256,896]{1,0:T(8,128)(2,1)S(1)} %get-tuple-element.37), channel_id=1, source_target_pairs={{0,48},{16,0},{32,16},{48,32},{1,49},{17,1},{33,17},{49,33},{2,50}... | collective-permute-start | bytes 1376264 | tf_op jit(solution)/shard_map/ppermute | solution.py:21
  225.4 44.9 %collective-permute-start.27 = (bf16[256,512]{1,0:T(8,128)(2,1)S(1)}, bf16[256,512]{1,0:T(8,128)(2,1)S(1)}, u32[]{:S(2)}, u32[]{:S(2)}) collective-permute-start(bf16[256,512]{1,0:T(8,128)(2,1)S(1)} %bitcast.30), channel_id=1, source_target_pairs={{0,16},{16,32},{32,48},{48,0},{1,17},{17,33},{33,49},{49,1},{2,18}... | collective-permute-start | bytes 786440 | tf_op jit(solution)/shard_map/ppermute | solution.py:21
  227.9 42.4 %collective-permute-start.26 = (bf16[256,512]{1,0:T(8,128)(2,1)S(1)}, bf16[256,512]{1,0:T(8,128)(2,1)S(1)}, u32[]{:S(2)}, u32[]{:S(2)}) collective-permute-start(bf16[256,512]{1,0:T(8,128)(2,1)S(1)} %bitcast.31), channel_id=1, source_target_pairs={{0,32},{16,48},{32,0},{48,16},{1,33},{17,49},{33,1},{49,17},{2,34}... | collective-permute-start | bytes 786440 | tf_op jit(solution)/shard_map/ppermute | solution.py:21
  235.5 34.8 %collective-permute-start.25 = (bf16[256,512]{1,0:T(8,128)(2,1)S(1)}, bf16[256,512]{1,0:T(8,128)(2,1)S(1)}, u32[]{:S(2)}, u32[]{:S(2)}) collective-permute-start(bf16[256,512]{1,0:T(8,128)(2,1)S(1)} %bitcast.32), channel_id=1, source_target_pairs={{0,48},{16,0},{32,16},{48,32},{1,49},{17,1},{33,17},{49,33},{2,50}... | collective-permute-start | bytes 786440 | tf_op jit(solution)/shard_map/ppermute | solution.py:21
  243.2 24.0 %collective-permute-start.21 = (bf16[128,896]{1,0:T(8,128)(2,1)S(1)}, bf16[128,896]{1,0:T(8,128)(2,1)S(1)}, u32[]{:S(2)}, u32[]{:S(2)}) collective-permute-start(bf16[128,896]{1,0:T(8,128)(2,1)S(1)} %add_convert_fusion.2), channel_id=1, source_target_pairs={{0,256},{256,0},{1,257},{257,1},{2,258},{258,2},{3,259},{259,3},{4... | collective-permute-start | bytes 688136 | tf_op jit(solution)/shard_map/ppermute | solution.py:25
  (24 other events, 429.1 us)

commit v5 on v2

v5 whole, which is shorter than its diff:
```python
import jax
import jax.numpy as jnp
from jax import lax
from jax.experimental import pallas as pl
from jax.experimental.pallas import tpu as pltpu
from jax.sharding import Mesh, PartitionSpec as P

corr_first = 1.0 - 0.9**10
corr_second = 1.0 - 0.999**10

NZ, NX, NY, NH, NC = 8, 4, 4, 2, 2
ORDER = (0, 2, 4, 6, 7, 5, 3, 1)
RING = [(ORDER[i], ORDER[(i + 1) % NZ]) for i in range(NZ)]
bf16, f32 = jnp.bfloat16, jnp.float32
VMEM = pl.BlockSpec(memory_space=pltpu.VMEM)
SMEM = pl.BlockSpec(memory_space=pltpu.SMEM)


def shift(value, axis, size, by):
    return lax.ppermute(value, axis, [(i, (i - by) % size) for i in range(size)])


def dot(a, b, contract):
    return lax.dot_general(a, b, (contract, ((), ())), preferred_element_type=f32)


def call(kernel, n_in, outs, scratch=(), flops=0, limit=20):
    return pl.pallas_call(
        kernel,
        out_shape=tuple(jax.ShapeDtypeStruct(*o) for o in outs),
        in_specs=[SMEM] + [VMEM] * n_in,
        out_specs=tuple(VMEM for _ in outs),
        scratch_shapes=[pltpu.VMEM(*s) for s in scratch],
        compiler_params=pltpu.CompilerParams(vmem_limit_bytes=limit << 20),
        cost_estimate=pl.CostEstimate(flops=flops, bytes_accessed=4 << 20, transcendentals=0),
    )


def ring_block(zl, hop):
    half = zl >> 1
    place = jnp.where((zl & 1) == 0, half, NZ - 1 - half)
    place = (place - hop) & (NZ - 1)
    return jnp.where(place < NZ // 2, 2 * place, 2 * NZ - 1 - 2 * place)


def prepare(pos, gate, up, cot, weight, basis, hidden, pack, both, plain):
    x, y, c = pos[0], pos[1], pos[2]
    for r in range(NX):
        block = lax.rem(x + r, NX) * 256
        for zl in range(NZ):
            piece = cot[:, pl.ds(pl.multiple_of(zl * 1024 + block, 256), 256)]
            for zh in range(NH):
                pack[zl * NH + zh, :, r * 256 : (r + 1) * 256] = piece
    both[:896, :] = weight[...]
    both[896:1152, :] = basis[:, :256]
    both[1152:, :] = basis[:, 256:]
    g = gate[...].astype(f32)
    plain[...] = g * jax.nn.sigmoid(g) * up[...].astype(f32)
    for cr in range(NC):
        for yr in range(NY):
            first = (lax.rem(y + yr, NY) * 4 + lax.rem(c + cr, NC)) * 8
            pair = [plain[pl.ds(pl.multiple_of(first + zh * 16, 8), 8), :] for zh in range(NH)]
            hidden[pl.ds((cr * NY + yr) * 16, 16), :] = jnp.concatenate(pair, 0).astype(bf16)


def backward(pos, *refs):
    cots, boths = refs[:8], refs[8:12]
    grad, reduced, tile = refs[12:]
    for piece in range(8):
        for zl in range(NZ):
            tile[pl.ds(zl * 128 + piece * 16, 16), :] = cots[piece][pl.ds(zl * 16, 16), :]

    def rows(step, _):
        at = pl.ds(pl.multiple_of(step * 256, 256), 256)
        total, left, right = None, None, None
        for r in range(NX):
            part = tile[at, r * 256 : (r + 1) * 256]
            more = dot(part, boths[r][:896, :], ((1,), (1,)))
            total = more if total is None else total + more
            more = dot(part, boths[r][896:1152, :], ((1,), (0,)))
            left = more if left is None else left + more
            more = dot(part, boths[r][1152:, :], ((1,), (0,)))
            right = more if right is None else right + more
        grad[at, :] = total.astype(bf16)
        reduced[at, :256] = left.astype(bf16)
        reduced[at, 256:] = right.astype(bf16)
        return 0

    lax.fori_loop(0, 4, rows, 0)


def project(pos, *refs):
    hiddens, reduced = refs[:8], refs[8]
    tile, outs, total, blocks = refs[9], refs[10:14], *refs[14:]
    x, zl_own = pos[0], pos[3]
    for hop in range(NZ):
        to = pl.ds(pl.multiple_of(ring_block(zl_own, hop) * 128, 128), 128)
        tile[to, :] = hiddens[hop][...]
    total[...] = dot(tile[...], reduced[...], ((0,), (0,)))
    spare = jnp.zeros((4, total.shape[1]), f32)
    for xs in range(NX):
        for zl in range(NZ):
            first = zl * 112 + xs * 28
            block = jnp.concatenate([total[first : first + 28, :], spare], 0)
            blocks[xs, zl * 32 : zl * 32 + 32, :] = block.astype(bf16)
    for xr, out in enumerate(outs):
        out[...] = blocks[lax.rem(x + xr, NX)]


def forward(pos, tile, b0, b1, b2, b3, o0, o1, o2, o3, leave):
    def rows(step, _):
        part = tile[pl.ds(pl.multiple_of(step * 256, 256), 256), :]
        for r, both in enumerate((b0, b1, b2, b3)):
            term = dot(part, both[:896, :], ((1,), (0,))).astype(bf16)
            for half in range(2):
                to = pl.ds(pl.multiple_of((step * 2 + half) * 16, 16), 16)
                for piece in range(8):
                    first = half * 128 + piece * 16
                    block = term[first : first + 16, :]
                    if piece < NY:
                        (o0, o1, o2, o3)[piece][to, r * 256 : (r + 1) * 256] = block
                    else:
                        leave[piece - NY, to, r * 256 : (r + 1) * 256] = block
        return 0

    lax.fori_loop(0, 4, rows, 0)


def finish_out(pos, parts, out):
    x = pos[0]
    for zl in range(NZ):
        both = (parts[zl * NH].astype(f32) + parts[zl * NH + 1].astype(f32)).astype(bf16)
        for r in range(NX):
            block = zl * 1024 + lax.rem(x + r, NX) * 256
            out[:, pl.ds(pl.multiple_of(block, 256), 256)] = both[:, r * 256 : (r + 1) * 256]


def finish_grad(pos, total, gate, up, grad_gate, grad_up, relative, plain):
    y, c = pos[1], pos[2]
    relative[...] = total[...].astype(f32)
    for ys in range(NY):
        yr = lax.rem(ys - y + NY, NY)
        for zh in range(NH):
            for cs in range(NC):
                cr = lax.rem(cs + c, NC)
                first = ((cr * NY + yr) * NH + zh) * 8
                to = ((ys * NH + zh) * NC + cs) * 8
                plain[to : to + 8, :] = relative[pl.ds(pl.multiple_of(first, 8), 8), :]
    g, u, d = gate[...].astype(f32), up[...].astype(f32), plain[...]
    s = jax.nn.sigmoid(g)
    grad_up[...] = (d * g * s).astype(bf16)
    grad_gate[...] = (d * u * s * (1.0 + g * (1.0 - s))).astype(bf16)


def expand(pos, s0, s1, s2, s3, basis, out, pieces, steps):
    x = pos[0]
    for xr, piece in enumerate((s0, s1, s2, s3)):
        pieces[lax.rem(x + xr, NX)] = piece[...].astype(f32)
    for xs in range(NX):
        for zl in range(NZ):
            first = zl * 112 + xs * 28
            steps[first : first + 28, :] = pieces[xs, zl * 32 : zl * 32 + 28, :]
    out[...] = dot(steps[...].astype(bf16), basis[...], ((1,), (1,)))


def body(gate, up, weight, basis, cotangent, moment1, moment2):
    pos = jnp.stack([lax.axis_index(a) for a in ("x", "y", "c", "zl")]).astype(jnp.int32)
    rows, ff = gate.shape
    mine, width = cotangent.shape
    cols = width // NZ
    deep, rank = basis.shape
    own, slot = moment1.shape[0], 32

    hidden, pack, both = call(
        prepare,
        5,
        [
            ((rows, ff), bf16),
            ((NZ * NH, mine, cols), bf16),
            ((ff + 2 * deep, deep), bf16),
        ],
        [((rows, ff), f32)],
    )(pos, gate, up, cotangent, weight, basis)

    got = lax.all_to_all(pack, ("zl", "zh"), 0, 0, tiled=True).reshape(rows, cols)
    boths = [both] + [shift(both, "x", NX, by) for by in range(1, NX)]
    got, *boths = lax.optimization_barrier((got, *boths))
    hiddens = [hidden]
    for _ in range(1, NZ - 2):
        hiddens.append(lax.ppermute(hiddens[-1], "zl", RING))
    cots = [got] + [shift(got, "y", NY, by) for by in range(1, NY)]
    cots = cots + [shift(piece, "c", NC, 1) for piece in cots]

    partial, reduced = call(
        backward,
        12,
        [((NZ * rows, ff), bf16), ((NZ * rows, rank), bf16)],
        [((NZ * rows, cols), bf16)],
        flops=3 * 10**9,
    )(pos, *cots, *boths)
    hiddens[-1], partial, reduced = lax.optimization_barrier((hiddens[-1], partial, reduced))
    for _ in range(2):
        hiddens.append(lax.ppermute(hiddens[-1], "zl", RING))
    grad_hidden = lax.psum_scatter(partial, "zl", scatter_dimension=0, tiled=True)
    grad_gate, grad_up = call(
        finish_grad,
        3,
        [((rows, ff), bf16), ((rows, ff), bf16)],
        [((rows, ff), f32), ((rows, ff), f32)],
    )(pos, grad_hidden, gate, up)

    tile, *parts = call(
        project,
        9,
        [((NZ * rows, ff), bf16)] + [((NZ * slot, rank), bf16)] * NX,
        [((ff, rank), f32), ((NX, NZ * slot, rank), bf16)],
        flops=10**9,
    )(pos, *hiddens, reduced)
    total = parts[0].astype(f32)
    for by in range(1, NX):
        total = total + shift(parts[by], "x", NX, -by).astype(f32)
    total, tile = lax.optimization_barrier((total.astype(bf16), tile))
    total = lax.all_to_all(total, "zl", 0, 0, tiled=True).reshape(NZ, slot, rank)
    projected = total.astype(f32).sum(0)[:own]
    moment1_new = 0.9 * moment1 + 0.1 * projected
    moment2_new = 0.999 * moment2 + 0.001 * projected * projected
    step = (moment1_new / corr_first / (jnp.sqrt(moment2_new / corr_second) + 1e-08)).astype(bf16)
    step = jnp.pad(step, ((0, slot - own), (0, 0)))
    *term, leave = call(
        forward, 5, [((rows, cols), bf16)] * NY + [((NY, rows, cols), bf16)], flops=2 * 10**9
    )(pos, tile, *boths)
    arrived = shift(leave, "c", NC, 1)
    term = [(term[yr].astype(f32) + arrived[yr].astype(f32)).astype(bf16) for yr in range(NY)]
    step, *term = lax.optimization_barrier((step, *term))
    step = jnp.broadcast_to(step[None], (NZ, slot, rank))
    step = lax.all_to_all(step, "zl", 0, 0, tiled=True).reshape(NZ * slot, rank)
    steps = [step] + [shift(step, "x", NX, by) for by in range(1, NX)]
    (expansion,) = call(
        expand,
        5,
        [((ff, deep), f32)],
        [((NX, NZ * slot, rank), f32), ((ff, rank), f32)],
        flops=3 * 10**8,
    )(pos, *steps, basis)

    total = term[0].astype(f32)
    for by in range(1, NY):
        total = total + shift(term[by], "y", NY, -by).astype(f32)
    total = total.astype(bf16).reshape(NZ * NH, mine, cols)
    total = lax.all_to_all(total, ("zl", "zh"), 0, 0, tiled=True)
    (layer_out,) = call(finish_out, 1, [((mine, width), bf16)])(pos, total)
    return (layer_out, grad_gate, grad_up, moment1_new, moment2_new, expansion)


def solution(mesh):
    fine = Mesh(mesh.devices.reshape(NZ, NX, NY, NH, NC), ("zl", "x", "y", "zh", "c"))
    dp, tensor = ("zl", "x"), ("y", "zh", "c")
    placed = (
        P(dp, tensor),
        P(dp, tensor),
        P(tensor, dp),
        P(dp, None),
        P(dp + tensor, None),
        P(tensor + dp, None),
        P(tensor + dp, None),
    )
    return jax.shard_map(
        body,
        mesh=fine,
        in_specs=placed,
        out_specs=(
            P(dp + tensor, None),
            P(dp, tensor),
            P(dp, tensor),
            P(tensor + dp, None),
            P(tensor + dp, None),
            P(tensor, dp),
        ),
        check_vma=False,
    )
```

time: 228 us -> 263 us (1.15)
  starting transfers between devices: 108 us -> 135 us
  waiting for transfers between devices: 62.5 us -> 68.2 us
    ppermute x0 -> x7, starting transfers between devices: none -> 35.1 us  [body(): hiddens.append(lax.ppermute(hiddens[-1], 'zl', RING))]
    ppermute x0 -> x7, waiting for transfers between devices: none -> 16.4 us  [body(): hiddens.append(lax.ppermute(hiddens[-1], 'zl', RING))]
    all_to_all x2, waiting for transfers between devices: 28.8 us -> 17.9 us  [the longest x1 12.6 us: body(): lax.all_to_all(total, 'zl', 0, 0, tiled=True).reshape(NZ, slot, rank)]
    ppermute x23 -> x20, starting transfers between devices: 72.9 us -> 63.2 us  [shift(): lax.ppermute(value, axis, [(i, (i - by) % size) for i in range(size)])]
    unnamed x44 -> x52, local copies, waits for them, and re-layouts: 14.6 us -> 18.5 us
    ppermute x23 -> x20, waiting for transfers between devices: 33.7 us -> 33.8 us  [shift(): lax.ppermute(value, axis, [(i, (i - by) % size) for i in range(size)])]
  transfers between devices with their start and end apart: 29 -> 32, of which waited for: 9 -> 17; matrix products, arithmetic and copies ran while one was open for 3% -> 2% of each run, Pallas kernels for 6% -> 5%
where the time goes in v5:
time: 263 us; the launch traced here: 259 us
  starting transfers between devices  135 us (51%)
  waiting for transfers between devices  68.2 us (26%)
  local copies, waits for them, and re-layouts  19.2 us (7%)
  Pallas kernels  18 us (7%)
  between operations  14.5 us (6%)
  other arithmetic  4.14 us (2%)
    ppermute x20, starting transfers between devices, shift(): lax.ppermute(value, axis, [(i, (i - by) % size) for i in range(size)])  63.2 us
    ppermute x7, starting transfers between devices, body(): hiddens.append(lax.ppermute(hiddens[-1], 'zl', RING))  35.1 us
    ppermute x20, waiting for transfers between devices, shift(): lax.ppermute(value, axis, [(i, (i - by) % size) for i in range(size)])  33.8 us
    unnamed x52, local copies, waits for them, and re-layouts  18.5 us
    ppermute x7, waiting for transfers between devices, body(): hiddens.append(lax.ppermute(hiddens[-1], 'zl', RING))  16.4 us
    all_to_all x1, starting transfers between devices, body(): lax.all_to_all(pack, ('zl', 'zh'), 0, 0, tiled=True).reshape(rows, cols)  15.2 us
    all_to_all x1, waiting for transfers between devices, body(): lax.all_to_all(total, 'zl', 0, 0, tiled=True).reshape(NZ, slot, rank)  12.6 us
    all_to_all x1, starting transfers between devices, body(): total = lax.all_to_all(total, ('zl', 'zh'), 0, 0, tiled=True)  8.53 us
  transfers between devices with their start and end apart: 32, of which 17 were waited for; matrix products, arithmetic and copies ran while one was open for 2% of the time, Pallas kernels for 5%

profile of v5, /device:TPU:24, one launch (start us, length us, event | category | flops | bytes accessed | tf_op | source)
XLA Modules:
  0.0 258.8 jit_solution(10779946484597755319)
XLA Ops:
  13.3 15.2 %all-to-all-start = ((bf16[16,8,1024]{2,1,0:T(8,128)(2,1)}), bf16[16,8,1024]{2,1,0:T(8,128)(2,1)S(1)}, u32[]{:S(2)}, u32[]{:S(2)}) async-start(bf16[16,8,1024]{2,1,0:T(8,128)(2,1)} %get-tuple-element.39), calls=%async_computation | async-start | bytes 524288 | tf_op jit(solution)/shard_map/all_to_all | solution.py:185
  32.0 4.6 %collective-permute-start.6 = (bf16[1408,256]{1,0:T(8,128)(2,1)S(1)}, bf16[1408,256]{1,0:T(8,128)(2,1)S(1)}, u32[]{:S(2)}, u32[]{:S(2)}) collective-permute-start(bf16[1408,256]{1,0:T(8,128)(2,1)S(1)} %get-tuple-element.42.refs_8_.b0), channel_id=1, source_target_pairs={{0,32},{16,48},{32,0},{48,16},{1,33},{17,49},{33,1},{49,17},{2,34}... | collective-permute-start | bytes 2162696 | tf_op jit(solution)/shard_map/ppermute | solution.py:20
  40.0 4.7 %collective-permute-start = (bf16[128,896]{1,0:T(8,128)(2,1)S(1)}, bf16[128,896]{1,0:T(8,128)(2,1)S(1)}, u32[]{:S(2)}, u32[]{:S(2)}) collective-permute-start(bf16[128,896]{1,0:T(8,128)(2,1)S(1)} %get-tuple-element.38.refs_0_), channel_id=1, source_target_pairs={{0,128},{128,256},{256,384},{384,448},{448,320},{320,192},{192,64}... | collective-permute-start | bytes 688136 | tf_op jit(solution)/shard_map/ppermute | solution.py:190
  44.7 4.7 %collective-permute-done.refs_1_ = bf16[128,896]{1,0:T(8,128)(2,1)S(1)} collective-permute-done((bf16[128,896]{1,0:T(8,128)(2,1)S(1)}, bf16[128,896]{1,0:T(8,128)(2,1)S(1)}, u32[]{:S(2)}, u32[]{:S(2)}) %collective-permute-start) | collective-permute-done | bytes 229408 | tf_op jit(solution)/shard_map/ppermute | solution.py:190
  49.4 4.4 %collective-permute-start.1 = (bf16[128,896]{1,0:T(8,128)(2,1)S(1)}, bf16[128,896]{1,0:T(8,128)(2,1)}, u32[]{:S(2)}, u32[]{:S(2)}) collective-permute-start(bf16[128,896]{1,0:T(8,128)(2,1)S(1)} %collective-permute-done.refs_1_), channel_id=1, source_target_pairs={{0,128},{128,256},{256,384},{384,448},{448,320},{320,192},{192,64}... | collective-permute-start | bytes 688136 | tf_op jit(solution)/shard_map/ppermute | solution.py:190
  53.8 11.9 %collective-permute-done.6.refs_10_.b2 = bf16[1408,256]{1,0:T(8,128)(2,1)S(1)} collective-permute-done((bf16[1408,256]{1,0:T(8,128)(2,1)S(1)}, bf16[1408,256]{1,0:T(8,128)(2,1)S(1)}, u32[]{:S(2)}, u32[]{:S(2)}) %collective-permute-start.6) | collective-permute-done | bytes 720928 | tf_op jit(solution)/shard_map/ppermute | solution.py:20
  70.3 4.5 %collective-permute-start.9 = (bf16[128,1024]{1,0:T(8,128)(2,1)S(1)}, bf16[128,1024]{1,0:T(8,128)(2,1)S(1)}, u32[]{:S(2)}, u32[]{:S(2)}) collective-permute-start(bf16[128,1024]{1,0:T(8,128)(2,1)S(1)} %bitcast.34), channel_id=1, source_target_pairs={{0,8},{4,12},{8,0},{12,4},{1,9},{5,13},{9,1},{13,5},{2,10},{6,14},... | collective-permute-start | bytes 786440 | tf_op jit(solution)/shard_map/ppermute | solution.py:20
  76.7 4.4 %collective-permute-start.2 = (bf16[128,896]{1,0:T(8,128)(2,1)}, bf16[128,896]{1,0:T(8,128)(2,1)S(1)}, u32[]{:S(2)}, u32[]{:S(2)}) collective-permute-start(bf16[128,896]{1,0:T(8,128)(2,1)} %collective-permute-done.1.refs_2_), channel_id=1, source_target_pairs={{0,128},{128,256},{256,384},{384,448},{448,320},{320,192},{192,64}... | collective-permute-start | bytes 688136 | tf_op jit(solution)/shard_map/ppermute | solution.py:190
  89.9 5.5 %collective-permute-start.3 = (bf16[128,896]{1,0:T(8,128)(2,1)S(1)}, bf16[128,896]{1,0:T(8,128)(2,1)S(1)}, u32[]{:S(2)}, u32[]{:S(2)}) collective-permute-start(bf16[128,896]{1,0:T(8,128)(2,1)S(1)} %collective-permute-done.2.refs_3_), channel_id=1, source_target_pairs={{0,128},{128,256},{256,384},{384,448},{448,320},{320,192},{192,64}... | collective-permute-start | bytes 688136 | tf_op jit(solution)/shard_map/ppermute | solution.py:190
  96.1 4.3 %collective-permute-done.3.refs_4_ = bf16[128,896]{1,0:T(8,128)(2,1)S(1)} collective-permute-done((bf16[128,896]{1,0:T(8,128)(2,1)S(1)}, bf16[128,896]{1,0:T(8,128)(2,1)S(1)}, u32[]{:S(2)}, u32[]{:S(2)}) %collective-permute-start.3) | collective-permute-done | bytes 229408 | tf_op jit(solution)/shard_map/ppermute | solution.py:190
  100.4 5.3 %collective-permute-start.4 = (bf16[128,896]{1,0:T(8,128)(2,1)S(1)}, bf16[128,896]{1,0:T(8,128)(2,1)S(1)}, u32[]{:S(2)}, u32[]{:S(2)}) collective-permute-start(bf16[128,896]{1,0:T(8,128)(2,1)S(1)} %collective-permute-done.3.refs_4_), channel_id=1, source_target_pairs={{0,128},{128,256},{256,384},{384,448},{448,320},{320,192},{192,64}... | collective-permute-start | bytes 688136 | tf_op jit(solution)/shard_map/ppermute | solution.py:190
  106.9 5.9 %shard_map.119 = (bf16[1024,896]{1,0:T(8,128)(2,1)}, bf16[1024,512]{1,0:T(8,128)(2,1)S(1)}) custom-call(s32[4]{0:T(128)S(1)} %pad_add_fusion.pos, bf16[128,1024]{1,0:T(8,128)(2,1)S(1)} %bitcast.37, bf16[128,1024]{1,0:T(8,128)(2,1)S(1)} %collective-permute-done.8.refs_1_, bf16[128,1024]{1,0:T(8,128)(2,1)S(1)} %collective-permute-done.9.refs_2_, ...), custom_call_target="tpu_custom_call" | custom-call | flops 3000000000 | bytes 4194304 | tf_op jit(solution)/shard_map/pallas_call | solution.py:194
  113.7 5.5 %collective-permute-start.15 = (bf16[128,896]{1,0:T(8,128)(2,1)S(1)}, bf16[128,896]{1,0:T(8,128)(2,1)S(1)}, u32[]{:S(2)}, u32[]{:S(2)}) collective-permute-start(bf16[128,896]{1,0:T(8,128)(2,1)S(1)} %collective-permute-done.4.refs_5_), channel_id=1, source_target_pairs={{0,128},{128,256},{256,384},{384,448},{448,320},{320,192},{192,64}... | collective-permute-start | bytes 688136 | tf_op jit(solution)/shard_map/ppermute | solution.py:203
  119.2 3.9 %collective-permute-done.15.refs_6_ = bf16[128,896]{1,0:T(8,128)(2,1)S(1)} collective-permute-done((bf16[128,896]{1,0:T(8,128)(2,1)S(1)}, bf16[128,896]{1,0:T(8,128)(2,1)S(1)}, u32[]{:S(2)}, u32[]{:S(2)}) %collective-permute-start.15) | collective-permute-done | bytes 229408 | tf_op jit(solution)/shard_map/ppermute | solution.py:203
  123.1 5.3 %collective-permute-start.16 = (bf16[128,896]{1,0:T(8,128)(2,1)S(1)}, bf16[128,896]{1,0:T(8,128)(2,1)S(1)}, u32[]{:S(2)}, u32[]{:S(2)}) collective-permute-start(bf16[128,896]{1,0:T(8,128)(2,1)S(1)} %collective-permute-done.15.refs_6_), channel_id=1, source_target_pairs={{0,128},{128,256},{256,384},{384,448},{448,320},{320,192},{192,64}... | collective-permute-start | bytes 688136 | tf_op jit(solution)/shard_map/ppermute | solution.py:203
  138.5 4.3 %collective-permute-start.17 = (bf16[256,512]{1,0:T(8,128)(2,1)S(1)}, bf16[256,512]{1,0:T(8,128)(2,1)S(1)}, u32[]{:S(2)}, u32[]{:S(2)}) collective-permute-start(bf16[256,512]{1,0:T(8,128)(2,1)S(1)} %get-tuple-element.51), channel_id=1, source_target_pairs={{0,16},{16,32},{32,48},{48,0},{1,17},{17,33},{33,49},{49,1},{2,18}... | collective-permute-start | bytes 786440 | tf_op jit(solution)/shard_map/ppermute | solution.py:20
  156.7 8.1 %all-to-all-start.1 = ((bf16[8,32,512]{2,1,0:T(8,128)(2,1)}), bf16[8,32,512]{2,1,0:T(8,128)(2,1)S(1)}, u32[]{:S(2)}, u32[]{:S(2)}) async-start(bf16[8,32,512]{2,1,0:T(8,128)(2,1)} %bitcast.5), calls=%async_computation.1 | async-start | bytes 524288 | tf_op jit(solution)/shard_map/all_to_all | solution.py:223
  175.0 12.6 %all-to-all-done.1 = bf16[8,32,512]{2,1,0:T(8,128)(2,1)S(1)} async-done(((bf16[8,32,512]{2,1,0:T(8,128)(2,1)}), bf16[8,32,512]{2,1,0:T(8,128)(2,1)S(1)}, u32[]{:S(2)}, u32[]{:S(2)}) %all-to-all-start.1) | async-done | bytes 262176 | tf_op jit(solution)/shard_map/all_to_all | solution.py:223
  190.7 4.6 %all-to-all-start.3 = ((bf16[8,32,512]{2,1,0:T(8,128)(2,1)}), bf16[8,32,512]{2,1,0:T(8,128)(2,1)S(1)}, u32[]{:S(2)}, u32[]{:S(2)}) async-start(bf16[8,32,512]{2,1,0:T(8,128)(2,1)} %broadcast_in_dim.2), calls=%async_computation.4 | async-start | bytes 524288 | tf_op jit(solution)/shard_map/all_to_all | solution.py:236
  197.2 5.9 %collective-permute-start.22 = (bf16[128,1024]{1,0:T(8,128)(2,1)S(1)}, bf16[128,1024]{1,0:T(8,128)(2,1)S(1)}, u32[]{:S(2)}, u32[]{:S(2)}) collective-permute-start(bf16[128,1024]{1,0:T(8,128)(2,1)S(1)} %get-tuple-element.64), channel_id=1, source_target_pairs={{0,8},{4,12},{8,0},{12,4},{1,9},{5,13},{9,1},{13,5},{2,10},{6,14},... | collective-permute-start | bytes 786440 | tf_op jit(solution)/shard_map/ppermute | solution.py:20
  205.4 4.7 %collective-permute-done.22 = bf16[128,1024]{1,0:T(8,128)(2,1)S(1)} collective-permute-done((bf16[128,1024]{1,0:T(8,128)(2,1)S(1)}, bf16[128,1024]{1,0:T(8,128)(2,1)S(1)}, u32[]{:S(2)}, u32[]{:S(2)}) %collective-permute-start.22) | collective-permute-done | bytes 262176 | tf_op jit(solution)/shard_map/ppermute | solution.py:20
  214.2 5.4 %all-to-all-done.3 = bf16[8,32,512]{2,1,0:T(8,128)(2,1)S(1)} async-done(((bf16[8,32,512]{2,1,0:T(8,128)(2,1)}), bf16[8,32,512]{2,1,0:T(8,128)(2,1)S(1)}, u32[]{:S(2)}, u32[]{:S(2)}) %all-to-all-start.3) | async-done | bytes 262176 | tf_op jit(solution)/shard_map/all_to_all | solution.py:236
  219.6 8.5 %all-to-all-start.2 = ((bf16[16,8,1024]{2,1,0:T(8,128)(2,1)}), bf16[16,8,1024]{2,1,0:T(8,128)(2,1)S(1)}, u32[]{:S(2)}, u32[]{:S(2)}) async-start(bf16[16,8,1024]{2,1,0:T(8,128)(2,1)} %fusion.4), calls=%async_computation.2 | async-start | bytes 524288 | tf_op jit(solution)/shard_map/all_to_all | solution.py:250
  228.1 5.1 %collective-permute-start.26 = (bf16[256,512]{1,0:T(8,128)(2,1)S(1)}, bf16[256,512]{1,0:T(8,128)(2,1)S(1)}, u32[]{:S(2)}, u32[]{:S(2)}) collective-permute-start(bf16[256,512]{1,0:T(8,128)(2,1)S(1)} %bitcast.29), channel_id=1, source_target_pairs={{0,16},{16,32},{32,48},{48,0},{1,17},{17,33},{33,49},{49,1},{2,18}... | collective-permute-start | bytes 786440 | tf_op jit(solution)/shard_map/ppermute | solution.py:20
  (108 shorter events, 95.2 us)
Async XLA Ops:
  13.3 54.8 %all-to-all-start = ((bf16[16,8,1024]{2,1,0:T(8,128)(2,1)}), bf16[16,8,1024]{2,1,0:T(8,128)(2,1)S(1)}, u32[]{:S(2)}, u32[]{:S(2)}) async-start(bf16[16,8,1024]{2,1,0:T(8,128)(2,1)} %get-tuple-element.39), calls=%async_computation | async-start | bytes 524288 | tf_op jit(solution)/shard_map/all_to_all | solution.py:185
  28.6 220.8 %reduce-scatter.2.cloned.1.call-start = ((), (), s32[]{:S(2)}) async-start(), calls=%async_computation.5 | async-start | bytes 2064384 | tf_op jit(solution)/shard_map/reduce_scatter | solution.py:204
  28.6 25.2 %collective-permute-start.7 = (bf16[1408,256]{1,0:T(8,128)(2,1)S(1)}, bf16[1408,256]{1,0:T(8,128)(2,1)S(1)}, u32[]{:S(2)}, u32[]{:S(2)}) collective-permute-start(bf16[1408,256]{1,0:T(8,128)(2,1)S(1)} %get-tuple-element.42.refs_8_.b0), channel_id=1, source_target_pairs={{0,16},{16,32},{32,48},{48,0},{1,17},{17,33},{33,49},{49,1},{2,18}... | collective-permute-start | bytes 2162696 | tf_op jit(solution)/shard_map/ppermute | solution.py:20
  32.0 33.7 %collective-permute-start.6 = (bf16[1408,256]{1,0:T(8,128)(2,1)S(1)}, bf16[1408,256]{1,0:T(8,128)(2,1)S(1)}, u32[]{:S(2)}, u32[]{:S(2)}) collective-permute-start(bf16[1408,256]{1,0:T(8,128)(2,1)S(1)} %get-tuple-element.42.refs_8_.b0), channel_id=1, source_target_pairs={{0,32},{16,48},{32,0},{48,16},{1,33},{17,49},{33,1},{49,17},{2,34}... | collective-permute-start | bytes 2162696 | tf_op jit(solution)/shard_map/ppermute | solution.py:20
  36.7 30.6 %collective-permute-start.5 = (bf16[1408,256]{1,0:T(8,128)(2,1)S(1)}, bf16[1408,256]{1,0:T(8,128)(2,1)S(1)}, u32[]{:S(2)}, u32[]{:S(2)}) collective-permute-start(bf16[1408,256]{1,0:T(8,128)(2,1)S(1)} %get-tuple-element.42.refs_8_.b0), channel_id=1, source_target_pairs={{0,48},{16,0},{32,16},{48,32},{1,49},{17,1},{33,17},{49,33},{2,50}... | collective-permute-start | bytes 2162696 | tf_op jit(solution)/shard_map/ppermute | solution.py:20
  49.4 27.3 %collective-permute-start.1 = (bf16[128,896]{1,0:T(8,128)(2,1)S(1)}, bf16[128,896]{1,0:T(8,128)(2,1)}, u32[]{:S(2)}, u32[]{:S(2)}) collective-permute-start(bf16[128,896]{1,0:T(8,128)(2,1)S(1)} %collective-permute-done.refs_1_), channel_id=1, source_target_pairs={{0,128},{128,256},{256,384},{384,448},{448,320},{320,192},{192,64}... | collective-permute-start | bytes 688136 | tf_op jit(solution)/shard_map/ppermute | solution.py:190
  68.1 15.0 %collective-permute-start.10 = (bf16[128,1024]{1,0:T(8,128)(2,1)S(1)}, bf16[128,1024]{1,0:T(8,128)(2,1)S(1)}, u32[]{:S(2)}, u32[]{:S(2)}) collective-permute-start(bf16[128,1024]{1,0:T(8,128)(2,1)S(1)} %bitcast.33), channel_id=1, source_target_pairs={{0,4},{4,8},{8,12},{12,0},{1,5},{5,9},{9,13},{13,1},{2,6},{6,10},{... | collective-permute-start | bytes 786440 | tf_op jit(solution)/shard_map/ppermute | solution.py:20
  70.3 15.3 %collective-permute-start.9 = (bf16[128,1024]{1,0:T(8,128)(2,1)S(1)}, bf16[128,1024]{1,0:T(8,128)(2,1)S(1)}, u32[]{:S(2)}, u32[]{:S(2)}) collective-permute-start(bf16[128,1024]{1,0:T(8,128)(2,1)S(1)} %bitcast.34), channel_id=1, source_target_pairs={{0,8},{4,12},{8,0},{12,4},{1,9},{5,13},{9,1},{13,5},{2,10},{6,14},... | collective-permute-start | bytes 786440 | tf_op jit(solution)/shard_map/ppermute | solution.py:20
  74.8 12.7 %collective-permute-start.8 = (bf16[128,1024]{1,0:T(8,128)(2,1)S(1)}, bf16[128,1024]{1,0:T(8,128)(2,1)S(1)}, u32[]{:S(2)}, u32[]{:S(2)}) collective-permute-start(bf16[128,1024]{1,0:T(8,128)(2,1)S(1)} %bitcast.35), channel_id=1, source_target_pairs={{0,12},{4,0},{8,4},{12,8},{1,13},{5,1},{9,5},{13,9},{2,14},{6,2},{... | collective-permute-start | bytes 786440 | tf_op jit(solution)/shard_map/ppermute | solution.py:20
  76.7 13.2 %collective-permute-start.2 = (bf16[128,896]{1,0:T(8,128)(2,1)}, bf16[128,896]{1,0:T(8,128)(2,1)S(1)}, u32[]{:S(2)}, u32[]{:S(2)}) collective-permute-start(bf16[128,896]{1,0:T(8,128)(2,1)} %collective-permute-done.1.refs_2_), channel_id=1, source_target_pairs={{0,128},{128,256},{256,384},{384,448},{448,320},{320,192},{192,64}... | collective-permute-start | bytes 688136 | tf_op jit(solution)/shard_map/ppermute | solution.py:190
  81.2 24.5 %collective-permute-start.11 = (bf16[128,1024]{1,0:T(8,128)(2,1)S(1)}, bf16[128,1024]{1,0:T(8,128)(2,1)S(1)}, u32[]{:S(2)}, u32[]{:S(2)}) collective-permute-start(bf16[128,1024]{1,0:T(8,128)(2,1)S(1)} %bitcast.36), channel_id=1, source_target_pairs={{0,1},{1,0},{2,3},{3,2},{4,5},{5,4},{6,7},{7,6},{8,9},{9,8},{10,11... | collective-permute-start | bytes 786440 | tf_op jit(solution)/shard_map/ppermute | solution.py:20
  83.1 22.6 %collective-permute-start.14 = (bf16[128,1024]{1,0:T(8,128)(2,1)S(1)}, bf16[128,1024]{1,0:T(8,128)(2,1)S(1)}, u32[]{:S(2)}, u32[]{:S(2)}) collective-permute-start(bf16[128,1024]{1,0:T(8,128)(2,1)S(1)} %collective-permute-done.10.refs_3_), channel_id=1, source_target_pairs={{0,1},{1,0},{2,3},{3,2},{4,5},{5,4},{6,7},{7,6},{8,9},{9,8},{10,11... | collective-permute-start | bytes 786440 | tf_op jit(solution)/shard_map/ppermute | solution.py:20
  85.5 20.2 %collective-permute-start.13 = (bf16[128,1024]{1,0:T(8,128)(2,1)S(1)}, bf16[128,1024]{1,0:T(8,128)(2,1)S(1)}, u32[]{:S(2)}, u32[]{:S(2)}) collective-permute-start(bf16[128,1024]{1,0:T(8,128)(2,1)S(1)} %collective-permute-done.9.refs_2_), channel_id=1, source_target_pairs={{0,1},{1,0},{2,3},{3,2},{4,5},{5,4},{6,7},{7,6},{8,9},{9,8},{10,11... | collective-permute-start | bytes 786440 | tf_op jit(solution)/shard_map/ppermute | solution.py:20
  87.5 18.3 %collective-permute-start.12 = (bf16[128,1024]{1,0:T(8,128)(2,1)S(1)}, bf16[128,1024]{1,0:T(8,128)(2,1)S(1)}, u32[]{:S(2)}, u32[]{:S(2)}) collective-permute-start(bf16[128,1024]{1,0:T(8,128)(2,1)S(1)} %collective-permute-done.8.refs_1_), channel_id=1, source_target_pairs={{0,1},{1,0},{2,3},{3,2},{4,5},{5,4},{6,7},{7,6},{8,9},{9,8},{10,11... | collective-permute-start | bytes 786440 | tf_op jit(solution)/shard_map/ppermute | solution.py:20
  89.9 10.5 %collective-permute-start.3 = (bf16[128,896]{1,0:T(8,128)(2,1)S(1)}, bf16[128,896]{1,0:T(8,128)(2,1)S(1)}, u32[]{:S(2)}, u32[]{:S(2)}) collective-permute-start(bf16[128,896]{1,0:T(8,128)(2,1)S(1)} %collective-permute-done.2.refs_3_), channel_id=1, source_target_pairs={{0,128},{128,256},{256,384},{384,448},{448,320},{320,192},{192,64}... | collective-permute-start | bytes 688136 | tf_op jit(solution)/shard_map/ppermute | solution.py:190
  100.4 13.3 %collective-permute-start.4 = (bf16[128,896]{1,0:T(8,128)(2,1)S(1)}, bf16[128,896]{1,0:T(8,128)(2,1)S(1)}, u32[]{:S(2)}, u32[]{:S(2)}) collective-permute-start(bf16[128,896]{1,0:T(8,128)(2,1)S(1)} %collective-permute-done.3.refs_4_), channel_id=1, source_target_pairs={{0,128},{128,256},{256,384},{384,448},{448,320},{320,192},{192,64}... | collective-permute-start | bytes 688136 | tf_op jit(solution)/shard_map/ppermute | solution.py:190
  138.5 12.2 %collective-permute-start.17 = (bf16[256,512]{1,0:T(8,128)(2,1)S(1)}, bf16[256,512]{1,0:T(8,128)(2,1)S(1)}, u32[]{:S(2)}, u32[]{:S(2)}) collective-permute-start(bf16[256,512]{1,0:T(8,128)(2,1)S(1)} %get-tuple-element.51), channel_id=1, source_target_pairs={{0,16},{16,32},{32,48},{48,0},{1,17},{17,33},{33,49},{49,1},{2,18}... | collective-permute-start | bytes 786440 | tf_op jit(solution)/shard_map/ppermute | solution.py:20
  142.8 11.2 %collective-permute-start.18 = (bf16[256,512]{1,0:T(8,128)(2,1)S(1)}, bf16[256,512]{1,0:T(8,128)(2,1)S(1)}, u32[]{:S(2)}, u32[]{:S(2)}) collective-permute-start(bf16[256,512]{1,0:T(8,128)(2,1)S(1)} %get-tuple-element.52), channel_id=1, source_target_pairs={{0,32},{16,48},{32,0},{48,16},{1,33},{17,49},{33,1},{49,17},{2,34}... | collective-permute-start | bytes 786440 | tf_op jit(solution)/shard_map/ppermute | solution.py:20
  156.7 30.9 %all-to-all-start.1 = ((bf16[8,32,512]{2,1,0:T(8,128)(2,1)}), bf16[8,32,512]{2,1,0:T(8,128)(2,1)S(1)}, u32[]{:S(2)}, u32[]{:S(2)}) async-start(bf16[8,32,512]{2,1,0:T(8,128)(2,1)} %bitcast.5), calls=%async_computation.1 | async-start | bytes 524288 | tf_op jit(solution)/shard_map/all_to_all | solution.py:223
  173.1 15.3 %collective-permute-start.20 = (bf16[4,128,1024]{2,1,0:T(8,128)(2,1)S(1)}, bf16[4,128,1024]{2,1,0:T(8,128)(2,1)}, u32[]{:S(2)}, u32[]{:S(2)}) collective-permute-start(bf16[4,128,1024]{2,1,0:T(8,128)(2,1)S(1)} %get-tuple-element.58), channel_id=1, source_target_pairs={{0,1},{1,0},{2,3},{3,2},{4,5},{5,4},{6,7},{7,6},{8,9},{9,8},{10,11... | collective-permute-start | bytes 3145736 | tf_op jit(solution)/shard_map/ppermute | solution.py:20
  190.7 28.9 %all-to-all-start.3 = ((bf16[8,32,512]{2,1,0:T(8,128)(2,1)}), bf16[8,32,512]{2,1,0:T(8,128)(2,1)S(1)}, u32[]{:S(2)}, u32[]{:S(2)}) async-start(bf16[8,32,512]{2,1,0:T(8,128)(2,1)} %broadcast_in_dim.2), calls=%async_computation.4 | async-start | bytes 524288 | tf_op jit(solution)/shard_map/all_to_all | solution.py:236
  197.2 12.9 %collective-permute-start.22 = (bf16[128,1024]{1,0:T(8,128)(2,1)S(1)}, bf16[128,1024]{1,0:T(8,128)(2,1)S(1)}, u32[]{:S(2)}, u32[]{:S(2)}) collective-permute-start(bf16[128,1024]{1,0:T(8,128)(2,1)S(1)} %get-tuple-element.64), channel_id=1, source_target_pairs={{0,8},{4,12},{8,0},{12,4},{1,9},{5,13},{9,1},{13,5},{2,10},{6,14},... | collective-permute-start | bytes 786440 | tf_op jit(solution)/shard_map/ppermute | solution.py:20
  219.6 28.5 %all-to-all-start.2 = ((bf16[16,8,1024]{2,1,0:T(8,128)(2,1)}), bf16[16,8,1024]{2,1,0:T(8,128)(2,1)S(1)}, u32[]{:S(2)}, u32[]{:S(2)}) async-start(bf16[16,8,1024]{2,1,0:T(8,128)(2,1)} %fusion.4), calls=%async_computation.2 | async-start | bytes 524288 | tf_op jit(solution)/shard_map/all_to_all | solution.py:250
  228.1 12.4 %collective-permute-start.26 = (bf16[256,512]{1,0:T(8,128)(2,1)S(1)}, bf16[256,512]{1,0:T(8,128)(2,1)S(1)}, u32[]{:S(2)}, u32[]{:S(2)}) collective-permute-start(bf16[256,512]{1,0:T(8,128)(2,1)S(1)} %bitcast.29), channel_id=1, source_target_pairs={{0,16},{16,32},{32,48},{48,0},{1,17},{17,33},{33,49},{49,1},{2,18}... | collective-permute-start | bytes 786440 | tf_op jit(solution)/shard_map/ppermute | solution.py:20
  (34 other events, 375.3 us)
Sparse Core Ops, SparseCore 0:
  150.1 72.9 reduce-scatter.1

commit v6 on v5

--- a/solution.py
+++ b/solution.py
@@ -9,11 +9,10 @@
 corr_second = 1.0 - 0.999**10
 
 NZ, NX, NY, NH, NC = 8, 4, 4, 2, 2
-ORDER = (0, 2, 4, 6, 7, 5, 3, 1)
-RING = [(ORDER[i], ORDER[(i + 1) % NZ]) for i in range(NZ)]
 bf16, f32 = jnp.bfloat16, jnp.float32
 VMEM = pl.BlockSpec(memory_space=pltpu.VMEM)
 SMEM = pl.BlockSpec(memory_space=pltpu.SMEM)
+DMA = pltpu.SemaphoreType.DMA((6,))
 
 
 def shift(value, axis, size, by):
@@ -24,43 +23,49 @@
     return lax.dot_general(a, b, (contract, ((), ())), preferred_element_type=f32)
 
 
-def call(kernel, n_in, outs, scratch=(), flops=0, limit=20):
+def call(kernel, n_in, outs, scratch=(), flops=0, limit=20, place=VMEM):
     return pl.pallas_call(
         kernel,
         out_shape=tuple(jax.ShapeDtypeStruct(*o) for o in outs),
-        in_specs=[SMEM] + [VMEM] * n_in,
+        in_specs=[SMEM] + [place] * n_in,
         out_specs=tuple(VMEM for _ in outs),
-        scratch_shapes=[pltpu.VMEM(*s) for s in scratch],
+        scratch_shapes=[s if isinstance(s, type(DMA)) else pltpu.VMEM(*s) for s in scratch],
         compiler_params=pltpu.CompilerParams(vmem_limit_bytes=limit << 20),
         cost_estimate=pl.CostEstimate(flops=flops, bytes_accessed=4 << 20, transcendentals=0),
     )
 
 
-def ring_block(zl, hop):
-    half = zl >> 1
-    place = jnp.where((zl & 1) == 0, half, NZ - 1 - half)
-    place = (place - hop) & (NZ - 1)
-    return jnp.where(place < NZ // 2, 2 * place, 2 * NZ - 1 - 2 * place)
-
-
-def prepare(pos, gate, up, cot, weight, basis, hidden, pack, both, plain):
+def prepare(pos, gate, up, cot, weight, basis, hidden, pack, both, g_in, u_in, c_in, plain, sems):
     x, y, c = pos[0], pos[1], pos[2]
+    moves = (
+        (cot, c_in),
+        (gate, g_in),
+        (up, u_in),
+        (weight, both.at[:896]),
+        (basis.at[:, :256], both.at[896:1152]),
+        (basis.at[:, 256:], both.at[1152:]),
+    )
+    copies = [pltpu.make_async_copy(a, b, sems.at[i]) for i, (a, b) in enumerate(moves)]
+    for copy in copies:
+        copy.start()
+    copies[0].wait()
     for r in range(NX):
         block = lax.rem(x + r, NX) * 256
         for zl in range(NZ):
-            piece = cot[:, pl.ds(pl.multiple_of(zl * 1024 + block, 256), 256)]
+            piece = c_in[:, pl.ds(pl.multiple_of(zl * 1024 + block, 256), 256)]
             for zh in range(NH):
                 pack[zl * NH + zh, :, r * 256 : (r + 1) * 256] = piece
-    both[:896, :] = weight[...]
-    both[896:1152, :] = basis[:, :256]
-    both[1152:, :] = basis[:, 256:]
-    g = gate[...].astype(f32)
-    plain[...] = g * jax.nn.sigmoid(g) * up[...].astype(f32)
+    copies[1].wait()
+    copies[2].wait()
+    g = g_in[...].astype(f32)
+    plain[...] = g * jax.nn.sigmoid(g) * u_in[...].astype(f32)
     for cr in range(NC):
         for yr in range(NY):
             first = (lax.rem(y + yr, NY) * 4 + lax.rem(c + cr, NC)) * 8
             pair = [plain[pl.ds(pl.multiple_of(first + zh * 16, 8), 8), :] for zh in range(NH)]
             hidden[pl.ds((cr * NY + yr) * 16, 16), :] = jnp.concatenate(pair, 0).astype(bf16)
+    for copy in copies[3:]:
+        copy.wait()
 
 
 def backward(pos, *refs):
@@ -89,13 +94,8 @@
     lax.fori_loop(0, 4, rows, 0)
 
 
-def project(pos, *refs):
-    hiddens, reduced = refs[:8], refs[8]
-    tile, outs, total, blocks = refs[9], refs[10:14], *refs[14:]
-    x, zl_own = pos[0], pos[3]
-    for hop in range(NZ):
-        to = pl.ds(pl.multiple_of(ring_block(zl_own, hop) * 128, 128), 128)
-        tile[to, :] = hiddens[hop][...]
+def project(pos, tile, reduced, o0, o1, o2, o3, total, blocks):
+    x = pos[0]
     total[...] = dot(tile[...], reduced[...], ((0,), (0,)))
     spare = jnp.zeros((4, total.shape[1]), f32)
     for xs in range(NX):
@@ -103,7 +103,7 @@
             first = zl * 112 + xs * 28
             block = jnp.concatenate([total[first : first + 28, :], spare], 0)
             blocks[xs, zl * 32 : zl * 32 + 32, :] = block.astype(bf16)
-    for xr, out in enumerate(outs):
+    for xr, out in enumerate((o0, o1, o2, o3)):
         out[...] = blocks[lax.rem(x + xr, NX)]
 
 
@@ -164,7 +164,7 @@
 
 
 def body(gate, up, weight, basis, cotangent, moment1, moment2):
-    pos = jnp.stack([lax.axis_index(a) for a in ("x", "y", "c", "zl")]).astype(jnp.int32)
+    pos = jnp.stack([lax.axis_index(a) for a in ("x", "y", "c")]).astype(jnp.int32)
     rows, ff = gate.shape
     mine, width = cotangent.shape
     cols = width // NZ
@@ -179,15 +179,20 @@
             ((NZ * NH, mine, cols), bf16),
             ((ff + 2 * deep, deep), bf16),
         ],
-        [((rows, ff), f32)],
+        [
+            ((rows, ff), bf16),
+            ((rows, ff), bf16),
+            ((mine, width), bf16),
+            ((rows, ff), f32),
+            DMA,
+        ],
+        place=pl.BlockSpec(memory_space=pl.ANY),
     )(pos, gate, up, cotangent, weight, basis)
 
+    tile = lax.all_gather(hidden, "zl", axis=0, tiled=True)
     got = lax.all_to_all(pack, ("zl", "zh"), 0, 0, tiled=True).reshape(rows, cols)
     boths = [both] + [shift(both, "x", NX, by) for by in range(1, NX)]
     got, *boths = lax.optimization_barrier((got, *boths))
-    hiddens = [hidden]
-    for _ in range(1, NZ - 2):
-        hiddens.append(lax.ppermute(hiddens[-1], "zl", RING))
     cots = [got] + [shift(got, "y", NY, by) for by in range(1, NY)]
     cots = cots + [shift(piece, "c", NC, 1) for piece in cots]
 
@@ -198,9 +203,6 @@
         [((NZ * rows, cols), bf16)],
         flops=3 * 10**9,
     )(pos, *cots, *boths)
-    hiddens[-1], partial, reduced = lax.optimization_barrier((hiddens[-1], partial, reduced))
-    for _ in range(2):
-        hiddens.append(lax.ppermute(hiddens[-1], "zl", RING))
     grad_hidden = lax.psum_scatter(partial, "zl", scatter_dimension=0, tiled=True)
     grad_gate, grad_up = call(
         finish_grad,
@@ -209,13 +211,13 @@
         [((rows, ff), f32), ((rows, ff), f32)],
     )(pos, grad_hidden, gate, up)
 
-    tile, *parts = call(
+    parts = call(
         project,
-        9,
-        [((NZ * rows, ff), bf16)] + [((NZ * slot, rank), bf16)] * NX,
+        2,
+        [((NZ * slot, rank), bf16)] * NX,
         [((ff, rank), f32), ((NX, NZ * slot, rank), bf16)],
         flops=10**9,
-    )(pos, *hiddens, reduced)
+    )(pos, tile, reduced)
     total = parts[0].astype(f32)
     for by in range(1, NX):
         total = total + shift(parts[by], "x", NX, -by).astype(f32)

time: 263 us -> 233 us (0.89); the launches traced: 259 us -> 232 us
  starting transfers between devices: 135 us -> 91.7 us
  waiting for transfers between devices: 68.2 us -> 88 us
  local copies, waits for them, and re-layouts: 19.2 us -> 15 us
    ppermute x7 -> x0, starting transfers between devices: 35.1 us -> none  [body(): hiddens.append(lax.ppermute(hiddens[-1], 'zl', RING))]
    ppermute x20, waiting for transfers between devices: 33.8 us -> 64.4 us  [shift(): lax.ppermute(value, axis, [(i, (i - by) % size) for i in range(size)])]
    ppermute x7 -> x0, waiting for transfers between devices: 16.4 us -> none  [body(): hiddens.append(lax.ppermute(hiddens[-1], 'zl', RING))]
    ppermute x20, starting transfers between devices: 63.2 us -> 56.9 us  [shift(): lax.ppermute(value, axis, [(i, (i - by) % size) for i in range(size)])]
    all_to_all x1, waiting for transfers between devices: 12.6 us -> 17.7 us  [body(): lax.all_to_all(total, 'zl', 0, 0, tiled=True).reshape(NZ, slot, rank)]
    unnamed x52 -> x42, local copies, waits for them, and re-layouts: 18.5 us -> 14.3 us
  transfers between devices with their start and end apart: 32 -> 26, of which waited for: 17 -> 14; matrix products, arithmetic and copies ran while one was open for 2% -> 2% of each run, Pallas kernels for 5% -> 6%
where the time goes in v6:
time: 233 us; the launch traced here: 232 us
  starting transfers between devices  91.7 us (39%)
  waiting for transfers between devices  88 us (38%)
  Pallas kernels  18.8 us (8%)
  local copies, waits for them, and re-layouts  15 us (6%)
  between operations  14.4 us (6%)
  other arithmetic  4.1 us (2%)
    ppermute x20, waiting for transfers between devices, shift(): lax.ppermute(value, axis, [(i, (i - by) % size) for i in range(size)])  64.4 us
    ppermute x20, starting transfers between devices, shift(): lax.ppermute(value, axis, [(i, (i - by) % size) for i in range(size)])  56.9 us
    all_to_all x1, waiting for transfers between devices, body(): lax.all_to_all(total, 'zl', 0, 0, tiled=True).reshape(NZ, slot, rank)  17.7 us
    all_to_all x1, starting transfers between devices, body(): lax.all_to_all(pack, ('zl', 'zh'), 0, 0, tiled=True).reshape(rows, cols)  15.2 us
    unnamed x42, local copies, waits for them, and re-layouts  14.3 us
    all_to_all x1, starting transfers between devices, body(): lax.all_to_all(total, 'zl', 0, 0, tiled=True).reshape(NZ, slot, rank)  9.52 us
    all_to_all x1, starting transfers between devices, body(): total = lax.all_to_all(total, ('zl', 'zh'), 0, 0, tiled=True)  6.59 us
    pallas_call x1, Pallas kernels, body(): call(backward, 12, [((NZ * rows, ff), bf16), ((NZ * rows, rank), bf16)],...  5.92 us
  transfers between devices with their start and end apart: 26, of which 14 were waited for; matrix products, arithmetic and copies ran while one was open for 2% of the time, Pallas kernels for 6%

profile of v6, /device:TPU:24, one launch (start us, length us, event | category | flops | bytes accessed | tf_op | source)
XLA Modules:
  0.0 232.0 jit_solution(13632555458410430345)
XLA Ops:
  14.7 15.2 %all-to-all-start = ((bf16[16,8,1024]{2,1,0:T(8,128)(2,1)}), bf16[16,8,1024]{2,1,0:T(8,128)(2,1)S(1)}, u32[]{:S(2)}, u32[]{:S(2)}) async-start(bf16[16,8,1024]{2,1,0:T(8,128)(2,1)} %get-tuple-element.35), calls=%async_computation | async-start | bytes 524288 | tf_op jit(solution)/shard_map/all_to_all | solution.py:193
  30.0 4.7 %collective-permute-start = (bf16[1408,256]{1,0:T(8,128)(2,1)S(1)}, bf16[1408,256]{1,0:T(8,128)(2,1)S(1)}, u32[]{:S(2)}, u32[]{:S(2)}) collective-permute-start(bf16[1408,256]{1,0:T(8,128)(2,1)S(1)} %get-tuple-element.38.refs_8_.b0), channel_id=1, source_target_pairs={{0,48},{16,0},{32,16},{48,32},{1,49},{17,1},{33,17},{49,33},{2,50}... | collective-permute-start | bytes 2162696 | tf_op jit(solution)/shard_map/ppermute | solution.py:19
  37.4 2.8 %collective-permute-start.2 = (bf16[1408,256]{1,0:T(8,128)(2,1)S(1)}, bf16[1408,256]{1,0:T(8,128)(2,1)S(1)}, u32[]{:S(2)}, u32[]{:S(2)}) collective-permute-start(bf16[1408,256]{1,0:T(8,128)(2,1)S(1)} %get-tuple-element.38.refs_8_.b0), channel_id=1, source_target_pairs={{0,16},{16,32},{32,48},{48,0},{1,17},{17,33},{33,49},{49,1},{2,18}... | collective-permute-start | bytes 2162696 | tf_op jit(solution)/shard_map/ppermute | solution.py:19
  40.2 25.1 %collective-permute-done.refs_9_.b1 = bf16[1408,256]{1,0:T(8,128)(2,1)S(1)} collective-permute-done((bf16[1408,256]{1,0:T(8,128)(2,1)S(1)}, bf16[1408,256]{1,0:T(8,128)(2,1)S(1)}, u32[]{:S(2)}, u32[]{:S(2)}) %collective-permute-start) | collective-permute-done | bytes 720928 | tf_op jit(solution)/shard_map/ppermute | solution.py:19
  65.2 5.6 %collective-permute-done.2.refs_11_.b3 = bf16[1408,256]{1,0:T(8,128)(2,1)S(1)} collective-permute-done((bf16[1408,256]{1,0:T(8,128)(2,1)S(1)}, bf16[1408,256]{1,0:T(8,128)(2,1)S(1)}, u32[]{:S(2)}, u32[]{:S(2)}) %collective-permute-start.2) | collective-permute-done | bytes 720928 | tf_op jit(solution)/shard_map/ppermute | solution.py:19
  73.5 2.8 %collective-permute-start.4 = (bf16[128,1024]{1,0:T(8,128)(2,1)S(1)}, bf16[128,1024]{1,0:T(8,128)(2,1)S(1)}, u32[]{:S(2)}, u32[]{:S(2)}) collective-permute-start(bf16[128,1024]{1,0:T(8,128)(2,1)S(1)} %bitcast.33), channel_id=1, source_target_pairs={{0,8},{4,12},{8,0},{12,4},{1,9},{5,13},{9,1},{13,5},{2,10},{6,14},... | collective-permute-start | bytes 786440 | tf_op jit(solution)/shard_map/ppermute | solution.py:19
  76.3 4.1 %collective-permute-start.5 = (bf16[128,1024]{1,0:T(8,128)(2,1)S(1)}, bf16[128,1024]{1,0:T(8,128)(2,1)S(1)}, u32[]{:S(2)}, u32[]{:S(2)}) collective-permute-start(bf16[128,1024]{1,0:T(8,128)(2,1)S(1)} %bitcast.34), channel_id=1, source_target_pairs={{0,4},{4,8},{8,12},{12,0},{1,5},{5,9},{9,13},{13,1},{2,6},{6,10},{... | collective-permute-start | bytes 786440 | tf_op jit(solution)/shard_map/ppermute | solution.py:19
  82.4 5.5 %collective-permute-done.3.refs_1_ = bf16[128,1024]{1,0:T(8,128)(2,1)S(1)} collective-permute-done((bf16[128,1024]{1,0:T(8,128)(2,1)S(1)}, bf16[128,1024]{1,0:T(8,128)(2,1)S(1)}, u32[]{:S(2)}, u32[]{:S(2)}) %collective-permute-start.3) | collective-permute-done | bytes 262176 | tf_op jit(solution)/shard_map/ppermute | solution.py:19
  95.7 5.9 %shard_map.119 = (bf16[1024,896]{1,0:T(8,128)(2,1)}, bf16[1024,512]{1,0:T(8,128)(2,1)S(1)}) custom-call(s32[3]{0:T(128)S(1)} %pad_add_fusion.pos, bf16[128,1024]{1,0:T(8,128)(2,1)S(1)} %bitcast.36, bf16[128,1024]{1,0:T(8,128)(2,1)S(1)} %collective-permute-done.3.refs_1_, bf16[128,1024]{1,0:T(8,128)(2,1)S(1)} %collective-permute-done.4.refs_2_, ...), custom_call_target="tpu_custom_call" | custom-call | flops 3000000000 | bytes 4194304 | tf_op jit(solution)/shard_map/pallas_call | solution.py:199
  109.0 2.8 %collective-permute-start.11 = (bf16[256,512]{1,0:T(8,128)(2,1)S(1)}, bf16[256,512]{1,0:T(8,128)(2,1)S(1)}, u32[]{:S(2)}, u32[]{:S(2)}) collective-permute-start(bf16[256,512]{1,0:T(8,128)(2,1)S(1)} %get-tuple-element.45), channel_id=1, source_target_pairs={{0,32},{16,48},{32,0},{48,16},{1,33},{17,49},{33,1},{49,17},{2,34}... | collective-permute-start | bytes 786440 | tf_op jit(solution)/shard_map/ppermute | solution.py:19
  111.8 4.4 %collective-permute-start.12 = (bf16[256,512]{1,0:T(8,128)(2,1)S(1)}, bf16[256,512]{1,0:T(8,128)(2,1)S(1)}, u32[]{:S(2)}, u32[]{:S(2)}) collective-permute-start(bf16[256,512]{1,0:T(8,128)(2,1)S(1)} %get-tuple-element.46), channel_id=1, source_target_pairs={{0,48},{16,0},{32,16},{48,32},{1,49},{17,1},{33,17},{49,33},{2,50}... | collective-permute-start | bytes 786440 | tf_op jit(solution)/shard_map/ppermute | solution.py:19
  116.3 7.9 %collective-permute-done.10 = bf16[256,512]{1,0:T(8,128)(2,1)S(1)} collective-permute-done((bf16[256,512]{1,0:T(8,128)(2,1)S(1)}, bf16[256,512]{1,0:T(8,128)(2,1)S(1)}, u32[]{:S(2)}, u32[]{:S(2)}) %collective-permute-start.10) | collective-permute-done | bytes 262176 | tf_op jit(solution)/shard_map/ppermute | solution.py:19
  127.5 9.5 %all-to-all-start.1 = ((bf16[8,32,512]{2,1,0:T(8,128)(2,1)}), bf16[8,32,512]{2,1,0:T(8,128)(2,1)S(1)}, u32[]{:S(2)}, u32[]{:S(2)}) async-start(bf16[8,32,512]{2,1,0:T(8,128)(2,1)} %bitcast.4), calls=%async_computation.1 | async-start | bytes 524288 | tf_op jit(solution)/shard_map/all_to_all | solution.py:225
  141.9 3.4 %shard_map.121 = (bf16[128,1024]{1,0:T(8,128)(2,1)S(1)}, bf16[128,1024]{1,0:T(8,128)(2,1)S(1)}, bf16[128,1024]{1,0:T(8,128)(2,1)S(1)}, bf16[128,1024]{1,0:T(8,128)(2,1)S(1)}, bf16[4,128,1024]{2,1,0:T(8,128)(2,1)S(1)}) custom-call(s32[3]{0:T(128)S(1)} %pad_add_fusion.pos, bf16[1024,896]{1,0:T(8,128)(2,1)S(1)} %copy-done.10, ...), custom_call_target="tpu_custom_call" | custom-call | flops 2000000000 | bytes 4194304 | tf_op jit(solution)/shard_map/pallas_call | solution.py:231
  147.3 17.7 %all-to-all-done.1 = bf16[8,32,512]{2,1,0:T(8,128)(2,1)S(1)} async-done(((bf16[8,32,512]{2,1,0:T(8,128)(2,1)}), bf16[8,32,512]{2,1,0:T(8,128)(2,1)S(1)}, u32[]{:S(2)}, u32[]{:S(2)}) %all-to-all-start.1) | async-done | bytes 262176 | tf_op jit(solution)/shard_map/all_to_all | solution.py:225
  168.1 3.4 %all-to-all-start.3 = ((bf16[8,32,512]{2,1,0:T(8,128)(2,1)}), bf16[8,32,512]{2,1,0:T(8,128)(2,1)S(1)}, u32[]{:S(2)}, u32[]{:S(2)}) async-start(bf16[8,32,512]{2,1,0:T(8,128)(2,1)} %broadcast_in_dim.2), calls=%async_computation.4 | async-start | bytes 524288 | tf_op jit(solution)/shard_map/all_to_all | solution.py:238
  171.5 3.1 %collective-permute-start.14 = (bf16[128,1024]{1,0:T(8,128)(2,1)S(1)}, bf16[128,1024]{1,0:T(8,128)(2,1)S(1)}, u32[]{:S(2)}, u32[]{:S(2)}) collective-permute-start(bf16[128,1024]{1,0:T(8,128)(2,1)S(1)} %get-tuple-element.55), channel_id=1, source_target_pairs={{0,4},{4,8},{8,12},{12,0},{1,5},{5,9},{9,13},{13,1},{2,6},{6,10},{... | collective-permute-start | bytes 786440 | tf_op jit(solution)/shard_map/ppermute | solution.py:19
  176.5 2.8 %collective-permute-start.16 = (bf16[128,1024]{1,0:T(8,128)(2,1)S(1)}, bf16[128,1024]{1,0:T(8,128)(2,1)S(1)}, u32[]{:S(2)}, u32[]{:S(2)}) collective-permute-start(bf16[128,1024]{1,0:T(8,128)(2,1)S(1)} %get-tuple-element.57), channel_id=1, source_target_pairs={{0,12},{4,0},{8,4},{12,8},{1,13},{5,1},{9,5},{13,9},{2,14},{6,2},{... | collective-permute-start | bytes 786440 | tf_op jit(solution)/shard_map/ppermute | solution.py:19
  180.9 4.7 %collective-permute-done.15 = bf16[128,1024]{1,0:T(8,128)(2,1)S(1)} collective-permute-done((bf16[128,1024]{1,0:T(8,128)(2,1)S(1)}, bf16[128,1024]{1,0:T(8,128)(2,1)S(1)}, u32[]{:S(2)}, u32[]{:S(2)}) %collective-permute-start.15) | collective-permute-done | bytes 262176 | tf_op jit(solution)/shard_map/ppermute | solution.py:19
  189.0 5.8 %all-to-all-done.3 = bf16[8,32,512]{2,1,0:T(8,128)(2,1)S(1)} async-done(((bf16[8,32,512]{2,1,0:T(8,128)(2,1)}), bf16[8,32,512]{2,1,0:T(8,128)(2,1)S(1)}, u32[]{:S(2)}, u32[]{:S(2)}) %all-to-all-start.3) | async-done | bytes 262176 | tf_op jit(solution)/shard_map/all_to_all | solution.py:238
  194.8 6.6 %all-to-all-start.2 = ((bf16[16,8,1024]{2,1,0:T(8,128)(2,1)}), bf16[16,8,1024]{2,1,0:T(8,128)(2,1)S(1)}, u32[]{:S(2)}, u32[]{:S(2)}) async-start(bf16[16,8,1024]{2,1,0:T(8,128)(2,1)} %fusion.4), calls=%async_computation.2 | async-start | bytes 524288 | tf_op jit(solution)/shard_map/all_to_all | solution.py:252
  201.4 5.4 %collective-permute-start.17 = (bf16[256,512]{1,0:T(8,128)(2,1)S(1)}, bf16[256,512]{1,0:T(8,128)(2,1)S(1)}, u32[]{:S(2)}, u32[]{:S(2)}) collective-permute-start(bf16[256,512]{1,0:T(8,128)(2,1)S(1)} %bitcast.28), channel_id=1, source_target_pairs={{0,48},{16,0},{32,16},{48,32},{1,49},{17,1},{33,17},{49,33},{2,50}... | collective-permute-start | bytes 786440 | tf_op jit(solution)/shard_map/ppermute | solution.py:19
  208.8 2.8 %collective-permute-start.19 = (bf16[256,512]{1,0:T(8,128)(2,1)S(1)}, bf16[256,512]{1,0:T(8,128)(2,1)S(1)}, u32[]{:S(2)}, u32[]{:S(2)}) collective-permute-start(bf16[256,512]{1,0:T(8,128)(2,1)S(1)} %bitcast.30), channel_id=1, source_target_pairs={{0,16},{16,32},{32,48},{48,0},{1,17},{17,33},{33,49},{49,1},{2,18}... | collective-permute-start | bytes 786440 | tf_op jit(solution)/shard_map/ppermute | solution.py:19
  216.1 2.9 %collective-permute-done.18.s2 = bf16[256,512]{1,0:T(8,128)(2,1)S(1)} collective-permute-done((bf16[256,512]{1,0:T(8,128)(2,1)S(1)}, bf16[256,512]{1,0:T(8,128)(2,1)S(1)}, u32[]{:S(2)}, u32[]{:S(2)}) %collective-permute-start.18) | collective-permute-done | bytes 262176 | tf_op jit(solution)/shard_map/ppermute | solution.py:19
  (87 shorter events, 62.7 us)
Async XLA Ops:
  7.2 95.4 %all-gather.2.cloned.1.call-start = ((), (), s32[]{:S(2)}) async-start(), calls=%async_computation.5 | async-start | bytes 2064384 | tf_op jit(solution)/shard_map/all_gather | solution.py:192
  14.7 56.1 %all-to-all-start = ((bf16[16,8,1024]{2,1,0:T(8,128)(2,1)}), bf16[16,8,1024]{2,1,0:T(8,128)(2,1)S(1)}, u32[]{:S(2)}, u32[]{:S(2)}) async-start(bf16[16,8,1024]{2,1,0:T(8,128)(2,1)} %get-tuple-element.35), calls=%async_computation | async-start | bytes 524288 | tf_op jit(solution)/shard_map/all_to_all | solution.py:193
  29.9 181.6 %reduce-scatter.2.cloned.1.call-start = ((), (), s32[]{:S(2)}) async-start(), calls=%async_computation.6 | async-start | bytes 2064384 | tf_op jit(solution)/shard_map/reduce_scatter | solution.py:206
  30.0 35.3 %collective-permute-start = (bf16[1408,256]{1,0:T(8,128)(2,1)S(1)}, bf16[1408,256]{1,0:T(8,128)(2,1)S(1)}, u32[]{:S(2)}, u32[]{:S(2)}) collective-permute-start(bf16[1408,256]{1,0:T(8,128)(2,1)S(1)} %get-tuple-element.38.refs_8_.b0), channel_id=1, source_target_pairs={{0,48},{16,0},{32,16},{48,32},{1,49},{17,1},{33,17},{49,33},{2,50}... | collective-permute-start | bytes 2162696 | tf_op jit(solution)/shard_map/ppermute | solution.py:19
  34.7 30.6 %collective-permute-start.1 = (bf16[1408,256]{1,0:T(8,128)(2,1)S(1)}, bf16[1408,256]{1,0:T(8,128)(2,1)S(1)}, u32[]{:S(2)}, u32[]{:S(2)}) collective-permute-start(bf16[1408,256]{1,0:T(8,128)(2,1)S(1)} %get-tuple-element.38.refs_8_.b0), channel_id=1, source_target_pairs={{0,32},{16,48},{32,0},{48,16},{1,33},{17,49},{33,1},{49,17},{2,34}... | collective-permute-start | bytes 2162696 | tf_op jit(solution)/shard_map/ppermute | solution.py:19
  37.4 33.4 %collective-permute-start.2 = (bf16[1408,256]{1,0:T(8,128)(2,1)S(1)}, bf16[1408,256]{1,0:T(8,128)(2,1)S(1)}, u32[]{:S(2)}, u32[]{:S(2)}) collective-permute-start(bf16[1408,256]{1,0:T(8,128)(2,1)S(1)} %get-tuple-element.38.refs_8_.b0), channel_id=1, source_target_pairs={{0,16},{16,32},{32,48},{48,0},{1,17},{17,33},{33,49},{49,1},{2,18}... | collective-permute-start | bytes 2162696 | tf_op jit(solution)/shard_map/ppermute | solution.py:19
  70.8 17.0 %collective-permute-start.3 = (bf16[128,1024]{1,0:T(8,128)(2,1)S(1)}, bf16[128,1024]{1,0:T(8,128)(2,1)S(1)}, u32[]{:S(2)}, u32[]{:S(2)}) collective-permute-start(bf16[128,1024]{1,0:T(8,128)(2,1)S(1)} %bitcast.32), channel_id=1, source_target_pairs={{0,12},{4,0},{8,4},{12,8},{1,13},{5,1},{9,5},{13,9},{2,14},{6,2},{... | collective-permute-start | bytes 786440 | tf_op jit(solution)/shard_map/ppermute | solution.py:19
  73.5 16.3 %collective-permute-start.4 = (bf16[128,1024]{1,0:T(8,128)(2,1)S(1)}, bf16[128,1024]{1,0:T(8,128)(2,1)S(1)}, u32[]{:S(2)}, u32[]{:S(2)}) collective-permute-start(bf16[128,1024]{1,0:T(8,128)(2,1)S(1)} %bitcast.33), channel_id=1, source_target_pairs={{0,8},{4,12},{8,0},{12,4},{1,9},{5,13},{9,1},{13,5},{2,10},{6,14},... | collective-permute-start | bytes 786440 | tf_op jit(solution)/shard_map/ppermute | solution.py:19
  76.3 15.9 %collective-permute-start.5 = (bf16[128,1024]{1,0:T(8,128)(2,1)S(1)}, bf16[128,1024]{1,0:T(8,128)(2,1)S(1)}, u32[]{:S(2)}, u32[]{:S(2)}) collective-permute-start(bf16[128,1024]{1,0:T(8,128)(2,1)S(1)} %bitcast.34), channel_id=1, source_target_pairs={{0,4},{4,8},{8,12},{12,0},{1,5},{5,9},{9,13},{13,1},{2,6},{6,10},{... | collective-permute-start | bytes 786440 | tf_op jit(solution)/shard_map/ppermute | solution.py:19
  80.4 13.7 %collective-permute-start.6 = (bf16[128,1024]{1,0:T(8,128)(2,1)S(1)}, bf16[128,1024]{1,0:T(8,128)(2,1)S(1)}, u32[]{:S(2)}, u32[]{:S(2)}) collective-permute-start(bf16[128,1024]{1,0:T(8,128)(2,1)S(1)} %bitcast.35), channel_id=1, source_target_pairs={{0,1},{1,0},{2,3},{3,2},{4,5},{5,4},{6,7},{7,6},{8,9},{9,8},{10,11... | collective-permute-start | bytes 786440 | tf_op jit(solution)/shard_map/ppermute | solution.py:19
  87.9 6.3 %collective-permute-start.7 = (bf16[128,1024]{1,0:T(8,128)(2,1)S(1)}, bf16[128,1024]{1,0:T(8,128)(2,1)S(1)}, u32[]{:S(2)}, u32[]{:S(2)}) collective-permute-start(bf16[128,1024]{1,0:T(8,128)(2,1)S(1)} %collective-permute-done.3.refs_1_), channel_id=1, source_target_pairs={{0,1},{1,0},{2,3},{3,2},{4,5},{5,4},{6,7},{7,6},{8,9},{9,8},{10,11... | collective-permute-start | bytes 786440 | tf_op jit(solution)/shard_map/ppermute | solution.py:19
  107.1 17.1 %collective-permute-start.10 = (bf16[256,512]{1,0:T(8,128)(2,1)S(1)}, bf16[256,512]{1,0:T(8,128)(2,1)S(1)}, u32[]{:S(2)}, u32[]{:S(2)}) collective-permute-start(bf16[256,512]{1,0:T(8,128)(2,1)S(1)} %get-tuple-element.44), channel_id=1, source_target_pairs={{0,16},{16,32},{32,48},{48,0},{1,17},{17,33},{33,49},{49,1},{2,18}... | collective-permute-start | bytes 786440 | tf_op jit(solution)/shard_map/ppermute | solution.py:19
  109.0 15.2 %collective-permute-start.11 = (bf16[256,512]{1,0:T(8,128)(2,1)S(1)}, bf16[256,512]{1,0:T(8,128)(2,1)S(1)}, u32[]{:S(2)}, u32[]{:S(2)}) collective-permute-start(bf16[256,512]{1,0:T(8,128)(2,1)S(1)} %get-tuple-element.45), channel_id=1, source_target_pairs={{0,32},{16,48},{32,0},{48,16},{1,33},{17,49},{33,1},{49,17},{2,34}... | collective-permute-start | bytes 786440 | tf_op jit(solution)/shard_map/ppermute | solution.py:19
  111.8 14.9 %collective-permute-start.12 = (bf16[256,512]{1,0:T(8,128)(2,1)S(1)}, bf16[256,512]{1,0:T(8,128)(2,1)S(1)}, u32[]{:S(2)}, u32[]{:S(2)}) collective-permute-start(bf16[256,512]{1,0:T(8,128)(2,1)S(1)} %get-tuple-element.46), channel_id=1, source_target_pairs={{0,48},{16,0},{32,16},{48,32},{1,49},{17,1},{33,17},{49,33},{2,50}... | collective-permute-start | bytes 786440 | tf_op jit(solution)/shard_map/ppermute | solution.py:19
  127.5 37.4 %all-to-all-start.1 = ((bf16[8,32,512]{2,1,0:T(8,128)(2,1)}), bf16[8,32,512]{2,1,0:T(8,128)(2,1)S(1)}, u32[]{:S(2)}, u32[]{:S(2)}) async-start(bf16[8,32,512]{2,1,0:T(8,128)(2,1)} %bitcast.4), calls=%async_computation.1 | async-start | bytes 524288 | tf_op jit(solution)/shard_map/all_to_all | solution.py:225
  145.3 20.4 %collective-permute-start.13 = (bf16[4,128,1024]{2,1,0:T(8,128)(2,1)S(1)}, bf16[4,128,1024]{2,1,0:T(8,128)(2,1)}, u32[]{:S(2)}, u32[]{:S(2)}) collective-permute-start(bf16[4,128,1024]{2,1,0:T(8,128)(2,1)S(1)} %get-tuple-element.50), channel_id=1, source_target_pairs={{0,1},{1,0},{2,3},{3,2},{4,5},{5,4},{6,7},{7,6},{8,9},{9,8},{10,11... | collective-permute-start | bytes 3145736 | tf_op jit(solution)/shard_map/ppermute | solution.py:19
  168.1 26.8 %all-to-all-start.3 = ((bf16[8,32,512]{2,1,0:T(8,128)(2,1)}), bf16[8,32,512]{2,1,0:T(8,128)(2,1)S(1)}, u32[]{:S(2)}, u32[]{:S(2)}) async-start(bf16[8,32,512]{2,1,0:T(8,128)(2,1)} %broadcast_in_dim.2), calls=%async_computation.4 | async-start | bytes 524288 | tf_op jit(solution)/shard_map/all_to_all | solution.py:238
  171.5 9.4 %collective-permute-start.14 = (bf16[128,1024]{1,0:T(8,128)(2,1)S(1)}, bf16[128,1024]{1,0:T(8,128)(2,1)S(1)}, u32[]{:S(2)}, u32[]{:S(2)}) collective-permute-start(bf16[128,1024]{1,0:T(8,128)(2,1)S(1)} %get-tuple-element.55), channel_id=1, source_target_pairs={{0,4},{4,8},{8,12},{12,0},{1,5},{5,9},{9,13},{13,1},{2,6},{6,10},{... | collective-permute-start | bytes 786440 | tf_op jit(solution)/shard_map/ppermute | solution.py:19
  174.6 11.0 %collective-permute-start.15 = (bf16[128,1024]{1,0:T(8,128)(2,1)S(1)}, bf16[128,1024]{1,0:T(8,128)(2,1)S(1)}, u32[]{:S(2)}, u32[]{:S(2)}) collective-permute-start(bf16[128,1024]{1,0:T(8,128)(2,1)S(1)} %get-tuple-element.56), channel_id=1, source_target_pairs={{0,8},{4,12},{8,0},{12,4},{1,9},{5,13},{9,1},{13,5},{2,10},{6,14},... | collective-permute-start | bytes 786440 | tf_op jit(solution)/shard_map/ppermute | solution.py:19
  176.5 11.6 %collective-permute-start.16 = (bf16[128,1024]{1,0:T(8,128)(2,1)S(1)}, bf16[128,1024]{1,0:T(8,128)(2,1)S(1)}, u32[]{:S(2)}, u32[]{:S(2)}) collective-permute-start(bf16[128,1024]{1,0:T(8,128)(2,1)S(1)} %get-tuple-element.57), channel_id=1, source_target_pairs={{0,12},{4,0},{8,4},{12,8},{1,13},{5,1},{9,5},{13,9},{2,14},{6,2},{... | collective-permute-start | bytes 786440 | tf_op jit(solution)/shard_map/ppermute | solution.py:19
  194.8 29.1 %all-to-all-start.2 = ((bf16[16,8,1024]{2,1,0:T(8,128)(2,1)}), bf16[16,8,1024]{2,1,0:T(8,128)(2,1)S(1)}, u32[]{:S(2)}, u32[]{:S(2)}) async-start(bf16[16,8,1024]{2,1,0:T(8,128)(2,1)} %fusion.4), calls=%async_computation.2 | async-start | bytes 524288 | tf_op jit(solution)/shard_map/all_to_all | solution.py:252
  201.4 14.7 %collective-permute-start.17 = (bf16[256,512]{1,0:T(8,128)(2,1)S(1)}, bf16[256,512]{1,0:T(8,128)(2,1)S(1)}, u32[]{:S(2)}, u32[]{:S(2)}) collective-permute-start(bf16[256,512]{1,0:T(8,128)(2,1)S(1)} %bitcast.28), channel_id=1, source_target_pairs={{0,48},{16,0},{32,16},{48,32},{1,49},{17,1},{33,17},{49,33},{2,50}... | collective-permute-start | bytes 786440 | tf_op jit(solution)/shard_map/ppermute | solution.py:19
  206.9 12.1 %collective-permute-start.18 = (bf16[256,512]{1,0:T(8,128)(2,1)S(1)}, bf16[256,512]{1,0:T(8,128)(2,1)S(1)}, u32[]{:S(2)}, u32[]{:S(2)}) collective-permute-start(bf16[256,512]{1,0:T(8,128)(2,1)S(1)} %bitcast.29), channel_id=1, source_target_pairs={{0,32},{16,48},{32,0},{48,16},{1,33},{17,49},{33,1},{49,17},{2,34}... | collective-permute-start | bytes 786440 | tf_op jit(solution)/shard_map/ppermute | solution.py:19
  208.8 13.0 %collective-permute-start.19 = (bf16[256,512]{1,0:T(8,128)(2,1)S(1)}, bf16[256,512]{1,0:T(8,128)(2,1)S(1)}, u32[]{:S(2)}, u32[]{:S(2)}) collective-permute-start(bf16[256,512]{1,0:T(8,128)(2,1)S(1)} %bitcast.30), channel_id=1, source_target_pairs={{0,16},{16,32},{32,48},{48,0},{1,17},{17,33},{33,49},{49,1},{2,18}... | collective-permute-start | bytes 786440 | tf_op jit(solution)/shard_map/ppermute | solution.py:19
  (23 other events, 314.7 us)
Sparse Core Ops, SparseCore 0:
  14.8 76.8 all-gather.1
  116.4 76.6 reduce-scatter.1

commit v7 on v5

--- a/solution.py
+++ b/solution.py
@@ -9,8 +9,6 @@
 corr_second = 1.0 - 0.999**10
 
 NZ, NX, NY, NH, NC = 8, 4, 4, 2, 2
-ORDER = (0, 2, 4, 6, 7, 5, 3, 1)
-RING = [(ORDER[i], ORDER[(i + 1) % NZ]) for i in range(NZ)]
 bf16, f32 = jnp.bfloat16, jnp.float32
 VMEM = pl.BlockSpec(memory_space=pltpu.VMEM)
 SMEM = pl.BlockSpec(memory_space=pltpu.SMEM)
@@ -34,13 +32,6 @@
         compiler_params=pltpu.CompilerParams(vmem_limit_bytes=limit << 20),
         cost_estimate=pl.CostEstimate(flops=flops, bytes_accessed=4 << 20, transcendentals=0),
     )
-
-
-def ring_block(zl, hop):
-    half = zl >> 1
-    place = jnp.where((zl & 1) == 0, half, NZ - 1 - half)
-    place = (place - hop) & (NZ - 1)
-    return jnp.where(place < NZ // 2, 2 * place, 2 * NZ - 1 - 2 * place)
 
 
 def prepare(pos, gate, up, cot, weight, basis, hidden, pack, both, plain):
@@ -63,39 +54,42 @@
             hidden[pl.ds((cr * NY + yr) * 16, 16), :] = jnp.concatenate(pair, 0).astype(bf16)
 
 
-def backward(pos, *refs):
+def reduce(pos, *refs):
     cots, boths = refs[:8], refs[8:12]
-    grad, reduced, tile = refs[12:]
+    tile, reduced = refs[12:]
     for piece in range(8):
         for zl in range(NZ):
             tile[pl.ds(zl * 128 + piece * 16, 16), :] = cots[piece][pl.ds(zl * 16, 16), :]
 
     def rows(step, _):
         at = pl.ds(pl.multiple_of(step * 256, 256), 256)
-        total, left, right = None, None, None
-        for r in range(NX):
-            part = tile[at, r * 256 : (r + 1) * 256]
-            more = dot(part, boths[r][:896, :], ((1,), (1,)))
+        for side in range(2):
+            total = None
+            for r in range(NX):
+                part = boths[r][896 + side * 256 : 1152 + side * 256, :]
+                more = dot(tile[at, r * 256 : (r + 1) * 256], part, ((1,), (0,)))
+                total = more if total is None else total + more
+            reduced[at, side * 256 : (side + 1) * 256] = total.astype(bf16)
+        return 0
+
+    lax.fori_loop(0, 4, rows, 0)
+
+
+def backward(pos, tile, b0, b1, b2, b3, grad):
+    def rows(step, _):
+        at = pl.ds(pl.multiple_of(step * 256, 256), 256)
+        total = None
+        for r, both in enumerate((b0, b1, b2, b3)):
+            more = dot(tile[at, r * 256 : (r + 1) * 256], both[:896, :], ((1,), (1,)))
             total = more if total is None else total + more
-            more = dot(part, boths[r][896:1152, :], ((1,), (0,)))
-            left = more if left is None else left + more
-            more = dot(part, boths[r][1152:, :], ((1,), (0,)))
-            right = more if right is None else right + more
         grad[at, :] = total.astype(bf16)
-        reduced[at, :256] = left.astype(bf16)
-        reduced[at, 256:] = right.astype(bf16)
         return 0
 
     lax.fori_loop(0, 4, rows, 0)
 
 
-def project(pos, *refs):
-    hiddens, reduced = refs[:8], refs[8]
-    tile, outs, total, blocks = refs[9], refs[10:14], *refs[14:]
-    x, zl_own = pos[0], pos[3]
-    for hop in range(NZ):
-        to = pl.ds(pl.multiple_of(ring_block(zl_own, hop) * 128, 128), 128)
-        tile[to, :] = hiddens[hop][...]
+def project(pos, tile, reduced, o0, o1, o2, o3, total, blocks):
+    x = pos[0]
     total[...] = dot(tile[...], reduced[...], ((0,), (0,)))
     spare = jnp.zeros((4, total.shape[1]), f32)
     for xs in range(NX):
@@ -103,7 +97,7 @@
             first = zl * 112 + xs * 28
             block = jnp.concatenate([total[first : first + 28, :], spare], 0)
             blocks[xs, zl * 32 : zl * 32 + 32, :] = block.astype(bf16)
-    for xr, out in enumerate(outs):
+    for xr, out in enumerate((o0, o1, o2, o3)):
         out[...] = blocks[lax.rem(x + xr, NX)]
 
 
@@ -164,7 +158,7 @@
 
 
 def body(gate, up, weight, basis, cotangent, moment1, moment2):
-    pos = jnp.stack([lax.axis_index(a) for a in ("x", "y", "c", "zl")]).astype(jnp.int32)
+    pos = jnp.stack([lax.axis_index(a) for a in ("x", "y", "c")]).astype(jnp.int32)
     rows, ff = gate.shape
     mine, width = cotangent.shape
     cols = width // NZ
@@ -182,59 +176,55 @@
         [((rows, ff), f32)],
     )(pos, gate, up, cotangent, weight, basis)
 
+    tile = lax.all_gather(hidden, "zl", axis=0, tiled=True)
     got = lax.all_to_all(pack, ("zl", "zh"), 0, 0, tiled=True).reshape(rows, cols)
     boths = [both] + [shift(both, "x", NX, by) for by in range(1, NX)]
-    got, *boths = lax.optimization_barrier((got, *boths))
-    hiddens = [hidden]
-    for _ in range(1, NZ - 2):
-        hiddens.append(lax.ppermute(hiddens[-1], "zl", RING))
+    got, boths[1], boths[3] = lax.optimization_barrier((got, boths[1], boths[3]))
     cots = [got] + [shift(got, "y", NY, by) for by in range(1, NY)]
     cots = cots + [shift(piece, "c", NC, 1) for piece in cots]
 
-    partial, reduced = call(
-        backward,
+    tile_cot, reduced = call(
+        reduce,
         12,
-        [((NZ * rows, ff), bf16), ((NZ * rows, rank), bf16)],
-        [((NZ * rows, cols), bf16)],
-        flops=3 * 10**9,
+        [((NZ * rows, cols), bf16), ((NZ * rows, rank), bf16)],
+        flops=10**9,
     )(pos, *cots, *boths)
-    hiddens[-1], partial, reduced = lax.optimization_barrier((hiddens[-1], partial, reduced))
-    for _ in range(2):
-        hiddens.append(lax.ppermute(hiddens[-1], "zl", RING))
-    grad_hidden = lax.psum_scatter(partial, "zl", scatter_dimension=0, tiled=True)
-    grad_gate, grad_up = call(
-        finish_grad,
-        3,
-        [((rows, ff), bf16), ((rows, ff), bf16)],
-        [((rows, ff), f32), ((rows, ff), f32)],
-    )(pos, grad_hidden, gate, up)
-
-    tile, *parts = call(
+
+    parts = call(
         project,
-        9,
-        [((NZ * rows, ff), bf16)] + [((NZ * slot, rank), bf16)] * NX,
+        2,
+        [((NZ * slot, rank), bf16)] * NX,
         [((ff, rank), f32), ((NX, NZ * slot, rank), bf16)],
         flops=10**9,
-    )(pos, *hiddens, reduced)
+    )(pos, tile, reduced)
+    tile_cot, *parts = lax.optimization_barrier((tile_cot, *parts))
+    (partial,) = call(backward, 5, [((NZ * rows, ff), bf16)], flops=2 * 10**9)(
+        pos, tile_cot, *boths
+    )
+    grad_hidden = lax.psum_scatter(partial, "zl", scatter_dimension=0, tiled=True)
     total = parts[0].astype(f32)
     for by in range(1, NX):
         total = total + shift(parts[by], "x", NX, -by).astype(f32)
-    total, tile = lax.optimization_barrier((total.astype(bf16), tile))
+    total, tile, partial = lax.optimization_barrier((total.astype(bf16), tile, partial))
+    *term, leave = call(
+        forward, 5, [((rows, cols), bf16)] * NY + [((NY, rows, cols), bf16)], flops=2 * 10**9
+    )(pos, tile, *boths)
+    arrived = shift(leave, "c", NC, 1)
+    term = [(term[yr].astype(f32) + arrived[yr].astype(f32)).astype(bf16) for yr in range(NY)]
+    outer = term[0].astype(f32)
+    for by in range(1, NY):
+        outer = outer + shift(term[by], "y", NY, -by).astype(f32)
+    outer = outer.astype(bf16).reshape(NZ * NH, mine, cols)
     total = lax.all_to_all(total, "zl", 0, 0, tiled=True).reshape(NZ, slot, rank)
     projected = total.astype(f32).sum(0)[:own]
     moment1_new = 0.9 * moment1 + 0.1 * projected
     moment2_new = 0.999 * moment2 + 0.001 * projected * projected
     step = (moment1_new / corr_first / (jnp.sqrt(moment2_new / corr_second) + 1e-08)).astype(bf16)
     step = jnp.pad(step, ((0, slot - own), (0, 0)))
-    *term, leave = call(
-        forward, 5, [((rows, cols), bf16)] * NY + [((NY, rows, cols), bf16)], flops=2 * 10**9
-    )(pos, tile, *boths)
-    arrived = shift(leave, "c", NC, 1)
-    term = [(term[yr].astype(f32) + arrived[yr].astype(f32)).astype(bf16) for yr in range(NY)]
-    step, *term = lax.optimization_barrier((step, *term))
     step = jnp.broadcast_to(step[None], (NZ, slot, rank))
     step = lax.all_to_all(step, "zl", 0, 0, tiled=True).reshape(NZ * slot, rank)
     steps = [step] + [shift(step, "x", NX, by) for by in range(1, NX)]
+    outer, steps[1] = lax.optimization_barrier((outer, steps[1]))
     (expansion,) = call(
         expand,
         5,
@@ -243,12 +233,14 @@
         flops=3 * 10**8,
     )(pos, *steps, basis)
 
-    total = term[0].astype(f32)
-    for by in range(1, NY):
-        total = total + shift(term[by], "y", NY, -by).astype(f32)
-    total = total.astype(bf16).reshape(NZ * NH, mine, cols)
-    total = lax.all_to_all(total, ("zl", "zh"), 0, 0, tiled=True)
-    (layer_out,) = call(finish_out, 1, [((mine, width), bf16)])(pos, total)
+    outer = lax.all_to_all(outer, ("zl", "zh"), 0, 0, tiled=True)
+    (layer_out,) = call(finish_out, 1, [((mine, width), bf16)])(pos, outer)
+    grad_gate, grad_up = call(
+        finish_grad,
+        3,
+        [((rows, ff), bf16), ((rows, ff), bf16)],
+        [((rows, ff), f32), ((rows, ff), f32)],
+    )(pos, grad_hidden, gate, up)
     return (layer_out, grad_gate, grad_up, moment1_new, moment2_new, expansion)
 
 

time: 263 us -> 237 us (0.901)
  starting transfers between devices: 135 us -> 95.7 us
  waiting for transfers between devices: 68.2 us -> 81.6 us
  local copies, waits for them, and re-layouts: 19.2 us -> 15.1 us
  Pallas kernels: 18 us -> 20.7 us
    ppermute x7 -> x0, starting transfers between devices: 35.1 us -> none  [body(): hiddens.append(lax.ppermute(hiddens[-1], 'zl', RING))]
    ppermute x20, waiting for transfers between devices: 33.8 us -> 51.8 us  [shift(): lax.ppermute(value, axis, [(i, (i - by) % size) for i in range(size)])]
    ppermute x7 -> x0, waiting for transfers between devices: 16.4 us -> none  [body(): hiddens.append(lax.ppermute(hiddens[-1], 'zl', RING))]
    all_to_all x1, waiting for transfers between devices: 5.37 us -> 14 us  [body(): step = lax.all_to_all(step, 'zl', 0, 0, tiled=True).reshape(NZ * slot, rank)]
    ppermute x20, starting transfers between devices: 63.2 us -> 57.7 us  [shift(): lax.ppermute(value, axis, [(i, (i - by) % size) for i in range(size)])]
    unnamed x52 -> x42, local copies, waits for them, and re-layouts: 18.5 us -> 14.4 us
    pallas_call x3 -> x4, Pallas kernels: 9.42 us -> 11 us  [the longest x1 4.79 us: body(): call(backward, 5, [((NZ * rows, ff), bf16)], flops=2 * 10 ** 9)]
  transfers between devices with their start and end apart: 32 -> 26, of which waited for: 17 -> 11; matrix products, arithmetic and copies ran while one was open for 2% -> 3% of each run, Pallas kernels for 5% -> 6%
where the time goes in v7:
time: 237 us; the launch traced here: 234 us
  starting transfers between devices  95.7 us (40%)
  waiting for transfers between devices  81.6 us (34%)
  Pallas kernels  20.7 us (9%)
  local copies, waits for them, and re-layouts  15.1 us (6%)
  between operations  14.4 us (6%)
  other arithmetic  6.07 us (3%)
    ppermute x20, starting transfers between devices, shift(): lax.ppermute(value, axis, [(i, (i - by) % size) for i in range(size)])  57.7 us
    ppermute x20, waiting for transfers between devices, shift(): lax.ppermute(value, axis, [(i, (i - by) % size) for i in range(size)])  51.8 us
    all_to_all x1, starting transfers between devices, body(): lax.all_to_all(pack, ('zl', 'zh'), 0, 0, tiled=True).reshape(rows, cols)  15.2 us
    all_to_all x1, waiting for transfers between devices, body(): lax.all_to_all(total, 'zl', 0, 0, tiled=True).reshape(NZ, slot, rank)  14.9 us
    unnamed x42, local copies, waits for them, and re-layouts  14.4 us
    all_to_all x1, waiting for transfers between devices, body(): step = lax.all_to_all(step, 'zl', 0, 0, tiled=True).reshape(NZ * slot, rank)  14 us
    all_to_all x1, starting transfers between devices, body(): lax.all_to_all(total, 'zl', 0, 0, tiled=True).reshape(NZ, slot, rank)  9.53 us
    all_to_all x1, starting transfers between devices, body(): outer = lax.all_to_all(outer, ('zl', 'zh'), 0, 0, tiled=True)  7.08 us
  transfers between devices with their start and end apart: 26, of which 11 were waited for; matrix products, arithmetic and copies ran while one was open for 3% of the time, Pallas kernels for 6%

profile of v7, /device:TPU:24, one launch (start us, length us, event | category | flops | bytes accessed | tf_op | source)
XLA Modules:
  0.0 233.7 jit_solution(4681642852622960780)
XLA Ops:
  13.5 15.2 %all-to-all-start = ((bf16[16,8,1024]{2,1,0:T(8,128)(2,1)}), bf16[16,8,1024]{2,1,0:T(8,128)(2,1)S(1)}, u32[]{:S(2)}, u32[]{:S(2)}) async-start(bf16[16,8,1024]{2,1,0:T(8,128)(2,1)} %get-tuple-element.34), calls=%async_computation | async-start | bytes 524288 | tf_op jit(solution)/shard_map/all_to_all | solution.py:180
  28.8 4.7 %collective-permute-start = (bf16[1408,256]{1,0:T(8,128)(2,1)S(1)}, bf16[1408,256]{1,0:T(8,128)(2,1)S(1)}, u32[]{:S(2)}, u32[]{:S(2)}) collective-permute-start(bf16[1408,256]{1,0:T(8,128)(2,1)S(1)} %get-tuple-element.35.refs_8_.b0), channel_id=1, source_target_pairs={{0,48},{16,0},{32,16},{48,32},{1,49},{17,1},{33,17},{49,33},{2,50}... | collective-permute-start | bytes 2162696 | tf_op jit(solution)/shard_map/ppermute | solution.py:18
  35.4 4.2 %collective-permute-start.9 = (bf16[1408,256]{1,0:T(8,128)(2,1)S(1)}, bf16[1408,256]{1,0:T(8,128)(2,1)S(1)}, u32[]{:S(2)}, u32[]{:S(2)}) collective-permute-start(bf16[1408,256]{1,0:T(8,128)(2,1)S(1)} %get-tuple-element.35.refs_8_.b0), channel_id=1, source_target_pairs={{0,32},{16,48},{32,0},{48,16},{1,33},{17,49},{33,1},{49,17},{2,34}... | collective-permute-start | bytes 2162696 | tf_op jit(solution)/shard_map/ppermute | solution.py:18
  39.6 24.5 %collective-permute-done.refs_9_.b1 = bf16[1408,256]{1,0:T(8,128)(2,1)S(1)} collective-permute-done((bf16[1408,256]{1,0:T(8,128)(2,1)S(1)}, bf16[1408,256]{1,0:T(8,128)(2,1)S(1)}, u32[]{:S(2)}, u32[]{:S(2)}) %collective-permute-start) | collective-permute-done | bytes 720928 | tf_op jit(solution)/shard_map/ppermute | solution.py:18
  64.0 5.3 %collective-permute-done.1.refs_11_.b3 = bf16[1408,256]{1,0:T(8,128)(2,1)S(1)} collective-permute-done((bf16[1408,256]{1,0:T(8,128)(2,1)S(1)}, bf16[1408,256]{1,0:T(8,128)(2,1)S(1)}, u32[]{:S(2)}, u32[]{:S(2)}) %collective-permute-start.1) | collective-permute-done | bytes 720928 | tf_op jit(solution)/shard_map/ppermute | solution.py:18
  69.3 2.6 %collective-permute-start.2 = (bf16[128,1024]{1,0:T(8,128)(2,1)S(1)}, bf16[128,1024]{1,0:T(8,128)(2,1)S(1)}, u32[]{:S(2)}, u32[]{:S(2)}) collective-permute-start(bf16[128,1024]{1,0:T(8,128)(2,1)S(1)} %bitcast.28), channel_id=1, source_target_pairs={{0,12},{4,0},{8,4},{12,8},{1,13},{5,1},{9,5},{13,9},{2,14},{6,2},{... | collective-permute-start | bytes 786440 | tf_op jit(solution)/shard_map/ppermute | solution.py:18
  72.0 2.8 %collective-permute-start.3 = (bf16[128,1024]{1,0:T(8,128)(2,1)S(1)}, bf16[128,1024]{1,0:T(8,128)(2,1)S(1)}, u32[]{:S(2)}, u32[]{:S(2)}) collective-permute-start(bf16[128,1024]{1,0:T(8,128)(2,1)S(1)} %bitcast.29), channel_id=1, source_target_pairs={{0,8},{4,12},{8,0},{12,4},{1,9},{5,13},{9,1},{13,5},{2,10},{6,14},... | collective-permute-start | bytes 786440 | tf_op jit(solution)/shard_map/ppermute | solution.py:18
  74.8 4.1 %collective-permute-start.4 = (bf16[128,1024]{1,0:T(8,128)(2,1)S(1)}, bf16[128,1024]{1,0:T(8,128)(2,1)S(1)}, u32[]{:S(2)}, u32[]{:S(2)}) collective-permute-start(bf16[128,1024]{1,0:T(8,128)(2,1)S(1)} %bitcast.30), channel_id=1, source_target_pairs={{0,4},{4,8},{8,12},{12,0},{1,5},{5,9},{9,13},{13,1},{2,6},{6,10},{... | collective-permute-start | bytes 786440 | tf_op jit(solution)/shard_map/ppermute | solution.py:18
  100.8 2.5 %collective-permute-start.11 = (bf16[256,512]{1,0:T(8,128)(2,1)}, bf16[256,512]{1,0:T(8,128)(2,1)}, u32[]{:S(2)}, u32[]{:S(2)}) collective-permute-start(bf16[256,512]{1,0:T(8,128)(2,1)} %get-tuple-element.48), channel_id=1, source_target_pairs={{0,32},{16,48},{32,0},{48,16},{1,33},{17,49},{33,1},{49,17},{2,34}... | collective-permute-start | bytes 786440 | tf_op jit(solution)/shard_map/ppermute | solution.py:18
  103.3 3.3 %collective-permute-start.10 = (bf16[256,512]{1,0:T(8,128)(2,1)S(1)}, bf16[256,512]{1,0:T(8,128)(2,1)}, u32[]{:S(2)}, u32[]{:S(2)}) collective-permute-start(bf16[256,512]{1,0:T(8,128)(2,1)S(1)} %get-tuple-element.47), channel_id=1, source_target_pairs={{0,16},{16,32},{32,48},{48,0},{1,17},{17,33},{33,49},{49,1},{2,18}... | collective-permute-start | bytes 786440 | tf_op jit(solution)/shard_map/ppermute | solution.py:18
  106.7 4.8 %shard_map.121 = bf16[1024,896]{1,0:T(8,128)(2,1)} custom-call(s32[3]{0:T(128)S(1)} %pad_add_fusion.pos, bf16[1024,1024]{1,0:T(8,128)(2,1)S(1)} %copy-done.14, bf16[1408,256]{1,0:T(8,128)(2,1)S(1)} %get-tuple-element.35.refs_8_.b0, bf16[1408,256]{1,0:T(8,128)(2,1)S(1)} %collective-permute-done.refs_9_.b1, ...), custom_call_target="tpu_custom_call" | custom-call | flops 2000000000 | bytes 4194304 | tf_op jit(solution)/shard_map/pallas_call | solution.py:201
  113.7 5.0 %collective-permute-done.10 = bf16[256,512]{1,0:T(8,128)(2,1)} collective-permute-done((bf16[256,512]{1,0:T(8,128)(2,1)S(1)}, bf16[256,512]{1,0:T(8,128)(2,1)}, u32[]{:S(2)}, u32[]{:S(2)}) %collective-permute-start.10) | collective-permute-done | bytes 262176 | tf_op jit(solution)/shard_map/ppermute | solution.py:18
  120.7 9.5 %all-to-all-start.1 = ((bf16[8,32,512]{2,1,0:T(8,128)(2,1)}), bf16[8,32,512]{2,1,0:T(8,128)(2,1)S(1)}, u32[]{:S(2)}, u32[]{:S(2)}) async-start(bf16[8,32,512]{2,1,0:T(8,128)(2,1)} %bitcast.9), calls=%async_computation.1 | async-start | bytes 524288 | tf_op jit(solution)/shard_map/all_to_all | solution.py:218
  131.7 4.4 %shard_map.122 = (bf16[128,1024]{1,0:T(8,128)(2,1)S(1)}, bf16[128,1024]{1,0:T(8,128)(2,1)S(1)}, bf16[128,1024]{1,0:T(8,128)(2,1)S(1)}, bf16[128,1024]{1,0:T(8,128)(2,1)S(1)}, bf16[4,128,1024]{2,1,0:T(8,128)(2,1)}) custom-call(s32[3]{0:T(128)S(1)} %pad_add_fusion.pos, bf16[1024,896]{1,0:T(8,128)(2,1)S(1)} %copy-done.16, ...), custom_call_target="tpu_custom_call" | custom-call | flops 2000000000 | bytes 4194304 | tf_op jit(solution)/shard_map/pallas_call | solution.py:209
  140.1 14.9 %all-to-all-done.1 = bf16[8,32,512]{2,1,0:T(8,128)(2,1)S(1)} async-done(((bf16[8,32,512]{2,1,0:T(8,128)(2,1)}), bf16[8,32,512]{2,1,0:T(8,128)(2,1)S(1)}, u32[]{:S(2)}, u32[]{:S(2)}) %all-to-all-start.1) | async-done | bytes 262176 | tf_op jit(solution)/shard_map/all_to_all | solution.py:218
  156.5 6.1 %all-to-all-start.2 = ((bf16[8,32,512]{2,1,0:T(8,128)(2,1)}), bf16[8,32,512]{2,1,0:T(8,128)(2,1)S(1)}, u32[]{:S(2)}, u32[]{:S(2)}) async-start(bf16[8,32,512]{2,1,0:T(8,128)(2,1)} %broadcast_in_dim.2), calls=%async_computation.2 | async-start | bytes 524288 | tf_op jit(solution)/shard_map/all_to_all | solution.py:225
  166.0 5.1 %collective-permute-start.15 = (bf16[128,1024]{1,0:T(8,128)(2,1)S(1)}, bf16[128,1024]{1,0:T(8,128)(2,1)}, u32[]{:S(2)}, u32[]{:S(2)}) collective-permute-start(bf16[128,1024]{1,0:T(8,128)(2,1)S(1)} %get-tuple-element.67), channel_id=1, source_target_pairs={{0,8},{4,12},{8,0},{12,4},{1,9},{5,13},{9,1},{13,5},{2,10},{6,14},... | collective-permute-start | bytes 786440 | tf_op jit(solution)/shard_map/ppermute | solution.py:18
  171.1 3.9 %collective-permute-start.14 = (bf16[128,1024]{1,0:T(8,128)(2,1)S(1)}, bf16[128,1024]{1,0:T(8,128)(2,1)}, u32[]{:S(2)}, u32[]{:S(2)}) collective-permute-start(bf16[128,1024]{1,0:T(8,128)(2,1)S(1)} %get-tuple-element.65), channel_id=1, source_target_pairs={{0,4},{4,8},{8,12},{12,0},{1,5},{5,9},{9,13},{13,1},{2,6},{6,10},{... | collective-permute-start | bytes 786440 | tf_op jit(solution)/shard_map/ppermute | solution.py:18
  175.0 14.0 %all-to-all-done.2 = bf16[8,32,512]{2,1,0:T(8,128)(2,1)S(1)} async-done(((bf16[8,32,512]{2,1,0:T(8,128)(2,1)}), bf16[8,32,512]{2,1,0:T(8,128)(2,1)S(1)}, u32[]{:S(2)}, u32[]{:S(2)}) %all-to-all-start.2) | async-done | bytes 262176 | tf_op jit(solution)/shard_map/all_to_all | solution.py:225
  192.9 4.3 %collective-permute-done.17.s1 = bf16[256,512]{1,0:T(8,128)(2,1)S(1)} collective-permute-done((bf16[256,512]{1,0:T(8,128)(2,1)S(1)}, bf16[256,512]{1,0:T(8,128)(2,1)S(1)}, u32[]{:S(2)}, u32[]{:S(2)}) %collective-permute-start.17) | collective-permute-done | bytes 262176 | tf_op jit(solution)/shard_map/ppermute | solution.py:18
  197.2 7.1 %all-to-all-start.3 = ((bf16[16,8,1024]{2,1,0:T(8,128)(2,1)}), bf16[16,8,1024]{2,1,0:T(8,128)(2,1)S(1)}, u32[]{:S(2)}, u32[]{:S(2)}) async-start(bf16[16,8,1024]{2,1,0:T(8,128)(2,1)} %fusion.4), calls=%async_computation.3 | async-start | bytes 524288 | tf_op jit(solution)/shard_map/all_to_all | solution.py:236
  206.3 4.3 %collective-permute-start.19 = (bf16[256,512]{1,0:T(8,128)(2,1)S(1)}, bf16[256,512]{1,0:T(8,128)(2,1)S(1)}, u32[]{:S(2)}, u32[]{:S(2)}) collective-permute-start(bf16[256,512]{1,0:T(8,128)(2,1)S(1)} %bitcast.35), channel_id=1, source_target_pairs={{0,16},{16,32},{32,48},{48,0},{1,17},{17,33},{33,49},{49,1},{2,18}... | collective-permute-start | bytes 786440 | tf_op jit(solution)/shard_map/ppermute | solution.py:18
  210.5 6.4 %collective-permute-done.18.s2 = bf16[256,512]{1,0:T(8,128)(2,1)S(1)} collective-permute-done((bf16[256,512]{1,0:T(8,128)(2,1)S(1)}, bf16[256,512]{1,0:T(8,128)(2,1)S(1)}, u32[]{:S(2)}, u32[]{:S(2)}) %collective-permute-start.18) | collective-permute-done | bytes 262176 | tf_op jit(solution)/shard_map/ppermute | solution.py:18
  217.0 2.9 %collective-permute-done.19.s3 = bf16[256,512]{1,0:T(8,128)(2,1)S(1)} collective-permute-done((bf16[256,512]{1,0:T(8,128)(2,1)S(1)}, bf16[256,512]{1,0:T(8,128)(2,1)S(1)}, u32[]{:S(2)}, u32[]{:S(2)}) %collective-permute-start.19) | collective-permute-done | bytes 262176 | tf_op jit(solution)/shard_map/ppermute | solution.py:18
  (88 shorter events, 57.2 us)
Async XLA Ops:
  7.2 86.4 %all-gather.2.cloned.1.call-start = ((), (), s32[]{:S(2)}) async-start(), calls=%async_computation.5 | async-start | bytes 2064384 | tf_op jit(solution)/shard_map/all_gather | solution.py:179
  13.5 55.8 %all-to-all-start = ((bf16[16,8,1024]{2,1,0:T(8,128)(2,1)}), bf16[16,8,1024]{2,1,0:T(8,128)(2,1)S(1)}, u32[]{:S(2)}, u32[]{:S(2)}) async-start(bf16[16,8,1024]{2,1,0:T(8,128)(2,1)} %get-tuple-element.34), calls=%async_computation | async-start | bytes 524288 | tf_op jit(solution)/shard_map/all_to_all | solution.py:180
  28.7 195.5 %reduce-scatter.2.cloned.1.call-start = ((), (), s32[]{:S(2)}) async-start(), calls=%async_computation.6 | async-start | bytes 2064384 | tf_op jit(solution)/shard_map/reduce_scatter | solution.py:204
  28.8 35.3 %collective-permute-start = (bf16[1408,256]{1,0:T(8,128)(2,1)S(1)}, bf16[1408,256]{1,0:T(8,128)(2,1)S(1)}, u32[]{:S(2)}, u32[]{:S(2)}) collective-permute-start(bf16[1408,256]{1,0:T(8,128)(2,1)S(1)} %get-tuple-element.35.refs_8_.b0), channel_id=1, source_target_pairs={{0,48},{16,0},{32,16},{48,32},{1,49},{17,1},{33,17},{49,33},{2,50}... | collective-permute-start | bytes 2162696 | tf_op jit(solution)/shard_map/ppermute | solution.py:18
  33.5 35.9 %collective-permute-start.1 = (bf16[1408,256]{1,0:T(8,128)(2,1)S(1)}, bf16[1408,256]{1,0:T(8,128)(2,1)S(1)}, u32[]{:S(2)}, u32[]{:S(2)}) collective-permute-start(bf16[1408,256]{1,0:T(8,128)(2,1)S(1)} %get-tuple-element.35.refs_8_.b0), channel_id=1, source_target_pairs={{0,16},{16,32},{32,48},{48,0},{1,17},{17,33},{33,49},{49,1},{2,18}... | collective-permute-start | bytes 2162696 | tf_op jit(solution)/shard_map/ppermute | solution.py:18
  35.4 52.3 %collective-permute-start.9 = (bf16[1408,256]{1,0:T(8,128)(2,1)S(1)}, bf16[1408,256]{1,0:T(8,128)(2,1)S(1)}, u32[]{:S(2)}, u32[]{:S(2)}) collective-permute-start(bf16[1408,256]{1,0:T(8,128)(2,1)S(1)} %get-tuple-element.35.refs_8_.b0), channel_id=1, source_target_pairs={{0,32},{16,48},{32,0},{48,16},{1,33},{17,49},{33,1},{49,17},{2,34}... | collective-permute-start | bytes 2162696 | tf_op jit(solution)/shard_map/ppermute | solution.py:18
  69.3 11.5 %collective-permute-start.2 = (bf16[128,1024]{1,0:T(8,128)(2,1)S(1)}, bf16[128,1024]{1,0:T(8,128)(2,1)S(1)}, u32[]{:S(2)}, u32[]{:S(2)}) collective-permute-start(bf16[128,1024]{1,0:T(8,128)(2,1)S(1)} %bitcast.28), channel_id=1, source_target_pairs={{0,12},{4,0},{8,4},{12,8},{1,13},{5,1},{9,5},{13,9},{2,14},{6,2},{... | collective-permute-start | bytes 786440 | tf_op jit(solution)/shard_map/ppermute | solution.py:18
  72.0 11.3 %collective-permute-start.3 = (bf16[128,1024]{1,0:T(8,128)(2,1)S(1)}, bf16[128,1024]{1,0:T(8,128)(2,1)S(1)}, u32[]{:S(2)}, u32[]{:S(2)}) collective-permute-start(bf16[128,1024]{1,0:T(8,128)(2,1)S(1)} %bitcast.29), channel_id=1, source_target_pairs={{0,8},{4,12},{8,0},{12,4},{1,9},{5,13},{9,1},{13,5},{2,10},{6,14},... | collective-permute-start | bytes 786440 | tf_op jit(solution)/shard_map/ppermute | solution.py:18
  74.8 10.4 %collective-permute-start.4 = (bf16[128,1024]{1,0:T(8,128)(2,1)S(1)}, bf16[128,1024]{1,0:T(8,128)(2,1)S(1)}, u32[]{:S(2)}, u32[]{:S(2)}) collective-permute-start(bf16[128,1024]{1,0:T(8,128)(2,1)S(1)} %bitcast.30), channel_id=1, source_target_pairs={{0,4},{4,8},{8,12},{12,0},{1,5},{5,9},{9,13},{13,1},{2,6},{6,10},{... | collective-permute-start | bytes 786440 | tf_op jit(solution)/shard_map/ppermute | solution.py:18
  78.9 8.7 %collective-permute-start.5 = (bf16[128,1024]{1,0:T(8,128)(2,1)S(1)}, bf16[128,1024]{1,0:T(8,128)(2,1)S(1)}, u32[]{:S(2)}, u32[]{:S(2)}) collective-permute-start(bf16[128,1024]{1,0:T(8,128)(2,1)S(1)} %bitcast.31), channel_id=1, source_target_pairs={{0,1},{1,0},{2,3},{3,2},{4,5},{5,4},{6,7},{7,6},{8,9},{9,8},{10,11... | collective-permute-start | bytes 786440 | tf_op jit(solution)/shard_map/ppermute | solution.py:18
  80.9 6.8 %collective-permute-start.6 = (bf16[128,1024]{1,0:T(8,128)(2,1)S(1)}, bf16[128,1024]{1,0:T(8,128)(2,1)S(1)}, u32[]{:S(2)}, u32[]{:S(2)}) collective-permute-start(bf16[128,1024]{1,0:T(8,128)(2,1)S(1)} %collective-permute-done.2.refs_1_), channel_id=1, source_target_pairs={{0,1},{1,0},{2,3},{3,2},{4,5},{5,4},{6,7},{7,6},{8,9},{9,8},{10,11... | collective-permute-start | bytes 786440 | tf_op jit(solution)/shard_map/ppermute | solution.py:18
  98.9 12.6 %collective-permute-start.12 = (bf16[256,512]{1,0:T(8,128)(2,1)}, bf16[256,512]{1,0:T(8,128)(2,1)}, u32[]{:S(2)}, u32[]{:S(2)}) collective-permute-start(bf16[256,512]{1,0:T(8,128)(2,1)} %get-tuple-element.49), channel_id=1, source_target_pairs={{0,48},{16,0},{32,16},{48,32},{1,49},{17,1},{33,17},{49,33},{2,50}... | collective-permute-start | bytes 786440 | tf_op jit(solution)/shard_map/ppermute | solution.py:18
  100.8 12.9 %collective-permute-start.11 = (bf16[256,512]{1,0:T(8,128)(2,1)}, bf16[256,512]{1,0:T(8,128)(2,1)}, u32[]{:S(2)}, u32[]{:S(2)}) collective-permute-start(bf16[256,512]{1,0:T(8,128)(2,1)} %get-tuple-element.48), channel_id=1, source_target_pairs={{0,32},{16,48},{32,0},{48,16},{1,33},{17,49},{33,1},{49,17},{2,34}... | collective-permute-start | bytes 786440 | tf_op jit(solution)/shard_map/ppermute | solution.py:18
  103.3 15.4 %collective-permute-start.10 = (bf16[256,512]{1,0:T(8,128)(2,1)S(1)}, bf16[256,512]{1,0:T(8,128)(2,1)}, u32[]{:S(2)}, u32[]{:S(2)}) collective-permute-start(bf16[256,512]{1,0:T(8,128)(2,1)S(1)} %get-tuple-element.47), channel_id=1, source_target_pairs={{0,16},{16,32},{32,48},{48,0},{1,17},{17,33},{33,49},{49,1},{2,18}... | collective-permute-start | bytes 786440 | tf_op jit(solution)/shard_map/ppermute | solution.py:18
  120.7 34.3 %all-to-all-start.1 = ((bf16[8,32,512]{2,1,0:T(8,128)(2,1)}), bf16[8,32,512]{2,1,0:T(8,128)(2,1)S(1)}, u32[]{:S(2)}, u32[]{:S(2)}) async-start(bf16[8,32,512]{2,1,0:T(8,128)(2,1)} %bitcast.9), calls=%async_computation.1 | async-start | bytes 524288 | tf_op jit(solution)/shard_map/all_to_all | solution.py:218
  138.2 24.5 %collective-permute-start.13 = (bf16[4,128,1024]{2,1,0:T(8,128)(2,1)}, bf16[4,128,1024]{2,1,0:T(8,128)(2,1)S(1)}, u32[]{:S(2)}, u32[]{:S(2)}) collective-permute-start(bf16[4,128,1024]{2,1,0:T(8,128)(2,1)} %get-tuple-element.53), channel_id=1, source_target_pairs={{0,1},{1,0},{2,3},{3,2},{4,5},{5,4},{6,7},{7,6},{8,9},{9,8},{10,11... | collective-permute-start | bytes 3145736 | tf_op jit(solution)/shard_map/ppermute | solution.py:18
  156.5 32.5 %all-to-all-start.2 = ((bf16[8,32,512]{2,1,0:T(8,128)(2,1)}), bf16[8,32,512]{2,1,0:T(8,128)(2,1)S(1)}, u32[]{:S(2)}, u32[]{:S(2)}) async-start(bf16[8,32,512]{2,1,0:T(8,128)(2,1)} %broadcast_in_dim.2), calls=%async_computation.2 | async-start | bytes 524288 | tf_op jit(solution)/shard_map/all_to_all | solution.py:225
  164.0 26.9 %collective-permute-start.16 = (bf16[128,1024]{1,0:T(8,128)(2,1)S(1)}, bf16[128,1024]{1,0:T(8,128)(2,1)S(1)}, u32[]{:S(2)}, u32[]{:S(2)}) collective-permute-start(bf16[128,1024]{1,0:T(8,128)(2,1)S(1)} %get-tuple-element.66), channel_id=1, source_target_pairs={{0,12},{4,0},{8,4},{12,8},{1,13},{5,1},{9,5},{13,9},{2,14},{6,2},{... | collective-permute-start | bytes 786440 | tf_op jit(solution)/shard_map/ppermute | solution.py:18
  166.0 25.0 %collective-permute-start.15 = (bf16[128,1024]{1,0:T(8,128)(2,1)S(1)}, bf16[128,1024]{1,0:T(8,128)(2,1)}, u32[]{:S(2)}, u32[]{:S(2)}) collective-permute-start(bf16[128,1024]{1,0:T(8,128)(2,1)S(1)} %get-tuple-element.67), channel_id=1, source_target_pairs={{0,8},{4,12},{8,0},{12,4},{1,9},{5,13},{9,1},{13,5},{2,10},{6,14},... | collective-permute-start | bytes 786440 | tf_op jit(solution)/shard_map/ppermute | solution.py:18
  171.1 19.9 %collective-permute-start.14 = (bf16[128,1024]{1,0:T(8,128)(2,1)S(1)}, bf16[128,1024]{1,0:T(8,128)(2,1)}, u32[]{:S(2)}, u32[]{:S(2)}) collective-permute-start(bf16[128,1024]{1,0:T(8,128)(2,1)S(1)} %get-tuple-element.65), channel_id=1, source_target_pairs={{0,4},{4,8},{8,12},{12,0},{1,5},{5,9},{9,13},{13,1},{2,6},{6,10},{... | collective-permute-start | bytes 786440 | tf_op jit(solution)/shard_map/ppermute | solution.py:18
  189.0 8.3 %collective-permute-start.17 = (bf16[256,512]{1,0:T(8,128)(2,1)S(1)}, bf16[256,512]{1,0:T(8,128)(2,1)S(1)}, u32[]{:S(2)}, u32[]{:S(2)}) collective-permute-start(bf16[256,512]{1,0:T(8,128)(2,1)S(1)} %bitcast.33), channel_id=1, source_target_pairs={{0,48},{16,0},{32,16},{48,32},{1,49},{17,1},{33,17},{49,33},{2,50}... | collective-permute-start | bytes 786440 | tf_op jit(solution)/shard_map/ppermute | solution.py:18
  197.2 25.7 %all-to-all-start.3 = ((bf16[16,8,1024]{2,1,0:T(8,128)(2,1)}), bf16[16,8,1024]{2,1,0:T(8,128)(2,1)S(1)}, u32[]{:S(2)}, u32[]{:S(2)}) async-start(bf16[16,8,1024]{2,1,0:T(8,128)(2,1)} %fusion.4), calls=%async_computation.3 | async-start | bytes 524288 | tf_op jit(solution)/shard_map/all_to_all | solution.py:236
  204.3 12.6 %collective-permute-start.18 = (bf16[256,512]{1,0:T(8,128)(2,1)S(1)}, bf16[256,512]{1,0:T(8,128)(2,1)S(1)}, u32[]{:S(2)}, u32[]{:S(2)}) collective-permute-start(bf16[256,512]{1,0:T(8,128)(2,1)S(1)} %bitcast.34), channel_id=1, source_target_pairs={{0,32},{16,48},{32,0},{48,16},{1,33},{17,49},{33,1},{49,17},{2,34}... | collective-permute-start | bytes 786440 | tf_op jit(solution)/shard_map/ppermute | solution.py:18
  206.3 13.6 %collective-permute-start.19 = (bf16[256,512]{1,0:T(8,128)(2,1)S(1)}, bf16[256,512]{1,0:T(8,128)(2,1)S(1)}, u32[]{:S(2)}, u32[]{:S(2)}) collective-permute-start(bf16[256,512]{1,0:T(8,128)(2,1)S(1)} %bitcast.35), channel_id=1, source_target_pairs={{0,16},{16,32},{32,48},{48,0},{1,17},{17,33},{33,49},{49,1},{2,18}... | collective-permute-start | bytes 786440 | tf_op jit(solution)/shard_map/ppermute | solution.py:18
  (23 other events, 235.1 us)
Sparse Core Ops, SparseCore 0:
  13.6 76.9 all-gather.1
  111.6 77.6 reduce-scatter.1

commit v8 on v4

--- a/solution.py
+++ b/solution.py
@@ -25,11 +25,16 @@
     return lax.ppermute(value, axis, [(0, 1), (1, 0)])
 
 
+def spread(value, axis, size):
+    copies = jnp.broadcast_to(value[None], (size,) + value.shape)
+    return lax.all_to_all(copies, axis, 0, 0, tiled=True)
+
+
 def dot(a, b, contract):
     return lax.dot_general(a, b, (contract, ((), ())), preferred_element_type=f32)
 
 
-def call(kernel, n_in, outs, scratch=(), flops=0, limit=32):
+def call(kernel, n_in, outs, scratch=(), flops=0, limit=20):
     return pl.pallas_call(
         kernel,
         out_shape=tuple(jax.ShapeDtypeStruct(*o) for o in outs),
@@ -47,7 +52,7 @@
 
 
 def prepare(pos, gate, up, cot, weight, basis, hidden, pack, both, plain):
-    y, c = pos[2], pos[3]
+    c = pos[3]
     for za in range(NA):
         for x in range(NX):
             for r in range(NB):
@@ -61,15 +66,15 @@
     g = gate[...].astype(f32)
     plain[...] = g * jax.nn.sigmoid(g) * up[...].astype(f32)
     for cr in range(NC):
-        for yr in range(NY):
-            first = (lax.rem(y + yr, NY) * 4 + lax.rem(c + cr, NC)) * 8
+        for y in range(NY):
+            first = (y * 4 + lax.rem(c + cr, NC)) * 8
             pair = [plain[pl.ds(pl.multiple_of(first + zh * 16, 8), 8), :] for zh in range(NH)]
-            hidden[pl.ds((cr * NY + yr) * 16, 16), :] = jnp.concatenate(pair, 0).astype(bf16)
+            hidden[pl.ds((cr * NY + y) * 16, 16), :] = jnp.concatenate(pair, 0).astype(bf16)
 
 
 def project(pos, *refs):
-    cots, boths, hiddens = refs[:8], refs[8:12], refs[12:16]
-    tile, outs, reduced, total, blocks = refs[16], refs[17:21], *refs[21:]
+    cots, boths, hiddens = refs[:2], refs[2:6], refs[6:10]
+    tile, out, reduced, total = refs[10:]
     za, x = pos[0], pos[1]
     for xr in range(NX):
         for ar in range(NA):
@@ -77,7 +82,7 @@
             at = pl.ds(pl.multiple_of(at, 16), 16)
             for piece in range(8):
                 to = (xr * NA + ar) * 128 + piece * 16
-                tile[to : to + 16, :] = cots[piece][at, :]
+                tile[to : to + 16, :] = cots[piece // NY][piece % NY, at, :]
 
     def rows(step, _):
         at = pl.ds(pl.multiple_of(step * 256, 256), 256)
@@ -99,9 +104,7 @@
         for zl in range(NZ):
             first = zl * 112 + xs * 28
             block = jnp.concatenate([total[first : first + 28, :], spare], 0)
-            blocks[xs, zl * 32 : zl * 32 + 32, :] = block.astype(bf16)
-    for xr, out in enumerate(outs):
-        out[...] = blocks[lax.rem(x + xr, NX)]
+            out[xs, zl * 32 : zl * 32 + 32, :] = block.astype(bf16)
 
 
 def backward(pos, tile, b0, b1, b2, b3, *outs):
@@ -114,8 +117,8 @@
         out[...] = total.astype(bf16)
 
 
-def forward(pos, b0, b1, b2, b3, h0, h1, h2, h3, o0, o1, o2, o3, leave):
-    za, x = pos[0], pos[1]
+def forward(pos, b0, b1, b2, b3, h0, h1, h2, h3, o0, o1, o2, o3, leave, stay):
+    za, x, y = pos[0], pos[1], pos[2]
     for xr, hidden in enumerate((h0, h1, h2, h3)):
         for r, both in enumerate((b0, b1, b2, b3)):
             term = dot(hidden[...], both[:896, :], ((1,), (0,))).astype(bf16)
@@ -125,10 +128,10 @@
                 for piece in range(8):
                     first = ar * 128 + piece * 16
                     block = term[first : first + 16, :]
-                    if piece < NY:
-                        (o0, o1, o2, o3)[piece][to, r * 256 : (r + 1) * 256] = block
-                    else:
-                        leave[piece - NY, to, r * 256 : (r + 1) * 256] = block
+                    side = (stay, leave)[piece // NY]
+                    side[lax.rem(piece % NY - y + NY, NY), to, r * 256 : (r + 1) * 256] = block
+    for yr, out in enumerate((o0, o1, o2, o3)):
+        out[...] = stay[yr]
 
 
 def finish_out(pos, parts, out):
@@ -143,17 +146,16 @@
 
 
 def finish_grad(pos, p0, p1, p2, p3, arrived, gate, up, grad_gate, grad_up, relative, plain):
-    y, c = pos[2], pos[3]
+    c = pos[3]
     total = arrived[...].astype(f32)
     for part in (p0, p1, p2, p3):
         total = total + part[:128, :].astype(f32)
     relative[...] = total
     for ys in range(NY):
-        yr = lax.rem(ys - y + NY, NY)
         for zh in range(NH):
             for cs in range(NC):
                 cr = lax.rem(cs + c, NC)
-                first = ((cr * NY + yr) * NH + zh) * 8
+                first = ((cr * NY + ys) * NH + zh) * 8
                 to = ((ys * NH + zh) * NC + cs) * 8
                 plain[to : to + 8, :] = relative[pl.ds(pl.multiple_of(first, 8), 8), :]
     g, u, d = gate[...].astype(f32), up[...].astype(f32), plain[...]
@@ -195,26 +197,51 @@
     )(pos, gate, up, cotangent, weight, basis)
 
     cot = lax.all_to_all(pack, square, 0, 0, tiled=True).reshape(rows, cols)
-    pair = jnp.concatenate([hidden, swap(hidden, "za")], 0)
-    boths = [both]
-    for _ in range(1, NB):
-        boths.append(lax.ppermute(boths[-1], "zb", RING))
+    boths = [both, lax.ppermute(both, "zb", RING)]
+    twin = swap(hidden, "za")
+    cot, boths[1], twin = lax.optimization_barrier((cot, boths[1], twin))
+    pair = jnp.concatenate([hidden, twin], 0)
+    boths.append(lax.ppermute(boths[1], "zb", RING))
+    cot = spread(cot, "y", NY)
+    cot, boths[2] = lax.optimization_barrier((cot, boths[2]))
+    boths.append(lax.ppermute(boths[2], "zb", RING))
     hiddens = [pair] + [shift(pair, "x", NX, by) for by in range(1, NX)]
-    cots = [cot] + [shift(cot, "y", NY, by) for by in range(1, NY)]
-    cots = cots + [swap(piece, "c") for piece in cots]
-
-    tile, *parts = call(
+
+    tile, parts = call(
         project,
-        16,
-        [((NX * NA * rows, cols), bf16)] + [((NZ * slot, rank), bf16)] * NX,
-        [((NX * NA * rows, rank), bf16), ((ff, rank), f32), ((NX, NZ * slot, rank), bf16)],
+        10,
+        [((NX * NA * rows, cols), bf16), ((NX, NZ * slot, rank), bf16)],
+        [((NX * NA * rows, rank), bf16), ((ff, rank), f32)],
         flops=2 * 10**9,
-    )(pos, *cots, *boths, *hiddens)
-
-    total = parts[0].astype(f32)
-    for by in range(1, NX):
-        total = total + shift(parts[by], "x", NX, -by).astype(f32)
-    total = lax.all_to_all(total.astype(bf16), line, 0, 0, tiled=True).reshape(NZ, slot, rank)
+    )(pos, cot, swap(cot, "c"), *boths, *hiddens)
+    tile, parts = lax.optimization_barrier((tile, parts))
+
+    partial = call(backward, 5, [((NA * rows, ff), bf16)] * NX, flops=2 * 10**9)(
+        pos, tile, *boths
+    )
+    partials = [partial[0]] + [shift(partial[by], "x", NX, -by) for by in range(1, NX)]
+    leave = partials[0][rows:].astype(f32)
+    for part in partials[1:]:
+        leave = leave + part[rows:].astype(f32)
+    leave = leave.astype(bf16)
+
+    total = lax.all_to_all(parts, "x", 0, 0, tiled=True).astype(f32).sum(0).astype(bf16)
+    total, leave, *hiddens = lax.optimization_barrier((total, leave, *hiddens))
+    arrived = swap(leave, "za")
+    *term, leave = call(
+        forward,
+        8,
+        [((rows, cols), bf16)] * NY + [((NY, rows, cols), bf16)],
+        [((NY, rows, cols), bf16)],
+        flops=2 * 10**9,
+    )(pos, *boths, *hiddens)
+    other = swap(leave, "c")
+    term = [(term[yr].astype(f32) + other[yr].astype(f32)).astype(bf16) for yr in range(NY)]
+    outer = term[0].astype(f32)
+    for by in range(1, NY):
+        outer = outer + shift(term[by], "y", NY, -by).astype(f32)
+    outer = outer.astype(bf16).reshape(NA * NX * NH, mine, cols)
+    total = lax.all_to_all(total, line, 0, 0, tiled=True).reshape(NZ, slot, rank)
     projected = total.astype(f32).sum(0)[:own]
     moment1_new = 0.9 * moment1 + 0.1 * projected
     moment2_new = 0.999 * moment2 + 0.001 * projected * projected
@@ -223,6 +250,7 @@
     step = jnp.broadcast_to(step[None], (NZ, slot, rank))
     step = lax.all_to_all(step, line, 0, 0, tiled=True).reshape(NZ * slot, rank)
     steps = [step] + [shift(step, "x", NX, by) for by in range(1, NX)]
+    outer, steps[1] = lax.optimization_barrier((outer, steps[1]))
     (expansion,) = call(
         expand,
         5,
@@ -231,14 +259,6 @@
         flops=3 * 10**8,
     )(pos, *steps, basis)
 
-    partial = call(backward, 5, [((NA * rows, ff), bf16)] * NX, flops=2 * 10**9)(
-        pos, tile, *boths
-    )
-    partials = [partial[0]] + [shift(partial[by], "x", NX, -by) for by in range(1, NX)]
-    leave = partials[0][rows:].astype(f32)
-    for part in partials[1:]:
-        leave = leave + part[rows:].astype(f32)
-    arrived = swap(leave.astype(bf16), "za")
     grad_gate, grad_up = call(
         finish_grad,
         7,
@@ -246,17 +266,8 @@
         [((rows, ff), f32), ((rows, ff), f32)],
     )(pos, *partials, arrived, gate, up)
 
-    *term, leave = call(
-        forward, 8, [((rows, cols), bf16)] * NY + [((NY, rows, cols), bf16)], flops=2 * 10**9
-    )(pos, *boths, *hiddens)
-    arrived = swap(leave, "c")
-    term = [(term[yr].astype(f32) + arrived[yr].astype(f32)).astype(bf16) for yr in range(NY)]
-    total = term[0].astype(f32)
-    for by in range(1, NY):
-        total = total + shift(term[by], "y", NY, -by).astype(f32)
-    total = total.astype(bf16).reshape(NA * NX * NH, mine, cols)
-    total = lax.all_to_all(total, square, 0, 0, tiled=True)
-    (layer_out,) = call(finish_out, 1, [((mine, width), bf16)])(pos, total)
+    outer = lax.all_to_all(outer, square, 0, 0, tiled=True)
+    (layer_out,) = call(finish_out, 1, [((mine, width), bf16)])(pos, outer)
     return (layer_out, grad_gate, grad_up, moment1_new, moment2_new, expansion)
 
 

time: 278 us -> 292 us (1.050); the launches traced: 273 us -> 290 us
  waiting for transfers between devices: 72.7 us -> 102 us
  starting transfers between devices: 162 us -> 139 us
  local copies, waits for them, and re-layouts: 11.9 us -> 18.4 us
  other arithmetic: 5.87 us -> 9.01 us
    ppermute x3, waiting for transfers between devices: 0.71 us -> 18.5 us  [the longest x1 16.2 us: body(): boths.append(lax.ppermute(boths[1], 'zb', RING))]
    ppermute x18 -> x12, starting transfers between devices: 57.4 us -> 45.1 us  [shift(): lax.ppermute(value, axis, [(i, (i - by) % size) for i in range(size)])]
    ppermute x7 -> x4, waiting for transfers between devices: 28.9 us -> 39.6 us  [swap(): return lax.ppermute(value, axis, [(0, 1), (1, 0)])]
    ppermute x7 -> x4, starting transfers between devices: 29.2 us -> 18.8 us  [swap(): return lax.ppermute(value, axis, [(0, 1), (1, 0)])]
    ppermute x3, starting transfers between devices: 30.8 us -> 23.5 us  [the longest x1 17.8 us: body(): boths.append(lax.ppermute(boths[1], 'zb', RING))]
    unnamed x33 -> x63, local copies, waits for them, and re-layouts: 11 us -> 16.3 us
    all_to_all x2 -> x4, waiting for transfers between devices: 7.78 us -> 2.82 us  [the longest x1 2.82 us: body(): lax.all_to_all(total, line, 0, 0, tiled=True).reshape(NZ, slot, rank)]
    all_to_all x1, waiting for transfers between devices: 0.01 us -> 4.96 us  [body(): step = lax.all_to_all(step, line, 0, 0, tiled=True).reshape(NZ * slot, rank)]
  transfers between devices with their start and end apart: 32 -> 25, of which waited for: 15 -> 13; matrix products, arithmetic and copies ran while one was open for 2% -> 3% of each run, Pallas kernels for 4% -> 4%
where the time goes in v8:
time: 292 us; the launch traced here: 290 us
  starting transfers between devices  139 us (48%)
  waiting for transfers between devices  102 us (35%)
  Pallas kernels  19.9 us (7%)
  local copies, waits for them, and re-layouts  18.4 us (6%)
  other arithmetic  9.01 us (3%)
    ppermute x12, starting transfers between devices, shift(): lax.ppermute(value, axis, [(i, (i - by) % size) for i in range(size)])  45.1 us
    ppermute x4, waiting for transfers between devices, swap(): return lax.ppermute(value, axis, [(0, 1), (1, 0)])  39.6 us
    ppermute x12, waiting for transfers between devices, shift(): lax.ppermute(value, axis, [(i, (i - by) % size) for i in range(size)])  36.4 us
    ppermute x4, starting transfers between devices, swap(): return lax.ppermute(value, axis, [(0, 1), (1, 0)])  18.8 us
    ppermute x1, starting transfers between devices, body(): boths.append(lax.ppermute(boths[1], 'zb', RING))  17.8 us
    all_to_all x1, starting transfers between devices, body(): cot = lax.all_to_all(pack, square, 0, 0, tiled=True).reshape(rows, cols)  17.7 us
    unnamed x63, local copies, waits for them, and re-layouts  16.3 us
    ppermute x1, waiting for transfers between devices, body(): boths.append(lax.ppermute(boths[1], 'zb', RING))  16.2 us
  transfers between devices with their start and end apart: 25, of which 13 were waited for; matrix products, arithmetic and copies ran while one was open for 3% of the time, Pallas kernels for 4%

profile of v8, /device:TPU:24, one launch (start us, length us, event | category | flops | bytes accessed | tf_op | source)
XLA Modules:
  0.0 289.6 jit_solution(11557771952778405156)
XLA Ops:
  6.9 17.7 %all-to-all-start = ((bf16[16,8,1024]{2,1,0:T(8,128)(2,1)}), bf16[16,8,1024]{2,1,0:T(8,128)(2,1)S(1)}, u32[]{:S(2)}, u32[]{:S(2)}) async-start(bf16[16,8,1024]{2,1,0:T(8,128)(2,1)} %get-tuple-element.36), calls=%async_computation | async-start | bytes 524288 | tf_op jit(solution)/shard_map/all_to_all | solution.py:199
  27.5 7.7 %collective-permute-start.1 = (bf16[128,896]{1,0:T(8,128)(2,1)S(1)}, bf16[128,896]{1,0:T(8,128)(2,1)S(1)}, u32[]{:S(2)}, u32[]{:S(2)}) collective-permute-start(bf16[128,896]{1,0:T(8,128)(2,1)S(1)} %get-tuple-element.37), channel_id=1, source_target_pairs={{0,256},{256,0},{1,257},{257,1},{2,258},{258,2},{3,259},{259,3},{4... | collective-permute-start | bytes 688136 | tf_op jit(solution)/shard_map/ppermute | solution.py:25
  35.2 19.7 %collective-permute-done.1 = bf16[128,896]{1,0:T(8,128)(2,1)S(1)} collective-permute-done((bf16[128,896]{1,0:T(8,128)(2,1)S(1)}, bf16[128,896]{1,0:T(8,128)(2,1)S(1)}, u32[]{:S(2)}, u32[]{:S(2)}) %collective-permute-start.1) | collective-permute-done | bytes 229408 | tf_op jit(solution)/shard_map/ppermute | solution.py:25
  58.6 4.7 %all-to-all-start.1 = ((bf16[4,128,1024]{2,1,0:T(8,128)(2,1)}), bf16[4,128,1024]{2,1,0:T(8,128)(2,1)S(1)}, u32[]{:S(2)}, u32[]{:S(2)}) async-start(bf16[4,128,1024]{2,1,0:T(8,128)(2,1)} %broadcast_in_dim.4), calls=%async_computation.1 | async-start | bytes 2097152 | tf_op jit(solution)/shard_map/all_to_all | solution.py:30
  63.3 17.8 %collective-permute-start.2 = (bf16[1408,256]{1,0:T(8,128)(2,1)S(1)}, bf16[1408,256]{1,0:T(8,128)(2,1)}, u32[]{:S(2)}, u32[]{:S(2)}) collective-permute-start(bf16[1408,256]{1,0:T(8,128)(2,1)S(1)} %collective-permute-done.refs_3_.b1), channel_id=1, source_target_pairs={{0,64},{64,192},{192,128},{128,0},{1,65},{65,193},{193,129},{129,1... | collective-permute-start | bytes 2162696 | tf_op jit(solution)/shard_map/ppermute | solution.py:204
  81.1 16.2 %collective-permute-done.2.refs_4_.b2 = bf16[1408,256]{1,0:T(8,128)(2,1)} collective-permute-done((bf16[1408,256]{1,0:T(8,128)(2,1)S(1)}, bf16[1408,256]{1,0:T(8,128)(2,1)}, u32[]{:S(2)}, u32[]{:S(2)}) %collective-permute-start.2) | collective-permute-done | bytes 720928 | tf_op jit(solution)/shard_map/ppermute | solution.py:204
  105.4 4.6 %collective-permute-start.6 = (bf16[256,896]{1,0:T(8,128)(2,1)S(1)}, bf16[256,896]{1,0:T(8,128)(2,1)S(1)}, u32[]{:S(2)}, u32[]{:S(2)}) collective-permute-start(bf16[256,896]{1,0:T(8,128)(2,1)S(1)} %constant_dynamic-update-slice_fusion.refs_6_.h0), channel_id=1, source_target_pairs={{0,32},{16,48},{32,0},{48,16},{1,33},{17,49},{33,1},{49,17},{2,34}... | collective-permute-start | bytes 1376264 | tf_op jit(solution)/shard_map/ppermute | solution.py:21
  113.4 4.4 %collective-permute-done.7.refs_9_.h3 = bf16[256,896]{1,0:T(8,128)(2,1)S(1)} collective-permute-done((bf16[256,896]{1,0:T(8,128)(2,1)S(1)}, bf16[256,896]{1,0:T(8,128)(2,1)S(1)}, u32[]{:S(2)}, u32[]{:S(2)}) %collective-permute-start.7) | collective-permute-done | bytes 458784 | tf_op jit(solution)/shard_map/ppermute | solution.py:21
  117.8 10.7 %collective-permute-done.6.refs_8_.h2 = bf16[256,896]{1,0:T(8,128)(2,1)S(1)} collective-permute-done((bf16[256,896]{1,0:T(8,128)(2,1)S(1)}, bf16[256,896]{1,0:T(8,128)(2,1)S(1)}, u32[]{:S(2)}, u32[]{:S(2)}) %collective-permute-start.6) | collective-permute-done | bytes 458784 | tf_op jit(solution)/shard_map/ppermute | solution.py:21
  131.7 5.2 %shard_map.119 = (bf16[1024,1024]{1,0:T(8,128)(2,1)S(1)}, bf16[4,256,512]{2,1,0:T(8,128)(2,1)}) custom-call(s32[5]{0:T(128)S(1)} %stack.23.pos, bf16[4,128,1024]{2,1,0:T(8,128)(2,1)S(1)} %all-to-all-done.1.refs_0_, bf16[4,128,1024]{2,1,0:T(8,128)(2,1)S(1)} %collective-permute-done.4.refs_1_, bf16[1408,256]{1,0:T(8,128)(2,1)S(1)} %get-tuple-element.35.refs_2_.b0, ...), custom_call_target="tpu_custom_call" | custom-call | flops 2000000000 | bytes 4194304 | tf_op jit(solution)/shard_map/pallas_call | solution.py:210
  138.3 4.4 %all-to-all-start.2 = ((bf16[4,256,512]{2,1,0:T(8,128)(2,1)}), bf16[4,256,512]{2,1,0:T(8,128)(2,1)}, u32[]{:S(2)}, u32[]{:S(2)}) async-start(bf16[4,256,512]{2,1,0:T(8,128)(2,1)} %get-tuple-element.43), calls=%async_computation.2 | async-start | bytes 2097152 | tf_op jit(solution)/shard_map/all_to_all | solution.py:228
  147.8 4.3 %collective-permute-start.8 = (bf16[256,896]{1,0:T(8,128)(2,1)S(1)}, bf16[256,896]{1,0:T(8,128)(2,1)S(1)}, u32[]{:S(2)}, u32[]{:S(2)}) collective-permute-start(bf16[256,896]{1,0:T(8,128)(2,1)S(1)} %get-tuple-element.46), channel_id=1, source_target_pairs={{0,16},{16,32},{32,48},{48,0},{1,17},{17,33},{33,49},{49,1},{2,18}... | collective-permute-start | bytes 1376264 | tf_op jit(solution)/shard_map/ppermute | solution.py:21
  152.1 4.3 %collective-permute-start.9 = (bf16[256,896]{1,0:T(8,128)(2,1)S(1)}, bf16[256,896]{1,0:T(8,128)(2,1)S(1)}, u32[]{:S(2)}, u32[]{:S(2)}) collective-permute-start(bf16[256,896]{1,0:T(8,128)(2,1)S(1)} %get-tuple-element.47), channel_id=1, source_target_pairs={{0,32},{16,48},{32,0},{48,16},{1,33},{17,49},{33,1},{49,17},{2,34}... | collective-permute-start | bytes 1376264 | tf_op jit(solution)/shard_map/ppermute | solution.py:21
  159.8 9.2 %collective-permute-done.8.p1 = bf16[256,896]{1,0:T(8,128)(2,1)S(1)} collective-permute-done((bf16[256,896]{1,0:T(8,128)(2,1)S(1)}, bf16[256,896]{1,0:T(8,128)(2,1)S(1)}, u32[]{:S(2)}, u32[]{:S(2)}) %collective-permute-start.8) | collective-permute-done | bytes 458784 | tf_op jit(solution)/shard_map/ppermute | solution.py:21
  168.9 8.3 %collective-permute-done.9.p2 = bf16[256,896]{1,0:T(8,128)(2,1)S(1)} collective-permute-done((bf16[256,896]{1,0:T(8,128)(2,1)S(1)}, bf16[256,896]{1,0:T(8,128)(2,1)S(1)}, u32[]{:S(2)}, u32[]{:S(2)}) %collective-permute-start.9) | collective-permute-done | bytes 458784 | tf_op jit(solution)/shard_map/ppermute | solution.py:21
  180.2 4.0 %all-to-all-start.3 = ((bf16[8,32,512]{2,1,0:T(8,128)(2,1)}), bf16[8,32,512]{2,1,0:T(8,128)(2,1)}, u32[]{:S(2)}, u32[]{:S(2)}) async-start(bf16[8,32,512]{2,1,0:T(8,128)(2,1)} %bitcast.11), calls=%async_computation.3 | async-start | bytes 524288 | tf_op jit(solution)/shard_map/all_to_all | solution.py:244
  190.6 4.5 %shard_map.121 = (bf16[128,1024]{1,0:T(8,128)(2,1)S(1)}, bf16[128,1024]{1,0:T(8,128)(2,1)S(1)}, bf16[128,1024]{1,0:T(8,128)(2,1)S(1)}, bf16[128,1024]{1,0:T(8,128)(2,1)S(1)}, bf16[4,128,1024]{2,1,0:T(8,128)(2,1)}) custom-call(s32[5]{0:T(128)S(1)} %stack.23.pos, bf16[1408,256]{1,0:T(8,128)(2,1)S(1)} %copy-done.12, bf16[1408,256]{1,0:T(8,128)(2,1)S(1)} %copy-done.16, ...), custom_call_target="tpu_custom_call" | custom-call | flops 2000000000 | bytes 4194304 | tf_op jit(solution)/shard_map/pallas_call | solution.py:231
  203.0 7.0 %all-to-all-start.4 = ((bf16[8,32,512]{2,1,0:T(8,128)(2,1)}), bf16[8,32,512]{2,1,0:T(8,128)(2,1)S(1)}, u32[]{:S(2)}, u32[]{:S(2)}) async-start(bf16[8,32,512]{2,1,0:T(8,128)(2,1)} %broadcast_in_dim.5), calls=%async_computation.4 | async-start | bytes 524288 | tf_op jit(solution)/shard_map/all_to_all | solution.py:251
  221.5 5.0 %all-to-all-done.4 = bf16[8,32,512]{2,1,0:T(8,128)(2,1)S(1)} async-done(((bf16[8,32,512]{2,1,0:T(8,128)(2,1)}), bf16[8,32,512]{2,1,0:T(8,128)(2,1)S(1)}, u32[]{:S(2)}, u32[]{:S(2)}) %all-to-all-start.4) | async-done | bytes 262176 | tf_op jit(solution)/shard_map/all_to_all | solution.py:251
  226.5 4.2 %collective-permute-start.15 = (bf16[256,512]{1,0:T(8,128)(2,1)S(1)}, bf16[256,512]{1,0:T(8,128)(2,1)S(1)}, u32[]{:S(2)}, u32[]{:S(2)}) collective-permute-start(bf16[256,512]{1,0:T(8,128)(2,1)S(1)} %bitcast.30), channel_id=1, source_target_pairs={{0,48},{16,0},{32,16},{48,32},{1,49},{17,1},{33,17},{49,33},{2,50}... | collective-permute-start | bytes 786440 | tf_op jit(solution)/shard_map/ppermute | solution.py:21
  235.0 13.7 %all-to-all-start.5 = ((bf16[16,8,1024]{2,1,0:T(8,128)(2,1)}), bf16[16,8,1024]{2,1,0:T(8,128)(2,1)S(1)}, u32[]{:S(2)}, u32[]{:S(2)}) async-start(bf16[16,8,1024]{2,1,0:T(8,128)(2,1)} %fusion.4), calls=%async_computation.5 | async-start | bytes 524288 | tf_op jit(solution)/shard_map/all_to_all | solution.py:269
  252.5 4.6 %collective-permute-start.17 = (bf16[256,512]{1,0:T(8,128)(2,1)S(1)}, bf16[256,512]{1,0:T(8,128)(2,1)S(1)}, u32[]{:S(2)}, u32[]{:S(2)}) collective-permute-start(bf16[256,512]{1,0:T(8,128)(2,1)S(1)} %bitcast.32), channel_id=1, source_target_pairs={{0,32},{16,48},{32,0},{48,16},{1,33},{17,49},{33,1},{49,17},{2,34}... | collective-permute-start | bytes 786440 | tf_op jit(solution)/shard_map/ppermute | solution.py:21
  257.1 7.3 %collective-permute-start.16 = (bf16[128,896]{1,0:T(8,128)(2,1)}, bf16[128,896]{1,0:T(8,128)(2,1)S(1)}, u32[]{:S(2)}, u32[]{:S(2)}) collective-permute-start(bf16[128,896]{1,0:T(8,128)(2,1)} %add_convert_fusion.1), channel_id=1, source_target_pairs={{0,256},{256,0},{1,257},{257,1},{2,258},{258,2},{3,259},{259,3},{4... | collective-permute-start | bytes 688136 | tf_op jit(solution)/shard_map/ppermute | solution.py:25
  264.4 19.9 %collective-permute-done.16.arrived = bf16[128,896]{1,0:T(8,128)(2,1)S(1)} collective-permute-done((bf16[128,896]{1,0:T(8,128)(2,1)}, bf16[128,896]{1,0:T(8,128)(2,1)S(1)}, u32[]{:S(2)}, u32[]{:S(2)}) %collective-permute-start.16) | collective-permute-done | bytes 229408 | tf_op jit(solution)/shard_map/ppermute | solution.py:25
  (107 shorter events, 79.2 us)
Async XLA Ops:
  6.9 50.5 %all-to-all-start = ((bf16[16,8,1024]{2,1,0:T(8,128)(2,1)}), bf16[16,8,1024]{2,1,0:T(8,128)(2,1)S(1)}, u32[]{:S(2)}, u32[]{:S(2)}) async-start(bf16[16,8,1024]{2,1,0:T(8,128)(2,1)} %get-tuple-element.36), calls=%async_computation | async-start | bytes 524288 | tf_op jit(solution)/shard_map/all_to_all | solution.py:199
  24.6 32.8 %collective-permute-start = (bf16[1408,256]{1,0:T(8,128)(2,1)S(1)}, bf16[1408,256]{1,0:T(8,128)(2,1)S(1)}, u32[]{:S(2)}, u32[]{:S(2)}) collective-permute-start(bf16[1408,256]{1,0:T(8,128)(2,1)S(1)} %get-tuple-element.35.refs_2_.b0), channel_id=1, source_target_pairs={{0,64},{64,192},{192,128},{128,0},{1,65},{65,193},{193,129},{129,1... | collective-permute-start | bytes 2162696 | tf_op jit(solution)/shard_map/ppermute | solution.py:200
  27.5 27.5 %collective-permute-start.1 = (bf16[128,896]{1,0:T(8,128)(2,1)S(1)}, bf16[128,896]{1,0:T(8,128)(2,1)S(1)}, u32[]{:S(2)}, u32[]{:S(2)}) collective-permute-start(bf16[128,896]{1,0:T(8,128)(2,1)S(1)} %get-tuple-element.37), channel_id=1, source_target_pairs={{0,256},{256,0},{1,257},{257,1},{2,258},{258,2},{3,259},{259,3},{4... | collective-permute-start | bytes 688136 | tf_op jit(solution)/shard_map/ppermute | solution.py:25
  58.6 38.6 %all-to-all-start.1 = ((bf16[4,128,1024]{2,1,0:T(8,128)(2,1)}), bf16[4,128,1024]{2,1,0:T(8,128)(2,1)S(1)}, u32[]{:S(2)}, u32[]{:S(2)}) async-start(bf16[4,128,1024]{2,1,0:T(8,128)(2,1)} %broadcast_in_dim.4), calls=%async_computation.1 | async-start | bytes 2097152 | tf_op jit(solution)/shard_map/all_to_all | solution.py:30
  63.3 33.9 %collective-permute-start.2 = (bf16[1408,256]{1,0:T(8,128)(2,1)S(1)}, bf16[1408,256]{1,0:T(8,128)(2,1)}, u32[]{:S(2)}, u32[]{:S(2)}) collective-permute-start(bf16[1408,256]{1,0:T(8,128)(2,1)S(1)} %collective-permute-done.refs_3_.b1), channel_id=1, source_target_pairs={{0,64},{64,192},{192,128},{128,0},{1,65},{65,193},{193,129},{129,1... | collective-permute-start | bytes 2162696 | tf_op jit(solution)/shard_map/ppermute | solution.py:204
  97.2 32.9 %collective-permute-start.4 = (bf16[4,128,1024]{2,1,0:T(8,128)(2,1)S(1)}, bf16[4,128,1024]{2,1,0:T(8,128)(2,1)S(1)}, u32[]{:S(2)}, u32[]{:S(2)}) collective-permute-start(bf16[4,128,1024]{2,1,0:T(8,128)(2,1)S(1)} %all-to-all-done.1.refs_0_), channel_id=1, source_target_pairs={{0,1},{1,0},{2,3},{3,2},{4,5},{5,4},{6,7},{7,6},{8,9},{9,8},{10,11... | collective-permute-start | bytes 3145736 | tf_op jit(solution)/shard_map/ppermute | solution.py:25
  99.2 31.0 %collective-permute-start.3 = (bf16[1408,256]{1,0:T(8,128)(2,1)}, bf16[1408,256]{1,0:T(8,128)(2,1)S(1)}, u32[]{:S(2)}, u32[]{:S(2)}) collective-permute-start(bf16[1408,256]{1,0:T(8,128)(2,1)} %collective-permute-done.2.refs_4_.b2), channel_id=1, source_target_pairs={{0,64},{64,192},{192,128},{128,0},{1,65},{65,193},{193,129},{129,1... | collective-permute-start | bytes 2162696 | tf_op jit(solution)/shard_map/ppermute | solution.py:207
  102.1 15.7 %collective-permute-start.7 = (bf16[256,896]{1,0:T(8,128)(2,1)S(1)}, bf16[256,896]{1,0:T(8,128)(2,1)S(1)}, u32[]{:S(2)}, u32[]{:S(2)}) collective-permute-start(bf16[256,896]{1,0:T(8,128)(2,1)S(1)} %constant_dynamic-update-slice_fusion.refs_6_.h0), channel_id=1, source_target_pairs={{0,16},{16,32},{32,48},{48,0},{1,17},{17,33},{33,49},{49,1},{2,18}... | collective-permute-start | bytes 1376264 | tf_op jit(solution)/shard_map/ppermute | solution.py:21
  105.4 23.1 %collective-permute-start.6 = (bf16[256,896]{1,0:T(8,128)(2,1)S(1)}, bf16[256,896]{1,0:T(8,128)(2,1)S(1)}, u32[]{:S(2)}, u32[]{:S(2)}) collective-permute-start(bf16[256,896]{1,0:T(8,128)(2,1)S(1)} %constant_dynamic-update-slice_fusion.refs_6_.h0), channel_id=1, source_target_pairs={{0,32},{16,48},{32,0},{48,16},{1,33},{17,49},{33,1},{49,17},{2,34}... | collective-permute-start | bytes 1376264 | tf_op jit(solution)/shard_map/ppermute | solution.py:21
  110.0 20.1 %collective-permute-start.5 = (bf16[256,896]{1,0:T(8,128)(2,1)S(1)}, bf16[256,896]{1,0:T(8,128)(2,1)S(1)}, u32[]{:S(2)}, u32[]{:S(2)}) collective-permute-start(bf16[256,896]{1,0:T(8,128)(2,1)S(1)} %constant_dynamic-update-slice_fusion.refs_6_.h0), channel_id=1, source_target_pairs={{0,48},{16,0},{32,16},{48,32},{1,49},{17,1},{33,17},{49,33},{2,50}... | collective-permute-start | bytes 1376264 | tf_op jit(solution)/shard_map/ppermute | solution.py:21
  138.3 39.8 %all-to-all-start.2 = ((bf16[4,256,512]{2,1,0:T(8,128)(2,1)}), bf16[4,256,512]{2,1,0:T(8,128)(2,1)}, u32[]{:S(2)}, u32[]{:S(2)}) async-start(bf16[4,256,512]{2,1,0:T(8,128)(2,1)} %get-tuple-element.43), calls=%async_computation.2 | async-start | bytes 2097152 | tf_op jit(solution)/shard_map/all_to_all | solution.py:228
  147.8 21.2 %collective-permute-start.8 = (bf16[256,896]{1,0:T(8,128)(2,1)S(1)}, bf16[256,896]{1,0:T(8,128)(2,1)S(1)}, u32[]{:S(2)}, u32[]{:S(2)}) collective-permute-start(bf16[256,896]{1,0:T(8,128)(2,1)S(1)} %get-tuple-element.46), channel_id=1, source_target_pairs={{0,16},{16,32},{32,48},{48,0},{1,17},{17,33},{33,49},{49,1},{2,18}... | collective-permute-start | bytes 1376264 | tf_op jit(solution)/shard_map/ppermute | solution.py:21
  152.1 25.2 %collective-permute-start.9 = (bf16[256,896]{1,0:T(8,128)(2,1)S(1)}, bf16[256,896]{1,0:T(8,128)(2,1)S(1)}, u32[]{:S(2)}, u32[]{:S(2)}) collective-permute-start(bf16[256,896]{1,0:T(8,128)(2,1)S(1)} %get-tuple-element.47), channel_id=1, source_target_pairs={{0,32},{16,48},{32,0},{48,16},{1,33},{17,49},{33,1},{49,17},{2,34}... | collective-permute-start | bytes 1376264 | tf_op jit(solution)/shard_map/ppermute | solution.py:21
  156.4 20.9 %collective-permute-start.10 = (bf16[256,896]{1,0:T(8,128)(2,1)S(1)}, bf16[256,896]{1,0:T(8,128)(2,1)S(1)}, u32[]{:S(2)}, u32[]{:S(2)}) collective-permute-start(bf16[256,896]{1,0:T(8,128)(2,1)S(1)} %get-tuple-element.48), channel_id=1, source_target_pairs={{0,48},{16,0},{32,16},{48,32},{1,49},{17,1},{33,17},{49,33},{2,50}... | collective-permute-start | bytes 1376264 | tf_op jit(solution)/shard_map/ppermute | solution.py:21
  180.2 20.3 %all-to-all-start.3 = ((bf16[8,32,512]{2,1,0:T(8,128)(2,1)}), bf16[8,32,512]{2,1,0:T(8,128)(2,1)}, u32[]{:S(2)}, u32[]{:S(2)}) async-start(bf16[8,32,512]{2,1,0:T(8,128)(2,1)} %bitcast.11), calls=%async_computation.3 | async-start | bytes 524288 | tf_op jit(solution)/shard_map/all_to_all | solution.py:244
  195.8 14.2 %collective-permute-start.11 = (bf16[4,128,1024]{2,1,0:T(8,128)(2,1)}, bf16[4,128,1024]{2,1,0:T(8,128)(2,1)}, u32[]{:S(2)}, u32[]{:S(2)}) collective-permute-start(bf16[4,128,1024]{2,1,0:T(8,128)(2,1)} %get-tuple-element.54), channel_id=1, source_target_pairs={{0,1},{1,0},{2,3},{3,2},{4,5},{5,4},{6,7},{7,6},{8,9},{9,8},{10,11... | collective-permute-start | bytes 3145736 | tf_op jit(solution)/shard_map/ppermute | solution.py:25
  203.0 23.4 %all-to-all-start.4 = ((bf16[8,32,512]{2,1,0:T(8,128)(2,1)}), bf16[8,32,512]{2,1,0:T(8,128)(2,1)S(1)}, u32[]{:S(2)}, u32[]{:S(2)}) async-start(bf16[8,32,512]{2,1,0:T(8,128)(2,1)} %broadcast_in_dim.5), calls=%async_computation.4 | async-start | bytes 524288 | tf_op jit(solution)/shard_map/all_to_all | solution.py:251
  212.3 18.4 %collective-permute-start.12 = (bf16[128,1024]{1,0:T(8,128)(2,1)}, bf16[128,1024]{1,0:T(8,128)(2,1)S(1)}, u32[]{:S(2)}, u32[]{:S(2)}) collective-permute-start(bf16[128,1024]{1,0:T(8,128)(2,1)} %get-tuple-element.67), channel_id=1, source_target_pairs={{0,4},{4,8},{8,12},{12,0},{1,5},{5,9},{9,13},{13,1},{2,6},{6,10},{... | collective-permute-start | bytes 786440 | tf_op jit(solution)/shard_map/ppermute | solution.py:21
  214.5 16.2 %collective-permute-start.14 = (bf16[128,1024]{1,0:T(8,128)(2,1)}, bf16[128,1024]{1,0:T(8,128)(2,1)S(1)}, u32[]{:S(2)}, u32[]{:S(2)}) collective-permute-start(bf16[128,1024]{1,0:T(8,128)(2,1)} %get-tuple-element.68), channel_id=1, source_target_pairs={{0,12},{4,0},{8,4},{12,8},{1,13},{5,1},{9,5},{13,9},{2,14},{6,2},{... | collective-permute-start | bytes 786440 | tf_op jit(solution)/shard_map/ppermute | solution.py:21
  218.1 13.5 %collective-permute-start.13 = (bf16[128,1024]{1,0:T(8,128)(2,1)}, bf16[128,1024]{1,0:T(8,128)(2,1)}, u32[]{:S(2)}, u32[]{:S(2)}) collective-permute-start(bf16[128,1024]{1,0:T(8,128)(2,1)} %get-tuple-element.69), channel_id=1, source_target_pairs={{0,8},{4,12},{8,0},{12,4},{1,9},{5,13},{9,1},{13,5},{2,10},{6,14},... | collective-permute-start | bytes 786440 | tf_op jit(solution)/shard_map/ppermute | solution.py:21
  235.0 53.4 %all-to-all-start.5 = ((bf16[16,8,1024]{2,1,0:T(8,128)(2,1)}), bf16[16,8,1024]{2,1,0:T(8,128)(2,1)S(1)}, u32[]{:S(2)}, u32[]{:S(2)}) async-start(bf16[16,8,1024]{2,1,0:T(8,128)(2,1)} %fusion.4), calls=%async_computation.5 | async-start | bytes 524288 | tf_op jit(solution)/shard_map/all_to_all | solution.py:269
  248.6 37.4 %collective-permute-start.18 = (bf16[256,512]{1,0:T(8,128)(2,1)S(1)}, bf16[256,512]{1,0:T(8,128)(2,1)S(1)}, u32[]{:S(2)}, u32[]{:S(2)}) collective-permute-start(bf16[256,512]{1,0:T(8,128)(2,1)S(1)} %bitcast.31), channel_id=1, source_target_pairs={{0,16},{16,32},{32,48},{48,0},{1,17},{17,33},{33,49},{49,1},{2,18}... | collective-permute-start | bytes 786440 | tf_op jit(solution)/shard_map/ppermute | solution.py:21
  252.5 33.6 %collective-permute-start.17 = (bf16[256,512]{1,0:T(8,128)(2,1)S(1)}, bf16[256,512]{1,0:T(8,128)(2,1)S(1)}, u32[]{:S(2)}, u32[]{:S(2)}) collective-permute-start(bf16[256,512]{1,0:T(8,128)(2,1)S(1)} %bitcast.32), channel_id=1, source_target_pairs={{0,32},{16,48},{32,0},{48,16},{1,33},{17,49},{33,1},{49,17},{2,34}... | collective-permute-start | bytes 786440 | tf_op jit(solution)/shard_map/ppermute | solution.py:21
  257.1 27.2 %collective-permute-start.16 = (bf16[128,896]{1,0:T(8,128)(2,1)}, bf16[128,896]{1,0:T(8,128)(2,1)S(1)}, u32[]{:S(2)}, u32[]{:S(2)}) collective-permute-start(bf16[128,896]{1,0:T(8,128)(2,1)} %add_convert_fusion.1), channel_id=1, source_target_pairs={{0,256},{256,0},{1,257},{257,1},{2,258},{258,2},{3,259},{259,3},{4... | collective-permute-start | bytes 688136 | tf_op jit(solution)/shard_map/ppermute | solution.py:25
  (32 other events, 547.2 us)

commit v9 on v7

--- a/solution.py
+++ b/solution.py
@@ -54,35 +54,27 @@
             hidden[pl.ds((cr * NY + yr) * 16, 16), :] = jnp.concatenate(pair, 0).astype(bf16)
 
 
-def reduce(pos, *refs):
+def backward(pos, *refs):
     cots, boths = refs[:8], refs[8:12]
-    tile, reduced = refs[12:]
+    grad, reduced, tile = refs[12:]
     for piece in range(8):
         for zl in range(NZ):
             tile[pl.ds(zl * 128 + piece * 16, 16), :] = cots[piece][pl.ds(zl * 16, 16), :]
 
     def rows(step, _):
         at = pl.ds(pl.multiple_of(step * 256, 256), 256)
-        for side in range(2):
-            total = None
-            for r in range(NX):
-                part = boths[r][896 + side * 256 : 1152 + side * 256, :]
-                more = dot(tile[at, r * 256 : (r + 1) * 256], part, ((1,), (0,)))
-                total = more if total is None else total + more
-            reduced[at, side * 256 : (side + 1) * 256] = total.astype(bf16)
-        return 0
-
-    lax.fori_loop(0, 4, rows, 0)
-
-
-def backward(pos, tile, b0, b1, b2, b3, grad):
-    def rows(step, _):
-        at = pl.ds(pl.multiple_of(step * 256, 256), 256)
-        total = None
-        for r, both in enumerate((b0, b1, b2, b3)):
-            more = dot(tile[at, r * 256 : (r + 1) * 256], both[:896, :], ((1,), (1,)))
+        total, left, right = None, None, None
+        for r in range(NX):
+            part = tile[at, r * 256 : (r + 1) * 256]
+            more = dot(part, boths[r][:896, :], ((1,), (1,)))
             total = more if total is None else total + more
+            more = dot(part, boths[r][896:1152, :], ((1,), (0,)))
+            left = more if left is None else left + more
+            more = dot(part, boths[r][1152:, :], ((1,), (0,)))
+            right = more if right is None else right + more
         grad[at, :] = total.astype(bf16)
+        reduced[at, :256] = left.astype(bf16)
+        reduced[at, 256:] = right.astype(bf16)
         return 0
 
     lax.fori_loop(0, 4, rows, 0)
@@ -178,18 +170,20 @@
 
     tile = lax.all_gather(hidden, "zl", axis=0, tiled=True)
     got = lax.all_to_all(pack, ("zl", "zh"), 0, 0, tiled=True).reshape(rows, cols)
-    boths = [both] + [shift(both, "x", NX, by) for by in range(1, NX)]
-    got, boths[1], boths[3] = lax.optimization_barrier((got, boths[1], boths[3]))
+    boths = [both, shift(both, "x", NX, 1), both, shift(both, "x", NX, 3)]
+    got, *boths = lax.optimization_barrier((got, *boths))
+    boths[2] = shift(boths[2], "x", NX, 2)
     cots = [got] + [shift(got, "y", NY, by) for by in range(1, NY)]
     cots = cots + [shift(piece, "c", NC, 1) for piece in cots]
 
-    tile_cot, reduced = call(
-        reduce,
+    partial, reduced = call(
+        backward,
         12,
-        [((NZ * rows, cols), bf16), ((NZ * rows, rank), bf16)],
-        flops=10**9,
+        [((NZ * rows, ff), bf16), ((NZ * rows, rank), bf16)],
+        [((NZ * rows, cols), bf16)],
+        flops=3 * 10**9,
     )(pos, *cots, *boths)
-
+    grad_hidden = lax.psum_scatter(partial, "zl", scatter_dimension=0, tiled=True)
     parts = call(
         project,
         2,
@@ -197,20 +191,16 @@
         [((ff, rank), f32), ((NX, NZ * slot, rank), bf16)],
         flops=10**9,
     )(pos, tile, reduced)
-    tile_cot, *parts = lax.optimization_barrier((tile_cot, *parts))
-    (partial,) = call(backward, 5, [((NZ * rows, ff), bf16)], flops=2 * 10**9)(
-        pos, tile_cot, *boths
-    )
-    grad_hidden = lax.psum_scatter(partial, "zl", scatter_dimension=0, tiled=True)
+    *term, leave = call(
+        forward, 5, [((rows, cols), bf16)] * NY + [((NY, rows, cols), bf16)], flops=2 * 10**9
+    )(pos, tile, *boths)
+    leave, *parts = lax.optimization_barrier((leave, *parts))
+    arrived = shift(leave, "c", NC, 1)
+    term = [(term[yr].astype(f32) + arrived[yr].astype(f32)).astype(bf16) for yr in range(NY)]
     total = parts[0].astype(f32)
     for by in range(1, NX):
         total = total + shift(parts[by], "x", NX, -by).astype(f32)
-    total, tile, partial = lax.optimization_barrier((total.astype(bf16), tile, partial))
-    *term, leave = call(
-        forward, 5, [((rows, cols), bf16)] * NY + [((NY, rows, cols), bf16)], flops=2 * 10**9
-    )(pos, tile, *boths)
-    arrived = shift(leave, "c", NC, 1)
-    term = [(term[yr].astype(f32) + arrived[yr].astype(f32)).astype(bf16) for yr in range(NY)]
+    total, grad_hidden, *term = lax.optimization_barrier((total.astype(bf16), grad_hidden, *term))
     outer = term[0].astype(f32)
     for by in range(1, NY):
         outer = outer + shift(term[by], "y", NY, -by).astype(f32)

time: 237 us -> 247 us (1.042)
  blocking collectives: 0 us -> 17.6 us
  waiting for transfers between devices: 81.6 us -> 93.1 us
  local copies, waits for them, and re-layouts: 15.1 us -> 9.22 us
  starting transfers between devices: 95.7 us -> 90.2 us
  other arithmetic: 6.07 us -> 2.22 us
  Pallas kernels: 20.7 us -> 17.6 us
    reduce_scatter x1, waiting for transfers between devices: 0.01 us -> 42.1 us  [body(): lax.psum_scatter(partial, 'zl', scatter_dimension=0, tiled=True)]
    all_to_all x0 -> x1, blocking collectives: none -> 17.6 us  [body(): lax.all_to_all(total, 'zl', 0, 0, tiled=True).reshape(NZ, slot, rank)]
    all_to_all x1 -> x0, waiting for transfers between devices: 14.9 us -> none  [body(): lax.all_to_all(total, 'zl', 0, 0, tiled=True).reshape(NZ, slot, rank)]
    ppermute x20, waiting for transfers between devices: 51.8 us -> 37.9 us  [shift(): lax.ppermute(value, axis, [(i, (i - by) % size) for i in range(size)])]
    all_to_all x1 -> x0, starting transfers between devices: 9.53 us -> none  [body(): lax.all_to_all(total, 'zl', 0, 0, tiled=True).reshape(NZ, slot, rank)]
    all_to_all x1, waiting for transfers between devices: 14 us -> 6.25 us  [body(): step = lax.all_to_all(step, 'zl', 0, 0, tiled=True).reshape(NZ * slot, rank)]
    all_gather x1, waiting for transfers between devices: 0.01 us -> 6.7 us  [body(): tile = lax.all_gather(hidden, 'zl', axis=0, tiled=True)]
    ppermute x20, starting transfers between devices: 57.7 us -> 64.4 us  [shift(): lax.ppermute(value, axis, [(i, (i - by) % size) for i in range(size)])]
  transfers between devices with their start and end apart: 26 -> 25, of which waited for: 11 -> 16; matrix products, arithmetic and copies ran while one was open for 3% -> 1% of each run, Pallas kernels for 6% -> 6%
where the time goes in v9:
time: 247 us; the launch traced here: 244 us
  waiting for transfers between devices  93.1 us (38%)
  starting transfers between devices  90.2 us (37%)
  Pallas kernels  17.6 us (7%)
  blocking collectives  17.6 us (7%)
  between operations  14.4 us (6%)
  local copies, waits for them, and re-layouts  9.22 us (4%)
    ppermute x20, starting transfers between devices, shift(): lax.ppermute(value, axis, [(i, (i - by) % size) for i in range(size)])  64.4 us
    reduce_scatter x1, waiting for transfers between devices, body(): lax.psum_scatter(partial, 'zl', scatter_dimension=0, tiled=True)  42.1 us
    ppermute x20, waiting for transfers between devices, shift(): lax.ppermute(value, axis, [(i, (i - by) % size) for i in range(size)])  37.9 us
    all_to_all x1, blocking collectives, body(): lax.all_to_all(total, 'zl', 0, 0, tiled=True).reshape(NZ, slot, rank)  17.6 us
    all_to_all x1, starting transfers between devices, body(): lax.all_to_all(pack, ('zl', 'zh'), 0, 0, tiled=True).reshape(rows, cols)  15.2 us
    unnamed x30, local copies, waits for them, and re-layouts  8.49 us
    all_to_all x1, starting transfers between devices, body(): outer = lax.all_to_all(outer, ('zl', 'zh'), 0, 0, tiled=True)  6.83 us
    all_gather x1, waiting for transfers between devices, body(): tile = lax.all_gather(hidden, 'zl', axis=0, tiled=True)  6.7 us
  transfers between devices with their start and end apart: 25, of which 16 were waited for; matrix products, arithmetic and copies ran while one was open for 1% of the time, Pallas kernels for 6%

profile of v9, /device:TPU:24, one launch (start us, length us, event | category | flops | bytes accessed | tf_op | source)
XLA Modules:
  0.0 244.4 jit_solution(18182004300593199254)
XLA Ops:
  13.5 15.2 %all-to-all-start = ((bf16[16,8,1024]{2,1,0:T(8,128)(2,1)}), bf16[16,8,1024]{2,1,0:T(8,128)(2,1)S(1)}, u32[]{:S(2)}, u32[]{:S(2)}) async-start(bf16[16,8,1024]{2,1,0:T(8,128)(2,1)} %get-tuple-element.41), calls=%async_computation | async-start | bytes 524288 | tf_op jit(solution)/shard_map/all_to_all | solution.py:172
  28.8 3.4 %collective-permute-start.1 = (bf16[1408,256]{1,0:T(8,128)(2,1)S(1)}, bf16[1408,256]{1,0:T(8,128)(2,1)S(1)}, u32[]{:S(2)}, u32[]{:S(2)}) collective-permute-start(bf16[1408,256]{1,0:T(8,128)(2,1)S(1)} %get-tuple-element.45.b0.refs_8_), channel_id=1, source_target_pairs={{0,16},{16,32},{32,48},{48,0},{1,17},{17,33},{33,49},{49,1},{2,18}... | collective-permute-start | bytes 2162696 | tf_op jit(solution)/shard_map/ppermute | solution.py:18
  32.2 3.7 %collective-permute-start = (bf16[1408,256]{1,0:T(8,128)(2,1)S(1)}, bf16[1408,256]{1,0:T(8,128)(2,1)S(1)}, u32[]{:S(2)}, u32[]{:S(2)}) collective-permute-start(bf16[1408,256]{1,0:T(8,128)(2,1)S(1)} %get-tuple-element.45.b0.refs_8_), channel_id=1, source_target_pairs={{0,48},{16,0},{32,16},{48,32},{1,49},{17,1},{33,17},{49,33},{2,50}... | collective-permute-start | bytes 2162696 | tf_op jit(solution)/shard_map/ppermute | solution.py:18
  35.9 13.6 %collective-permute-done.1.b3.refs_11_ = bf16[1408,256]{1,0:T(8,128)(2,1)S(1)} collective-permute-done((bf16[1408,256]{1,0:T(8,128)(2,1)S(1)}, bf16[1408,256]{1,0:T(8,128)(2,1)S(1)}, u32[]{:S(2)}, u32[]{:S(2)}) %collective-permute-start.1) | collective-permute-done | bytes 720928 | tf_op jit(solution)/shard_map/ppermute | solution.py:18
  51.4 4.6 %collective-permute-start.2 = (bf16[1408,256]{1,0:T(8,128)(2,1)S(1)}, bf16[1408,256]{1,0:T(8,128)(2,1)S(1)}, u32[]{:S(2)}, u32[]{:S(2)}) collective-permute-start(bf16[1408,256]{1,0:T(8,128)(2,1)S(1)} %get-tuple-element.45.b0.refs_8_), channel_id=1, source_target_pairs={{0,32},{16,48},{32,0},{48,16},{1,33},{17,49},{33,1},{49,17},{2,34}... | collective-permute-start | bytes 2162696 | tf_op jit(solution)/shard_map/ppermute | solution.py:18
  58.2 4.4 %collective-permute-start.4 = (bf16[128,1024]{1,0:T(8,128)(2,1)S(1)}, bf16[128,1024]{1,0:T(8,128)(2,1)S(1)}, u32[]{:S(2)}, u32[]{:S(2)}) collective-permute-start(bf16[128,1024]{1,0:T(8,128)(2,1)S(1)} %bitcast.33), channel_id=1, source_target_pairs={{0,8},{4,12},{8,0},{12,4},{1,9},{5,13},{9,1},{13,5},{2,10},{6,14},... | collective-permute-start | bytes 786440 | tf_op jit(solution)/shard_map/ppermute | solution.py:18
  77.1 5.9 %shard_map.120 = (bf16[1024,896]{1,0:T(8,128)(2,1)}, bf16[1024,512]{1,0:T(8,128)(2,1)S(1)}) custom-call(s32[3]{0:T(128)S(1)} %pad_add_fusion.pos, bf16[128,1024]{1,0:T(8,128)(2,1)S(1)} %bitcast.36, bf16[128,1024]{1,0:T(8,128)(2,1)S(1)} %collective-permute-done.3.refs_1_, bf16[128,1024]{1,0:T(8,128)(2,1)S(1)} %collective-permute-done.4.refs_2_, ...), custom_call_target="tpu_custom_call" | custom-call | flops 3000000000 | bytes 4194304 | tf_op jit(solution)/shard_map/pallas_call | solution.py:179
  84.0 6.7 %all-gather.2.cloned.1.call-done.tile = bf16[1024,896]{1,0:T(8,128)(2,1)} async-done(((bf16[128,896]{1,0:T(8,128)(2,1)}), bf16[1024,896]{1,0:T(8,128)(2,1)}) %all-gather.2.cloned.1.call-update) | async-done | bytes 1835024 | tf_op jit(solution)/shard_map/all_gather | solution.py:171
  95.1 3.4 %shard_map.119 = (bf16[128,1024]{1,0:T(8,128)(2,1)S(1)}, bf16[128,1024]{1,0:T(8,128)(2,1)S(1)}, bf16[128,1024]{1,0:T(8,128)(2,1)S(1)}, bf16[128,1024]{1,0:T(8,128)(2,1)S(1)}, bf16[4,128,1024]{2,1,0:T(8,128)(2,1)S(1)}) custom-call(s32[3]{0:T(128)S(1)} %pad_add_fusion.pos, bf16[1024,896]{1,0:T(8,128)(2,1)S(1)} %copy-done.10, ...), custom_call_target="tpu_custom_call" | custom-call | flops 2000000000 | bytes 4194304 | tf_op jit(solution)/shard_map/pallas_call | solution.py:194
  100.5 3.4 %collective-permute-start.10 = (bf16[256,512]{1,0:T(8,128)(2,1)S(1)}, bf16[256,512]{1,0:T(8,128)(2,1)S(1)}, u32[]{:S(2)}, u32[]{:S(2)}) collective-permute-start(bf16[256,512]{1,0:T(8,128)(2,1)S(1)} %get-tuple-element.55), channel_id=1, source_target_pairs={{0,16},{16,32},{32,48},{48,0},{1,17},{17,33},{33,49},{49,1},{2,18}... | collective-permute-start | bytes 786440 | tf_op jit(solution)/shard_map/ppermute | solution.py:18
  103.9 4.7 %collective-permute-start.11 = (bf16[256,512]{1,0:T(8,128)(2,1)S(1)}, bf16[256,512]{1,0:T(8,128)(2,1)S(1)}, u32[]{:S(2)}, u32[]{:S(2)}) collective-permute-start(bf16[256,512]{1,0:T(8,128)(2,1)S(1)} %get-tuple-element.56), channel_id=1, source_target_pairs={{0,32},{16,48},{32,0},{48,16},{1,33},{17,49},{33,1},{49,17},{2,34}... | collective-permute-start | bytes 786440 | tf_op jit(solution)/shard_map/ppermute | solution.py:18
  108.6 3.2 %collective-permute-start.12 = (bf16[256,512]{1,0:T(8,128)(2,1)S(1)}, bf16[256,512]{1,0:T(8,128)(2,1)S(1)}, u32[]{:S(2)}, u32[]{:S(2)}) collective-permute-start(bf16[256,512]{1,0:T(8,128)(2,1)S(1)} %get-tuple-element.57), channel_id=1, source_target_pairs={{0,48},{16,0},{32,16},{48,32},{1,49},{17,1},{33,17},{49,33},{2,50}... | collective-permute-start | bytes 786440 | tf_op jit(solution)/shard_map/ppermute | solution.py:18
  112.3 6.6 %collective-permute-done.11 = bf16[256,512]{1,0:T(8,128)(2,1)S(1)} collective-permute-done((bf16[256,512]{1,0:T(8,128)(2,1)S(1)}, bf16[256,512]{1,0:T(8,128)(2,1)S(1)}, u32[]{:S(2)}, u32[]{:S(2)}) %collective-permute-start.11) | collective-permute-done | bytes 262176 | tf_op jit(solution)/shard_map/ppermute | solution.py:18
  121.0 42.1 %reduce-scatter.2.cloned.1.call-done.total = bf16[128,896]{1,0:T(8,128)(2,1)} async-done(((bf16[1024,896]{1,0:T(8,128)(2,1)}), bf16[128,896]{1,0:T(8,128)(2,1)}) %reduce-scatter.2.cloned.1.call-update) | async-done | bytes 229392 | tf_op jit(solution)/shard_map/reduce_scatter | solution.py:186
  163.1 17.6 %all_to_all.24 = bf16[8,32,512]{2,1,0:T(8,128)(2,1)S(1)} all-to-all(bf16[8,32,512]{2,1,0:T(8,128)(2,1)S(1)} %bitcast.37), channel_id=1, replica_groups=mesh['zl'=8,'x'=4,'y'=4,'zh'=2,'c'=2] {'zl'}, dimensions={0} | all-to-all | bytes 524288 | tf_op jit(solution)/shard_map/all_to_all | solution.py:208
  182.3 3.7 %all-to-all-start.2 = ((bf16[8,32,512]{2,1,0:T(8,128)(2,1)}), bf16[8,32,512]{2,1,0:T(8,128)(2,1)S(1)}, u32[]{:S(2)}, u32[]{:S(2)}) async-start(bf16[8,32,512]{2,1,0:T(8,128)(2,1)} %broadcast_in_dim.2), calls=%async_computation.3 | async-start | bytes 524288 | tf_op jit(solution)/shard_map/all_to_all | solution.py:215
  188.7 4.7 %collective-permute-start.15 = (bf16[128,1024]{1,0:T(8,128)(2,1)S(1)}, bf16[128,1024]{1,0:T(8,128)(2,1)S(1)}, u32[]{:S(2)}, u32[]{:S(2)}) collective-permute-start(bf16[128,1024]{1,0:T(8,128)(2,1)S(1)} %get-tuple-element.66), channel_id=1, source_target_pairs={{0,8},{4,12},{8,0},{12,4},{1,9},{5,13},{9,1},{13,5},{2,10},{6,14},... | collective-permute-start | bytes 786440 | tf_op jit(solution)/shard_map/ppermute | solution.py:18
  195.3 6.2 %all-to-all-done.2 = bf16[8,32,512]{2,1,0:T(8,128)(2,1)S(1)} async-done(((bf16[8,32,512]{2,1,0:T(8,128)(2,1)}), bf16[8,32,512]{2,1,0:T(8,128)(2,1)S(1)}, u32[]{:S(2)}, u32[]{:S(2)}) %all-to-all-start.2) | async-done | bytes 262176 | tf_op jit(solution)/shard_map/all_to_all | solution.py:215
  201.6 5.1 %collective-permute-start.17 = (bf16[256,512]{1,0:T(8,128)(2,1)S(1)}, bf16[256,512]{1,0:T(8,128)(2,1)S(1)}, u32[]{:S(2)}, u32[]{:S(2)}) collective-permute-start(bf16[256,512]{1,0:T(8,128)(2,1)S(1)} %bitcast.28), channel_id=1, source_target_pairs={{0,48},{16,0},{32,16},{48,32},{1,49},{17,1},{33,17},{49,33},{2,50}... | collective-permute-start | bytes 786440 | tf_op jit(solution)/shard_map/ppermute | solution.py:18
  207.6 3.0 %collective-permute-done.17.s1 = bf16[256,512]{1,0:T(8,128)(2,1)S(1)} collective-permute-done((bf16[256,512]{1,0:T(8,128)(2,1)S(1)}, bf16[256,512]{1,0:T(8,128)(2,1)S(1)}, u32[]{:S(2)}, u32[]{:S(2)}) %collective-permute-start.17) | collective-permute-done | bytes 262176 | tf_op jit(solution)/shard_map/ppermute | solution.py:18
  210.5 6.8 %all-to-all-start.3 = ((bf16[16,8,1024]{2,1,0:T(8,128)(2,1)}), bf16[16,8,1024]{2,1,0:T(8,128)(2,1)S(1)}, u32[]{:S(2)}, u32[]{:S(2)}) async-start(bf16[16,8,1024]{2,1,0:T(8,128)(2,1)} %fusion.4), calls=%async_computation.4 | async-start | bytes 524288 | tf_op jit(solution)/shard_map/all_to_all | solution.py:226
  217.4 3.2 %collective-permute-start.19 = (bf16[256,512]{1,0:T(8,128)(2,1)S(1)}, bf16[256,512]{1,0:T(8,128)(2,1)S(1)}, u32[]{:S(2)}, u32[]{:S(2)}) collective-permute-start(bf16[256,512]{1,0:T(8,128)(2,1)S(1)} %bitcast.29), channel_id=1, source_target_pairs={{0,16},{16,32},{32,48},{48,0},{1,17},{17,33},{33,49},{49,1},{2,18}... | collective-permute-start | bytes 786440 | tf_op jit(solution)/shard_map/ppermute | solution.py:18
  220.6 5.8 %collective-permute-start.18 = (bf16[256,512]{1,0:T(8,128)(2,1)S(1)}, bf16[256,512]{1,0:T(8,128)(2,1)S(1)}, u32[]{:S(2)}, u32[]{:S(2)}) collective-permute-start(bf16[256,512]{1,0:T(8,128)(2,1)S(1)} %bitcast.30), channel_id=1, source_target_pairs={{0,32},{16,48},{32,0},{48,16},{1,33},{17,49},{33,1},{49,17},{2,34}... | collective-permute-start | bytes 786440 | tf_op jit(solution)/shard_map/ppermute | solution.py:18
  229.5 4.5 %collective-permute-done.18.s2 = bf16[256,512]{1,0:T(8,128)(2,1)S(1)} collective-permute-done((bf16[256,512]{1,0:T(8,128)(2,1)S(1)}, bf16[256,512]{1,0:T(8,128)(2,1)S(1)}, u32[]{:S(2)}, u32[]{:S(2)}) %collective-permute-start.18) | collective-permute-done | bytes 262176 | tf_op jit(solution)/shard_map/ppermute | solution.py:18
  (74 shorter events, 48.5 us)
Async XLA Ops:
  7.2 83.5 %all-gather.2.cloned.1.call-start = ((), (), s32[]{:S(2)}) async-start(), calls=%async_computation.5 | async-start | bytes 2064384 | tf_op jit(solution)/shard_map/all_gather | solution.py:171
  13.5 37.9 %all-to-all-start = ((bf16[16,8,1024]{2,1,0:T(8,128)(2,1)}), bf16[16,8,1024]{2,1,0:T(8,128)(2,1)S(1)}, u32[]{:S(2)}, u32[]{:S(2)}) async-start(bf16[16,8,1024]{2,1,0:T(8,128)(2,1)} %get-tuple-element.41), calls=%async_computation | async-start | bytes 524288 | tf_op jit(solution)/shard_map/all_to_all | solution.py:172
  28.7 134.4 %reduce-scatter.2.cloned.1.call-start = ((), (), s32[]{:S(2)}) async-start(), calls=%async_computation.6 | async-start | bytes 2064384 | tf_op jit(solution)/shard_map/reduce_scatter | solution.py:186
  28.8 20.7 %collective-permute-start.1 = (bf16[1408,256]{1,0:T(8,128)(2,1)S(1)}, bf16[1408,256]{1,0:T(8,128)(2,1)S(1)}, u32[]{:S(2)}, u32[]{:S(2)}) collective-permute-start(bf16[1408,256]{1,0:T(8,128)(2,1)S(1)} %get-tuple-element.45.b0.refs_8_), channel_id=1, source_target_pairs={{0,16},{16,32},{32,48},{48,0},{1,17},{17,33},{33,49},{49,1},{2,18}... | collective-permute-start | bytes 2162696 | tf_op jit(solution)/shard_map/ppermute | solution.py:18
  32.2 19.2 %collective-permute-start = (bf16[1408,256]{1,0:T(8,128)(2,1)S(1)}, bf16[1408,256]{1,0:T(8,128)(2,1)S(1)}, u32[]{:S(2)}, u32[]{:S(2)}) collective-permute-start(bf16[1408,256]{1,0:T(8,128)(2,1)S(1)} %get-tuple-element.45.b0.refs_8_), channel_id=1, source_target_pairs={{0,48},{16,0},{32,16},{48,32},{1,49},{17,1},{33,17},{49,33},{2,50}... | collective-permute-start | bytes 2162696 | tf_op jit(solution)/shard_map/ppermute | solution.py:18
  51.4 25.6 %collective-permute-start.2 = (bf16[1408,256]{1,0:T(8,128)(2,1)S(1)}, bf16[1408,256]{1,0:T(8,128)(2,1)S(1)}, u32[]{:S(2)}, u32[]{:S(2)}) collective-permute-start(bf16[1408,256]{1,0:T(8,128)(2,1)S(1)} %get-tuple-element.45.b0.refs_8_), channel_id=1, source_target_pairs={{0,32},{16,48},{32,0},{48,16},{1,33},{17,49},{33,1},{49,17},{2,34}... | collective-permute-start | bytes 2162696 | tf_op jit(solution)/shard_map/ppermute | solution.py:18
  56.0 11.1 %collective-permute-start.5 = (bf16[128,1024]{1,0:T(8,128)(2,1)S(1)}, bf16[128,1024]{1,0:T(8,128)(2,1)S(1)}, u32[]{:S(2)}, u32[]{:S(2)}) collective-permute-start(bf16[128,1024]{1,0:T(8,128)(2,1)S(1)} %bitcast.32), channel_id=1, source_target_pairs={{0,4},{4,8},{8,12},{12,0},{1,5},{5,9},{9,13},{13,1},{2,6},{6,10},{... | collective-permute-start | bytes 786440 | tf_op jit(solution)/shard_map/ppermute | solution.py:18
  58.2 11.7 %collective-permute-start.4 = (bf16[128,1024]{1,0:T(8,128)(2,1)S(1)}, bf16[128,1024]{1,0:T(8,128)(2,1)S(1)}, u32[]{:S(2)}, u32[]{:S(2)}) collective-permute-start(bf16[128,1024]{1,0:T(8,128)(2,1)S(1)} %bitcast.33), channel_id=1, source_target_pairs={{0,8},{4,12},{8,0},{12,4},{1,9},{5,13},{9,1},{13,5},{2,10},{6,14},... | collective-permute-start | bytes 786440 | tf_op jit(solution)/shard_map/ppermute | solution.py:18
  62.7 10.9 %collective-permute-start.3 = (bf16[128,1024]{1,0:T(8,128)(2,1)S(1)}, bf16[128,1024]{1,0:T(8,128)(2,1)S(1)}, u32[]{:S(2)}, u32[]{:S(2)}) collective-permute-start(bf16[128,1024]{1,0:T(8,128)(2,1)S(1)} %bitcast.34), channel_id=1, source_target_pairs={{0,12},{4,0},{8,4},{12,8},{1,13},{5,1},{9,5},{13,9},{2,14},{6,2},{... | collective-permute-start | bytes 786440 | tf_op jit(solution)/shard_map/ppermute | solution.py:18
  64.6 10.9 %collective-permute-start.6 = (bf16[128,1024]{1,0:T(8,128)(2,1)S(1)}, bf16[128,1024]{1,0:T(8,128)(2,1)S(1)}, u32[]{:S(2)}, u32[]{:S(2)}) collective-permute-start(bf16[128,1024]{1,0:T(8,128)(2,1)S(1)} %bitcast.35), channel_id=1, source_target_pairs={{0,1},{1,0},{2,3},{3,2},{4,5},{5,4},{6,7},{7,6},{8,9},{9,8},{10,11... | collective-permute-start | bytes 786440 | tf_op jit(solution)/shard_map/ppermute | solution.py:18
  67.1 8.4 %collective-permute-start.9 = (bf16[128,1024]{1,0:T(8,128)(2,1)S(1)}, bf16[128,1024]{1,0:T(8,128)(2,1)S(1)}, u32[]{:S(2)}, u32[]{:S(2)}) collective-permute-start(bf16[128,1024]{1,0:T(8,128)(2,1)S(1)} %collective-permute-done.5.refs_3_), channel_id=1, source_target_pairs={{0,1},{1,0},{2,3},{3,2},{4,5},{5,4},{6,7},{7,6},{8,9},{9,8},{10,11... | collective-permute-start | bytes 786440 | tf_op jit(solution)/shard_map/ppermute | solution.py:18
  69.9 5.6 %collective-permute-start.8 = (bf16[128,1024]{1,0:T(8,128)(2,1)S(1)}, bf16[128,1024]{1,0:T(8,128)(2,1)S(1)}, u32[]{:S(2)}, u32[]{:S(2)}) collective-permute-start(bf16[128,1024]{1,0:T(8,128)(2,1)S(1)} %collective-permute-done.4.refs_2_), channel_id=1, source_target_pairs={{0,1},{1,0},{2,3},{3,2},{4,5},{5,4},{6,7},{7,6},{8,9},{9,8},{10,11... | collective-permute-start | bytes 786440 | tf_op jit(solution)/shard_map/ppermute | solution.py:18
  98.6 22.0 %collective-permute-start.13 = (bf16[4,128,1024]{2,1,0:T(8,128)(2,1)S(1)}, bf16[4,128,1024]{2,1,0:T(8,128)(2,1)S(1)}, u32[]{:S(2)}, u32[]{:S(2)}) collective-permute-start(bf16[4,128,1024]{2,1,0:T(8,128)(2,1)S(1)} %get-tuple-element.60), channel_id=1, source_target_pairs={{0,1},{1,0},{2,3},{3,2},{4,5},{5,4},{6,7},{7,6},{8,9},{9,8},{10,11... | collective-permute-start | bytes 3145736 | tf_op jit(solution)/shard_map/ppermute | solution.py:18
  100.5 11.8 %collective-permute-start.10 = (bf16[256,512]{1,0:T(8,128)(2,1)S(1)}, bf16[256,512]{1,0:T(8,128)(2,1)S(1)}, u32[]{:S(2)}, u32[]{:S(2)}) collective-permute-start(bf16[256,512]{1,0:T(8,128)(2,1)S(1)} %get-tuple-element.55), channel_id=1, source_target_pairs={{0,16},{16,32},{32,48},{48,0},{1,17},{17,33},{33,49},{49,1},{2,18}... | collective-permute-start | bytes 786440 | tf_op jit(solution)/shard_map/ppermute | solution.py:18
  103.9 15.0 %collective-permute-start.11 = (bf16[256,512]{1,0:T(8,128)(2,1)S(1)}, bf16[256,512]{1,0:T(8,128)(2,1)S(1)}, u32[]{:S(2)}, u32[]{:S(2)}) collective-permute-start(bf16[256,512]{1,0:T(8,128)(2,1)S(1)} %get-tuple-element.56), channel_id=1, source_target_pairs={{0,32},{16,48},{32,0},{48,16},{1,33},{17,49},{33,1},{49,17},{2,34}... | collective-permute-start | bytes 786440 | tf_op jit(solution)/shard_map/ppermute | solution.py:18
  108.6 11.9 %collective-permute-start.12 = (bf16[256,512]{1,0:T(8,128)(2,1)S(1)}, bf16[256,512]{1,0:T(8,128)(2,1)S(1)}, u32[]{:S(2)}, u32[]{:S(2)}) collective-permute-start(bf16[256,512]{1,0:T(8,128)(2,1)S(1)} %get-tuple-element.57), channel_id=1, source_target_pairs={{0,48},{16,0},{32,16},{48,32},{1,49},{17,1},{33,17},{49,33},{2,50}... | collective-permute-start | bytes 786440 | tf_op jit(solution)/shard_map/ppermute | solution.py:18
  182.3 19.3 %all-to-all-start.2 = ((bf16[8,32,512]{2,1,0:T(8,128)(2,1)}), bf16[8,32,512]{2,1,0:T(8,128)(2,1)S(1)}, u32[]{:S(2)}, u32[]{:S(2)}) async-start(bf16[8,32,512]{2,1,0:T(8,128)(2,1)} %broadcast_in_dim.2), calls=%async_computation.3 | async-start | bytes 524288 | tf_op jit(solution)/shard_map/all_to_all | solution.py:215
  186.0 20.7 %collective-permute-start.14 = (bf16[128,1024]{1,0:T(8,128)(2,1)S(1)}, bf16[128,1024]{1,0:T(8,128)(2,1)S(1)}, u32[]{:S(2)}, u32[]{:S(2)}) collective-permute-start(bf16[128,1024]{1,0:T(8,128)(2,1)S(1)} %get-tuple-element.65), channel_id=1, source_target_pairs={{0,4},{4,8},{8,12},{12,0},{1,5},{5,9},{9,13},{13,1},{2,6},{6,10},{... | collective-permute-start | bytes 786440 | tf_op jit(solution)/shard_map/ppermute | solution.py:18
  188.7 18.0 %collective-permute-start.15 = (bf16[128,1024]{1,0:T(8,128)(2,1)S(1)}, bf16[128,1024]{1,0:T(8,128)(2,1)S(1)}, u32[]{:S(2)}, u32[]{:S(2)}) collective-permute-start(bf16[128,1024]{1,0:T(8,128)(2,1)S(1)} %get-tuple-element.66), channel_id=1, source_target_pairs={{0,8},{4,12},{8,0},{12,4},{1,9},{5,13},{9,1},{13,5},{2,10},{6,14},... | collective-permute-start | bytes 786440 | tf_op jit(solution)/shard_map/ppermute | solution.py:18
  193.4 13.3 %collective-permute-start.16 = (bf16[128,1024]{1,0:T(8,128)(2,1)S(1)}, bf16[128,1024]{1,0:T(8,128)(2,1)S(1)}, u32[]{:S(2)}, u32[]{:S(2)}) collective-permute-start(bf16[128,1024]{1,0:T(8,128)(2,1)S(1)} %get-tuple-element.67), channel_id=1, source_target_pairs={{0,12},{4,0},{8,4},{12,8},{1,13},{5,1},{9,5},{13,9},{2,14},{6,2},{... | collective-permute-start | bytes 786440 | tf_op jit(solution)/shard_map/ppermute | solution.py:18
  201.6 9.0 %collective-permute-start.17 = (bf16[256,512]{1,0:T(8,128)(2,1)S(1)}, bf16[256,512]{1,0:T(8,128)(2,1)S(1)}, u32[]{:S(2)}, u32[]{:S(2)}) collective-permute-start(bf16[256,512]{1,0:T(8,128)(2,1)S(1)} %bitcast.28), channel_id=1, source_target_pairs={{0,48},{16,0},{32,16},{48,32},{1,49},{17,1},{33,17},{49,33},{2,50}... | collective-permute-start | bytes 786440 | tf_op jit(solution)/shard_map/ppermute | solution.py:18
  210.5 25.8 %all-to-all-start.3 = ((bf16[16,8,1024]{2,1,0:T(8,128)(2,1)}), bf16[16,8,1024]{2,1,0:T(8,128)(2,1)S(1)}, u32[]{:S(2)}, u32[]{:S(2)}) async-start(bf16[16,8,1024]{2,1,0:T(8,128)(2,1)} %fusion.4), calls=%async_computation.4 | async-start | bytes 524288 | tf_op jit(solution)/shard_map/all_to_all | solution.py:226
  217.4 12.2 %collective-permute-start.19 = (bf16[256,512]{1,0:T(8,128)(2,1)S(1)}, bf16[256,512]{1,0:T(8,128)(2,1)S(1)}, u32[]{:S(2)}, u32[]{:S(2)}) collective-permute-start(bf16[256,512]{1,0:T(8,128)(2,1)S(1)} %bitcast.29), channel_id=1, source_target_pairs={{0,16},{16,32},{32,48},{48,0},{1,17},{17,33},{33,49},{49,1},{2,18}... | collective-permute-start | bytes 786440 | tf_op jit(solution)/shard_map/ppermute | solution.py:18
  220.6 13.4 %collective-permute-start.18 = (bf16[256,512]{1,0:T(8,128)(2,1)S(1)}, bf16[256,512]{1,0:T(8,128)(2,1)S(1)}, u32[]{:S(2)}, u32[]{:S(2)}) collective-permute-start(bf16[256,512]{1,0:T(8,128)(2,1)S(1)} %bitcast.30), channel_id=1, source_target_pairs={{0,32},{16,48},{32,0},{48,16},{1,33},{17,49},{33,1},{49,17},{2,34}... | collective-permute-start | bytes 786440 | tf_op jit(solution)/shard_map/ppermute | solution.py:18
  (16 other events, 324.0 us)
Sparse Core Ops, SparseCore 0:
  13.6 76.9 all-gather.1
  93.5 69.5 reduce-scatter.1

commit v10 on v9

--- a/solution.py
+++ b/solution.py
@@ -9,6 +9,7 @@
 corr_second = 1.0 - 0.999**10
 
 NZ, NX, NY, NH, NC = 8, 4, 4, 2, 2
+ORDER = (0, 2, 4, 6, 7, 5, 3, 1)
 bf16, f32 = jnp.bfloat16, jnp.float32
 VMEM = pl.BlockSpec(memory_space=pltpu.VMEM)
 SMEM = pl.BlockSpec(memory_space=pltpu.SMEM)
@@ -58,8 +59,8 @@
     cots, boths = refs[:8], refs[8:12]
     grad, reduced, tile = refs[12:]
     for piece in range(8):
-        for zl in range(NZ):
-            tile[pl.ds(zl * 128 + piece * 16, 16), :] = cots[piece][pl.ds(zl * 16, 16), :]
+        for at, zl in enumerate(ORDER):
+            tile[pl.ds(at * 128 + piece * 16, 16), :] = cots[piece][pl.ds(zl * 16, 16), :]
 
     def rows(step, _):
         at = pl.ds(pl.multiple_of(step * 256, 256), 256)
@@ -80,26 +81,24 @@
     lax.fori_loop(0, 4, rows, 0)
 
 
-def project(pos, tile, reduced, o0, o1, o2, o3, total, blocks):
-    x = pos[0]
+def project(pos, tile, reduced, out, total):
     total[...] = dot(tile[...], reduced[...], ((0,), (0,)))
     spare = jnp.zeros((4, total.shape[1]), f32)
     for xs in range(NX):
         for zl in range(NZ):
             first = zl * 112 + xs * 28
             block = jnp.concatenate([total[first : first + 28, :], spare], 0)
-            blocks[xs, zl * 32 : zl * 32 + 32, :] = block.astype(bf16)
-    for xr, out in enumerate((o0, o1, o2, o3)):
-        out[...] = blocks[lax.rem(x + xr, NX)]
+            out[xs, zl * 32 : zl * 32 + 32, :] = block.astype(bf16)
 
 
 def forward(pos, tile, b0, b1, b2, b3, o0, o1, o2, o3, leave):
-    def rows(step, _):
-        part = tile[pl.ds(pl.multiple_of(step * 256, 256), 256), :]
+    for step in range(4):
+        part = tile[step * 256 : (step + 1) * 256, :]
         for r, both in enumerate((b0, b1, b2, b3)):
             term = dot(part, both[:896, :], ((1,), (0,))).astype(bf16)
             for half in range(2):
-                to = pl.ds(pl.multiple_of((step * 2 + half) * 16, 16), 16)
+                zl = ORDER[step * 2 + half]
+                to = pl.ds(zl * 16, 16)
                 for piece in range(8):
                     first = half * 128 + piece * 16
                     block = term[first : first + 16, :]
@@ -107,9 +106,6 @@
                         (o0, o1, o2, o3)[piece][to, r * 256 : (r + 1) * 256] = block
                     else:
                         leave[piece - NY, to, r * 256 : (r + 1) * 256] = block
-        return 0
-
-    lax.fori_loop(0, 4, rows, 0)
 
 
 def finish_out(pos, parts, out):
@@ -168,7 +164,7 @@
         [((rows, ff), f32)],
     )(pos, gate, up, cotangent, weight, basis)
 
-    tile = lax.all_gather(hidden, "zl", axis=0, tiled=True)
+    tile = lax.all_gather(hidden, "zl", axis=0, tiled=True, axis_index_groups=[ORDER])
     got = lax.all_to_all(pack, ("zl", "zh"), 0, 0, tiled=True).reshape(rows, cols)
     boths = [both, shift(both, "x", NX, 1), both, shift(both, "x", NX, 3)]
     got, *boths = lax.optimization_barrier((got, *boths))
@@ -183,24 +179,19 @@
         [((NZ * rows, cols), bf16)],
         flops=3 * 10**9,
     )(pos, *cots, *boths)
-    grad_hidden = lax.psum_scatter(partial, "zl", scatter_dimension=0, tiled=True)
-    parts = call(
-        project,
-        2,
-        [((NZ * slot, rank), bf16)] * NX,
-        [((ff, rank), f32), ((NX, NZ * slot, rank), bf16)],
-        flops=10**9,
+    grad_hidden = lax.psum_scatter(
+        partial, "zl", scatter_dimension=0, tiled=True, axis_index_groups=[ORDER]
+    )
+    (parts,) = call(
+        project, 2, [((NX, NZ * slot, rank), bf16)], [((ff, rank), f32)], flops=10**9
     )(pos, tile, reduced)
+    total = lax.all_to_all(parts, "x", 0, 0, tiled=True).astype(f32).sum(0)
+    total, tile = lax.optimization_barrier((total.astype(bf16), tile))
     *term, leave = call(
         forward, 5, [((rows, cols), bf16)] * NY + [((NY, rows, cols), bf16)], flops=2 * 10**9
     )(pos, tile, *boths)
-    leave, *parts = lax.optimization_barrier((leave, *parts))
     arrived = shift(leave, "c", NC, 1)
     term = [(term[yr].astype(f32) + arrived[yr].astype(f32)).astype(bf16) for yr in range(NY)]
-    total = parts[0].astype(f32)
-    for by in range(1, NX):
-        total = total + shift(parts[by], "x", NX, -by).astype(f32)
-    total, grad_hidden, *term = lax.optimization_barrier((total.astype(bf16), grad_hidden, *term))
     outer = term[0].astype(f32)
     for by in range(1, NY):
         outer = outer + shift(term[by], "y", NY, -by).astype(f32)

time: 247 us -> 219 us (0.89)
  waiting for transfers between devices: 93.1 us -> 75.3 us
  blocking collectives: 17.6 us -> 0 us
  local copies, waits for them, and re-layouts: 9.22 us -> 15.2 us
  other arithmetic: 2.22 us -> 5.03 us
  starting transfers between devices: 90.2 us -> 87.7 us
    reduce_scatter x1, waiting for transfers between devices: 42.1 us -> 0.02 us  [body(): lax.psum_scatter(partial, 'zl', scatter_dimension=0, tiled=True, axis_ind...]
    all_to_all x0 -> x2, waiting for transfers between devices: none -> 29.3 us  [the longest x1 14.7 us: body(): total = lax.all_to_all(parts, 'x', 0, 0, tiled=True).astype(f32).sum(0)]
    ppermute x20 -> x17, starting transfers between devices: 64.4 us -> 45.3 us  [shift(): lax.ppermute(value, axis, [(i, (i - by) % size) for i in range(size)])]
    all_to_all x1 -> x0, blocking collectives: 17.6 us -> none  [body(): lax.all_to_all(total, 'zl', 0, 0, tiled=True).reshape(NZ, slot, rank)]
    all_to_all x0 -> x2, starting transfers between devices: none -> 13.9 us  [the longest x1 9.38 us: body(): lax.all_to_all(total, 'zl', 0, 0, tiled=True).reshape(NZ, slot, rank)]
    all_gather x1, waiting for transfers between devices: 6.7 us -> 0.01 us  [body(): lax.all_gather(hidden, 'zl', axis=0, tiled=True, axis_index_groups=[ORDER])]
    all_to_all x1, waiting for transfers between devices: 6.25 us -> 12.8 us  [body(): step = lax.all_to_all(step, 'zl', 0, 0, tiled=True).reshape(NZ * slot, rank)]
    ppermute x20 -> x17, waiting for transfers between devices: 37.9 us -> 31.6 us  [shift(): lax.ppermute(value, axis, [(i, (i - by) % size) for i in range(size)])]
  transfers between devices with their start and end apart: 25 -> 24, of which waited for: 16 -> 11; matrix products, arithmetic and copies ran while one was open for 1% -> 3% of each run, Pallas kernels for 6% -> 6%
where the time goes in v10:
time: 219 us; the launch traced here: 217 us
  starting transfers between devices  87.7 us (40%)
  waiting for transfers between devices  75.3 us (34%)
  Pallas kernels  19 us (9%)
  local copies, waits for them, and re-layouts  15.2 us (7%)
  between operations  14.4 us (7%)
  other arithmetic  5.03 us (2%)
    ppermute x17, starting transfers between devices, shift(): lax.ppermute(value, axis, [(i, (i - by) % size) for i in range(size)])  45.3 us
    ppermute x17, waiting for transfers between devices, shift(): lax.ppermute(value, axis, [(i, (i - by) % size) for i in range(size)])  31.6 us
    all_to_all x1, starting transfers between devices, body(): lax.all_to_all(pack, ('zl', 'zh'), 0, 0, tiled=True).reshape(rows, cols)  15.2 us
    all_to_all x1, waiting for transfers between devices, body(): total = lax.all_to_all(parts, 'x', 0, 0, tiled=True).astype(f32).sum(0)  14.7 us
    all_to_all x1, waiting for transfers between devices, body(): lax.all_to_all(total, 'zl', 0, 0, tiled=True).reshape(NZ, slot, rank)  14.6 us
    unnamed x44, local copies, waits for them, and re-layouts  14.5 us
    all_to_all x1, waiting for transfers between devices, body(): step = lax.all_to_all(step, 'zl', 0, 0, tiled=True).reshape(NZ * slot, rank)  12.8 us
    all_to_all x1, starting transfers between devices, body(): lax.all_to_all(total, 'zl', 0, 0, tiled=True).reshape(NZ, slot, rank)  9.38 us
  transfers between devices with their start and end apart: 24, of which 11 were waited for; matrix products, arithmetic and copies ran while one was open for 3% of the time, Pallas kernels for 6%

profile of v10, /device:TPU:24, one launch (start us, length us, event | category | flops | bytes accessed | tf_op | source)
XLA Modules:
  0.0 216.6 jit_solution(3239324457332768041)
XLA Ops:
  13.5 15.2 %all-to-all-start = ((bf16[16,8,1024]{2,1,0:T(8,128)(2,1)}), bf16[16,8,1024]{2,1,0:T(8,128)(2,1)S(1)}, u32[]{:S(2)}, u32[]{:S(2)}) async-start(bf16[16,8,1024]{2,1,0:T(8,128)(2,1)} %get-tuple-element.28), calls=%async_computation | async-start | bytes 524288 | tf_op jit(solution)/shard_map/all_to_all | solution.py:168
  28.7 4.7 %collective-permute-start = (bf16[1408,256]{1,0:T(8,128)(2,1)S(1)}, bf16[1408,256]{1,0:T(8,128)(2,1)S(1)}, u32[]{:S(2)}, u32[]{:S(2)}) collective-permute-start(bf16[1408,256]{1,0:T(8,128)(2,1)S(1)} %get-tuple-element.33.refs_8_.b0), channel_id=1, source_target_pairs={{0,48},{16,0},{32,16},{48,32},{1,49},{17,1},{33,17},{49,33},{2,50}... | collective-permute-start | bytes 2162696 | tf_op jit(solution)/shard_map/ppermute | solution.py:19
  35.3 13.2 %collective-permute-done.refs_9_.b1 = bf16[1408,256]{1,0:T(8,128)(2,1)S(1)} collective-permute-done((bf16[1408,256]{1,0:T(8,128)(2,1)S(1)}, bf16[1408,256]{1,0:T(8,128)(2,1)S(1)}, u32[]{:S(2)}, u32[]{:S(2)}) %collective-permute-start) | collective-permute-done | bytes 720928 | tf_op jit(solution)/shard_map/ppermute | solution.py:19
  48.5 5.3 %collective-permute-done.1.refs_11_.b3 = bf16[1408,256]{1,0:T(8,128)(2,1)S(1)} collective-permute-done((bf16[1408,256]{1,0:T(8,128)(2,1)S(1)}, bf16[1408,256]{1,0:T(8,128)(2,1)S(1)}, u32[]{:S(2)}, u32[]{:S(2)}) %collective-permute-start.1) | collective-permute-done | bytes 720928 | tf_op jit(solution)/shard_map/ppermute | solution.py:19
  56.6 2.6 %collective-permute-start.2 = (bf16[128,1024]{1,0:T(8,128)(2,1)S(1)}, bf16[128,1024]{1,0:T(8,128)(2,1)S(1)}, u32[]{:S(2)}, u32[]{:S(2)}) collective-permute-start(bf16[128,1024]{1,0:T(8,128)(2,1)S(1)} %bitcast.32), channel_id=1, source_target_pairs={{0,12},{4,0},{8,4},{12,8},{1,13},{5,1},{9,5},{13,9},{2,14},{6,2},{... | collective-permute-start | bytes 786440 | tf_op jit(solution)/shard_map/ppermute | solution.py:19
  59.3 2.8 %collective-permute-start.3 = (bf16[128,1024]{1,0:T(8,128)(2,1)S(1)}, bf16[128,1024]{1,0:T(8,128)(2,1)S(1)}, u32[]{:S(2)}, u32[]{:S(2)}) collective-permute-start(bf16[128,1024]{1,0:T(8,128)(2,1)S(1)} %bitcast.33), channel_id=1, source_target_pairs={{0,8},{4,12},{8,0},{12,4},{1,9},{5,13},{9,1},{13,5},{2,10},{6,14},... | collective-permute-start | bytes 786440 | tf_op jit(solution)/shard_map/ppermute | solution.py:19
  62.1 4.1 %collective-permute-start.4 = (bf16[128,1024]{1,0:T(8,128)(2,1)S(1)}, bf16[128,1024]{1,0:T(8,128)(2,1)S(1)}, u32[]{:S(2)}, u32[]{:S(2)}) collective-permute-start(bf16[128,1024]{1,0:T(8,128)(2,1)S(1)} %bitcast.34), channel_id=1, source_target_pairs={{0,4},{4,8},{8,12},{12,0},{1,5},{5,9},{9,13},{13,1},{2,6},{6,10},{... | collective-permute-start | bytes 786440 | tf_op jit(solution)/shard_map/ppermute | solution.py:19
  68.2 3.7 %collective-permute-done.2.refs_1_ = bf16[128,1024]{1,0:T(8,128)(2,1)S(1)} collective-permute-done((bf16[128,1024]{1,0:T(8,128)(2,1)S(1)}, bf16[128,1024]{1,0:T(8,128)(2,1)S(1)}, u32[]{:S(2)}, u32[]{:S(2)}) %collective-permute-start.2) | collective-permute-done | bytes 262176 | tf_op jit(solution)/shard_map/ppermute | solution.py:19
  80.8 5.9 %shard_map.119 = (bf16[1024,896]{1,0:T(8,128)(2,1)}, bf16[1024,512]{1,0:T(8,128)(2,1)S(1)}) custom-call(s32[3]{0:T(128)S(1)} %pad_add_fusion.pos, bf16[128,1024]{1,0:T(8,128)(2,1)S(1)} %bitcast.36, bf16[128,1024]{1,0:T(8,128)(2,1)S(1)} %collective-permute-done.2.refs_1_, bf16[128,1024]{1,0:T(8,128)(2,1)S(1)} %collective-permute-done.3.refs_2_, ...), custom_call_target="tpu_custom_call" | custom-call | flops 3000000000 | bytes 4194304 | tf_op jit(solution)/shard_map/pallas_call | solution.py:175
  89.1 2.7 %shard_map.120 = bf16[4,256,512]{2,1,0:T(8,128)(2,1)} custom-call(s32[3]{0:T(128)S(1)} %pad_add_fusion.pos, bf16[1024,896]{1,0:T(8,128)(2,1)S(1)} %copy-done, bf16[1024,512]{1,0:T(8,128)(2,1)S(1)} %get-tuple-element.35.reduced), custom_call_target="tpu_custom_call" | custom-call | flops 1000000000 | bytes 4194304 | tf_op jit(solution)/shard_map/pallas_call | solution.py:185
  91.8 4.5 %all-to-all-start.1 = ((bf16[4,256,512]{2,1,0:T(8,128)(2,1)}), bf16[4,256,512]{2,1,0:T(8,128)(2,1)S(1)}, u32[]{:S(2)}, u32[]{:S(2)}) async-start(bf16[4,256,512]{2,1,0:T(8,128)(2,1)} %shard_map.120), calls=%async_computation.1 | async-start | bytes 2097152 | tf_op jit(solution)/shard_map/all_to_all | solution.py:188
  97.0 14.7 %all-to-all-done.1 = bf16[4,256,512]{2,1,0:T(8,128)(2,1)S(1)} async-done(((bf16[4,256,512]{2,1,0:T(8,128)(2,1)}), bf16[4,256,512]{2,1,0:T(8,128)(2,1)S(1)}, u32[]{:S(2)}, u32[]{:S(2)}) %all-to-all-start.1) | async-done | bytes 1048608 | tf_op jit(solution)/shard_map/all_to_all | solution.py:188
  112.6 9.4 %all-to-all-start.2 = ((bf16[8,32,512]{2,1,0:T(8,128)(2,1)}), bf16[8,32,512]{2,1,0:T(8,128)(2,1)S(1)}, u32[]{:S(2)}, u32[]{:S(2)}) async-start(bf16[8,32,512]{2,1,0:T(8,128)(2,1)} %bitcast.9), calls=%async_computation.2 | async-start | bytes 524288 | tf_op jit(solution)/shard_map/all_to_all | solution.py:199
  126.4 3.9 %shard_map.121 = (bf16[128,1024]{1,0:T(8,128)(2,1)S(1)}, bf16[128,1024]{1,0:T(8,128)(2,1)S(1)}, bf16[128,1024]{1,0:T(8,128)(2,1)S(1)}, bf16[128,1024]{1,0:T(8,128)(2,1)S(1)}, bf16[4,128,1024]{2,1,0:T(8,128)(2,1)}) custom-call(s32[3]{0:T(128)S(1)} %pad_add_fusion.pos, bf16[1024,896]{1,0:T(8,128)(2,1)S(1)} %copy-done.1, bf16[1408,256]{1,0:T(8,128)(2,1)S(1)} %copy-done.12, ...), custom_call_target="tpu_custom_call" | custom-call | flops 2000000000 | bytes 4194304 | tf_op jit(solution)/shard_map/pallas_call | solution.py:190
  132.2 14.6 %all-to-all-done.2 = bf16[8,32,512]{2,1,0:T(8,128)(2,1)S(1)} async-done(((bf16[8,32,512]{2,1,0:T(8,128)(2,1)}), bf16[8,32,512]{2,1,0:T(8,128)(2,1)S(1)}, u32[]{:S(2)}, u32[]{:S(2)}) %all-to-all-start.2) | async-done | bytes 262176 | tf_op jit(solution)/shard_map/all_to_all | solution.py:199
  148.4 4.7 %all-to-all-start.3 = ((bf16[8,32,512]{2,1,0:T(8,128)(2,1)}), bf16[8,32,512]{2,1,0:T(8,128)(2,1)S(1)}, u32[]{:S(2)}, u32[]{:S(2)}) async-start(bf16[8,32,512]{2,1,0:T(8,128)(2,1)} %broadcast_in_dim.2), calls=%async_computation.3 | async-start | bytes 524288 | tf_op jit(solution)/shard_map/all_to_all | solution.py:206
  156.9 2.5 %collective-permute-start.12 = (bf16[128,1024]{1,0:T(8,128)(2,1)S(1)}, bf16[128,1024]{1,0:T(8,128)(2,1)S(1)}, u32[]{:S(2)}, u32[]{:S(2)}) collective-permute-start(bf16[128,1024]{1,0:T(8,128)(2,1)S(1)} %get-tuple-element.53), channel_id=1, source_target_pairs={{0,8},{4,12},{8,0},{12,4},{1,9},{5,13},{9,1},{13,5},{2,10},{6,14},... | collective-permute-start | bytes 786440 | tf_op jit(solution)/shard_map/ppermute | solution.py:19
  159.4 3.1 %collective-permute-start.13 = (bf16[128,1024]{1,0:T(8,128)(2,1)S(1)}, bf16[128,1024]{1,0:T(8,128)(2,1)S(1)}, u32[]{:S(2)}, u32[]{:S(2)}) collective-permute-start(bf16[128,1024]{1,0:T(8,128)(2,1)S(1)} %get-tuple-element.52), channel_id=1, source_target_pairs={{0,12},{4,0},{8,4},{12,8},{1,13},{5,1},{9,5},{13,9},{2,14},{6,2},{... | collective-permute-start | bytes 786440 | tf_op jit(solution)/shard_map/ppermute | solution.py:19
  162.5 12.8 %all-to-all-done.3 = bf16[8,32,512]{2,1,0:T(8,128)(2,1)S(1)} async-done(((bf16[8,32,512]{2,1,0:T(8,128)(2,1)}), bf16[8,32,512]{2,1,0:T(8,128)(2,1)S(1)}, u32[]{:S(2)}, u32[]{:S(2)}) %all-to-all-start.3) | async-done | bytes 262176 | tf_op jit(solution)/shard_map/all_to_all | solution.py:206
  175.4 3.3 %collective-permute-start.14 = (bf16[256,512]{1,0:T(8,128)(2,1)S(1)}, bf16[256,512]{1,0:T(8,128)(2,1)S(1)}, u32[]{:S(2)}, u32[]{:S(2)}) collective-permute-start(bf16[256,512]{1,0:T(8,128)(2,1)S(1)} %bitcast.28), channel_id=1, source_target_pairs={{0,48},{16,0},{32,16},{48,32},{1,49},{17,1},{33,17},{49,33},{2,50}... | collective-permute-start | bytes 786440 | tf_op jit(solution)/shard_map/ppermute | solution.py:19
  180.6 3.0 %collective-permute-done.14.s1 = bf16[256,512]{1,0:T(8,128)(2,1)S(1)} collective-permute-done((bf16[256,512]{1,0:T(8,128)(2,1)S(1)}, bf16[256,512]{1,0:T(8,128)(2,1)S(1)}, u32[]{:S(2)}, u32[]{:S(2)}) %collective-permute-start.14) | collective-permute-done | bytes 262176 | tf_op jit(solution)/shard_map/ppermute | solution.py:19
  183.6 8.5 %all-to-all-start.4 = ((bf16[16,8,1024]{2,1,0:T(8,128)(2,1)}), bf16[16,8,1024]{2,1,0:T(8,128)(2,1)S(1)}, u32[]{:S(2)}, u32[]{:S(2)}) async-start(bf16[16,8,1024]{2,1,0:T(8,128)(2,1)} %fusion.4), calls=%async_computation.4 | async-start | bytes 524288 | tf_op jit(solution)/shard_map/all_to_all | solution.py:217
  194.1 4.0 %collective-permute-start.16 = (bf16[256,512]{1,0:T(8,128)(2,1)S(1)}, bf16[256,512]{1,0:T(8,128)(2,1)S(1)}, u32[]{:S(2)}, u32[]{:S(2)}) collective-permute-start(bf16[256,512]{1,0:T(8,128)(2,1)S(1)} %bitcast.30), channel_id=1, source_target_pairs={{0,16},{16,32},{32,48},{48,0},{1,17},{17,33},{33,49},{49,1},{2,18}... | collective-permute-start | bytes 786440 | tf_op jit(solution)/shard_map/ppermute | solution.py:19
  202.5 3.0 %collective-permute-done.16.s3 = bf16[256,512]{1,0:T(8,128)(2,1)S(1)} collective-permute-done((bf16[256,512]{1,0:T(8,128)(2,1)S(1)}, bf16[256,512]{1,0:T(8,128)(2,1)S(1)}, u32[]{:S(2)}, u32[]{:S(2)}) %collective-permute-start.16) | collective-permute-done | bytes 262176 | tf_op jit(solution)/shard_map/ppermute | solution.py:19
  (85 shorter events, 49.8 us)
Async XLA Ops:
  7.2 80.4 %all-gather.2.cloned.1.call-start = ((), (), s32[]{:S(2)}) async-start(), calls=%async_computation.6 | async-start | bytes 2064384 | tf_op jit(solution)/shard_map/all_gather | solution.py:167
  13.5 41.2 %all-to-all-start = ((bf16[16,8,1024]{2,1,0:T(8,128)(2,1)}), bf16[16,8,1024]{2,1,0:T(8,128)(2,1)S(1)}, u32[]{:S(2)}, u32[]{:S(2)}) async-start(bf16[16,8,1024]{2,1,0:T(8,128)(2,1)} %get-tuple-element.28), calls=%async_computation | async-start | bytes 524288 | tf_op jit(solution)/shard_map/all_to_all | solution.py:168
  28.7 19.8 %collective-permute-start = (bf16[1408,256]{1,0:T(8,128)(2,1)S(1)}, bf16[1408,256]{1,0:T(8,128)(2,1)S(1)}, u32[]{:S(2)}, u32[]{:S(2)}) collective-permute-start(bf16[1408,256]{1,0:T(8,128)(2,1)S(1)} %get-tuple-element.33.refs_8_.b0), channel_id=1, source_target_pairs={{0,48},{16,0},{32,16},{48,32},{1,49},{17,1},{33,17},{49,33},{2,50}... | collective-permute-start | bytes 2162696 | tf_op jit(solution)/shard_map/ppermute | solution.py:19
  33.4 20.4 %collective-permute-start.1 = (bf16[1408,256]{1,0:T(8,128)(2,1)S(1)}, bf16[1408,256]{1,0:T(8,128)(2,1)S(1)}, u32[]{:S(2)}, u32[]{:S(2)}) collective-permute-start(bf16[1408,256]{1,0:T(8,128)(2,1)S(1)} %get-tuple-element.33.refs_8_.b0), channel_id=1, source_target_pairs={{0,16},{16,32},{32,48},{48,0},{1,17},{17,33},{33,49},{49,1},{2,18}... | collective-permute-start | bytes 2162696 | tf_op jit(solution)/shard_map/ppermute | solution.py:19
  54.7 25.0 %collective-permute-start.9 = (bf16[1408,256]{1,0:T(8,128)(2,1)S(1)}, bf16[1408,256]{1,0:T(8,128)(2,1)S(1)}, u32[]{:S(2)}, u32[]{:S(2)}) collective-permute-start(bf16[1408,256]{1,0:T(8,128)(2,1)S(1)} %get-tuple-element.33.refs_8_.b0), channel_id=1, source_target_pairs={{0,32},{16,48},{32,0},{48,16},{1,33},{17,49},{33,1},{49,17},{2,34}... | collective-permute-start | bytes 2162696 | tf_op jit(solution)/shard_map/ppermute | solution.py:19
  56.6 15.3 %collective-permute-start.2 = (bf16[128,1024]{1,0:T(8,128)(2,1)S(1)}, bf16[128,1024]{1,0:T(8,128)(2,1)S(1)}, u32[]{:S(2)}, u32[]{:S(2)}) collective-permute-start(bf16[128,1024]{1,0:T(8,128)(2,1)S(1)} %bitcast.32), channel_id=1, source_target_pairs={{0,12},{4,0},{8,4},{12,8},{1,13},{5,1},{9,5},{13,9},{2,14},{6,2},{... | collective-permute-start | bytes 786440 | tf_op jit(solution)/shard_map/ppermute | solution.py:19
  59.3 14.6 %collective-permute-start.3 = (bf16[128,1024]{1,0:T(8,128)(2,1)S(1)}, bf16[128,1024]{1,0:T(8,128)(2,1)S(1)}, u32[]{:S(2)}, u32[]{:S(2)}) collective-permute-start(bf16[128,1024]{1,0:T(8,128)(2,1)S(1)} %bitcast.33), channel_id=1, source_target_pairs={{0,8},{4,12},{8,0},{12,4},{1,9},{5,13},{9,1},{13,5},{2,10},{6,14},... | collective-permute-start | bytes 786440 | tf_op jit(solution)/shard_map/ppermute | solution.py:19
  62.1 14.1 %collective-permute-start.4 = (bf16[128,1024]{1,0:T(8,128)(2,1)S(1)}, bf16[128,1024]{1,0:T(8,128)(2,1)S(1)}, u32[]{:S(2)}, u32[]{:S(2)}) collective-permute-start(bf16[128,1024]{1,0:T(8,128)(2,1)S(1)} %bitcast.34), channel_id=1, source_target_pairs={{0,4},{4,8},{8,12},{12,0},{1,5},{5,9},{9,13},{13,1},{2,6},{6,10},{... | collective-permute-start | bytes 786440 | tf_op jit(solution)/shard_map/ppermute | solution.py:19
  66.2 12.0 %collective-permute-start.5 = (bf16[128,1024]{1,0:T(8,128)(2,1)S(1)}, bf16[128,1024]{1,0:T(8,128)(2,1)S(1)}, u32[]{:S(2)}, u32[]{:S(2)}) collective-permute-start(bf16[128,1024]{1,0:T(8,128)(2,1)S(1)} %bitcast.35), channel_id=1, source_target_pairs={{0,1},{1,0},{2,3},{3,2},{4,5},{5,4},{6,7},{7,6},{8,9},{9,8},{10,11... | collective-permute-start | bytes 786440 | tf_op jit(solution)/shard_map/ppermute | solution.py:19
  71.9 6.3 %collective-permute-start.6 = (bf16[128,1024]{1,0:T(8,128)(2,1)S(1)}, bf16[128,1024]{1,0:T(8,128)(2,1)S(1)}, u32[]{:S(2)}, u32[]{:S(2)}) collective-permute-start(bf16[128,1024]{1,0:T(8,128)(2,1)S(1)} %collective-permute-done.2.refs_1_), channel_id=1, source_target_pairs={{0,1},{1,0},{2,3},{3,2},{4,5},{5,4},{6,7},{7,6},{8,9},{9,8},{10,11... | collective-permute-start | bytes 786440 | tf_op jit(solution)/shard_map/ppermute | solution.py:19
  73.8 4.4 %collective-permute-start.7 = (bf16[128,1024]{1,0:T(8,128)(2,1)S(1)}, bf16[128,1024]{1,0:T(8,128)(2,1)S(1)}, u32[]{:S(2)}, u32[]{:S(2)}) collective-permute-start(bf16[128,1024]{1,0:T(8,128)(2,1)S(1)} %collective-permute-done.3.refs_2_), channel_id=1, source_target_pairs={{0,1},{1,0},{2,3},{3,2},{4,5},{5,4},{6,7},{7,6},{8,9},{9,8},{10,11... | collective-permute-start | bytes 786440 | tf_op jit(solution)/shard_map/ppermute | solution.py:19
  76.3 3.4 %collective-permute-start.8 = (bf16[128,1024]{1,0:T(8,128)(2,1)S(1)}, bf16[128,1024]{1,0:T(8,128)(2,1)S(1)}, u32[]{:S(2)}, u32[]{:S(2)}) collective-permute-start(bf16[128,1024]{1,0:T(8,128)(2,1)S(1)} %collective-permute-done.4.refs_3_), channel_id=1, source_target_pairs={{0,1},{1,0},{2,3},{3,2},{4,5},{5,4},{6,7},{7,6},{8,9},{9,8},{10,11... | collective-permute-start | bytes 786440 | tf_op jit(solution)/shard_map/ppermute | solution.py:19
  91.8 19.9 %all-to-all-start.1 = ((bf16[4,256,512]{2,1,0:T(8,128)(2,1)}), bf16[4,256,512]{2,1,0:T(8,128)(2,1)S(1)}, u32[]{:S(2)}, u32[]{:S(2)}) async-start(bf16[4,256,512]{2,1,0:T(8,128)(2,1)} %shard_map.120), calls=%async_computation.1 | async-start | bytes 2097152 | tf_op jit(solution)/shard_map/all_to_all | solution.py:188
  96.3 101.8 %reduce-scatter.2.cloned.1.call-start = ((), (), s32[]{:S(2)}) async-start(), calls=%async_computation.7 | async-start | bytes 2064384 | tf_op jit(solution)/shard_map/reduce_scatter | solution.py:182
  112.6 34.3 %all-to-all-start.2 = ((bf16[8,32,512]{2,1,0:T(8,128)(2,1)}), bf16[8,32,512]{2,1,0:T(8,128)(2,1)S(1)}, u32[]{:S(2)}, u32[]{:S(2)}) async-start(bf16[8,32,512]{2,1,0:T(8,128)(2,1)} %bitcast.9), calls=%async_computation.2 | async-start | bytes 524288 | tf_op jit(solution)/shard_map/all_to_all | solution.py:199
  130.3 22.8 %collective-permute-start.10 = (bf16[4,128,1024]{2,1,0:T(8,128)(2,1)}, bf16[4,128,1024]{2,1,0:T(8,128)(2,1)}, u32[]{:S(2)}, u32[]{:S(2)}) collective-permute-start(bf16[4,128,1024]{2,1,0:T(8,128)(2,1)} %get-tuple-element.38), channel_id=1, source_target_pairs={{0,1},{1,0},{2,3},{3,2},{4,5},{5,4},{6,7},{7,6},{8,9},{9,8},{10,11... | collective-permute-start | bytes 3145736 | tf_op jit(solution)/shard_map/ppermute | solution.py:19
  148.4 27.0 %all-to-all-start.3 = ((bf16[8,32,512]{2,1,0:T(8,128)(2,1)}), bf16[8,32,512]{2,1,0:T(8,128)(2,1)S(1)}, u32[]{:S(2)}, u32[]{:S(2)}) async-start(bf16[8,32,512]{2,1,0:T(8,128)(2,1)} %broadcast_in_dim.2), calls=%async_computation.3 | async-start | bytes 524288 | tf_op jit(solution)/shard_map/all_to_all | solution.py:206
  154.6 24.1 %collective-permute-start.11 = (bf16[128,1024]{1,0:T(8,128)(2,1)S(1)}, bf16[128,1024]{1,0:T(8,128)(2,1)S(1)}, u32[]{:S(2)}, u32[]{:S(2)}) collective-permute-start(bf16[128,1024]{1,0:T(8,128)(2,1)S(1)} %get-tuple-element.51), channel_id=1, source_target_pairs={{0,4},{4,8},{8,12},{12,0},{1,5},{5,9},{9,13},{13,1},{2,6},{6,10},{... | collective-permute-start | bytes 786440 | tf_op jit(solution)/shard_map/ppermute | solution.py:19
  156.9 21.8 %collective-permute-start.12 = (bf16[128,1024]{1,0:T(8,128)(2,1)S(1)}, bf16[128,1024]{1,0:T(8,128)(2,1)S(1)}, u32[]{:S(2)}, u32[]{:S(2)}) collective-permute-start(bf16[128,1024]{1,0:T(8,128)(2,1)S(1)} %get-tuple-element.53), channel_id=1, source_target_pairs={{0,8},{4,12},{8,0},{12,4},{1,9},{5,13},{9,1},{13,5},{2,10},{6,14},... | collective-permute-start | bytes 786440 | tf_op jit(solution)/shard_map/ppermute | solution.py:19
  159.4 19.3 %collective-permute-start.13 = (bf16[128,1024]{1,0:T(8,128)(2,1)S(1)}, bf16[128,1024]{1,0:T(8,128)(2,1)S(1)}, u32[]{:S(2)}, u32[]{:S(2)}) collective-permute-start(bf16[128,1024]{1,0:T(8,128)(2,1)S(1)} %get-tuple-element.52), channel_id=1, source_target_pairs={{0,12},{4,0},{8,4},{12,8},{1,13},{5,1},{9,5},{13,9},{2,14},{6,2},{... | collective-permute-start | bytes 786440 | tf_op jit(solution)/shard_map/ppermute | solution.py:19
  175.4 8.3 %collective-permute-start.14 = (bf16[256,512]{1,0:T(8,128)(2,1)S(1)}, bf16[256,512]{1,0:T(8,128)(2,1)S(1)}, u32[]{:S(2)}, u32[]{:S(2)}) collective-permute-start(bf16[256,512]{1,0:T(8,128)(2,1)S(1)} %bitcast.28), channel_id=1, source_target_pairs={{0,48},{16,0},{32,16},{48,32},{1,49},{17,1},{33,17},{49,33},{2,50}... | collective-permute-start | bytes 786440 | tf_op jit(solution)/shard_map/ppermute | solution.py:19
  183.6 24.9 %all-to-all-start.4 = ((bf16[16,8,1024]{2,1,0:T(8,128)(2,1)}), bf16[16,8,1024]{2,1,0:T(8,128)(2,1)S(1)}, u32[]{:S(2)}, u32[]{:S(2)}) async-start(bf16[16,8,1024]{2,1,0:T(8,128)(2,1)} %fusion.4), calls=%async_computation.4 | async-start | bytes 524288 | tf_op jit(solution)/shard_map/all_to_all | solution.py:217
  192.1 10.4 %collective-permute-start.15 = (bf16[256,512]{1,0:T(8,128)(2,1)S(1)}, bf16[256,512]{1,0:T(8,128)(2,1)S(1)}, u32[]{:S(2)}, u32[]{:S(2)}) collective-permute-start(bf16[256,512]{1,0:T(8,128)(2,1)S(1)} %bitcast.29), channel_id=1, source_target_pairs={{0,32},{16,48},{32,0},{48,16},{1,33},{17,49},{33,1},{49,17},{2,34}... | collective-permute-start | bytes 786440 | tf_op jit(solution)/shard_map/ppermute | solution.py:19
  194.1 11.5 %collective-permute-start.16 = (bf16[256,512]{1,0:T(8,128)(2,1)S(1)}, bf16[256,512]{1,0:T(8,128)(2,1)S(1)}, u32[]{:S(2)}, u32[]{:S(2)}) collective-permute-start(bf16[256,512]{1,0:T(8,128)(2,1)S(1)} %bitcast.30), channel_id=1, source_target_pairs={{0,16},{16,32},{32,48},{48,0},{1,17},{17,33},{33,49},{49,1},{2,18}... | collective-permute-start | bytes 786440 | tf_op jit(solution)/shard_map/ppermute | solution.py:19
  (22 other events, 333.5 us)
Sparse Core Ops, SparseCore 0:
  13.6 66.0 all-gather.1
  100.0 77.2 reduce-scatter.1

commit v11 on v7

--- a/solution.py
+++ b/solution.py
@@ -9,6 +9,7 @@
 corr_second = 1.0 - 0.999**10
 
 NZ, NX, NY, NH, NC = 8, 4, 4, 2, 2
+ORDER = (0, 2, 4, 6, 7, 5, 3, 1)
 bf16, f32 = jnp.bfloat16, jnp.float32
 VMEM = pl.BlockSpec(memory_space=pltpu.VMEM)
 SMEM = pl.BlockSpec(memory_space=pltpu.SMEM)
@@ -34,7 +35,13 @@
     )
 
 
-def prepare(pos, gate, up, cot, weight, basis, hidden, pack, both, plain):
+def join(pos, weight, basis, both):
+    both[:896, :] = weight[...]
+    both[896:1152, :] = basis[:, :256]
+    both[1152:, :] = basis[:, 256:]
+
+
+def prepare(pos, gate, up, cot, hidden, pack, plain):
     x, y, c = pos[0], pos[1], pos[2]
     for r in range(NX):
         block = lax.rem(x + r, NX) * 256
@@ -42,9 +49,6 @@
             piece = cot[:, pl.ds(pl.multiple_of(zl * 1024 + block, 256), 256)]
             for zh in range(NH):
                 pack[zl * NH + zh, :, r * 256 : (r + 1) * 256] = piece
-    both[:896, :] = weight[...]
-    both[896:1152, :] = basis[:, :256]
-    both[1152:, :] = basis[:, 256:]
     g = gate[...].astype(f32)
     plain[...] = g * jax.nn.sigmoid(g) * up[...].astype(f32)
     for cr in range(NC):
@@ -58,8 +62,8 @@
     cots, boths = refs[:8], refs[8:12]
     tile, reduced = refs[12:]
     for piece in range(8):
-        for zl in range(NZ):
-            tile[pl.ds(zl * 128 + piece * 16, 16), :] = cots[piece][pl.ds(zl * 16, 16), :]
+        for at, zl in enumerate(ORDER):
+            tile[pl.ds(at * 128 + piece * 16, 16), :] = cots[piece][pl.ds(zl * 16, 16), :]
 
     def rows(step, _):
         at = pl.ds(pl.multiple_of(step * 256, 256), 256)
@@ -88,26 +92,24 @@
     lax.fori_loop(0, 4, rows, 0)
 
 
-def project(pos, tile, reduced, o0, o1, o2, o3, total, blocks):
-    x = pos[0]
+def project(pos, tile, reduced, out, total):
     total[...] = dot(tile[...], reduced[...], ((0,), (0,)))
     spare = jnp.zeros((4, total.shape[1]), f32)
     for xs in range(NX):
         for zl in range(NZ):
             first = zl * 112 + xs * 28
             block = jnp.concatenate([total[first : first + 28, :], spare], 0)
-            blocks[xs, zl * 32 : zl * 32 + 32, :] = block.astype(bf16)
-    for xr, out in enumerate((o0, o1, o2, o3)):
-        out[...] = blocks[lax.rem(x + xr, NX)]
+            out[xs, zl * 32 : zl * 32 + 32, :] = block.astype(bf16)
 
 
 def forward(pos, tile, b0, b1, b2, b3, o0, o1, o2, o3, leave):
-    def rows(step, _):
-        part = tile[pl.ds(pl.multiple_of(step * 256, 256), 256), :]
+    for step in range(4):
+        part = tile[step * 256 : (step + 1) * 256, :]
         for r, both in enumerate((b0, b1, b2, b3)):
             term = dot(part, both[:896, :], ((1,), (0,))).astype(bf16)
             for half in range(2):
-                to = pl.ds(pl.multiple_of((step * 2 + half) * 16, 16), 16)
+                zl = ORDER[step * 2 + half]
+                to = pl.ds(zl * 16, 16)
                 for piece in range(8):
                     first = half * 128 + piece * 16
                     block = term[first : first + 16, :]
@@ -115,9 +117,6 @@
                         (o0, o1, o2, o3)[piece][to, r * 256 : (r + 1) * 256] = block
                     else:
                         leave[piece - NY, to, r * 256 : (r + 1) * 256] = block
-        return 0
-
-    lax.fori_loop(0, 4, rows, 0)
 
 
 def finish_out(pos, parts, out):
@@ -165,21 +164,17 @@
     deep, rank = basis.shape
     own, slot = moment1.shape[0], 32
 
-    hidden, pack, both = call(
-        prepare,
-        5,
-        [
-            ((rows, ff), bf16),
-            ((NZ * NH, mine, cols), bf16),
-            ((ff + 2 * deep, deep), bf16),
-        ],
-        [((rows, ff), f32)],
-    )(pos, gate, up, cotangent, weight, basis)
-
-    tile = lax.all_gather(hidden, "zl", axis=0, tiled=True)
+    hidden, pack = call(
+        prepare, 3, [((rows, ff), bf16), ((NZ * NH, mine, cols), bf16)], [((rows, ff), f32)]
+    )(pos, gate, up, cotangent)
+    pack, hidden, weight = lax.optimization_barrier((pack, hidden, weight))
+    (both,) = call(join, 2, [((ff + 2 * deep, deep), bf16)])(pos, weight, basis)
+
+    tile = lax.all_gather(hidden, "zl", axis=0, tiled=True, axis_index_groups=[ORDER])
     got = lax.all_to_all(pack, ("zl", "zh"), 0, 0, tiled=True).reshape(rows, cols)
-    boths = [both] + [shift(both, "x", NX, by) for by in range(1, NX)]
-    got, boths[1], boths[3] = lax.optimization_barrier((got, boths[1], boths[3]))
+    boths = [both, shift(both, "x", NX, 1), both, shift(both, "x", NX, 3)]
+    got, *boths = lax.optimization_barrier((got, *boths))
+    boths[2] = shift(boths[2], "x", NX, 2)
     cots = [got] + [shift(got, "y", NY, by) for by in range(1, NY)]
     cots = cots + [shift(piece, "c", NC, 1) for piece in cots]
 
@@ -190,41 +185,38 @@
         flops=10**9,
     )(pos, *cots, *boths)
 
-    parts = call(
-        project,
-        2,
-        [((NZ * slot, rank), bf16)] * NX,
-        [((ff, rank), f32), ((NX, NZ * slot, rank), bf16)],
-        flops=10**9,
+    (parts,) = call(
+        project, 2, [((NX, NZ * slot, rank), bf16)], [((ff, rank), f32)], flops=10**9
     )(pos, tile, reduced)
-    tile_cot, *parts = lax.optimization_barrier((tile_cot, *parts))
+    tile_cot, parts = lax.optimization_barrier((tile_cot, parts))
     (partial,) = call(backward, 5, [((NZ * rows, ff), bf16)], flops=2 * 10**9)(
         pos, tile_cot, *boths
     )
-    grad_hidden = lax.psum_scatter(partial, "zl", scatter_dimension=0, tiled=True)
-    total = parts[0].astype(f32)
-    for by in range(1, NX):
-        total = total + shift(parts[by], "x", NX, -by).astype(f32)
+    grad_hidden = lax.psum_scatter(
+        partial, "zl", scatter_dimension=0, tiled=True, axis_index_groups=[ORDER]
+    )
+    total = lax.all_to_all(parts, "x", 0, 0, tiled=True).astype(f32).sum(0)
     total, tile, partial = lax.optimization_barrier((total.astype(bf16), tile, partial))
     *term, leave = call(
         forward, 5, [((rows, cols), bf16)] * NY + [((NY, rows, cols), bf16)], flops=2 * 10**9
     )(pos, tile, *boths)
     arrived = shift(leave, "c", NC, 1)
     term = [(term[yr].astype(f32) + arrived[yr].astype(f32)).astype(bf16) for yr in range(NY)]
-    outer = term[0].astype(f32)
-    for by in range(1, NY):
-        outer = outer + shift(term[by], "y", NY, -by).astype(f32)
-    outer = outer.astype(bf16).reshape(NZ * NH, mine, cols)
     total = lax.all_to_all(total, "zl", 0, 0, tiled=True).reshape(NZ, slot, rank)
     projected = total.astype(f32).sum(0)[:own]
     moment1_new = 0.9 * moment1 + 0.1 * projected
     moment2_new = 0.999 * moment2 + 0.001 * projected * projected
     step = (moment1_new / corr_first / (jnp.sqrt(moment2_new / corr_second) + 1e-08)).astype(bf16)
     step = jnp.pad(step, ((0, slot - own), (0, 0)))
+    step, *term = lax.optimization_barrier((step, *term))
     step = jnp.broadcast_to(step[None], (NZ, slot, rank))
     step = lax.all_to_all(step, "zl", 0, 0, tiled=True).reshape(NZ * slot, rank)
+    outer = term[0].astype(f32)
+    for by in range(1, NY):
+        outer = outer + shift(term[by], "y", NY, -by).astype(f32)
+    outer = outer.astype(bf16).reshape(NZ * NH, mine, cols)
+    step, outer = lax.optimization_barrier((step, outer))
     steps = [step] + [shift(step, "x", NX, by) for by in range(1, NX)]
-    outer, steps[1] = lax.optimization_barrier((outer, steps[1]))
     (expansion,) = call(
         expand,
         5,

time: 237 us -> 219 us (0.924)
  waiting for transfers between devices: 81.6 us -> 66.9 us
  starting transfers between devices: 95.7 us -> 89.5 us
  local copies, waits for them, and re-layouts: 15.1 us -> 18 us
    ppermute x20 -> x17, starting transfers between devices: 57.7 us -> 46 us  [shift(): lax.ppermute(value, axis, [(i, (i - by) % size) for i in range(size)])]
    all_to_all x1, waiting for transfers between devices: 14 us -> 2.39 us  [body(): step = lax.all_to_all(step, 'zl', 0, 0, tiled=True).reshape(NZ * slot, rank)]
    ppermute x20 -> x17, waiting for transfers between devices: 51.8 us -> 41.1 us  [shift(): lax.ppermute(value, axis, [(i, (i - by) % size) for i in range(size)])]
    all_to_all x0 -> x1, waiting for transfers between devices: none -> 9.11 us  [body(): total = lax.all_to_all(parts, 'x', 0, 0, tiled=True).astype(f32).sum(0)]
    all_to_all x0 -> x1, starting transfers between devices: none -> 4.64 us  [body(): total = lax.all_to_all(parts, 'x', 0, 0, tiled=True).astype(f32).sum(0)]
    unnamed x42 -> x46, local copies, waits for them, and re-layouts: 14.4 us -> 17.2 us
  transfers between devices with their start and end apart: 26 -> 24, of which waited for: 11 -> 12; matrix products, arithmetic and copies ran while one was open for 3% -> 4% of each run, Pallas kernels for 6% -> 7%
where the time goes in v11:
time: 219 us; the launch traced here: 217 us
  starting transfers between devices  89.5 us (41%)
  waiting for transfers between devices  66.9 us (31%)
  Pallas kernels  20.8 us (9%)
  local copies, waits for them, and re-layouts  18 us (8%)
  between operations  14.4 us (7%)
  other arithmetic  7.18 us (3%)
    ppermute x17, starting transfers between devices, shift(): lax.ppermute(value, axis, [(i, (i - by) % size) for i in range(size)])  46 us
    ppermute x17, waiting for transfers between devices, shift(): lax.ppermute(value, axis, [(i, (i - by) % size) for i in range(size)])  41.1 us
    unnamed x46, local copies, waits for them, and re-layouts  17.2 us
    all_to_all x1, starting transfers between devices, body(): lax.all_to_all(pack, ('zl', 'zh'), 0, 0, tiled=True).reshape(rows, cols)  15.2 us
    all_to_all x1, waiting for transfers between devices, body(): lax.all_to_all(total, 'zl', 0, 0, tiled=True).reshape(NZ, slot, rank)  14.2 us
    all_to_all x1, starting transfers between devices, body(): lax.all_to_all(total, 'zl', 0, 0, tiled=True).reshape(NZ, slot, rank)  9.35 us
    all_to_all x1, starting transfers between devices, body(): outer = lax.all_to_all(outer, ('zl', 'zh'), 0, 0, tiled=True)  9.2 us
    all_to_all x1, waiting for transfers between devices, body(): total = lax.all_to_all(parts, 'x', 0, 0, tiled=True).astype(f32).sum(0)  9.11 us
  transfers between devices with their start and end apart: 24, of which 12 were waited for; matrix products, arithmetic and copies ran while one was open for 4% of the time, Pallas kernels for 7%

profile of v11, /device:TPU:24, one launch (start us, length us, event | category | flops | bytes accessed | tf_op | source)
XLA Modules:
  0.0 216.8 jit_solution(4494027290579488823)
XLA Ops:
  11.5 15.2 %all-to-all-start = ((bf16[16,8,1024]{2,1,0:T(8,128)(2,1)}), bf16[16,8,1024]{2,1,0:T(8,128)(2,1)S(1)}, u32[]{:S(2)}, u32[]{:S(2)}) async-start(bf16[16,8,1024]{2,1,0:T(8,128)(2,1)} %get-tuple-element.38), calls=%async_computation | async-start | bytes 524288 | tf_op jit(solution)/shard_map/all_to_all | solution.py:174
  29.3 4.7 %collective-permute-start = (bf16[1408,256]{1,0:T(8,128)(2,1)S(1)}, bf16[1408,256]{1,0:T(8,128)(2,1)S(1)}, u32[]{:S(2)}, u32[]{:S(2)}) collective-permute-start(bf16[1408,256]{1,0:T(8,128)(2,1)S(1)} %shard_map.119.refs_8_.b0), channel_id=1, source_target_pairs={{0,48},{16,0},{32,16},{48,32},{1,49},{17,1},{33,17},{49,33},{2,50}... | collective-permute-start | bytes 2162696 | tf_op jit(solution)/shard_map/ppermute | solution.py:19
  35.9 13.2 %collective-permute-done.refs_9_.b1 = bf16[1408,256]{1,0:T(8,128)(2,1)S(1)} collective-permute-done((bf16[1408,256]{1,0:T(8,128)(2,1)S(1)}, bf16[1408,256]{1,0:T(8,128)(2,1)S(1)}, u32[]{:S(2)}, u32[]{:S(2)}) %collective-permute-start) | collective-permute-done | bytes 720928 | tf_op jit(solution)/shard_map/ppermute | solution.py:19
  49.1 5.3 %collective-permute-done.1.refs_11_.b3 = bf16[1408,256]{1,0:T(8,128)(2,1)S(1)} collective-permute-done((bf16[1408,256]{1,0:T(8,128)(2,1)S(1)}, bf16[1408,256]{1,0:T(8,128)(2,1)S(1)}, u32[]{:S(2)}, u32[]{:S(2)}) %collective-permute-start.1) | collective-permute-done | bytes 720928 | tf_op jit(solution)/shard_map/ppermute | solution.py:19
  57.2 2.6 %collective-permute-start.2 = (bf16[128,1024]{1,0:T(8,128)(2,1)S(1)}, bf16[128,1024]{1,0:T(8,128)(2,1)S(1)}, u32[]{:S(2)}, u32[]{:S(2)}) collective-permute-start(bf16[128,1024]{1,0:T(8,128)(2,1)S(1)} %bitcast.28), channel_id=1, source_target_pairs={{0,12},{4,0},{8,4},{12,8},{1,13},{5,1},{9,5},{13,9},{2,14},{6,2},{... | collective-permute-start | bytes 786440 | tf_op jit(solution)/shard_map/ppermute | solution.py:19
  59.8 2.8 %collective-permute-start.3 = (bf16[128,1024]{1,0:T(8,128)(2,1)S(1)}, bf16[128,1024]{1,0:T(8,128)(2,1)S(1)}, u32[]{:S(2)}, u32[]{:S(2)}) collective-permute-start(bf16[128,1024]{1,0:T(8,128)(2,1)S(1)} %bitcast.29), channel_id=1, source_target_pairs={{0,8},{4,12},{8,0},{12,4},{1,9},{5,13},{9,1},{13,5},{2,10},{6,14},... | collective-permute-start | bytes 786440 | tf_op jit(solution)/shard_map/ppermute | solution.py:19
  62.7 4.1 %collective-permute-start.4 = (bf16[128,1024]{1,0:T(8,128)(2,1)S(1)}, bf16[128,1024]{1,0:T(8,128)(2,1)S(1)}, u32[]{:S(2)}, u32[]{:S(2)}) collective-permute-start(bf16[128,1024]{1,0:T(8,128)(2,1)S(1)} %bitcast.30), channel_id=1, source_target_pairs={{0,4},{4,8},{8,12},{12,0},{1,5},{5,9},{9,13},{13,1},{2,6},{6,10},{... | collective-permute-start | bytes 786440 | tf_op jit(solution)/shard_map/ppermute | solution.py:19
  68.7 3.8 %collective-permute-done.2.refs_1_ = bf16[128,1024]{1,0:T(8,128)(2,1)S(1)} collective-permute-done((bf16[128,1024]{1,0:T(8,128)(2,1)S(1)}, bf16[128,1024]{1,0:T(8,128)(2,1)S(1)}, u32[]{:S(2)}, u32[]{:S(2)}) %collective-permute-start.2) | collective-permute-done | bytes 262176 | tf_op jit(solution)/shard_map/ppermute | solution.py:19
  87.5 2.7 %shard_map.121 = bf16[4,256,512]{2,1,0:T(8,128)(2,1)} custom-call(s32[3]{0:T(128)S(1)} %pad_add_fusion.pos, bf16[1024,896]{1,0:T(8,128)(2,1)S(1)} %copy-done, bf16[1024,512]{1,0:T(8,128)(2,1)S(1)} %get-tuple-element.47.reduced), custom_call_target="tpu_custom_call" | custom-call | flops 1000000000 | bytes 4194304 | tf_op jit(solution)/shard_map/pallas_call | solution.py:188
  90.2 4.6 %all-to-all-start.1 = ((bf16[4,256,512]{2,1,0:T(8,128)(2,1)}), bf16[4,256,512]{2,1,0:T(8,128)(2,1)}, u32[]{:S(2)}, u32[]{:S(2)}) async-start(bf16[4,256,512]{2,1,0:T(8,128)(2,1)} %shard_map.121), calls=%async_computation.1 | async-start | bytes 2097152 | tf_op jit(solution)/shard_map/all_to_all | solution.py:198
  96.5 4.8 %shard_map.122 = bf16[1024,896]{1,0:T(8,128)(2,1)} custom-call(s32[3]{0:T(128)S(1)} %pad_add_fusion.pos, bf16[1024,1024]{1,0:T(8,128)(2,1)S(1)} %copy-done.22, bf16[1408,256]{1,0:T(8,128)(2,1)S(1)} %shard_map.119.refs_8_.b0, bf16[1408,256]{1,0:T(8,128)(2,1)S(1)} %collective-permute-done.refs_9_.b1, bf16[1408,256]{1,0:T(8,128)(2,1)S(1)} %copy-done.13, ...), custom_call_target="tpu_custom_call" | custom-call | flops 2000000000 | bytes 4194304 | tf_op jit(solution)/shard_map/pallas_call | solution.py:192
  101.3 9.1 %all-to-all-done.1 = bf16[4,256,512]{2,1,0:T(8,128)(2,1)} async-done(((bf16[4,256,512]{2,1,0:T(8,128)(2,1)}), bf16[4,256,512]{2,1,0:T(8,128)(2,1)}, u32[]{:S(2)}, u32[]{:S(2)}) %all-to-all-start.1) | async-done | bytes 1048608 | tf_op jit(solution)/shard_map/all_to_all | solution.py:198
  112.5 9.3 %all-to-all-start.2 = ((bf16[8,32,512]{2,1,0:T(8,128)(2,1)}), bf16[8,32,512]{2,1,0:T(8,128)(2,1)}, u32[]{:S(2)}, u32[]{:S(2)}) async-start(bf16[8,32,512]{2,1,0:T(8,128)(2,1)} %bitcast.4), calls=%async_computation.2 | async-start | bytes 524288 | tf_op jit(solution)/shard_map/all_to_all | solution.py:205
  124.1 3.9 %shard_map.123 = (bf16[128,1024]{1,0:T(8,128)(2,1)S(1)}, bf16[128,1024]{1,0:T(8,128)(2,1)S(1)}, bf16[128,1024]{1,0:T(8,128)(2,1)S(1)}, bf16[128,1024]{1,0:T(8,128)(2,1)S(1)}, bf16[4,128,1024]{2,1,0:T(8,128)(2,1)}) custom-call(s32[3]{0:T(128)S(1)} %pad_add_fusion.pos, bf16[1024,896]{1,0:T(8,128)(2,1)S(1)} %copy-done.1, ...), custom_call_target="tpu_custom_call" | custom-call | flops 2000000000 | bytes 4194304 | tf_op jit(solution)/shard_map/pallas_call | solution.py:200
  132.0 14.2 %all-to-all-done.2 = bf16[8,32,512]{2,1,0:T(8,128)(2,1)} async-done(((bf16[8,32,512]{2,1,0:T(8,128)(2,1)}), bf16[8,32,512]{2,1,0:T(8,128)(2,1)}, u32[]{:S(2)}, u32[]{:S(2)}) %all-to-all-start.2) | async-done | bytes 262176 | tf_op jit(solution)/shard_map/all_to_all | solution.py:205
  151.0 5.1 %all-to-all-start.3 = ((bf16[8,32,512]{2,1,0:T(8,128)(2,1)}), bf16[8,32,512]{2,1,0:T(8,128)(2,1)S(1)}, u32[]{:S(2)}, u32[]{:S(2)}) async-start(bf16[8,32,512]{2,1,0:T(8,128)(2,1)} %broadcast_in_dim.2), calls=%async_computation.3 | async-start | bytes 524288 | tf_op jit(solution)/shard_map/all_to_all | solution.py:213
  158.2 4.0 %collective-permute-start.12 = (bf16[128,1024]{1,0:T(8,128)(2,1)S(1)}, bf16[128,1024]{1,0:T(8,128)(2,1)S(1)}, u32[]{:S(2)}, u32[]{:S(2)}) collective-permute-start(bf16[128,1024]{1,0:T(8,128)(2,1)S(1)} %get-tuple-element.60), channel_id=1, source_target_pairs={{0,8},{4,12},{8,0},{12,4},{1,9},{5,13},{9,1},{13,5},{2,10},{6,14},... | collective-permute-start | bytes 786440 | tf_op jit(solution)/shard_map/ppermute | solution.py:19
  162.2 3.1 %collective-permute-start.11 = (bf16[128,1024]{1,0:T(8,128)(2,1)S(1)}, bf16[128,1024]{1,0:T(8,128)(2,1)S(1)}, u32[]{:S(2)}, u32[]{:S(2)}) collective-permute-start(bf16[128,1024]{1,0:T(8,128)(2,1)S(1)} %get-tuple-element.59), channel_id=1, source_target_pairs={{0,4},{4,8},{8,12},{12,0},{1,5},{5,9},{9,13},{13,1},{2,6},{6,10},{... | collective-permute-start | bytes 786440 | tf_op jit(solution)/shard_map/ppermute | solution.py:19
  165.3 6.3 %collective-permute-done.13 = bf16[128,1024]{1,0:T(8,128)(2,1)S(1)} collective-permute-done((bf16[128,1024]{1,0:T(8,128)(2,1)S(1)}, bf16[128,1024]{1,0:T(8,128)(2,1)S(1)}, u32[]{:S(2)}, u32[]{:S(2)}) %collective-permute-start.13) | collective-permute-done | bytes 262176 | tf_op jit(solution)/shard_map/ppermute | solution.py:19
  171.6 2.5 %collective-permute-done.11 = bf16[128,1024]{1,0:T(8,128)(2,1)S(1)} collective-permute-done((bf16[128,1024]{1,0:T(8,128)(2,1)S(1)}, bf16[128,1024]{1,0:T(8,128)(2,1)S(1)}, u32[]{:S(2)}, u32[]{:S(2)}) %collective-permute-start.11) | collective-permute-done | bytes 262176 | tf_op jit(solution)/shard_map/ppermute | solution.py:19
  177.4 9.2 %all-to-all-start.4 = ((bf16[16,8,1024]{2,1,0:T(8,128)(2,1)}), bf16[16,8,1024]{2,1,0:T(8,128)(2,1)S(1)}, u32[]{:S(2)}, u32[]{:S(2)}) async-start(bf16[16,8,1024]{2,1,0:T(8,128)(2,1)} %fusion.4), calls=%async_computation.4 | async-start | bytes 524288 | tf_op jit(solution)/shard_map/all_to_all | solution.py:228
  186.6 3.0 %collective-permute-start.14 = (bf16[256,512]{1,0:T(8,128)(2,1)S(1)}, bf16[256,512]{1,0:T(8,128)(2,1)S(1)}, u32[]{:S(2)}, u32[]{:S(2)}) collective-permute-start(bf16[256,512]{1,0:T(8,128)(2,1)S(1)} %bitcast.33), channel_id=1, source_target_pairs={{0,48},{16,0},{32,16},{48,32},{1,49},{17,1},{33,17},{49,33},{2,50}... | collective-permute-start | bytes 786440 | tf_op jit(solution)/shard_map/ppermute | solution.py:19
  189.5 3.8 %collective-permute-start.15 = (bf16[256,512]{1,0:T(8,128)(2,1)S(1)}, bf16[256,512]{1,0:T(8,128)(2,1)S(1)}, u32[]{:S(2)}, u32[]{:S(2)}) collective-permute-start(bf16[256,512]{1,0:T(8,128)(2,1)S(1)} %bitcast.34), channel_id=1, source_target_pairs={{0,32},{16,48},{32,0},{48,16},{1,33},{17,49},{33,1},{49,17},{2,34}... | collective-permute-start | bytes 786440 | tf_op jit(solution)/shard_map/ppermute | solution.py:19
  196.8 4.7 %collective-permute-done.15.s2 = bf16[256,512]{1,0:T(8,128)(2,1)S(1)} collective-permute-done((bf16[256,512]{1,0:T(8,128)(2,1)S(1)}, bf16[256,512]{1,0:T(8,128)(2,1)S(1)}, u32[]{:S(2)}, u32[]{:S(2)}) %collective-permute-start.15) | collective-permute-done | bytes 262176 | tf_op jit(solution)/shard_map/ppermute | solution.py:19
  (89 shorter events, 60.4 us)
Async XLA Ops:
  7.2 78.9 %all-gather.2.cloned.1.call-start = ((), (), s32[]{:S(2)}) async-start(), calls=%async_computation.6 | async-start | bytes 2064384 | tf_op jit(solution)/shard_map/all_gather | solution.py:173
  11.5 43.7 %all-to-all-start = ((bf16[16,8,1024]{2,1,0:T(8,128)(2,1)}), bf16[16,8,1024]{2,1,0:T(8,128)(2,1)S(1)}, u32[]{:S(2)}, u32[]{:S(2)}) async-start(bf16[16,8,1024]{2,1,0:T(8,128)(2,1)} %get-tuple-element.38), calls=%async_computation | async-start | bytes 524288 | tf_op jit(solution)/shard_map/all_to_all | solution.py:174
  29.3 19.8 %collective-permute-start = (bf16[1408,256]{1,0:T(8,128)(2,1)S(1)}, bf16[1408,256]{1,0:T(8,128)(2,1)S(1)}, u32[]{:S(2)}, u32[]{:S(2)}) collective-permute-start(bf16[1408,256]{1,0:T(8,128)(2,1)S(1)} %shard_map.119.refs_8_.b0), channel_id=1, source_target_pairs={{0,48},{16,0},{32,16},{48,32},{1,49},{17,1},{33,17},{49,33},{2,50}... | collective-permute-start | bytes 2162696 | tf_op jit(solution)/shard_map/ppermute | solution.py:19
  34.0 20.4 %collective-permute-start.1 = (bf16[1408,256]{1,0:T(8,128)(2,1)S(1)}, bf16[1408,256]{1,0:T(8,128)(2,1)S(1)}, u32[]{:S(2)}, u32[]{:S(2)}) collective-permute-start(bf16[1408,256]{1,0:T(8,128)(2,1)S(1)} %shard_map.119.refs_8_.b0), channel_id=1, source_target_pairs={{0,16},{16,32},{32,48},{48,0},{1,17},{17,33},{33,49},{49,1},{2,18}... | collective-permute-start | bytes 2162696 | tf_op jit(solution)/shard_map/ppermute | solution.py:19
  55.2 25.0 %collective-permute-start.9 = (bf16[1408,256]{1,0:T(8,128)(2,1)S(1)}, bf16[1408,256]{1,0:T(8,128)(2,1)S(1)}, u32[]{:S(2)}, u32[]{:S(2)}) collective-permute-start(bf16[1408,256]{1,0:T(8,128)(2,1)S(1)} %shard_map.119.refs_8_.b0), channel_id=1, source_target_pairs={{0,32},{16,48},{32,0},{48,16},{1,33},{17,49},{33,1},{49,17},{2,34}... | collective-permute-start | bytes 2162696 | tf_op jit(solution)/shard_map/ppermute | solution.py:19
  57.2 15.3 %collective-permute-start.2 = (bf16[128,1024]{1,0:T(8,128)(2,1)S(1)}, bf16[128,1024]{1,0:T(8,128)(2,1)S(1)}, u32[]{:S(2)}, u32[]{:S(2)}) collective-permute-start(bf16[128,1024]{1,0:T(8,128)(2,1)S(1)} %bitcast.28), channel_id=1, source_target_pairs={{0,12},{4,0},{8,4},{12,8},{1,13},{5,1},{9,5},{13,9},{2,14},{6,2},{... | collective-permute-start | bytes 786440 | tf_op jit(solution)/shard_map/ppermute | solution.py:19
  59.8 14.6 %collective-permute-start.3 = (bf16[128,1024]{1,0:T(8,128)(2,1)S(1)}, bf16[128,1024]{1,0:T(8,128)(2,1)S(1)}, u32[]{:S(2)}, u32[]{:S(2)}) collective-permute-start(bf16[128,1024]{1,0:T(8,128)(2,1)S(1)} %bitcast.29), channel_id=1, source_target_pairs={{0,8},{4,12},{8,0},{12,4},{1,9},{5,13},{9,1},{13,5},{2,10},{6,14},... | collective-permute-start | bytes 786440 | tf_op jit(solution)/shard_map/ppermute | solution.py:19
  62.7 14.2 %collective-permute-start.4 = (bf16[128,1024]{1,0:T(8,128)(2,1)S(1)}, bf16[128,1024]{1,0:T(8,128)(2,1)S(1)}, u32[]{:S(2)}, u32[]{:S(2)}) collective-permute-start(bf16[128,1024]{1,0:T(8,128)(2,1)S(1)} %bitcast.30), channel_id=1, source_target_pairs={{0,4},{4,8},{8,12},{12,0},{1,5},{5,9},{9,13},{13,1},{2,6},{6,10},{... | collective-permute-start | bytes 786440 | tf_op jit(solution)/shard_map/ppermute | solution.py:19
  66.8 12.0 %collective-permute-start.5 = (bf16[128,1024]{1,0:T(8,128)(2,1)S(1)}, bf16[128,1024]{1,0:T(8,128)(2,1)S(1)}, u32[]{:S(2)}, u32[]{:S(2)}) collective-permute-start(bf16[128,1024]{1,0:T(8,128)(2,1)S(1)} %bitcast.31), channel_id=1, source_target_pairs={{0,1},{1,0},{2,3},{3,2},{4,5},{5,4},{6,7},{7,6},{8,9},{9,8},{10,11... | collective-permute-start | bytes 786440 | tf_op jit(solution)/shard_map/ppermute | solution.py:19
  72.5 6.3 %collective-permute-start.6 = (bf16[128,1024]{1,0:T(8,128)(2,1)S(1)}, bf16[128,1024]{1,0:T(8,128)(2,1)S(1)}, u32[]{:S(2)}, u32[]{:S(2)}) collective-permute-start(bf16[128,1024]{1,0:T(8,128)(2,1)S(1)} %collective-permute-done.2.refs_1_), channel_id=1, source_target_pairs={{0,1},{1,0},{2,3},{3,2},{4,5},{5,4},{6,7},{7,6},{8,9},{9,8},{10,11... | collective-permute-start | bytes 786440 | tf_op jit(solution)/shard_map/ppermute | solution.py:19
  74.4 4.4 %collective-permute-start.7 = (bf16[128,1024]{1,0:T(8,128)(2,1)S(1)}, bf16[128,1024]{1,0:T(8,128)(2,1)S(1)}, u32[]{:S(2)}, u32[]{:S(2)}) collective-permute-start(bf16[128,1024]{1,0:T(8,128)(2,1)S(1)} %collective-permute-done.3.refs_2_), channel_id=1, source_target_pairs={{0,1},{1,0},{2,3},{3,2},{4,5},{5,4},{6,7},{7,6},{8,9},{9,8},{10,11... | collective-permute-start | bytes 786440 | tf_op jit(solution)/shard_map/ppermute | solution.py:19
  76.8 3.4 %collective-permute-start.8 = (bf16[128,1024]{1,0:T(8,128)(2,1)S(1)}, bf16[128,1024]{1,0:T(8,128)(2,1)S(1)}, u32[]{:S(2)}, u32[]{:S(2)}) collective-permute-start(bf16[128,1024]{1,0:T(8,128)(2,1)S(1)} %collective-permute-done.4.refs_3_), channel_id=1, source_target_pairs={{0,1},{1,0},{2,3},{3,2},{4,5},{5,4},{6,7},{7,6},{8,9},{9,8},{10,11... | collective-permute-start | bytes 786440 | tf_op jit(solution)/shard_map/ppermute | solution.py:19
  90.2 20.1 %all-to-all-start.1 = ((bf16[4,256,512]{2,1,0:T(8,128)(2,1)}), bf16[4,256,512]{2,1,0:T(8,128)(2,1)}, u32[]{:S(2)}, u32[]{:S(2)}) async-start(bf16[4,256,512]{2,1,0:T(8,128)(2,1)} %shard_map.121), calls=%async_computation.1 | async-start | bytes 2097152 | tf_op jit(solution)/shard_map/all_to_all | solution.py:198
  94.9 111.2 %reduce-scatter.2.cloned.1.call-start = ((), (), s32[]{:S(2)}) async-start(), calls=%async_computation.7 | async-start | bytes 2064384 | tf_op jit(solution)/shard_map/reduce_scatter | solution.py:195
  112.5 33.7 %all-to-all-start.2 = ((bf16[8,32,512]{2,1,0:T(8,128)(2,1)}), bf16[8,32,512]{2,1,0:T(8,128)(2,1)}, u32[]{:S(2)}, u32[]{:S(2)}) async-start(bf16[8,32,512]{2,1,0:T(8,128)(2,1)} %bitcast.4), calls=%async_computation.2 | async-start | bytes 524288 | tf_op jit(solution)/shard_map/all_to_all | solution.py:205
  130.1 18.7 %collective-permute-start.10 = (bf16[4,128,1024]{2,1,0:T(8,128)(2,1)}, bf16[4,128,1024]{2,1,0:T(8,128)(2,1)S(1)}, u32[]{:S(2)}, u32[]{:S(2)}) collective-permute-start(bf16[4,128,1024]{2,1,0:T(8,128)(2,1)} %get-tuple-element.53), channel_id=1, source_target_pairs={{0,1},{1,0},{2,3},{3,2},{4,5},{5,4},{6,7},{7,6},{8,9},{9,8},{10,11... | collective-permute-start | bytes 3145736 | tf_op jit(solution)/shard_map/ppermute | solution.py:19
  151.0 26.3 %all-to-all-start.3 = ((bf16[8,32,512]{2,1,0:T(8,128)(2,1)}), bf16[8,32,512]{2,1,0:T(8,128)(2,1)S(1)}, u32[]{:S(2)}, u32[]{:S(2)}) async-start(bf16[8,32,512]{2,1,0:T(8,128)(2,1)} %broadcast_in_dim.2), calls=%async_computation.3 | async-start | bytes 524288 | tf_op jit(solution)/shard_map/all_to_all | solution.py:213
  156.1 15.4 %collective-permute-start.13 = (bf16[128,1024]{1,0:T(8,128)(2,1)S(1)}, bf16[128,1024]{1,0:T(8,128)(2,1)S(1)}, u32[]{:S(2)}, u32[]{:S(2)}) collective-permute-start(bf16[128,1024]{1,0:T(8,128)(2,1)S(1)} %get-tuple-element.61), channel_id=1, source_target_pairs={{0,12},{4,0},{8,4},{12,8},{1,13},{5,1},{9,5},{13,9},{2,14},{6,2},{... | collective-permute-start | bytes 786440 | tf_op jit(solution)/shard_map/ppermute | solution.py:19
  158.2 13.4 %collective-permute-start.12 = (bf16[128,1024]{1,0:T(8,128)(2,1)S(1)}, bf16[128,1024]{1,0:T(8,128)(2,1)S(1)}, u32[]{:S(2)}, u32[]{:S(2)}) collective-permute-start(bf16[128,1024]{1,0:T(8,128)(2,1)S(1)} %get-tuple-element.60), channel_id=1, source_target_pairs={{0,8},{4,12},{8,0},{12,4},{1,9},{5,13},{9,1},{13,5},{2,10},{6,14},... | collective-permute-start | bytes 786440 | tf_op jit(solution)/shard_map/ppermute | solution.py:19
  162.2 11.9 %collective-permute-start.11 = (bf16[128,1024]{1,0:T(8,128)(2,1)S(1)}, bf16[128,1024]{1,0:T(8,128)(2,1)S(1)}, u32[]{:S(2)}, u32[]{:S(2)}) collective-permute-start(bf16[128,1024]{1,0:T(8,128)(2,1)S(1)} %get-tuple-element.59), channel_id=1, source_target_pairs={{0,4},{4,8},{8,12},{12,0},{1,5},{5,9},{9,13},{13,1},{2,6},{6,10},{... | collective-permute-start | bytes 786440 | tf_op jit(solution)/shard_map/ppermute | solution.py:19
  177.4 31.3 %all-to-all-start.4 = ((bf16[16,8,1024]{2,1,0:T(8,128)(2,1)}), bf16[16,8,1024]{2,1,0:T(8,128)(2,1)S(1)}, u32[]{:S(2)}, u32[]{:S(2)}) async-start(bf16[16,8,1024]{2,1,0:T(8,128)(2,1)} %fusion.4), calls=%async_computation.4 | async-start | bytes 524288 | tf_op jit(solution)/shard_map/all_to_all | solution.py:228
  186.6 10.3 %collective-permute-start.14 = (bf16[256,512]{1,0:T(8,128)(2,1)S(1)}, bf16[256,512]{1,0:T(8,128)(2,1)S(1)}, u32[]{:S(2)}, u32[]{:S(2)}) collective-permute-start(bf16[256,512]{1,0:T(8,128)(2,1)S(1)} %bitcast.33), channel_id=1, source_target_pairs={{0,48},{16,0},{32,16},{48,32},{1,49},{17,1},{33,17},{49,33},{2,50}... | collective-permute-start | bytes 786440 | tf_op jit(solution)/shard_map/ppermute | solution.py:19
  189.5 11.9 %collective-permute-start.15 = (bf16[256,512]{1,0:T(8,128)(2,1)S(1)}, bf16[256,512]{1,0:T(8,128)(2,1)S(1)}, u32[]{:S(2)}, u32[]{:S(2)}) collective-permute-start(bf16[256,512]{1,0:T(8,128)(2,1)S(1)} %bitcast.34), channel_id=1, source_target_pairs={{0,32},{16,48},{32,0},{48,16},{1,33},{17,49},{33,1},{49,17},{2,34}... | collective-permute-start | bytes 786440 | tf_op jit(solution)/shard_map/ppermute | solution.py:19
  193.4 10.5 %collective-permute-start.16 = (bf16[256,512]{1,0:T(8,128)(2,1)S(1)}, bf16[256,512]{1,0:T(8,128)(2,1)S(1)}, u32[]{:S(2)}, u32[]{:S(2)}) collective-permute-start(bf16[256,512]{1,0:T(8,128)(2,1)S(1)} %bitcast.35), channel_id=1, source_target_pairs={{0,16},{16,32},{32,48},{48,0},{1,17},{17,33},{33,49},{49,1},{2,18}... | collective-permute-start | bytes 786440 | tf_op jit(solution)/shard_map/ppermute | solution.py:19
  (23 other events, 200.7 us)
Sparse Core Ops, SparseCore 0:
  11.6 66.0 all-gather.1
  101.4 75.0 reduce-scatter.1

commit v12 on v11

--- a/solution.py
+++ b/solution.py
@@ -217,6 +217,7 @@
     outer = outer.astype(bf16).reshape(NZ * NH, mine, cols)
     step, outer = lax.optimization_barrier((step, outer))
     steps = [step] + [shift(step, "x", NX, by) for by in range(1, NX)]
+    steps[1], grad_hidden = lax.optimization_barrier((steps[1], grad_hidden))
     (expansion,) = call(
         expand,
         5,

time: 219 us -> 217 us (level)
  waiting for transfers between devices: 66.9 us -> 64.5 us
    ppermute x17, waiting for transfers between devices: 41.1 us -> 38.5 us  [shift(): lax.ppermute(value, axis, [(i, (i - by) % size) for i in range(size)])]
where the time goes in v12:
time: 217 us; the launch traced here: 214 us
  starting transfers between devices  89.4 us (41%)
  waiting for transfers between devices  64.5 us (30%)
  Pallas kernels  20.8 us (10%)
  local copies, waits for them, and re-layouts  18 us (8%)
  between operations  14.4 us (7%)
  other arithmetic  7.18 us (3%)
    ppermute x17, starting transfers between devices, shift(): lax.ppermute(value, axis, [(i, (i - by) % size) for i in range(size)])  45.8 us
    ppermute x17, waiting for transfers between devices, shift(): lax.ppermute(value, axis, [(i, (i - by) % size) for i in range(size)])  38.5 us
    unnamed x46, local copies, waits for them, and re-layouts  17.2 us
    all_to_all x1, starting transfers between devices, body(): lax.all_to_all(pack, ('zl', 'zh'), 0, 0, tiled=True).reshape(rows, cols)  15.2 us
    all_to_all x1, waiting for transfers between devices, body(): lax.all_to_all(total, 'zl', 0, 0, tiled=True).reshape(NZ, slot, rank)  14.2 us
    all_to_all x1, starting transfers between devices, body(): lax.all_to_all(total, 'zl', 0, 0, tiled=True).reshape(NZ, slot, rank)  9.35 us
    all_to_all x1, starting transfers between devices, body(): outer = lax.all_to_all(outer, ('zl', 'zh'), 0, 0, tiled=True)  9.21 us
    all_to_all x1, waiting for transfers between devices, body(): total = lax.all_to_all(parts, 'x', 0, 0, tiled=True).astype(f32).sum(0)  9.11 us
  transfers between devices with their start and end apart: 24, of which 12 were waited for; matrix products, arithmetic and copies ran while one was open for 4% of the time, Pallas kernels for 7%

profile of v12, /device:TPU:24, one launch (start us, length us, event | category | flops | bytes accessed | tf_op | source)
XLA Modules:
  0.0 214.2 jit_solution(2146888396238899280)
XLA Ops:
  11.5 15.2 %all-to-all-start = ((bf16[16,8,1024]{2,1,0:T(8,128)(2,1)}), bf16[16,8,1024]{2,1,0:T(8,128)(2,1)S(1)}, u32[]{:S(2)}, u32[]{:S(2)}) async-start(bf16[16,8,1024]{2,1,0:T(8,128)(2,1)} %get-tuple-element.40), calls=%async_computation | async-start | bytes 524288 | tf_op jit(solution)/shard_map/all_to_all | solution.py:174
  29.3 4.7 %collective-permute-start = (bf16[1408,256]{1,0:T(8,128)(2,1)S(1)}, bf16[1408,256]{1,0:T(8,128)(2,1)S(1)}, u32[]{:S(2)}, u32[]{:S(2)}) collective-permute-start(bf16[1408,256]{1,0:T(8,128)(2,1)S(1)} %shard_map.119.refs_8_.b0), channel_id=1, source_target_pairs={{0,48},{16,0},{32,16},{48,32},{1,49},{17,1},{33,17},{49,33},{2,50}... | collective-permute-start | bytes 2162696 | tf_op jit(solution)/shard_map/ppermute | solution.py:19
  35.9 13.2 %collective-permute-done.refs_9_.b1 = bf16[1408,256]{1,0:T(8,128)(2,1)S(1)} collective-permute-done((bf16[1408,256]{1,0:T(8,128)(2,1)S(1)}, bf16[1408,256]{1,0:T(8,128)(2,1)S(1)}, u32[]{:S(2)}, u32[]{:S(2)}) %collective-permute-start) | collective-permute-done | bytes 720928 | tf_op jit(solution)/shard_map/ppermute | solution.py:19
  49.1 5.3 %collective-permute-done.1.refs_11_.b3 = bf16[1408,256]{1,0:T(8,128)(2,1)S(1)} collective-permute-done((bf16[1408,256]{1,0:T(8,128)(2,1)S(1)}, bf16[1408,256]{1,0:T(8,128)(2,1)S(1)}, u32[]{:S(2)}, u32[]{:S(2)}) %collective-permute-start.1) | collective-permute-done | bytes 720928 | tf_op jit(solution)/shard_map/ppermute | solution.py:19
  57.2 2.6 %collective-permute-start.2 = (bf16[128,1024]{1,0:T(8,128)(2,1)S(1)}, bf16[128,1024]{1,0:T(8,128)(2,1)S(1)}, u32[]{:S(2)}, u32[]{:S(2)}) collective-permute-start(bf16[128,1024]{1,0:T(8,128)(2,1)S(1)} %bitcast.28), channel_id=1, source_target_pairs={{0,12},{4,0},{8,4},{12,8},{1,13},{5,1},{9,5},{13,9},{2,14},{6,2},{... | collective-permute-start | bytes 786440 | tf_op jit(solution)/shard_map/ppermute | solution.py:19
  59.8 2.8 %collective-permute-start.3 = (bf16[128,1024]{1,0:T(8,128)(2,1)S(1)}, bf16[128,1024]{1,0:T(8,128)(2,1)S(1)}, u32[]{:S(2)}, u32[]{:S(2)}) collective-permute-start(bf16[128,1024]{1,0:T(8,128)(2,1)S(1)} %bitcast.29), channel_id=1, source_target_pairs={{0,8},{4,12},{8,0},{12,4},{1,9},{5,13},{9,1},{13,5},{2,10},{6,14},... | collective-permute-start | bytes 786440 | tf_op jit(solution)/shard_map/ppermute | solution.py:19
  62.7 4.1 %collective-permute-start.4 = (bf16[128,1024]{1,0:T(8,128)(2,1)S(1)}, bf16[128,1024]{1,0:T(8,128)(2,1)S(1)}, u32[]{:S(2)}, u32[]{:S(2)}) collective-permute-start(bf16[128,1024]{1,0:T(8,128)(2,1)S(1)} %bitcast.30), channel_id=1, source_target_pairs={{0,4},{4,8},{8,12},{12,0},{1,5},{5,9},{9,13},{13,1},{2,6},{6,10},{... | collective-permute-start | bytes 786440 | tf_op jit(solution)/shard_map/ppermute | solution.py:19
  68.7 3.8 %collective-permute-done.2.refs_1_ = bf16[128,1024]{1,0:T(8,128)(2,1)S(1)} collective-permute-done((bf16[128,1024]{1,0:T(8,128)(2,1)S(1)}, bf16[128,1024]{1,0:T(8,128)(2,1)S(1)}, u32[]{:S(2)}, u32[]{:S(2)}) %collective-permute-start.2) | collective-permute-done | bytes 262176 | tf_op jit(solution)/shard_map/ppermute | solution.py:19
  87.5 2.7 %shard_map.121 = bf16[4,256,512]{2,1,0:T(8,128)(2,1)} custom-call(s32[3]{0:T(128)S(1)} %pad_add_fusion.pos, bf16[1024,896]{1,0:T(8,128)(2,1)S(1)} %copy-done, bf16[1024,512]{1,0:T(8,128)(2,1)S(1)} %get-tuple-element.49.reduced), custom_call_target="tpu_custom_call" | custom-call | flops 1000000000 | bytes 4194304 | tf_op jit(solution)/shard_map/pallas_call | solution.py:188
  90.2 4.6 %all-to-all-start.1 = ((bf16[4,256,512]{2,1,0:T(8,128)(2,1)}), bf16[4,256,512]{2,1,0:T(8,128)(2,1)}, u32[]{:S(2)}, u32[]{:S(2)}) async-start(bf16[4,256,512]{2,1,0:T(8,128)(2,1)} %shard_map.121), calls=%async_computation.1 | async-start | bytes 2097152 | tf_op jit(solution)/shard_map/all_to_all | solution.py:198
  96.5 4.8 %shard_map.122 = bf16[1024,896]{1,0:T(8,128)(2,1)} custom-call(s32[3]{0:T(128)S(1)} %pad_add_fusion.pos, bf16[1024,1024]{1,0:T(8,128)(2,1)S(1)} %copy-done.22, bf16[1408,256]{1,0:T(8,128)(2,1)S(1)} %shard_map.119.refs_8_.b0, bf16[1408,256]{1,0:T(8,128)(2,1)S(1)} %collective-permute-done.refs_9_.b1, bf16[1408,256]{1,0:T(8,128)(2,1)S(1)} %copy-done.13, ...), custom_call_target="tpu_custom_call" | custom-call | flops 2000000000 | bytes 4194304 | tf_op jit(solution)/shard_map/pallas_call | solution.py:192
  101.3 9.1 %all-to-all-done.1 = bf16[4,256,512]{2,1,0:T(8,128)(2,1)} async-done(((bf16[4,256,512]{2,1,0:T(8,128)(2,1)}), bf16[4,256,512]{2,1,0:T(8,128)(2,1)}, u32[]{:S(2)}, u32[]{:S(2)}) %all-to-all-start.1) | async-done | bytes 1048608 | tf_op jit(solution)/shard_map/all_to_all | solution.py:198
  112.5 9.3 %all-to-all-start.2 = ((bf16[8,32,512]{2,1,0:T(8,128)(2,1)}), bf16[8,32,512]{2,1,0:T(8,128)(2,1)}, u32[]{:S(2)}, u32[]{:S(2)}) async-start(bf16[8,32,512]{2,1,0:T(8,128)(2,1)} %bitcast.4), calls=%async_computation.2 | async-start | bytes 524288 | tf_op jit(solution)/shard_map/all_to_all | solution.py:205
  124.1 3.9 %shard_map.123 = (bf16[128,1024]{1,0:T(8,128)(2,1)S(1)}, bf16[128,1024]{1,0:T(8,128)(2,1)S(1)}, bf16[128,1024]{1,0:T(8,128)(2,1)S(1)}, bf16[128,1024]{1,0:T(8,128)(2,1)S(1)}, bf16[4,128,1024]{2,1,0:T(8,128)(2,1)}) custom-call(s32[3]{0:T(128)S(1)} %pad_add_fusion.pos, bf16[1024,896]{1,0:T(8,128)(2,1)S(1)} %copy-done.1, ...), custom_call_target="tpu_custom_call" | custom-call | flops 2000000000 | bytes 4194304 | tf_op jit(solution)/shard_map/pallas_call | solution.py:200
  132.0 14.2 %all-to-all-done.2 = bf16[8,32,512]{2,1,0:T(8,128)(2,1)} async-done(((bf16[8,32,512]{2,1,0:T(8,128)(2,1)}), bf16[8,32,512]{2,1,0:T(8,128)(2,1)}, u32[]{:S(2)}, u32[]{:S(2)}) %all-to-all-start.2) | async-done | bytes 262176 | tf_op jit(solution)/shard_map/all_to_all | solution.py:205
  151.1 5.1 %all-to-all-start.3 = ((bf16[8,32,512]{2,1,0:T(8,128)(2,1)}), bf16[8,32,512]{2,1,0:T(8,128)(2,1)S(1)}, u32[]{:S(2)}, u32[]{:S(2)}) async-start(bf16[8,32,512]{2,1,0:T(8,128)(2,1)} %broadcast_in_dim.2), calls=%async_computation.3 | async-start | bytes 524288 | tf_op jit(solution)/shard_map/all_to_all | solution.py:213
  158.1 4.0 %collective-permute-start.12 = (bf16[128,1024]{1,0:T(8,128)(2,1)S(1)}, bf16[128,1024]{1,0:T(8,128)(2,1)S(1)}, u32[]{:S(2)}, u32[]{:S(2)}) collective-permute-start(bf16[128,1024]{1,0:T(8,128)(2,1)S(1)} %get-tuple-element.62), channel_id=1, source_target_pairs={{0,8},{4,12},{8,0},{12,4},{1,9},{5,13},{9,1},{13,5},{2,10},{6,14},... | collective-permute-start | bytes 786440 | tf_op jit(solution)/shard_map/ppermute | solution.py:19
  162.0 3.1 %collective-permute-start.11 = (bf16[128,1024]{1,0:T(8,128)(2,1)S(1)}, bf16[128,1024]{1,0:T(8,128)(2,1)S(1)}, u32[]{:S(2)}, u32[]{:S(2)}) collective-permute-start(bf16[128,1024]{1,0:T(8,128)(2,1)S(1)} %get-tuple-element.61), channel_id=1, source_target_pairs={{0,4},{4,8},{8,12},{12,0},{1,5},{5,9},{9,13},{13,1},{2,6},{6,10},{... | collective-permute-start | bytes 786440 | tf_op jit(solution)/shard_map/ppermute | solution.py:19
  165.1 6.3 %collective-permute-done.13 = bf16[128,1024]{1,0:T(8,128)(2,1)S(1)} collective-permute-done((bf16[128,1024]{1,0:T(8,128)(2,1)S(1)}, bf16[128,1024]{1,0:T(8,128)(2,1)S(1)}, u32[]{:S(2)}, u32[]{:S(2)}) %collective-permute-start.13) | collective-permute-done | bytes 262176 | tf_op jit(solution)/shard_map/ppermute | solution.py:19
  171.5 2.5 %collective-permute-done.11 = bf16[128,1024]{1,0:T(8,128)(2,1)S(1)} collective-permute-done((bf16[128,1024]{1,0:T(8,128)(2,1)S(1)}, bf16[128,1024]{1,0:T(8,128)(2,1)S(1)}, u32[]{:S(2)}, u32[]{:S(2)}) %collective-permute-start.11) | collective-permute-done | bytes 262176 | tf_op jit(solution)/shard_map/ppermute | solution.py:19
  174.8 2.5 %all-to-all-done.3 = bf16[8,32,512]{2,1,0:T(8,128)(2,1)S(1)} async-done(((bf16[8,32,512]{2,1,0:T(8,128)(2,1)}), bf16[8,32,512]{2,1,0:T(8,128)(2,1)S(1)}, u32[]{:S(2)}, u32[]{:S(2)}) %all-to-all-start.3) | async-done | bytes 262176 | tf_op jit(solution)/shard_map/all_to_all | solution.py:213
  177.4 9.2 %all-to-all-start.4 = ((bf16[16,8,1024]{2,1,0:T(8,128)(2,1)}), bf16[16,8,1024]{2,1,0:T(8,128)(2,1)S(1)}, u32[]{:S(2)}, u32[]{:S(2)}) async-start(bf16[16,8,1024]{2,1,0:T(8,128)(2,1)} %fusion.4), calls=%async_computation.4 | async-start | bytes 524288 | tf_op jit(solution)/shard_map/all_to_all | solution.py:229
  186.6 3.0 %collective-permute-start.14 = (bf16[256,512]{1,0:T(8,128)(2,1)S(1)}, bf16[256,512]{1,0:T(8,128)(2,1)S(1)}, u32[]{:S(2)}, u32[]{:S(2)}) collective-permute-start(bf16[256,512]{1,0:T(8,128)(2,1)S(1)} %bitcast.33), channel_id=1, source_target_pairs={{0,48},{16,0},{32,16},{48,32},{1,49},{17,1},{33,17},{49,33},{2,50}... | collective-permute-start | bytes 786440 | tf_op jit(solution)/shard_map/ppermute | solution.py:19
  189.6 3.8 %collective-permute-start.15 = (bf16[256,512]{1,0:T(8,128)(2,1)S(1)}, bf16[256,512]{1,0:T(8,128)(2,1)S(1)}, u32[]{:S(2)}, u32[]{:S(2)}) collective-permute-start(bf16[256,512]{1,0:T(8,128)(2,1)S(1)} %bitcast.34), channel_id=1, source_target_pairs={{0,32},{16,48},{32,0},{48,16},{1,33},{17,49},{33,1},{49,17},{2,34}... | collective-permute-start | bytes 786440 | tf_op jit(solution)/shard_map/ppermute | solution.py:19
  (89 shorter events, 59.9 us)
Async XLA Ops:
  7.2 78.9 %all-gather.2.cloned.1.call-start = ((), (), s32[]{:S(2)}) async-start(), calls=%async_computation.6 | async-start | bytes 2064384 | tf_op jit(solution)/shard_map/all_gather | solution.py:173
  11.5 43.7 %all-to-all-start = ((bf16[16,8,1024]{2,1,0:T(8,128)(2,1)}), bf16[16,8,1024]{2,1,0:T(8,128)(2,1)S(1)}, u32[]{:S(2)}, u32[]{:S(2)}) async-start(bf16[16,8,1024]{2,1,0:T(8,128)(2,1)} %get-tuple-element.40), calls=%async_computation | async-start | bytes 524288 | tf_op jit(solution)/shard_map/all_to_all | solution.py:174
  29.3 19.8 %collective-permute-start = (bf16[1408,256]{1,0:T(8,128)(2,1)S(1)}, bf16[1408,256]{1,0:T(8,128)(2,1)S(1)}, u32[]{:S(2)}, u32[]{:S(2)}) collective-permute-start(bf16[1408,256]{1,0:T(8,128)(2,1)S(1)} %shard_map.119.refs_8_.b0), channel_id=1, source_target_pairs={{0,48},{16,0},{32,16},{48,32},{1,49},{17,1},{33,17},{49,33},{2,50}... | collective-permute-start | bytes 2162696 | tf_op jit(solution)/shard_map/ppermute | solution.py:19
  34.0 20.4 %collective-permute-start.1 = (bf16[1408,256]{1,0:T(8,128)(2,1)S(1)}, bf16[1408,256]{1,0:T(8,128)(2,1)S(1)}, u32[]{:S(2)}, u32[]{:S(2)}) collective-permute-start(bf16[1408,256]{1,0:T(8,128)(2,1)S(1)} %shard_map.119.refs_8_.b0), channel_id=1, source_target_pairs={{0,16},{16,32},{32,48},{48,0},{1,17},{17,33},{33,49},{49,1},{2,18}... | collective-permute-start | bytes 2162696 | tf_op jit(solution)/shard_map/ppermute | solution.py:19
  55.2 25.0 %collective-permute-start.9 = (bf16[1408,256]{1,0:T(8,128)(2,1)S(1)}, bf16[1408,256]{1,0:T(8,128)(2,1)S(1)}, u32[]{:S(2)}, u32[]{:S(2)}) collective-permute-start(bf16[1408,256]{1,0:T(8,128)(2,1)S(1)} %shard_map.119.refs_8_.b0), channel_id=1, source_target_pairs={{0,32},{16,48},{32,0},{48,16},{1,33},{17,49},{33,1},{49,17},{2,34}... | collective-permute-start | bytes 2162696 | tf_op jit(solution)/shard_map/ppermute | solution.py:19
  57.2 15.3 %collective-permute-start.2 = (bf16[128,1024]{1,0:T(8,128)(2,1)S(1)}, bf16[128,1024]{1,0:T(8,128)(2,1)S(1)}, u32[]{:S(2)}, u32[]{:S(2)}) collective-permute-start(bf16[128,1024]{1,0:T(8,128)(2,1)S(1)} %bitcast.28), channel_id=1, source_target_pairs={{0,12},{4,0},{8,4},{12,8},{1,13},{5,1},{9,5},{13,9},{2,14},{6,2},{... | collective-permute-start | bytes 786440 | tf_op jit(solution)/shard_map/ppermute | solution.py:19
  59.8 14.6 %collective-permute-start.3 = (bf16[128,1024]{1,0:T(8,128)(2,1)S(1)}, bf16[128,1024]{1,0:T(8,128)(2,1)S(1)}, u32[]{:S(2)}, u32[]{:S(2)}) collective-permute-start(bf16[128,1024]{1,0:T(8,128)(2,1)S(1)} %bitcast.29), channel_id=1, source_target_pairs={{0,8},{4,12},{8,0},{12,4},{1,9},{5,13},{9,1},{13,5},{2,10},{6,14},... | collective-permute-start | bytes 786440 | tf_op jit(solution)/shard_map/ppermute | solution.py:19
  62.7 14.2 %collective-permute-start.4 = (bf16[128,1024]{1,0:T(8,128)(2,1)S(1)}, bf16[128,1024]{1,0:T(8,128)(2,1)S(1)}, u32[]{:S(2)}, u32[]{:S(2)}) collective-permute-start(bf16[128,1024]{1,0:T(8,128)(2,1)S(1)} %bitcast.30), channel_id=1, source_target_pairs={{0,4},{4,8},{8,12},{12,0},{1,5},{5,9},{9,13},{13,1},{2,6},{6,10},{... | collective-permute-start | bytes 786440 | tf_op jit(solution)/shard_map/ppermute | solution.py:19
  66.8 12.0 %collective-permute-start.5 = (bf16[128,1024]{1,0:T(8,128)(2,1)S(1)}, bf16[128,1024]{1,0:T(8,128)(2,1)S(1)}, u32[]{:S(2)}, u32[]{:S(2)}) collective-permute-start(bf16[128,1024]{1,0:T(8,128)(2,1)S(1)} %bitcast.31), channel_id=1, source_target_pairs={{0,1},{1,0},{2,3},{3,2},{4,5},{5,4},{6,7},{7,6},{8,9},{9,8},{10,11... | collective-permute-start | bytes 786440 | tf_op jit(solution)/shard_map/ppermute | solution.py:19
  72.5 6.3 %collective-permute-start.6 = (bf16[128,1024]{1,0:T(8,128)(2,1)S(1)}, bf16[128,1024]{1,0:T(8,128)(2,1)S(1)}, u32[]{:S(2)}, u32[]{:S(2)}) collective-permute-start(bf16[128,1024]{1,0:T(8,128)(2,1)S(1)} %collective-permute-done.2.refs_1_), channel_id=1, source_target_pairs={{0,1},{1,0},{2,3},{3,2},{4,5},{5,4},{6,7},{7,6},{8,9},{9,8},{10,11... | collective-permute-start | bytes 786440 | tf_op jit(solution)/shard_map/ppermute | solution.py:19
  74.4 4.4 %collective-permute-start.7 = (bf16[128,1024]{1,0:T(8,128)(2,1)S(1)}, bf16[128,1024]{1,0:T(8,128)(2,1)S(1)}, u32[]{:S(2)}, u32[]{:S(2)}) collective-permute-start(bf16[128,1024]{1,0:T(8,128)(2,1)S(1)} %collective-permute-done.3.refs_2_), channel_id=1, source_target_pairs={{0,1},{1,0},{2,3},{3,2},{4,5},{5,4},{6,7},{7,6},{8,9},{9,8},{10,11... | collective-permute-start | bytes 786440 | tf_op jit(solution)/shard_map/ppermute | solution.py:19
  76.8 3.4 %collective-permute-start.8 = (bf16[128,1024]{1,0:T(8,128)(2,1)S(1)}, bf16[128,1024]{1,0:T(8,128)(2,1)S(1)}, u32[]{:S(2)}, u32[]{:S(2)}) collective-permute-start(bf16[128,1024]{1,0:T(8,128)(2,1)S(1)} %collective-permute-done.4.refs_3_), channel_id=1, source_target_pairs={{0,1},{1,0},{2,3},{3,2},{4,5},{5,4},{6,7},{7,6},{8,9},{9,8},{10,11... | collective-permute-start | bytes 786440 | tf_op jit(solution)/shard_map/ppermute | solution.py:19
  90.2 20.1 %all-to-all-start.1 = ((bf16[4,256,512]{2,1,0:T(8,128)(2,1)}), bf16[4,256,512]{2,1,0:T(8,128)(2,1)}, u32[]{:S(2)}, u32[]{:S(2)}) async-start(bf16[4,256,512]{2,1,0:T(8,128)(2,1)} %shard_map.121), calls=%async_computation.1 | async-start | bytes 2097152 | tf_op jit(solution)/shard_map/all_to_all | solution.py:198
  94.9 102.0 %reduce-scatter.2.cloned.1.call-start = ((), (), s32[]{:S(2)}) async-start(), calls=%async_computation.7 | async-start | bytes 2064384 | tf_op jit(solution)/shard_map/reduce_scatter | solution.py:195
  112.5 33.7 %all-to-all-start.2 = ((bf16[8,32,512]{2,1,0:T(8,128)(2,1)}), bf16[8,32,512]{2,1,0:T(8,128)(2,1)}, u32[]{:S(2)}, u32[]{:S(2)}) async-start(bf16[8,32,512]{2,1,0:T(8,128)(2,1)} %bitcast.4), calls=%async_computation.2 | async-start | bytes 524288 | tf_op jit(solution)/shard_map/all_to_all | solution.py:205
  130.1 18.7 %collective-permute-start.10 = (bf16[4,128,1024]{2,1,0:T(8,128)(2,1)}, bf16[4,128,1024]{2,1,0:T(8,128)(2,1)S(1)}, u32[]{:S(2)}, u32[]{:S(2)}) collective-permute-start(bf16[4,128,1024]{2,1,0:T(8,128)(2,1)} %get-tuple-element.55), channel_id=1, source_target_pairs={{0,1},{1,0},{2,3},{3,2},{4,5},{5,4},{6,7},{7,6},{8,9},{9,8},{10,11... | collective-permute-start | bytes 3145736 | tf_op jit(solution)/shard_map/ppermute | solution.py:19
  151.1 26.3 %all-to-all-start.3 = ((bf16[8,32,512]{2,1,0:T(8,128)(2,1)}), bf16[8,32,512]{2,1,0:T(8,128)(2,1)S(1)}, u32[]{:S(2)}, u32[]{:S(2)}) async-start(bf16[8,32,512]{2,1,0:T(8,128)(2,1)} %broadcast_in_dim.2), calls=%async_computation.3 | async-start | bytes 524288 | tf_op jit(solution)/shard_map/all_to_all | solution.py:213
  156.2 15.3 %collective-permute-start.13 = (bf16[128,1024]{1,0:T(8,128)(2,1)S(1)}, bf16[128,1024]{1,0:T(8,128)(2,1)S(1)}, u32[]{:S(2)}, u32[]{:S(2)}) collective-permute-start(bf16[128,1024]{1,0:T(8,128)(2,1)S(1)} %get-tuple-element.63), channel_id=1, source_target_pairs={{0,12},{4,0},{8,4},{12,8},{1,13},{5,1},{9,5},{13,9},{2,14},{6,2},{... | collective-permute-start | bytes 786440 | tf_op jit(solution)/shard_map/ppermute | solution.py:19
  158.1 13.4 %collective-permute-start.12 = (bf16[128,1024]{1,0:T(8,128)(2,1)S(1)}, bf16[128,1024]{1,0:T(8,128)(2,1)S(1)}, u32[]{:S(2)}, u32[]{:S(2)}) collective-permute-start(bf16[128,1024]{1,0:T(8,128)(2,1)S(1)} %get-tuple-element.62), channel_id=1, source_target_pairs={{0,8},{4,12},{8,0},{12,4},{1,9},{5,13},{9,1},{13,5},{2,10},{6,14},... | collective-permute-start | bytes 786440 | tf_op jit(solution)/shard_map/ppermute | solution.py:19
  162.0 11.9 %collective-permute-start.11 = (bf16[128,1024]{1,0:T(8,128)(2,1)S(1)}, bf16[128,1024]{1,0:T(8,128)(2,1)S(1)}, u32[]{:S(2)}, u32[]{:S(2)}) collective-permute-start(bf16[128,1024]{1,0:T(8,128)(2,1)S(1)} %get-tuple-element.61), channel_id=1, source_target_pairs={{0,4},{4,8},{8,12},{12,0},{1,5},{5,9},{9,13},{13,1},{2,6},{6,10},{... | collective-permute-start | bytes 786440 | tf_op jit(solution)/shard_map/ppermute | solution.py:19
  177.4 28.7 %all-to-all-start.4 = ((bf16[16,8,1024]{2,1,0:T(8,128)(2,1)}), bf16[16,8,1024]{2,1,0:T(8,128)(2,1)S(1)}, u32[]{:S(2)}, u32[]{:S(2)}) async-start(bf16[16,8,1024]{2,1,0:T(8,128)(2,1)} %fusion.4), calls=%async_computation.4 | async-start | bytes 524288 | tf_op jit(solution)/shard_map/all_to_all | solution.py:229
  186.6 10.3 %collective-permute-start.14 = (bf16[256,512]{1,0:T(8,128)(2,1)S(1)}, bf16[256,512]{1,0:T(8,128)(2,1)S(1)}, u32[]{:S(2)}, u32[]{:S(2)}) collective-permute-start(bf16[256,512]{1,0:T(8,128)(2,1)S(1)} %bitcast.33), channel_id=1, source_target_pairs={{0,48},{16,0},{32,16},{48,32},{1,49},{17,1},{33,17},{49,33},{2,50}... | collective-permute-start | bytes 786440 | tf_op jit(solution)/shard_map/ppermute | solution.py:19
  189.6 11.9 %collective-permute-start.15 = (bf16[256,512]{1,0:T(8,128)(2,1)S(1)}, bf16[256,512]{1,0:T(8,128)(2,1)S(1)}, u32[]{:S(2)}, u32[]{:S(2)}) collective-permute-start(bf16[256,512]{1,0:T(8,128)(2,1)S(1)} %bitcast.34), channel_id=1, source_target_pairs={{0,32},{16,48},{32,0},{48,16},{1,33},{17,49},{33,1},{49,17},{2,34}... | collective-permute-start | bytes 786440 | tf_op jit(solution)/shard_map/ppermute | solution.py:19
  193.4 10.5 %collective-permute-start.16 = (bf16[256,512]{1,0:T(8,128)(2,1)S(1)}, bf16[256,512]{1,0:T(8,128)(2,1)S(1)}, u32[]{:S(2)}, u32[]{:S(2)}) collective-permute-start(bf16[256,512]{1,0:T(8,128)(2,1)S(1)} %bitcast.35), channel_id=1, source_target_pairs={{0,16},{16,32},{32,48},{48,0},{1,17},{17,33},{33,49},{49,1},{2,18}... | collective-permute-start | bytes 786440 | tf_op jit(solution)/shard_map/ppermute | solution.py:19
  (23 other events, 193.9 us)
Sparse Core Ops, SparseCore 0:
  11.6 66.0 all-gather.1
  101.4 75.0 reduce-scatter.1
